TPU v7x, 128 devices: a whole 4x4x4 slice. The times are simulated.
128 devices in a mesh: gx: 8 (over y, core), gy: 8 (over z, x_hi), gz: 2 (over x_lo).
Axes of the slice: x: 4 (x_hi: 2, x_lo: 2; x = x_hi * 2 + x_lo), y: 4, z: 4, core: 2. Of those that a mesh axis runs over, the one named last changes fastest.
Arguments:
- mode_fields: float32 [2, 3, 64, 256, 512], P(None, None, 'gx', 'gy', 'gz'), may hold values from -6 to 6
- design: float32 [64, 256, 512], P('gx', 'gy', 'gz'), may hold values from 0.05 to 1
- solid_mask: int32 [64, 256, 512], P('gx', 'gy', 'gz'), may hold values 0 or 1
- eigenvalues: float32 [6], replicated, may hold values from 0.5 to 5
- mode_order: int32 [6], replicated, may hold values from 0 to 5, each once
Outputs:
- sensitivity: float32 [2, 64, 256, 512], P(None, 'gx', 'gy', 'gz')
Inputs may be any that keep to these rules, and one draw needn't show every extreme that they name: `mode_order`: each of 0 to 5 appears once.
All inputs are finite; a program needn't handle non-finite values. No bound on the sum of `solid_mask` on one device may be relied on, other than what follows from the above.
Results may differ from a plain program's by a relative error of at most 0.0003.
Values sent between devices are 32-bit elements; how exact they have to be, the bound alone decides.
No kernel may reach another device: no remote copies, remote signals or barrier semaphores. Data moves between devices by JAX's collectives and lax.ppermute only.
A program may use at most 128 MiB of HBM per device.

v0:
```python
import jax
import jax.numpy as jnp
import numpy as np
from jax import lax
from jax.sharding import PartitionSpec as P

ITERS = 4


poisson = 0.3
radius_sq = 3.0
stiff_floor = 0.001


def padded_2(x, sides, width):
    for axis, dim in sides:
        peers, length = (lax.axis_size(axis), x.shape[dim])
        up = [(i, (i + 1) % peers) for i in range(peers - 1)]
        down = [(j, i) for i, j in up]
        last = lax.slice_in_dim(x, length - width, length, axis=dim)
        first = lax.slice_in_dim(x, 0, width, axis=dim)
        before = lax.ppermute(last, axis, up)
        after = lax.ppermute(first, axis, down)
        x = jnp.concatenate([before, x, after], axis=dim)
    return x


def from_behind(block, axis, distance):
    devices = range(lax.axis_size(axis))
    route = [(i - distance, i) for i in devices if i - distance in devices]
    return lax.ppermute(block, axis, route)


def hex_stiffness():
    lame_first = poisson / ((1.0 + poisson) * (1.0 - 2.0 * poisson))
    shear = 0.5 / (1.0 + poisson)
    elastic = np.zeros((6, 6))
    elastic[:3, :3] = lame_first
    for row in range(3):
        elastic[row, row] = lame_first + 2.0 * shear
        elastic[row + 3, row + 3] = shear
    points = [0.5 - 0.5 / np.sqrt(3.0), 0.5 + 0.5 / np.sqrt(3.0)]
    stiffness = np.zeros((24, 24))
    for point_x in points:
        for point_y in points:
            for point_z in points:
                coords = (point_x, point_y, point_z)
                grads = np.zeros((3, 8))
                for corner in range(8):
                    bits = (corner >> 2 & 1, corner >> 1 & 1, corner & 1)
                    for direction in range(3):
                        value = 1.0
                        for other in range(3):
                            if other == direction:
                                value *= 1.0 if bits[other] else -1.0
                            else:
                                value *= coords[other] if bits[other] else 1.0 - coords[other]
                        grads[direction, corner] = value
                strain = np.zeros((6, 24))
                strain[0, 0:8] = grads[0]
                strain[1, 8:16] = grads[1]
                strain[2, 16:24] = grads[2]
                strain[3, 0:8] = grads[1]
                strain[3, 8:16] = grads[0]
                strain[4, 8:16] = grads[2]
                strain[4, 16:24] = grads[1]
                strain[5, 0:8] = grads[2]
                strain[5, 16:24] = grads[0]
                stiffness += 0.125 * strain.T @ elastic @ strain
    return stiffness.astype(np.float32)


def neighbour_total(padded):
    total = padded[..., 2:, 1:-1, 1:-1] + padded[..., :-2, 1:-1, 1:-1]
    total = total + padded[..., 1:-1, 2:, 1:-1] + padded[..., 1:-1, :-2, 1:-1]
    return total + padded[..., 1:-1, 1:-1, 2:] + padded[..., 1:-1, 1:-1, :-2]


def local_scale(local_shape, margin):
    extents = (
        (lax.axis_size("gx"), lax.axis_index("gx")),
        (lax.axis_size("gy"), lax.axis_index("gy")),
        (lax.axis_size("gz"), lax.axis_index("gz")),
    )
    shape = tuple((length + 2 * margin for length in local_shape))
    counts = jnp.full(shape, 6.0, jnp.float32)
    inside = jnp.ones(shape, jnp.float32)
    for axis_pos in range(3):
        length = local_shape[axis_pos]
        devices, position = extents[axis_pos]
        whole = length * devices
        place = lax.broadcasted_iota(jnp.int32, shape, axis_pos) + position * length - margin
        counts = (
            counts - (place == 0).astype(jnp.float32) - (place == whole - 1).astype(jnp.float32)
        )
        inside = inside * ((place >= 0) & (place < whole)).astype(jnp.float32)
    return inside / (1.0 + radius_sq * counts)


def local(mode_fields, design, solid_mask, eigenvalues, mode_order):
    modes, comps, cells_x, cells_y, cells_z = mode_fields.shape
    mask = solid_mask.astype(jnp.float32)
    local_shape = (cells_x, cells_y, cells_z)
    source = mask * design
    scale = local_scale(local_shape, 0)
    physical = source * scale
    for step in range(ITERS):
        padded = padded_2(physical, (("gx", 0), ("gy", 1), ("gz", 2)), 1)
        physical = (source + radius_sq * neighbour_total(padded)) * scale
    extended = jnp.concatenate([mode_fields, from_behind(mode_fields[:, :, 0:1], "gx", -1)], axis=2)
    extended = jnp.concatenate([extended, from_behind(extended[:, :, :, 0:1], "gy", -1)], axis=3)
    extended = jnp.concatenate([extended, from_behind(extended[:, :, :, :, 0:1], "gz", -1)], axis=4)
    stiffness = jnp.asarray(hex_stiffness(), dtype=jnp.float32)
    selector = (
        mode_order[:modes, None] == jnp.arange(eigenvalues.shape[0], dtype=jnp.int32)[None, :]
    ).astype(jnp.float32)
    chosen = jnp.sum(selector * eigenvalues[None, :], axis=1)
    stiff_factor = 3.0 * (1.0 - stiff_floor) * physical * physical
    raw_list = []
    for mode in range(modes):
        corners = []
        for corner in range(8):
            off_x, off_y, off_z = (corner >> 2 & 1, corner >> 1 & 1, corner & 1)
            corners.append(
                extended[
                    mode,
                    :,
                    off_x : off_x + cells_x,
                    off_y : off_y + cells_y,
                    off_z : off_z + cells_z,
                ]
            )
        element = jnp.stack(corners, axis=1).reshape(24, cells_x * cells_y * cells_z)
        kinetic = jnp.dot(
            stiffness, element, precision=lax.Precision.HIGHEST, preferred_element_type=jnp.float32
        )
        energy_k = jnp.sum(element * kinetic, axis=0).reshape(local_shape)
        energy_m = (0.125 * jnp.sum(element * element, axis=0)).reshape(local_shape)
        raw_list.append(stiff_factor * energy_k - chosen[mode] * energy_m)
    raw = jnp.stack(raw_list, axis=0)
    filtered = raw * scale[None]
    for step in range(ITERS):
        padded = padded_2(filtered, (("gx", 1), ("gy", 2), ("gz", 3)), 1)
        filtered = (raw + radius_sq * neighbour_total(padded)) * scale[None]
    return mask[None] * filtered


def solution(mesh):
    return jax.shard_map(
        local,
        mesh=mesh,
        in_specs=(
            P(None, None, "gx", "gy", "gz"),
            P("gx", "gy", "gz"),
            P("gx", "gy", "gz"),
            P(),
            P(),
        ),
        out_specs=P(None, "gx", "gy", "gz"),
        check_vma=False,
    )
```

profile of v0, /device:TPU:0, one launch (start us, length us, event | category | flops | bytes accessed | tf_op | source)
XLA Modules:
  0.0 534.0 jit_solution(4449713004272622416)
XLA Ops:
  14.1 4.9 collective-permute-start.3
  20.4 5.7 %collective-permute-done.2 = f32[10,1,256]{2,1,0:T(1,128)S(1)} collective-permute-done((f32[10,1,256]{2,1,0:T(1,128)S(1)}, f32[10,1,256]{2,1,0:T(1,128)S(1)}, u32[]{:S(2)}, u32[]{:S(2)}) %collective-permute-start.2) | collective-permute-done | bytes 10272 | tf_op jit(solution)/shard_map/ppermute | solution.py:23
  28.3 5.9 %collective-permute-start.5 = (f32[10,34,1]{2,1,0:T(8,128)}, f32[10,34,1]{2,1,0:T(8,128)}, u32[]{:S(2)}, u32[]{:S(2)}) collective-permute-start(f32[10,34,1]{2,1,0:T(8,128)} %get-tuple-element.72), channel_id=1, source_target_pairs={{0,1},{2,3},{4,5},{6,7},{8,9},{10,11},{12,13},{14,15},{16,17},{18,... | collective-permute-start | bytes 4088 | tf_op jit(solution)/shard_map/ppermute | solution.py:22
  72.5 5.2 collective-permute-start.11
  98.0 5.7 %collective-permute-start.15 = (f32[10,1,256]{2,1,0:T(1,128)S(1)}, f32[10,1,256]{2,1,0:T(1,128)S(1)}, u32[]{:S(2)}, u32[]{:S(2)}) collective-permute-start(f32[10,1,256]{2,1,0:T(1,128)S(1)} %get-tuple-element.87), channel_id=1, source_target_pairs={{0,2},{2,4},{4,6},{6,8},{8,10},{10,12},{12,14},{1,3},{3,5},{5,7},{... | collective-permute-start | bytes 30728 | tf_op jit(solution)/shard_map/ppermute | solution.py:22
  112.9 5.9 %collective-permute-start.17 = (f32[10,34,1]{2,1,0:T(8,128)}, f32[10,34,1]{2,1,0:T(8,128)}, u32[]{:S(2)}, u32[]{:S(2)}) collective-permute-start(f32[10,34,1]{2,1,0:T(8,128)} %get-tuple-element.68), channel_id=1, source_target_pairs={{0,1},{2,3},{4,5},{6,7},{8,9},{10,11},{12,13},{14,15},{16,17},{18,... | collective-permute-start | bytes 4088 | tf_op jit(solution)/shard_map/ppermute | solution.py:22
  143.6 6.4 %collective-permute-start.21 = (f32[10,1,256]{2,1,0:T(1,128)S(1)}, f32[10,1,256]{2,1,0:T(1,128)S(1)}, u32[]{:S(2)}, u32[]{:S(2)}) collective-permute-start(f32[10,1,256]{2,1,0:T(1,128)S(1)} %get-tuple-element.85), channel_id=1, source_target_pairs={{0,2},{2,4},{4,6},{6,8},{8,10},{10,12},{12,14},{1,3},{3,5},{5,7},{... | collective-permute-start | bytes 30728 | tf_op jit(solution)/shard_map/ppermute | solution.py:22
  158.6 5.2 collective-permute-start.23
  166.9 11.3 %collective-permute-start.25 = (f32[2,3,9,1,256]{4,0,3,2,1:T(2,128)}, f32[2,3,9,1,256]{4,0,3,2,1:T(2,128)}, u32[]{:S(2)}, u32[]{:S(2)}) collective-permute-start(f32[2,3,9,1,256]{4,0,3,2,1:T(2,128)} %copy.289), channel_id=1, source_target_pairs={{2,0},{4,2},{6,4},{8,6},{10,8},{12,10},{14,12},{3,1},{5,3},{7,5},{... | collective-permute-start | bytes 165896 | tf_op jit(solution)/shard_map/ppermute | solution.py:31
  183.4 7.1 %copy.218 = f32[2,3,9,32,256]{3,0,4,2,1:T(2,128)} copy(f32[2,3,9,32,256]{4,3,2,1,0:T(8,128)S(1)} %constant_dynamic-update-slice_fusion) | data formatting | bytes 3538944 | tf_op jit(solution)/shard_map/concatenate | solution.py:110
  190.5 8.5 %copy.219 = f32[2,3,9,1,256]{3,0,4,2,1:T(2,128)} copy(f32[2,3,9,1,256]{4,0,3,2,1:T(2,128)} %collective-permute-done.25) | data formatting | bytes 110592 | tf_op jit(solution)/shard_map/ppermute | solution.py:31
  203.3 54.2 %slice_maximum_fusion.2 = (f32[1,3,8,32,256]{3,0,4,2,1:T(1,128)}, f32[1,3,8,32,256]{3,0,4,2,1:T(1,128)}, f32[1,3,8,32,256]{3,0,4,2,1:T(1,128)}, f32[1,3,8,32,256]{3,0,4,2,1:T(1,128)}) fusion(f32[2,3,9,1,256]{3,0,4,2,1:T(2,128)S(1)} %copy-done, f32[2,3,9,32,256]{3,0,4,2,1:T(2,128)S(1)} %bitcast.52), kind=kLoop, calls=%fused_computation.13 | loop fusion | flops 786432 | bytes 4970496 | tf_op jit(solution)/shard_map/concatenate | solution.py:111
  258.8 8.9 %pad_maximum_fusion.134 = f32[2,3,9,33,256]{3,0,4,2,1:T(2,128)} fusion(f32[2,3,9,1,256]{3,0,4,2,1:T(2,128)S(1)} %copy-done, f32[2,3,9,32,256]{3,0,4,2,1:T(2,128)S(1)} %bitcast.52), kind=kLoop, calls=%fused_computation.294 | loop fusion | flops 456192 | bytes 3649536 | tf_op jit(solution)/shard_map/concatenate | solution.py:111
  267.7 11.1 %copy.220 = f32[2,3,9,33,256]{4,0,3,2,1:T(2,128)} copy(f32[2,3,9,33,256]{3,0,4,2,1:T(2,128)} %pad_maximum_fusion.134) | data formatting | bytes 3649536 | tf_op jit(solution)/shard_map/concatenate | solution.py:111
  292.0 26.0 %fusion.46 = (f32[3,1,8,32,256]{4,1,3,2,0:T(1,128)S(1)}, f32[3,1,8,32,256]{4,1,3,2,0:T(1,128)S(1)}, f32[3,1,8,32,256]{4,1,3,2,0:T(1,128)S(1)}, f32[3,1,8,32,256]...) fusion(f32[2,3,9,33,1]{4,0,3,2,1:T(2,128)S(1)} %copy.221, ...), kind=kLoop, calls=%fused_computation.93 | loop fusion | flops 1572864 | bytes 8123352 | tf_op jit(solution)/shard_map/stack;squeeze | solution.py:133
  326.4 7.0 %reshape.36 = f32[24,65536]{1,0:T(8,128)} reshape(f32[3,8,8,32,256]{4,3,2,1,0:T(8,128)} %copy-done.1) | data formatting | bytes 12582912 | tf_op jit(solution)/shard_map/reshape | solution.py:133
  340.6 6.9 %reshape.38 = f32[24,65536]{1,0:T(8,128)} reshape(f32[3,8,8,32,256]{4,3,2,1,0:T(8,128)} %copy_dynamic-update-slice_fusion) | data formatting | bytes 12582912 | tf_op jit(solution)/shard_map/reshape | solution.py:133
  347.5 11.2 %fusion = f32[65536]{0:T(1024)} fusion(f32[24,65536]{1,0:T(8,128)} %reshape.36, f32[24,24]{1,0:T(8,128)S(1)} %copy-done.28), kind=kOutput, calls=%fused_computation.15 | convolution fusion | flops 456065024 | bytes 6555904 | tf_op jit(solution)/shard_map/dot_general | solution.py:134
  365.0 4.8 subtract_bitcast_fusion.1
  371.4 9.9 %fusion.1 = f32[65536]{0:T(1024)S(1)} fusion(f32[24,65536]{1,0:T(8,128)} %reshape.38, f32[24,24]{1,0:T(8,128)S(1)} %copy-done.28), kind=kOutput, calls=%fused_computation.16 | convolution fusion | flops 456065024 | bytes 6555904 | tf_op jit(solution)/shard_map/dot_general | solution.py:134
  394.2 6.1 %collective-permute-start.30 = (f32[2,10,1,256]{3,0,2,1:T(2,128)S(1)}, f32[2,10,1,256]{3,0,2,1:T(2,128)S(1)}, u32[]{:S(2)}, u32[]{:S(2)}) collective-permute-start(f32[2,10,1,256]{3,0,2,1:T(2,128)S(1)} %copy.318), channel_id=1, source_target_pairs={{0,2},{2,4},{4,6},{6,8},{8,10},{10,12},{12,14},{1,3},{3,5},{5,7},{... | collective-permute-start | bytes 61448 | tf_op jit(solution)/shard_map/ppermute | solution.py:22
  402.3 5.2 collective-permute-done.29
  409.2 4.8 collective-permute-start.32
  414.1 6.0 %collective-permute-done.31 = f32[2,10,34,1]{3,0,2,1:T(2,128)S(1)} collective-permute-done((f32[2,10,34,1]{3,0,2,1:T(2,128)S(1)}, f32[2,10,34,1]{3,0,2,1:T(2,128)S(1)}, u32[]{:S(2)}, u32[]{:S(2)}) %collective-permute-start.31) | collective-permute-done | bytes 2752 | tf_op jit(solution)/shard_map/ppermute | solution.py:23
  430.7 6.6 %collective-permute-start.36 = (f32[2,10,1,256]{3,0,2,1:T(2,128)S(1)}, f32[2,10,1,256]{3,0,2,1:T(2,128)S(1)}, u32[]{:S(2)}, u32[]{:S(2)}) collective-permute-start(f32[2,10,1,256]{3,0,2,1:T(2,128)S(1)} %copy.320), channel_id=1, source_target_pairs={{0,2},{2,4},{4,6},{6,8},{8,10},{10,12},{12,14},{1,3},{3,5},{5,7},{... | collective-permute-start | bytes 61448 | tf_op jit(solution)/shard_map/ppermute | solution.py:22
  439.3 5.2 collective-permute-done.35
  450.9 6.5 %collective-permute-done.37 = f32[2,10,34,1]{3,0,2,1:T(2,128)S(1)} collective-permute-done((f32[2,10,34,1]{3,0,2,1:T(2,128)S(1)}, f32[2,10,34,1]{3,0,2,1:T(2,128)S(1)}, u32[]{:S(2)}, u32[]{:S(2)}) %collective-permute-start.37) | collective-permute-done | bytes 2752 | tf_op jit(solution)/shard_map/ppermute | solution.py:23
  471.9 5.2 collective-permute-done.41
  483.5 6.8 %collective-permute-done.43 = f32[2,10,34,1]{3,0,2,1:T(2,128)S(1)} collective-permute-done((f32[2,10,34,1]{3,0,2,1:T(2,128)S(1)}, f32[2,10,34,1]{3,0,2,1:T(2,128)S(1)}, u32[]{:S(2)}, u32[]{:S(2)}) %collective-permute-start.43) | collective-permute-done | bytes 2752 | tf_op jit(solution)/shard_map/ppermute | solution.py:23
  498.7 6.6 %collective-permute-start.48 = (f32[2,10,1,256]{3,0,2,1:T(2,128)S(1)}, f32[2,10,1,256]{3,0,2,1:T(2,128)S(1)}, u32[]{:S(2)}, u32[]{:S(2)}) collective-permute-start(f32[2,10,1,256]{3,0,2,1:T(2,128)S(1)} %copy.324), channel_id=1, source_target_pairs={{0,2},{2,4},{4,6},{6,8},{8,10},{10,12},{12,14},{1,3},{3,5},{5,7},{... | collective-permute-start | bytes 61448 | tf_op jit(solution)/shard_map/ppermute | solution.py:22
  507.3 5.2 collective-permute-done.47
  515.2 6.0 %collective-permute-start.50 = (f32[2,10,34,1]{3,0,2,1:T(2,128)}, f32[2,10,34,1]{3,0,2,1:T(2,128)}, u32[]{:S(2)}, u32[]{:S(2)}) collective-permute-start(f32[2,10,34,1]{3,0,2,1:T(2,128)} %get-tuple-element.36), channel_id=1, source_target_pairs={{0,1},{2,3},{4,5},{6,7},{8,9},{10,11},{12,13},{14,15},{16,17},{18,... | collective-permute-start | bytes 8168 | tf_op jit(solution)/shard_map/ppermute | solution.py:22
  (332 shorter events, 249.3 us)
Async XLA Ops:
  19.1 7.1 %collective-permute-start.2 = (f32[10,1,256]{2,1,0:T(1,128)S(1)}, f32[10,1,256]{2,1,0:T(1,128)S(1)}, u32[]{:S(2)}, u32[]{:S(2)}) collective-permute-start(f32[10,1,256]{2,1,0:T(1,128)S(1)} %get-tuple-element.92), channel_id=1, source_target_pairs={{2,0},{4,2},{6,4},{8,6},{10,8},{12,10},{14,12},{3,1},{5,3},{7,5},{... | collective-permute-start | bytes 30728 | tf_op jit(solution)/shard_map/ppermute | solution.py:23
  27.0 10.2 %collective-permute-start.4 = (f32[10,34,1]{2,1,0:T(8,128)}, f32[10,34,1]{2,1,0:T(8,128)}, u32[]{:S(2)}, u32[]{:S(2)}) collective-permute-start(f32[10,34,1]{2,1,0:T(8,128)} %get-tuple-element.71), channel_id=1, source_target_pairs={{1,0},{3,2},{5,4},{7,6},{9,8},{11,10},{13,12},{15,14},{17,16},{19,... | collective-permute-start | bytes 4088 | tf_op jit(solution)/shard_map/ppermute | solution.py:23
  28.3 10.2 %collective-permute-start.5 = (f32[10,34,1]{2,1,0:T(8,128)}, f32[10,34,1]{2,1,0:T(8,128)}, u32[]{:S(2)}, u32[]{:S(2)}) collective-permute-start(f32[10,34,1]{2,1,0:T(8,128)} %get-tuple-element.72), channel_id=1, source_target_pairs={{0,1},{2,3},{4,5},{6,7},{8,9},{10,11},{12,13},{14,15},{16,17},{18,... | collective-permute-start | bytes 4088 | tf_op jit(solution)/shard_map/ppermute | solution.py:22
  58.7 8.9 %collective-permute-start.9 = (f32[10,1,256]{2,1,0:T(1,128)S(1)}, f32[10,1,256]{2,1,0:T(1,128)S(1)}, u32[]{:S(2)}, u32[]{:S(2)}) collective-permute-start(f32[10,1,256]{2,1,0:T(1,128)S(1)} %get-tuple-element.89), channel_id=1, source_target_pairs={{0,2},{2,4},{4,6},{6,8},{8,10},{10,12},{12,14},{1,3},{3,5},{5,7},{... | collective-permute-start | bytes 30728 | tf_op jit(solution)/shard_map/ppermute | solution.py:22
  63.4 7.1 %collective-permute-start.8 = (f32[10,1,256]{2,1,0:T(1,128)S(1)}, f32[10,1,256]{2,1,0:T(1,128)S(1)}, u32[]{:S(2)}, u32[]{:S(2)}) collective-permute-start(f32[10,1,256]{2,1,0:T(1,128)S(1)} %get-tuple-element.90), channel_id=1, source_target_pairs={{2,0},{4,2},{6,4},{8,6},{10,8},{12,10},{14,12},{3,1},{5,3},{7,5},{... | collective-permute-start | bytes 30728 | tf_op jit(solution)/shard_map/ppermute | solution.py:23
  66.3 98.9 %collective-permute-start.24 = (f32[2,3,1,32,256]{4,3,2,1,0:T(8,128)}, f32[2,3,1,32,256]{4,3,2,1,0:T(8,128)}, u32[]{:S(2)}, u32[]{:S(2)}) collective-permute-start(f32[2,3,1,32,256]{4,3,2,1,0:T(8,128)} %slice.451), channel_id=1, source_target_pairs={{16,0},{32,16},{48,32},{64,48},{80,64},{96,80},{112,96},{17,1},{33... | collective-permute-start | bytes 589832 | tf_op jit(solution)/shard_map/ppermute | solution.py:31
  71.2 8.9 %collective-permute-start.10 = (f32[10,34,1]{2,1,0:T(8,128)}, f32[10,34,1]{2,1,0:T(8,128)S(1)}, u32[]{:S(2)}, u32[]{:S(2)}) collective-permute-start(f32[10,34,1]{2,1,0:T(8,128)} %get-tuple-element.69), channel_id=1, source_target_pairs={{1,0},{3,2},{5,4},{7,6},{9,8},{11,10},{13,12},{15,14},{17,16},{19,... | collective-permute-start | bytes 4088 | tf_op jit(solution)/shard_map/ppermute | solution.py:23
  72.5 9.2 %collective-permute-start.11 = (f32[10,34,1]{2,1,0:T(8,128)S(1)}, f32[10,34,1]{2,1,0:T(8,128)}, u32[]{:S(2)}, u32[]{:S(2)}) collective-permute-start(f32[10,34,1]{2,1,0:T(8,128)S(1)} %get-tuple-element.70), channel_id=1, source_target_pairs={{0,1},{2,3},{4,5},{6,7},{8,9},{10,11},{12,13},{14,15},{16,17},{18,... | collective-permute-start | bytes 4088 | tf_op jit(solution)/shard_map/ppermute | solution.py:22
  98.0 8.5 %collective-permute-start.15 = (f32[10,1,256]{2,1,0:T(1,128)S(1)}, f32[10,1,256]{2,1,0:T(1,128)S(1)}, u32[]{:S(2)}, u32[]{:S(2)}) collective-permute-start(f32[10,1,256]{2,1,0:T(1,128)S(1)} %get-tuple-element.87), channel_id=1, source_target_pairs={{0,2},{2,4},{4,6},{6,8},{8,10},{10,12},{12,14},{1,3},{3,5},{5,7},{... | collective-permute-start | bytes 30728 | tf_op jit(solution)/shard_map/ppermute | solution.py:22
  103.7 7.1 %collective-permute-start.14 = (f32[10,1,256]{2,1,0:T(1,128)S(1)}, f32[10,1,256]{2,1,0:T(1,128)S(1)}, u32[]{:S(2)}, u32[]{:S(2)}) collective-permute-start(f32[10,1,256]{2,1,0:T(1,128)S(1)} %get-tuple-element.88), channel_id=1, source_target_pairs={{2,0},{4,2},{6,4},{8,6},{10,8},{12,10},{14,12},{3,1},{5,3},{7,5},{... | collective-permute-start | bytes 30728 | tf_op jit(solution)/shard_map/ppermute | solution.py:23
  111.6 9.0 %collective-permute-start.16 = (f32[10,34,1]{2,1,0:T(8,128)}, f32[10,34,1]{2,1,0:T(8,128)}, u32[]{:S(2)}, u32[]{:S(2)}) collective-permute-start(f32[10,34,1]{2,1,0:T(8,128)} %get-tuple-element.67), channel_id=1, source_target_pairs={{1,0},{3,2},{5,4},{7,6},{9,8},{11,10},{13,12},{15,14},{17,16},{19,... | collective-permute-start | bytes 4088 | tf_op jit(solution)/shard_map/ppermute | solution.py:23
  112.9 10.1 %collective-permute-start.17 = (f32[10,34,1]{2,1,0:T(8,128)}, f32[10,34,1]{2,1,0:T(8,128)}, u32[]{:S(2)}, u32[]{:S(2)}) collective-permute-start(f32[10,34,1]{2,1,0:T(8,128)} %get-tuple-element.68), channel_id=1, source_target_pairs={{0,1},{2,3},{4,5},{6,7},{8,9},{10,11},{12,13},{14,15},{16,17},{18,... | collective-permute-start | bytes 4088 | tf_op jit(solution)/shard_map/ppermute | solution.py:22
  143.6 11.1 %collective-permute-start.21 = (f32[10,1,256]{2,1,0:T(1,128)S(1)}, f32[10,1,256]{2,1,0:T(1,128)S(1)}, u32[]{:S(2)}, u32[]{:S(2)}) collective-permute-start(f32[10,1,256]{2,1,0:T(1,128)S(1)} %get-tuple-element.85), channel_id=1, source_target_pairs={{0,2},{2,4},{4,6},{6,8},{8,10},{10,12},{12,14},{1,3},{3,5},{5,7},{... | collective-permute-start | bytes 30728 | tf_op jit(solution)/shard_map/ppermute | solution.py:22
  157.3 20.9 %collective-permute-start.22 = (f32[10,34,1]{2,1,0:T(8,128)S(1)}, f32[10,34,1]{2,1,0:T(8,128)S(1)}, u32[]{:S(2)}, u32[]{:S(2)}) collective-permute-start(f32[10,34,1]{2,1,0:T(8,128)S(1)} %get-tuple-element.65), channel_id=1, source_target_pairs={{1,0},{3,2},{5,4},{7,6},{9,8},{11,10},{13,12},{15,14},{17,16},{19,... | collective-permute-start | bytes 4088 | tf_op jit(solution)/shard_map/ppermute | solution.py:23
  158.6 19.7 %collective-permute-start.23 = (f32[10,34,1]{2,1,0:T(8,128)S(1)}, f32[10,34,1]{2,1,0:T(8,128)}, u32[]{:S(2)}, u32[]{:S(2)}) collective-permute-start(f32[10,34,1]{2,1,0:T(8,128)S(1)} %get-tuple-element.66), channel_id=1, source_target_pairs={{0,1},{2,3},{4,5},{6,7},{8,9},{10,11},{12,13},{14,15},{16,17},{18,... | collective-permute-start | bytes 4088 | tf_op jit(solution)/shard_map/ppermute | solution.py:22
  166.9 23.6 %collective-permute-start.25 = (f32[2,3,9,1,256]{4,0,3,2,1:T(2,128)}, f32[2,3,9,1,256]{4,0,3,2,1:T(2,128)}, u32[]{:S(2)}, u32[]{:S(2)}) collective-permute-start(f32[2,3,9,1,256]{4,0,3,2,1:T(2,128)} %copy.289), channel_id=1, source_target_pairs={{2,0},{4,2},{6,4},{8,6},{10,8},{12,10},{14,12},{3,1},{5,3},{7,5},{... | collective-permute-start | bytes 165896 | tf_op jit(solution)/shard_map/ppermute | solution.py:31
  257.5 32.6 %collective-permute-start.26 = (f32[2,3,9,33,1]{3,0,4,2,1:T(2,128)}, f32[2,3,9,33,1]{3,0,4,2,1:T(2,128)}, u32[]{:S(2)}, u32[]{:S(2)}) collective-permute-start(f32[2,3,9,33,1]{3,0,4,2,1:T(2,128)} %slice_maximum_fusion.4), channel_id=1, source_target_pairs={{1,0},{3,2},{5,4},{7,6},{9,8},{11,10},{13,12},{15,14},{17,16},{19,... | collective-permute-start | bytes 21392 | tf_op jit(solution)/shard_map/ppermute | solution.py:31
  394.2 7.5 %collective-permute-start.30 = (f32[2,10,1,256]{3,0,2,1:T(2,128)S(1)}, f32[2,10,1,256]{3,0,2,1:T(2,128)S(1)}, u32[]{:S(2)}, u32[]{:S(2)}) collective-permute-start(f32[2,10,1,256]{3,0,2,1:T(2,128)S(1)} %copy.318), channel_id=1, source_target_pairs={{0,2},{2,4},{4,6},{6,8},{8,10},{10,12},{12,14},{1,3},{3,5},{5,7},{... | collective-permute-start | bytes 61448 | tf_op jit(solution)/shard_map/ppermute | solution.py:22
  400.3 7.2 %collective-permute-start.29 = (f32[2,10,1,256]{3,0,2,1:T(2,128)S(1)}, f32[2,10,1,256]{3,0,2,1:T(2,128)S(1)}, u32[]{:S(2)}, u32[]{:S(2)}) collective-permute-start(f32[2,10,1,256]{3,0,2,1:T(2,128)S(1)} %copy.319), channel_id=1, source_target_pairs={{2,0},{4,2},{6,4},{8,6},{10,8},{12,10},{14,12},{3,1},{5,3},{7,5},{... | collective-permute-start | bytes 61448 | tf_op jit(solution)/shard_map/ppermute | solution.py:23
  407.9 12.1 %collective-permute-start.31 = (f32[2,10,34,1]{3,0,2,1:T(2,128)S(1)}, f32[2,10,34,1]{3,0,2,1:T(2,128)S(1)}, u32[]{:S(2)}, u32[]{:S(2)}) collective-permute-start(f32[2,10,34,1]{3,0,2,1:T(2,128)S(1)} %get-tuple-element.47), channel_id=1, source_target_pairs={{1,0},{3,2},{5,4},{7,6},{9,8},{11,10},{13,12},{15,14},{17,16},{19,... | collective-permute-start | bytes 8168 | tf_op jit(solution)/shard_map/ppermute | solution.py:23
  409.2 12.6 %collective-permute-start.32 = (f32[2,10,34,1]{3,0,2,1:T(2,128)S(1)}, f32[2,10,34,1]{3,0,2,1:T(2,128)S(1)}, u32[]{:S(2)}, u32[]{:S(2)}) collective-permute-start(f32[2,10,34,1]{3,0,2,1:T(2,128)S(1)} %get-tuple-element.48), channel_id=1, source_target_pairs={{0,1},{2,3},{4,5},{6,7},{8,9},{10,11},{12,13},{14,15},{16,17},{18,... | collective-permute-start | bytes 8168 | tf_op jit(solution)/shard_map/ppermute | solution.py:22
  430.7 8.0 %collective-permute-start.36 = (f32[2,10,1,256]{3,0,2,1:T(2,128)S(1)}, f32[2,10,1,256]{3,0,2,1:T(2,128)S(1)}, u32[]{:S(2)}, u32[]{:S(2)}) collective-permute-start(f32[2,10,1,256]{3,0,2,1:T(2,128)S(1)} %copy.320), channel_id=1, source_target_pairs={{0,2},{2,4},{4,6},{6,8},{8,10},{10,12},{12,14},{1,3},{3,5},{5,7},{... | collective-permute-start | bytes 61448 | tf_op jit(solution)/shard_map/ppermute | solution.py:22
  437.3 7.2 %collective-permute-start.35 = (f32[2,10,1,256]{3,0,2,1:T(2,128)S(1)}, f32[2,10,1,256]{3,0,2,1:T(2,128)S(1)}, u32[]{:S(2)}, u32[]{:S(2)}) collective-permute-start(f32[2,10,1,256]{3,0,2,1:T(2,128)S(1)} %copy.321), channel_id=1, source_target_pairs={{2,0},{4,2},{6,4},{8,6},{10,8},{12,10},{14,12},{3,1},{5,3},{7,5},{... | collective-permute-start | bytes 61448 | tf_op jit(solution)/shard_map/ppermute | solution.py:23
  445.0 12.4 %collective-permute-start.37 = (f32[2,10,34,1]{3,0,2,1:T(2,128)S(1)}, f32[2,10,34,1]{3,0,2,1:T(2,128)S(1)}, u32[]{:S(2)}, u32[]{:S(2)}) collective-permute-start(f32[2,10,34,1]{3,0,2,1:T(2,128)S(1)} %get-tuple-element.43), channel_id=1, source_target_pairs={{1,0},{3,2},{5,4},{7,6},{9,8},{11,10},{13,12},{15,14},{17,16},{19,... | collective-permute-start | bytes 8168 | tf_op jit(solution)/shard_map/ppermute | solution.py:23
  446.3 12.8 %collective-permute-start.38 = (f32[2,10,34,1]{3,0,2,1:T(2,128)S(1)}, f32[2,10,34,1]{3,0,2,1:T(2,128)S(1)}, u32[]{:S(2)}, u32[]{:S(2)}) collective-permute-start(f32[2,10,34,1]{3,0,2,1:T(2,128)S(1)} %get-tuple-element.44), channel_id=1, source_target_pairs={{0,1},{2,3},{4,5},{6,7},{8,9},{10,11},{12,13},{14,15},{16,17},{18,... | collective-permute-start | bytes 8168 | tf_op jit(solution)/shard_map/ppermute | solution.py:22
  469.9 7.2 %collective-permute-start.41 = (f32[2,10,1,256]{3,0,2,1:T(2,128)S(1)}, f32[2,10,1,256]{3,0,2,1:T(2,128)S(1)}, u32[]{:S(2)}, u32[]{:S(2)}) collective-permute-start(f32[2,10,1,256]{3,0,2,1:T(2,128)S(1)} %copy.323), channel_id=1, source_target_pairs={{2,0},{4,2},{6,4},{8,6},{10,8},{12,10},{14,12},{3,1},{5,3},{7,5},{... | collective-permute-start | bytes 61448 | tf_op jit(solution)/shard_map/ppermute | solution.py:23
  477.6 12.8 %collective-permute-start.43 = (f32[2,10,34,1]{3,0,2,1:T(2,128)S(1)}, f32[2,10,34,1]{3,0,2,1:T(2,128)S(1)}, u32[]{:S(2)}, u32[]{:S(2)}) collective-permute-start(f32[2,10,34,1]{3,0,2,1:T(2,128)S(1)} %get-tuple-element.39), channel_id=1, source_target_pairs={{1,0},{3,2},{5,4},{7,6},{9,8},{11,10},{13,12},{15,14},{17,16},{19,... | collective-permute-start | bytes 8168 | tf_op jit(solution)/shard_map/ppermute | solution.py:23
  478.9 13.0 %collective-permute-start.44 = (f32[2,10,34,1]{3,0,2,1:T(2,128)S(1)}, f32[2,10,34,1]{3,0,2,1:T(2,128)S(1)}, u32[]{:S(2)}, u32[]{:S(2)}) collective-permute-start(f32[2,10,34,1]{3,0,2,1:T(2,128)S(1)} %get-tuple-element.40), channel_id=1, source_target_pairs={{0,1},{2,3},{4,5},{6,7},{8,9},{10,11},{12,13},{14,15},{16,17},{18,... | collective-permute-start | bytes 8168 | tf_op jit(solution)/shard_map/ppermute | solution.py:22
  498.7 8.1 %collective-permute-start.48 = (f32[2,10,1,256]{3,0,2,1:T(2,128)S(1)}, f32[2,10,1,256]{3,0,2,1:T(2,128)S(1)}, u32[]{:S(2)}, u32[]{:S(2)}) collective-permute-start(f32[2,10,1,256]{3,0,2,1:T(2,128)S(1)} %copy.324), channel_id=1, source_target_pairs={{0,2},{2,4},{4,6},{6,8},{8,10},{10,12},{12,14},{1,3},{3,5},{5,7},{... | collective-permute-start | bytes 61448 | tf_op jit(solution)/shard_map/ppermute | solution.py:22
  505.3 7.2 %collective-permute-start.47 = (f32[2,10,1,256]{3,0,2,1:T(2,128)S(1)}, f32[2,10,1,256]{3,0,2,1:T(2,128)S(1)}, u32[]{:S(2)}, u32[]{:S(2)}) collective-permute-start(f32[2,10,1,256]{3,0,2,1:T(2,128)S(1)} %copy.325), channel_id=1, source_target_pairs={{2,0},{4,2},{6,4},{8,6},{10,8},{12,10},{14,12},{3,1},{5,3},{7,5},{... | collective-permute-start | bytes 61448 | tf_op jit(solution)/shard_map/ppermute | solution.py:23
  513.9 13.2 %collective-permute-start.49 = (f32[2,10,34,1]{3,0,2,1:T(2,128)}, f32[2,10,34,1]{3,0,2,1:T(2,128)}, u32[]{:S(2)}, u32[]{:S(2)}) collective-permute-start(f32[2,10,34,1]{3,0,2,1:T(2,128)} %get-tuple-element.35), channel_id=1, source_target_pairs={{1,0},{3,2},{5,4},{7,6},{9,8},{11,10},{13,12},{15,14},{17,16},{19,... | collective-permute-start | bytes 8168 | tf_op jit(solution)/shard_map/ppermute | solution.py:23
  515.2 13.9 %collective-permute-start.50 = (f32[2,10,34,1]{3,0,2,1:T(2,128)}, f32[2,10,34,1]{3,0,2,1:T(2,128)}, u32[]{:S(2)}, u32[]{:S(2)}) collective-permute-start(f32[2,10,34,1]{3,0,2,1:T(2,128)} %get-tuple-element.36), channel_id=1, source_target_pairs={{0,1},{2,3},{4,5},{6,7},{8,9},{10,11},{12,13},{14,15},{16,17},{18,... | collective-permute-start | bytes 8168 | tf_op jit(solution)/shard_map/ppermute | solution.py:22
  (65 other events, 1245.1 us)
where the time goes:
time: 541 us; the launch traced here: 534 us
  starting transfers between devices  152 us (28%)
  other arithmetic  135 us (25%)
  local copies, waits for them, and re-layouts  133 us (25%)
  waiting for transfers between devices  90.5 us (17%)
  matrix products  21.1 us (4%)
    ppermute x24, starting transfers between devices, padded_2(): before = lax.ppermute(last, axis, up)  107 us
    ppermute x24, waiting for transfers between devices, padded_2(): after = lax.ppermute(first, axis, down)  78.2 us
    concatenate x3, other arithmetic, local(): jnp.concatenate([extended, from_behind(extended[:, :, :, 0:1], 'gy', -1)]...  64.8 us
    unnamed x141, local copies, waits for them, and re-layouts  52.5 us
    ppermute x24, starting transfers between devices, padded_2(): after = lax.ppermute(first, axis, down)  31 us
    another operation x1, other arithmetic, local(): jnp.stack(corners, axis=1).reshape(24, cells_x * cells_y * cells_z)  26 us
    dot_general x2, matrix products, local(): jnp.dot(stiffness, element, precision=lax.Precision.HIGHEST, preferred_el...  21.1 us
    concatenate x24, other arithmetic, padded_2(): x = jnp.concatenate([before, x, after], axis=dim)  15.1 us
  transfers between devices with their start and end apart: 51, of which 34 were waited for; matrix products, arithmetic and copies ran while one was open for 17% of the time, Pallas kernels for 0%

commit v1 on v0

v1 whole, which is shorter than its diff:
```python
import jax
import jax.numpy as jnp
from jax import lax
from jax.experimental import pallas as pl
from jax.experimental.pallas import tpu as pltpu
from jax.sharding import PartitionSpec as P

ITERS = 4
MODES = 2
CX, CY, CZ = 8, 32, 256
W = ITERS
PX = CX + 2 * W
PY = CY + 8
PZ = CZ + 128
LANES = 128

poisson = 0.3
radius_sq = 3.0
stiff_floor = 0.001
LAME = poisson / ((1.0 + poisson) * (1.0 - 2.0 * poisson))
SHEAR = 0.5 / (1.0 + poisson)

F32 = jnp.float32


def iota(shape, dim):
    return lax.broadcasted_iota(jnp.int32, shape, dim)


def pos(ref):
    return ref[0], ref[1], ref[2]


def fill_table(table, where):
    gx, gy, gz = where
    shape = (PY, PZ)
    y, z = iota(shape, 0), iota(shape, 1)
    y = jnp.where(y < CY + W, y, y - PY) + gy * CY
    z = jnp.where(z < CZ + LANES // 2, z, z - PZ)
    near = (z >= -W) & (z < CZ + W)
    z = z + gz * CZ
    inside = near & (y >= 0) & (y < 8 * CY) & (z >= 0) & (z < 2 * CZ)
    count = 4.0
    for place, last in ((y, 8 * CY - 1), (z, 2 * CZ - 1)):
        count = count - (place == 0).astype(F32) - (place == last).astype(F32)
    table[0] = jnp.zeros(shape, F32)
    table[1] = jnp.where(inside, 1.0 / (1.0 + radius_sq * (count + 1.0)), 0.0)
    table[2] = jnp.where(inside, 1.0 / (1.0 + radius_sq * (count + 2.0)), 0.0)


def row_of(gx, plane):
    x = gx * CX + plane - W
    out = (x < 0) | (x > 8 * CX - 1)
    end = (x == 0) | (x == 8 * CX - 1)
    return jnp.where(out, 0, jnp.where(end, 1, 2))


def sweep_plane(table, gx, p, sb, old):
    mid = old[p]
    total = old[p - 1] + old[p + 1]
    total = total + pltpu.roll(mid, 1, 0) + pltpu.roll(mid, PY - 1, 0)
    total = total + pltpu.roll(mid, 1, 1) + pltpu.roll(mid, PZ - 1, 1)
    return sb[p] + (radius_sq * table[row_of(gx, p)]) * total


def pack_x1(design, mask, modes, src, down, up):
    for x in range(CX):
        plane = design[x] * mask[x].astype(F32)
        src[x] = plane
        if x < W:
            down[x] = plane
        if x >= CX - W:
            up[x - (CX - W)] = plane
    for m in range(MODES):
        for c in range(3):
            down[W + 3 * m + c] = modes[m, c, 0]


def pick_plane(own, above, below, p):
    if p < W:
        return below, p
    if p < W + CX:
        return own, p - W
    return above, p - W - CX


def pack_y1(where, src, modes, above, below, down, up):
    gx, gy, gz = pos(where)
    low = iota((8, CZ), 0) < 4
    for q in range(8):
        a, i = pick_plane(src, above, below, q)
        b, j = pick_plane(src, above, below, q + 8)
        down[q] = jnp.where(low, a[i, 0:8, :], pltpu.roll(b[j, 0:8, :], 4, 0))
        up[q] = jnp.where(low, pltpu.roll(b[j, 24:32, :], 4, 0), a[i, 24:32, :])
    keep = jnp.where(gx < 7, 1.0, 0.0)
    for m in range(MODES):
        for c in range(3):
            for x in range(CX + 1):
                n = c * (CX + 1) + x
                if x < CX:
                    row = modes[m, c, x, 0:1, :]
                else:
                    row = above[W + 3 * m + c, 0:1, :] * keep
                down[8 + 4 * m + n // 8, n % 8 : n % 8 + 1, :] = row
        down[8 + 4 * m + 3, 3:8, :] = jnp.zeros((5, CZ), F32)


def halo_tile(y_above, y_below, p, lanes=slice(None)):
    a, b = y_above[p % 8, :, lanes], y_below[p % 8, :, lanes]
    if p >= 8:
        a, b = pltpu.roll(a, 4, 0), pltpu.roll(b, 4, 0)
    return jnp.where(iota(a.shape, 0) < 4, a, b)


def pack_z1(where, src, modes, above, below, y_above, y_below, out):
    gx, gy, gz = pos(where)
    start = pl.multiple_of((1 - gz) * LANES, LANES)
    edge = pl.ds(start, LANES)
    lane = iota((PY, LANES), 1)
    sub = iota((8, LANES), 0)
    acc = jnp.zeros((PY, LANES), F32)
    for p in range(PX):
        a, i = pick_plane(src, above, below, p)
        tile = jnp.concatenate([a[i, :, edge], halo_tile(y_above, y_below, p, edge)], axis=0)
        tile = pltpu.roll(tile, (4 * p + 4 * (1 - gz)) % LANES, 1)
        acc = jnp.where((lane >= 4 * p) & (lane < 4 * p + 4), tile, acc)
    keep_x = jnp.where(gx < 7, 1.0, 0.0)
    keep_y = jnp.where(gy < 7, 1.0, 0.0)
    for m in range(MODES):
        for c in range(3):
            for x in range(CX + 1):
                n = c * (CX + 1) + x
                t = 8 + 4 * m + n // 8
                rim = y_above[t, n % 8 : n % 8 + 1, 0:LANES] * keep_y
                rim = jnp.where(sub == 0, rim, 0.0)
                body = modes[m, c, x] if x < CX else above[W + 3 * m + c, :, 0:LANES] * keep_x
                tile = jnp.concatenate([body, rim], axis=0)
                to = 64 + 32 * m + n
                acc = jnp.where(lane == to, pltpu.roll(tile, to, 1), acc)
    out[...] = acc


def energy_terms(prev, cur):
    (paa, pad, pda, pdd), (caa, cad, cda, cdd) = prev, cur
    u, v, w = 0, 1, 2
    aad = [cad[i] + pad[i] for i in range(3)]
    ada = [cda[i] + pda[i] for i in range(3)]
    add = [cdd[i] + pdd[i] for i in range(3)]
    daa = [caa[i] - paa[i] for i in range(3)]
    dad = [cad[i] - pad[i] for i in range(3)]
    dda = [cda[i] - pda[i] for i in range(3)]
    ddd = [cdd[i] - pdd[i] for i in range(3)]

    def sq(x):
        return x * x

    trace = sq(daa[u] + ada[v] + aad[w])
    lines = sq(dda[v] + dad[w]) + sq(dda[u] + add[w]) + sq(dad[u] + add[v])
    diag = sq(daa[u]) + sq(ada[v]) + sq(aad[w])
    shear = sq(ada[u] + daa[v]) + sq(aad[u] + daa[w]) + sq(aad[v] + ada[w])
    mixed = sq(dda[u]) + sq(dda[v]) + sq(dad[u]) + sq(dad[w]) + sq(add[v]) + sq(add[w])
    cross = sq(add[u] + dad[v]) + sq(add[u] + dda[w]) + sq(dad[v] + dda[w])
    cubic = sq(ddd[u]) + sq(ddd[v]) + sq(ddd[w])
    return (
        LAME * (trace + lines * (1.0 / 3.0))
        + SHEAR * (2.0 * diag + shear + mixed + cross * (1.0 / 3.0))
        + ((LAME + 4.0 * SHEAR) / 9.0) * cubic
    )


def main_kernel(
    eigenvalues, order, where, src, modes, above, below, y_above, y_below, z_in,
    low, high, table, sb, one, two,
):
    gx, gy, gz = pos(where)
    fill_table(table, (gx, gy, gz))
    back = (LANES - 4) * gz
    for p in range(PX):
        a, i = pick_plane(src, above, below, p)
        scale = table.at[row_of(gx, p)]
        sb[p, 0:CY, 0:CZ] = a[i] * scale[0:CY, 0:CZ]
        sb[p, CY:PY, 0:CZ] = halo_tile(y_above, y_below, p) * scale[CY:PY, 0:CZ]
        sb[p, :, CZ:PZ] = pltpu.roll(z_in[...], (back + LANES - 4 * p) % LANES, 1) * scale[:, CZ:PZ]
    old = sb
    for k in range(1, ITERS + 1):
        new = one if k % 2 else two

        def body(p, carry, old=old, new=new):
            new[p] = sweep_plane(table, gx, p, sb, old)
            return carry

        lax.fori_loop(k, PX - k, body, 0)
        old = new
    physical = old

    keep_x = jnp.where(gx < 7, 1.0, 0.0)
    keep_y = jnp.where(gy < 7, 1.0, 0.0)
    keep_z = jnp.where(gz < 1, 1.0, 0.0)
    last_lane = iota((8, CZ), 1) == CZ - 1
    last_sub = iota((8, CZ), 0) == 7
    stiff = 3.0 * (1.0 - stiff_floor) / 16.0

    def mode_step(m, carry):
        lam = eigenvalues[order[m]] * (0.125 * 0.25)

        def along_z(x, c, chunk):
            n = c * (CX + 1) + x
            t, s = n // 8, n % 8
            if chunk == CY // 8:
                here = jnp.broadcast_to(y_above[8 + 4 * m + t, s : s + 1, :] * keep_y, (8, CZ))
            elif x < CX:
                here = modes[m, c, x, 8 * chunk : 8 * chunk + 8, :]
            else:
                here = above[W + 3 * m + c, 8 * chunk : 8 * chunk + 8, :] * keep_x
            col = pltpu.roll(
                z_in[8 * chunk : 8 * chunk + 8, :], LANES - 1 - (64 + 32 * m + n), 1
            ) * keep_z
            if chunk == CY // 8:
                col = jnp.broadcast_to(col[0:1], (8, LANES))
            col = jnp.concatenate([col, col], axis=1)
            after = jnp.where(last_lane, col, pltpu.roll(here, CZ - 1, 1))
            return here + after, after - here

        for chunk in range(CY // 8):
            prev = None
            prev_mass = None
            for x in range(CX + 1):
                aa, ad, da, dd = [], [], [], []
                mass = None
                for c in range(3):
                    a0, d0 = along_z(x, c, chunk)
                    a1, d1 = along_z(x, c, chunk + 1)

                    def next_row(t, n):
                        return jnp.where(last_sub, pltpu.roll(n, 7, 0), pltpu.roll(t, 7, 0))

                    a1, d1 = next_row(a0, a1), next_row(d0, d1)
                    aa.append(a0 + a1)
                    da.append(a1 - a0)
                    ad.append(d0 + d1)
                    dd.append(d1 - d0)
                    for part in (aa[-1], da[-1], ad[-1], dd[-1]):
                        mass = part * part if mass is None else mass + part * part
                cur = (aa, ad, da, dd)
                if x:
                    rows = slice(8 * chunk, 8 * chunk + 8)
                    phys = physical[W + x - 1, rows, 0:CZ]
                    energy = energy_terms(prev, cur)
                    raw = stiff * phys * phys * energy - lam * (mass + prev_mass)
                    if x - 1 < W:
                        low[x - 1, m, rows, :] = raw
                    else:
                        high[x - 1 - W, m, rows, :] = raw
                prev, prev_mass = cur, mass
        return carry

    lax.fori_loop(0, MODES, mode_step, 0)


def raw_plane(low, high, above, below, p):
    if p < W:
        return below, p
    if p < 2 * W:
        return low, p - W
    if p < 3 * W:
        return high, p - 2 * W
    return above, p - 3 * W


def pack_y2(low, high, above, below, down, up):
    first = iota((8, CZ), 0) < 4
    for p in range(PX):
        a, i = raw_plane(low, high, above, below, p)
        down[p] = jnp.where(first, a[i, 0, 0:8, :], pltpu.roll(a[i, 1, 0:8, :], 4, 0))
        up[p] = jnp.where(first, pltpu.roll(a[i, 0, 24:32, :], 4, 0), a[i, 1, 24:32, :])


def raw_halo(y_above, y_below, p, m, lanes=slice(None)):
    a, b = y_above[p, :, lanes], y_below[p, :, lanes]
    if m == 0:
        b = pltpu.roll(b, 4, 0)
    else:
        a = pltpu.roll(a, 4, 0)
    return jnp.where(iota(a.shape, 0) < 4, a, b)


def pack_z2(where, low, high, above, below, y_above, y_below, out):
    gx, gy, gz = pos(where)
    edge = pl.ds(pl.multiple_of((1 - gz) * LANES, LANES), LANES)
    lane = iota((PY, LANES), 1)
    acc = jnp.zeros((PY, LANES), F32)
    for p in range(PX):
        a, i = raw_plane(low, high, above, below, p)
        for m in range(MODES):
            tile = jnp.concatenate([a[i, m, :, edge], raw_halo(y_above, y_below, p, m, edge)], axis=0)
            to = 64 * m + 4 * p
            tile = pltpu.roll(tile, (to + 4 * (1 - gz)) % LANES, 1)
            acc = jnp.where((lane >= to) & (lane < to + 4), tile, acc)
    out[...] = acc


def final_kernel(
    where, mask, low, high, above, below, y_above, y_below, z_in,
    out, table, sb0, sb1, one0, one1, two0, two1,
):
    gx, gy, gz = pos(where)
    fill_table(table, (gx, gy, gz))
    back = (LANES - 4) * gz
    sbs, ones, twos = (sb0, sb1), (one0, one1), (two0, two1)
    for p in range(PX):
        a, i = raw_plane(low, high, above, below, p)
        scale = table.at[row_of(gx, p)]
        for m in range(MODES):
            sb = sbs[m]
            sb[p, 0:CY, 0:CZ] = a[i, m] * scale[0:CY, 0:CZ]
            sb[p, CY:PY, 0:CZ] = raw_halo(y_above, y_below, p, m) * scale[CY:PY, 0:CZ]
            turn = (back + 2 * LANES - 64 * m - 4 * p) % LANES
            sb[p, :, CZ:PZ] = pltpu.roll(z_in[...], turn, 1) * scale[:, CZ:PZ]
    old = sbs
    for k in range(1, ITERS + 1):
        new = ones if k % 2 else twos

        def body(p, carry, old=old, new=new, k=k):
            for m in range(MODES):
                plane = sweep_plane(table, gx, p, sbs[m], old[m])
                if k < ITERS:
                    new[m][p] = plane
                else:
                    out[m, p - W] = plane[0:CY, 0:CZ] * mask[p - W].astype(F32)
            return carry

        lax.fori_loop(k, PX - k, body, 0)
        old = new


def call(kernel, outs, specs, args, scratch=(), name=None):
    shapes = tuple(jax.ShapeDtypeStruct(s, F32) for s in outs)
    return pl.pallas_call(
        kernel,
        grid=(1,),
        out_shape=shapes if len(shapes) > 1 else shapes[0],
        in_specs=specs,
        scratch_shapes=scratch,
        compiler_params=pltpu.CompilerParams(vmem_limit_bytes=24 * 1024 * 1024),
        name=name,
    )(*args)


SMEM = pl.BlockSpec(memory_space=pltpu.SMEM)


def whole(x):
    return pl.BlockSpec(x.shape, lambda i: (0,) * x.ndim)


def ring(axis, step):
    size = lax.axis_size(axis)
    return [(i, (i + step) % size) for i in range(size)]


def shift(x, axis, step):
    return lax.ppermute(x, axis, ring(axis, step))


def local(mode_fields, design, solid_mask, eigenvalues, mode_order):
    where = jnp.stack([lax.axis_index(a) for a in ("gx", "gy", "gz")]).astype(jnp.int32)
    big = pltpu.VMEM((PX, PY, PZ), F32)
    table = pltpu.VMEM((3, PY, PZ), F32)

    first_x = pl.BlockSpec((MODES, 3, 1, CY, CZ), lambda i: (0, 0, 0, 0, 0))
    src, down, up = call(
        pack_x1, [(CX, CY, CZ), (W + 6, CY, CZ), (W, CY, CZ)],
        [whole(design), whole(solid_mask), first_x], (design, solid_mask, mode_fields), name="pack_x1",
    )
    above, below = shift(down, "gx", -1), shift(up, "gx", 1)

    first_y = pl.BlockSpec((MODES, 3, CX, 8, CZ), lambda i: (0, 0, 0, 0, 0))
    down, up = call(
        pack_y1, [(16, 8, CZ), (8, 8, CZ)],
        [SMEM, whole(src), first_y, whole(above), whole(below)],
        (where, src, mode_fields, above, below), name="pack_y1",
    )
    y_above, y_below = shift(down, "gy", -1), shift(up, "gy", 1)

    first_z = pl.BlockSpec((MODES, 3, CX, CY, LANES), lambda i: (0, 0, 0, 0, 0))
    halos = (above, below, y_above, y_below)
    edge = call(
        pack_z1, [(PY, LANES)],
        [SMEM, whole(src), first_z, *map(whole, halos)],
        (where, src, mode_fields, *halos), name="pack_z1",
    )
    z_in = shift(edge, "gz", 1)

    low, high = call(
        main_kernel, [(W, MODES, CY, CZ)] * 2,
        [SMEM, SMEM, SMEM, *map(whole, (src, mode_fields, *halos, z_in))],
        (eigenvalues, mode_order, where, src, mode_fields, *halos, z_in),
        [table, big, big, big], name="raw",
    )

    above, below = shift(low, "gx", -1), shift(high, "gx", 1)
    planes = (low, high, above, below)
    down, up = call(pack_y2, [(PX, 8, CZ)] * 2, list(map(whole, planes)), planes, name="pack_y2")
    y_above, y_below = shift(down, "gy", -1), shift(up, "gy", 1)
    args = (*planes, y_above, y_below)
    edge = call(pack_z2, [(PY, LANES)], [SMEM, *map(whole, args)], (where, *args), name="pack_z2")
    z_in = shift(edge, "gz", 1)
    return call(
        final_kernel, [(MODES, CX, CY, CZ)],
        [SMEM, *map(whole, (solid_mask, *args, z_in))],
        (where, solid_mask, *args, z_in),
        [table] + [big] * 6, name="filter",
    )


def solution(mesh):
    return jax.shard_map(
        local,
        mesh=mesh,
        in_specs=(
            P(None, None, "gx", "gy", "gz"),
            P("gx", "gy", "gz"),
            P("gx", "gy", "gz"),
            P(),
            P(),
        ),
        out_specs=P(None, "gx", "gy", "gz"),
        check_vma=False,
    )
```

time: 541 us -> 69.5 us (0.13); the launches traced: 534 us -> 69.4 us
  starting transfers between devices: 152 us -> 14.5 us
  other arithmetic: 135 us -> 0.08 us
  local copies, waits for them, and re-layouts: 133 us -> 3.33 us
  waiting for transfers between devices: 90.5 us -> 32.5 us
  matrix products: 21.1 us -> 0 us
  Pallas kernels: 0 us -> 18.9 us
    ppermute x51 -> x10, starting transfers between devices: 152 us -> 14.5 us  [shift(): return lax.ppermute(x, axis, ring(axis, step))]
    concatenate x27 -> x0, other arithmetic: 79.8 us -> none  [the longest x3 64.8 us: local(): jnp.concatenate([extended, from_behind(extended[:, :, :, 0:1], 'gy', -1)]...]
    ppermute x51 -> x10, waiting for transfers between devices: 90.5 us -> 32.5 us  [shift(): return lax.ppermute(x, axis, ring(axis, step))]
    unnamed x141 -> x14, local copies, waits for them, and re-layouts: 52.5 us -> 3.33 us
    another operation x3 -> x1, other arithmetic: 33.1 us -> 0.08 us  [local(): jnp.stack([lax.axis_index(a) for a in ('gx', 'gy', 'gz')]).astype(jnp.int32)]
    dot_general x2 -> x0, matrix products: 21.1 us -> none  [local(): jnp.dot(stiffness, element, precision=lax.Precision.HIGHEST, preferred_el...]
    concatenate x7 -> x0, local copies, waits for them, and re-layouts: 19.1 us -> none  [the longest x1 11.1 us: local(): jnp.concatenate([extended, from_behind(extended[:, :, :, 0:1], 'gy', -1)]...]
    pallas_call x0 -> x7, Pallas kernels: none -> 18.9 us  [call(): pl.pallas_call(kernel, grid=(1,), out_shape=shapes if len(shapes) > 1 els...]
  transfers between devices with their start and end apart: 51 -> 10, of which waited for: 34 -> 8; matrix products, arithmetic and copies ran while one was open for 17% -> 0% of each run, Pallas kernels for 0% -> 0%
where the time goes in v1:
time: 69.5 us; the launch traced here: 69.4 us
  waiting for transfers between devices  32.5 us (47%)
  Pallas kernels  18.9 us (27%)
  starting transfers between devices  14.5 us (21%)
  local copies, waits for them, and re-layouts  3.33 us (5%)
    ppermute x10, waiting for transfers between devices, shift(): return lax.ppermute(x, axis, ring(axis, step))  32.5 us
    pallas_call x7, Pallas kernels, call(): pl.pallas_call(kernel, grid=(1,), out_shape=shapes if len(shapes) > 1 els...  18.9 us
    ppermute x10, starting transfers between devices, shift(): return lax.ppermute(x, axis, ring(axis, step))  14.5 us
    unnamed x14, local copies, waits for them, and re-layouts  3.33 us
  transfers between devices with their start and end apart: 10, of which 8 were waited for; matrix products, arithmetic and copies ran while one was open for 0% of the time, Pallas kernels for 0%

profile of v1, /device:TPU:0, one launch (start us, length us, event | category | flops | bytes accessed | tf_op | source)
XLA Modules:
  0.0 69.4 jit_solution(13256030519298445242)
XLA Ops:
  0.0 1.4 %copy-done = f32[2,3,8,32,256]{4,3,2,1,0:T(8,128)S(1)} copy-done((f32[2,3,8,32,256]{4,3,2,1,0:T(8,128)S(1)}, f32[2,3,8,32,256]{4,3,2,1,0:T(8,128)}, u32[]{:S(2)}) %copy-start) | copy-done | bytes 1572888
  1.4 0.9 %copy-done.2 = s32[8,32,256]{2,1,0:T(8,128)S(1)} copy-done((s32[8,32,256]{2,1,0:T(8,128)S(1)}, s32[8,32,256]{2,1,0:T(8,128)}, u32[]{:S(2)}) %copy-start.2) | copy-done | bytes 262168
  2.4 0.9 %copy-done.4 = f32[8,32,256]{2,1,0:T(8,128)S(1)} copy-done((f32[8,32,256]{2,1,0:T(8,128)S(1)}, f32[8,32,256]{2,1,0:T(8,128)}, u32[]{:S(2)}) %copy-start.4) | copy-done | bytes 262168
  3.3 0.1 pack_x1.1
  3.4 2.5 %collective-permute-start = (f32[10,32,256]{2,1,0:T(8,128)S(1)}, f32[10,32,256]{2,1,0:T(8,128)S(1)}, u32[]{:S(2)}, u32[]{:S(2)}) collective-permute-start(f32[10,32,256]{2,1,0:T(8,128)S(1)} %get-tuple-element.15), channel_id=1, source_target_pairs={{0,112},{16,0},{32,16},{48,32},{64,48},{80,64},{96,80},{112,96},{1... | collective-permute-start | bytes 983048 | tf_op jit(solution)/shard_map/ppermute | solution.py:362
  5.9 0.0 collective-permute-start.1
  5.9 0.1 pad_add_fusion.where
  6.0 5.5 %collective-permute-done.1.below = f32[4,32,256]{2,1,0:T(8,128)S(1)} collective-permute-done((f32[4,32,256]{2,1,0:T(8,128)S(1)}, f32[4,32,256]{2,1,0:T(8,128)S(1)}, u32[]{:S(2)}, u32[]{:S(2)}) %collective-permute-start.1) | collective-permute-done | bytes 131104 | tf_op jit(solution)/shard_map/ppermute | solution.py:362
  11.5 0.0 collective-permute-done.above
  11.5 0.6 pack_y1.1
  12.1 0.0 copy-start.5
  12.1 0.0 copy-start.6
  12.1 6.6 %collective-permute-start.2 = (f32[16,8,256]{2,1,0:T(8,128)S(1)}, f32[16,8,256]{2,1,0:T(8,128)S(1)}, u32[]{:S(2)}, u32[]{:S(2)}) collective-permute-start(f32[16,8,256]{2,1,0:T(8,128)S(1)} %get-tuple-element.17), channel_id=1, source_target_pairs={{0,14},{2,0},{4,2},{6,4},{8,6},{10,8},{12,10},{14,12},{1,15},{3,1}... | collective-permute-start | bytes 393224 | tf_op jit(solution)/shard_map/ppermute | solution.py:362
  18.7 0.0 collective-permute-start.3
  18.7 7.9 %collective-permute-done.3.y_below = f32[8,8,256]{2,1,0:T(8,128)S(1)} collective-permute-done((f32[8,8,256]{2,1,0:T(8,128)S(1)}, f32[8,8,256]{2,1,0:T(8,128)S(1)}, u32[]{:S(2)}, u32[]{:S(2)}) %collective-permute-start.3) | collective-permute-done | bytes 65568 | tf_op jit(solution)/shard_map/ppermute | solution.py:362
  26.6 1.0 %pack_z1.1 = f32[40,128]{1,0:T(8,128)S(1)} custom-call(s32[3]{0:T(128)S(1)} %pad_add_fusion.where, f32[8,32,256]{2,1,0:T(8,128)S(1)} %get-tuple-element.14.src, f32[2,3,8,32,256]{4,3,2,1,0:T(8,128)S(1)} %copy-done.1, f32[10,32,256]{2,1,0:T(8,128)S(1)} %collective-permute-done.above, f32[4,32,256]{2,1,0:T(8,128)S(1)} %collective-permute-done.1.below, ...), custom_call_target="tpu_custom_call" | custom-call | tf_op jit(solution)/shard_map/pack_z1/pallas_call | solution.py:338
  27.6 0.7 collective-permute-start.4
  28.3 3.2 %collective-permute-done.4.z_in = f32[40,128]{1,0:T(8,128)S(1)} collective-permute-done((f32[40,128]{1,0:T(8,128)S(1)}, f32[40,128]{1,0:T(8,128)S(1)}, u32[]{:S(2)}, u32[]{:S(2)}) %collective-permute-start.4) | collective-permute-done | bytes 20512 | tf_op jit(solution)/shard_map/ppermute | solution.py:362
  31.5 8.6 %raw.1 = (f32[4,2,32,256]{3,2,1,0:T(8,128)S(1)}, f32[4,2,32,256]{3,2,1,0:T(8,128)S(1)}) custom-call(f32[6]{0:T(128)S(1)} %copy-done.5, s32[6]{0:T(128)S(1)} %copy-done.6, s32[3]{0:T(128)S(1)} %pad_add_fusion.where, f32[8,32,256]{2,1,0:T(8,128)S(1)} %get-tuple-element.14.src, f32[2,3,8,32,256]{4,3,2,1,0:T(8,128)S(1)} %copy-done.1, ...), custom_call_target="tpu_custom_call" | custom-call | tf_op jit(solution)/shard_map/raw/pallas_call | solution.py:338
  40.1 0.0 copy-start.3
  40.1 0.0 collective-permute-start.5
  40.1 0.5 collective-permute-start.6
  40.6 3.4 %collective-permute-done.5.above = f32[4,2,32,256]{3,2,1,0:T(8,128)S(1)} collective-permute-done((f32[4,2,32,256]{3,2,1,0:T(8,128)S(1)}, f32[4,2,32,256]{3,2,1,0:T(8,128)S(1)}, u32[]{:S(2)}, u32[]{:S(2)}) %collective-permute-start.5) | collective-permute-done | bytes 262176 | tf_op jit(solution)/shard_map/ppermute | solution.py:362
  44.0 3.1 %collective-permute-done.6.below = f32[4,2,32,256]{3,2,1,0:T(8,128)S(1)} collective-permute-done((f32[4,2,32,256]{3,2,1,0:T(8,128)S(1)}, f32[4,2,32,256]{3,2,1,0:T(8,128)S(1)}, u32[]{:S(2)}, u32[]{:S(2)}) %collective-permute-start.6) | collective-permute-done | bytes 262176 | tf_op jit(solution)/shard_map/ppermute | solution.py:362
  47.2 0.9 %collective-permute-start.7 = (f32[16,8,256]{2,1,0:T(8,128)S(1)}, f32[16,8,256]{2,1,0:T(8,128)S(1)}, u32[]{:S(2)}, u32[]{:S(2)}) collective-permute-start(f32[16,8,256]{2,1,0:T(8,128)S(1)} %get-tuple-element.21), channel_id=1, source_target_pairs={{0,14},{2,0},{4,2},{6,4},{8,6},{10,8},{12,10},{14,12},{1,15},{3,1}... | collective-permute-start | bytes 393224 | tf_op jit(solution)/shard_map/ppermute | solution.py:362
  48.0 2.7 %collective-permute-start.8 = (f32[16,8,256]{2,1,0:T(8,128)S(1)}, f32[16,8,256]{2,1,0:T(8,128)S(1)}, u32[]{:S(2)}, u32[]{:S(2)}) collective-permute-start(f32[16,8,256]{2,1,0:T(8,128)S(1)} %get-tuple-element.22), channel_id=1, source_target_pairs={{0,2},{2,4},{4,6},{6,8},{8,10},{10,12},{12,14},{14,0},{1,3},{3,5},... | collective-permute-start | bytes 393224 | tf_op jit(solution)/shard_map/ppermute | solution.py:362
  50.8 2.9 %collective-permute-done.7.y_above = f32[16,8,256]{2,1,0:T(8,128)S(1)} collective-permute-done((f32[16,8,256]{2,1,0:T(8,128)S(1)}, f32[16,8,256]{2,1,0:T(8,128)S(1)}, u32[]{:S(2)}, u32[]{:S(2)}) %collective-permute-start.7) | collective-permute-done | bytes 131104 | tf_op jit(solution)/shard_map/ppermute | solution.py:362
  53.7 3.1 %collective-permute-done.8.y_below = f32[16,8,256]{2,1,0:T(8,128)S(1)} collective-permute-done((f32[16,8,256]{2,1,0:T(8,128)S(1)}, f32[16,8,256]{2,1,0:T(8,128)S(1)}, u32[]{:S(2)}, u32[]{:S(2)}) %collective-permute-start.8) | collective-permute-done | bytes 131104 | tf_op jit(solution)/shard_map/ppermute | solution.py:362
  56.8 0.8 %pack_z2.1 = f32[40,128]{1,0:T(8,128)S(1)} custom-call(s32[3]{0:T(128)S(1)} %pad_add_fusion.where, f32[4,2,32,256]{3,2,1,0:T(8,128)S(1)} %get-tuple-element.19.low, f32[4,2,32,256]{3,2,1,0:T(8,128)S(1)} %get-tuple-element.20.high, f32[4,2,32,256]{3,2,1,0:T(8,128)S(1)} %collective-permute-done.5.above, f32[4,2,32,256]{3,2,1,0:T(8,128)S(1)} %collective-permute-done.6.below, ...), custom_call_target="tpu_custom_call" | custom-call | tf_op jit(solution)/shard_map/pack_z2/pallas_call | solution.py:338
  57.6 0.6 collective-permute-start.9
  58.2 3.3 %collective-permute-done.9.z_in = f32[40,128]{1,0:T(8,128)S(1)} collective-permute-done((f32[40,128]{1,0:T(8,128)S(1)}, f32[40,128]{1,0:T(8,128)S(1)}, u32[]{:S(2)}, u32[]{:S(2)}) %collective-permute-start.9) | collective-permute-done | bytes 20512 | tf_op jit(solution)/shard_map/ppermute | solution.py:362
  61.5 7.9 %filter.1 = f32[2,8,32,256]{3,2,1,0:T(8,128)} custom-call(s32[3]{0:T(128)S(1)} %pad_add_fusion.where, s32[8,32,256]{2,1,0:T(8,128)S(1)} %copy-done.3, f32[4,2,32,256]{3,2,1,0:T(8,128)S(1)} %get-tuple-element.19.low, f32[4,2,32,256]{3,2,1,0:T(8,128)S(1)} %get-tuple-element.20.high, f32[4,2,32,256]{3,2,1,0:T(8,128)S(1)} %collective-permute-done.5.above, ...), custom_call_target="tpu_custom_call" | custom-call | tf_op jit(solution)/shard_map/filter/pallas_call | solution.py:338
  (10 shorter events, 0.0 us)
Async XLA Ops:
  0.0 1.4 %copy-start = (f32[2,3,8,32,256]{4,3,2,1,0:T(8,128)S(1)}, f32[2,3,8,32,256]{4,3,2,1,0:T(8,128)}, u32[]{:S(2)}) copy-start(f32[2,3,8,32,256]{4,3,2,1,0:T(8,128)} %modes.7) | copy-start | bytes 4718596
  1.4 0.9 %copy-start.2 = (s32[8,32,256]{2,1,0:T(8,128)S(1)}, s32[8,32,256]{2,1,0:T(8,128)}, u32[]{:S(2)}) copy-start(s32[8,32,256]{2,1,0:T(8,128)} %mask.3) | copy-start | bytes 786436
  2.4 0.9 %copy-start.4 = (f32[8,32,256]{2,1,0:T(8,128)S(1)}, f32[8,32,256]{2,1,0:T(8,128)}, u32[]{:S(2)}) copy-start(f32[8,32,256]{2,1,0:T(8,128)} %design.1) | copy-start | bytes 786436
  3.3 8.2 %copy-start.1 = (f32[2,3,8,32,256]{4,3,2,1,0:T(8,128)S(1)}, f32[2,3,8,32,256]{4,3,2,1,0:T(8,128)}, u32[]{:S(2)}) copy-start(f32[2,3,8,32,256]{4,3,2,1,0:T(8,128)} %modes.7) | copy-start | bytes 4718596
  3.4 8.2 %collective-permute-start = (f32[10,32,256]{2,1,0:T(8,128)S(1)}, f32[10,32,256]{2,1,0:T(8,128)S(1)}, u32[]{:S(2)}, u32[]{:S(2)}) collective-permute-start(f32[10,32,256]{2,1,0:T(8,128)S(1)} %get-tuple-element.15), channel_id=1, source_target_pairs={{0,112},{16,0},{32,16},{48,32},{64,48},{80,64},{96,80},{112,96},{1... | collective-permute-start | bytes 983048 | tf_op jit(solution)/shard_map/ppermute | solution.py:362
  5.9 5.6 %collective-permute-start.1 = (f32[4,32,256]{2,1,0:T(8,128)S(1)}, f32[4,32,256]{2,1,0:T(8,128)S(1)}, u32[]{:S(2)}, u32[]{:S(2)}) collective-permute-start(f32[4,32,256]{2,1,0:T(8,128)S(1)} %get-tuple-element.16), channel_id=1, source_target_pairs={{0,16},{16,32},{32,48},{48,64},{64,80},{80,96},{96,112},{112,0},{1... | collective-permute-start | bytes 393224 | tf_op jit(solution)/shard_map/ppermute | solution.py:362
  12.1 19.3 %copy-start.5 = (f32[6]{0:T(128)S(1)}, f32[6]{0:T(128)}, u32[]{:S(2)}) copy-start(f32[6]{0:T(128)} %eigenvalues.1) | copy-start | bytes 76
  12.1 19.3 %copy-start.6 = (s32[6]{0:T(128)S(1)}, s32[6]{0:T(128)}, u32[]{:S(2)}) copy-start(s32[6]{0:T(128)} %order.1) | copy-start | bytes 76
  12.1 14.4 %collective-permute-start.2 = (f32[16,8,256]{2,1,0:T(8,128)S(1)}, f32[16,8,256]{2,1,0:T(8,128)S(1)}, u32[]{:S(2)}, u32[]{:S(2)}) collective-permute-start(f32[16,8,256]{2,1,0:T(8,128)S(1)} %get-tuple-element.17), channel_id=1, source_target_pairs={{0,14},{2,0},{4,2},{6,4},{8,6},{10,8},{12,10},{14,12},{1,15},{3,1}... | collective-permute-start | bytes 393224 | tf_op jit(solution)/shard_map/ppermute | solution.py:362
  18.7 7.9 %collective-permute-start.3 = (f32[8,8,256]{2,1,0:T(8,128)S(1)}, f32[8,8,256]{2,1,0:T(8,128)S(1)}, u32[]{:S(2)}, u32[]{:S(2)}) collective-permute-start(f32[8,8,256]{2,1,0:T(8,128)S(1)} %get-tuple-element.18), channel_id=1, source_target_pairs={{0,2},{2,4},{4,6},{6,8},{8,10},{10,12},{12,14},{14,0},{1,3},{3,5},... | collective-permute-start | bytes 196616 | tf_op jit(solution)/shard_map/ppermute | solution.py:362
  27.6 3.9 %collective-permute-start.4 = (f32[40,128]{1,0:T(8,128)S(1)}, f32[40,128]{1,0:T(8,128)S(1)}, u32[]{:S(2)}, u32[]{:S(2)}) collective-permute-start(f32[40,128]{1,0:T(8,128)S(1)} %pack_z1.1), channel_id=1, source_target_pairs={{0,1},{1,0},{2,3},{3,2},{4,5},{5,4},{6,7},{7,6},{8,9},{9,8},{10,11... | collective-permute-start | bytes 61448 | tf_op jit(solution)/shard_map/ppermute | solution.py:362
  40.1 21.4 %copy-start.3 = (s32[8,32,256]{2,1,0:T(8,128)S(1)}, s32[8,32,256]{2,1,0:T(8,128)}, u32[]{:S(2)}) copy-start(s32[8,32,256]{2,1,0:T(8,128)} %mask.3) | copy-start | bytes 786436
  40.1 3.9 %collective-permute-start.5 = (f32[4,2,32,256]{3,2,1,0:T(8,128)S(1)}, f32[4,2,32,256]{3,2,1,0:T(8,128)S(1)}, u32[]{:S(2)}, u32[]{:S(2)}) collective-permute-start(f32[4,2,32,256]{3,2,1,0:T(8,128)S(1)} %get-tuple-element.19.low), channel_id=1, source_target_pairs={{0,112},{16,0},{32,16},{48,32},{64,48},{80,64},{96,80},{112,96},{1... | collective-permute-start | bytes 786440 | tf_op jit(solution)/shard_map/ppermute | solution.py:362
  40.1 7.0 %collective-permute-start.6 = (f32[4,2,32,256]{3,2,1,0:T(8,128)S(1)}, f32[4,2,32,256]{3,2,1,0:T(8,128)S(1)}, u32[]{:S(2)}, u32[]{:S(2)}) collective-permute-start(f32[4,2,32,256]{3,2,1,0:T(8,128)S(1)} %get-tuple-element.20.high), channel_id=1, source_target_pairs={{0,16},{16,32},{32,48},{48,64},{64,80},{80,96},{96,112},{112,0},{1... | collective-permute-start | bytes 786440 | tf_op jit(solution)/shard_map/ppermute | solution.py:362
  47.2 6.5 %collective-permute-start.7 = (f32[16,8,256]{2,1,0:T(8,128)S(1)}, f32[16,8,256]{2,1,0:T(8,128)S(1)}, u32[]{:S(2)}, u32[]{:S(2)}) collective-permute-start(f32[16,8,256]{2,1,0:T(8,128)S(1)} %get-tuple-element.21), channel_id=1, source_target_pairs={{0,14},{2,0},{4,2},{6,4},{8,6},{10,8},{12,10},{14,12},{1,15},{3,1}... | collective-permute-start | bytes 393224 | tf_op jit(solution)/shard_map/ppermute | solution.py:362
  48.0 8.8 %collective-permute-start.8 = (f32[16,8,256]{2,1,0:T(8,128)S(1)}, f32[16,8,256]{2,1,0:T(8,128)S(1)}, u32[]{:S(2)}, u32[]{:S(2)}) collective-permute-start(f32[16,8,256]{2,1,0:T(8,128)S(1)} %get-tuple-element.22), channel_id=1, source_target_pairs={{0,2},{2,4},{4,6},{6,8},{8,10},{10,12},{12,14},{14,0},{1,3},{3,5},... | collective-permute-start | bytes 393224 | tf_op jit(solution)/shard_map/ppermute | solution.py:362
  57.6 3.9 %collective-permute-start.9 = (f32[40,128]{1,0:T(8,128)S(1)}, f32[40,128]{1,0:T(8,128)S(1)}, u32[]{:S(2)}, u32[]{:S(2)}) collective-permute-start(f32[40,128]{1,0:T(8,128)S(1)} %pack_z2.1), channel_id=1, source_target_pairs={{0,1},{1,0},{2,3},{3,2},{4,5},{5,4},{6,7},{7,6},{8,9},{9,8},{10,11... | collective-permute-start | bytes 61448 | tf_op jit(solution)/shard_map/ppermute | solution.py:362

commit v2 on v0

v2 whole, which is shorter than its diff:
```python
import jax
import jax.numpy as jnp
from jax import lax
from jax.experimental import pallas as pl
from jax.experimental.pallas import tpu as pltpu
from jax.sharding import PartitionSpec as P

ITERS = 4
MODES = 2
CX, CY, CZ = 8, 32, 256
W = ITERS
PX = CX + 2 * W
PY = CY + 8
NODES = CX + 1
LANES = 128

poisson = 0.3
radius_sq = 3.0
stiff_floor = 0.001
LAME = poisson / ((1.0 + poisson) * (1.0 - 2.0 * poisson))
SHEAR = 0.5 / (1.0 + poisson)

F32 = jnp.float32


def iota(shape, dim):
    return lax.broadcasted_iota(jnp.int32, shape, dim)


def pos(ref):
    return ref[0], ref[1], ref[2]


def sub_lane():
    return iota((8, LANES), 0), iota((8, LANES), 1)


def total_of(terms):
    terms = [t for t in terms if t is not None]
    while len(terms) > 1:
        pairs = [terms[i] + terms[i + 1] for i in range(0, len(terms) - 1, 2)]
        terms = pairs + ([terms[-1]] if len(terms) % 2 else [])
    return terms[0]


def scales(count, inside):
    outside = jnp.zeros(count.shape, F32)
    end = jnp.where(inside, radius_sq / (1.0 + radius_sq * (count + 1.0)), 0.0)
    mid = jnp.where(inside, radius_sq / (1.0 + radius_sq * (count + 2.0)), 0.0)
    return outside, end, mid


def yz_scales(y, z, gy, gz):
    y, z = y + gy * CY, z + gz * CZ
    inside = (y >= 0) & (y < 8 * CY)
    count = 4.0
    for place, last in ((y, 8 * CY - 1), (z, 2 * CZ - 1)):
        count = count - (place == 0).astype(F32) - (place == last).astype(F32)
    return scales(count, inside)


def kind_of(gx, plane):
    x = gx * CX + plane - W
    out = (x < 0) | (x > 8 * CX - 1)
    end = (x == 0) | (x == 8 * CX - 1)
    return jnp.where(out, 0, jnp.where(end, 1, 2))


def fill_bulk(table, gy, gz):
    shape = (CY, CZ)
    for i, part in enumerate(yz_scales(iota(shape, 0), iota(shape, 1), gy, gz)):
        table[i] = part


def fill_strips(table, gy, gz):
    shape = (16, CZ)
    row = iota(shape, 0)
    top = jnp.where(row < 4, row + CY, row + CY - 8)
    bottom = jnp.where(row < 12, row - 8, row - 16)
    for i, part in enumerate(yz_scales(jnp.where(row < 8, top, bottom), iota(shape, 1), gy, gz)):
        table[i] = part


def strip_scale(gx, gy):
    shape = (PY, LANES)
    row = iota(shape, 0)
    y = jnp.where(row < CY + W, row, row - PY) + gy * CY
    x = gx * CX - W + lax.div(iota(shape, 1), 8)
    inside = (y >= 0) & (y < 8 * CY) & (x >= 0) & (x < 8 * CX)
    count = 6.0
    for place, last in ((y, 8 * CY - 1), (x, 8 * CX - 1)):
        count = count - (place == 0).astype(F32) - (place == last).astype(F32)
    return jnp.where(inside, radius_sq / (1.0 + radius_sq * count), 0.0)


def tiles_of(ref, index, rows, cols):
    return [
        [ref[index + (slice(8 * i, 8 * i + 8), slice(LANES * j, LANES * j + LANES))] for j in range(cols)]
        for i in range(rows)
    ]


def along_lanes(row, lane):
    right = [pltpu.roll(t, 1, 1) for t in row]
    left = [pltpu.roll(t, LANES - 1, 1) for t in row]
    out = []
    for j in range(len(row)):
        before = right[j - 1] if j else 0.0
        after = left[j + 1] if j + 1 < len(row) else 0.0
        out.append(
            jnp.where(lane == 0, before, right[j]) + jnp.where(lane == LANES - 1, after, left[j])
        )
    return out


def along_rows(tiles, sub):
    rows, cols = len(tiles), len(tiles[0])
    down = [[pltpu.roll(t, 1, 0) for t in row] for row in tiles]
    up = [[pltpu.roll(t, 7, 0) for t in row] for row in tiles]
    out = []
    for i in range(rows):
        line = []
        for j in range(cols):
            before = down[i - 1][j] if i else 0.0
            after = up[i + 1][j] if i + 1 < rows else 0.0
            line.append(jnp.where(sub == 0, before, down[i][j]) + jnp.where(sub == 7, after, up[i][j]))
        out.append(line)
    return out


def send_edge(edges, index, tile, p, gz, lane):
    turned = pltpu.roll(tile, lax.rem(8 * p + 5 - 2 * gz, LANES), 1)
    edges[index] = jnp.where(lane == 8 * p + 4 - gz, turned, edges[index])


def bulk_sweeps(fields, where, table, source, states, ends, edges, out):
    gx, gy, gz = where
    sub, lane = sub_lane()
    sb = states[0]
    edges[...] = jnp.zeros(edges.shape, F32)
    ends[...] = jnp.zeros(ends.shape, F32)
    for p in range(PX):
        kind = kind_of(gx, p)
        for m in range(fields):
            for i in range(CY // 8):
                rows = slice(8 * i, 8 * i + 8)
                sb[m, p, rows, :] = source(m, p, i) * (table[kind, rows, :] * (1.0 / radius_sq))
    for k in range(ITERS):
        old = states[0] if k == 0 else states[1 + (k - 1) % 2]
        new = states[1 + k % 2]

        def body(p, carry, old=old, new=new, k=k):
            scale = tiles_of(table, (kind_of(gx, p),), CY // 8, 2)
            for m in range(fields):
                mid = tiles_of(old, (m, p), CY // 8, 2)
                low = tiles_of(old, (m, p - 1), CY // 8, 2)
                high = tiles_of(old, (m, p + 1), CY // 8, 2)
                base = tiles_of(sb, (m, p), CY // 8, 2)
                yy = along_rows(mid, sub)
                for i in range(CY // 8):
                    zz = along_lanes(mid[i], lane)
                    rows = slice(8 * i, 8 * i + 8)
                    for j in range(2):
                        total = (low[i][j] + high[i][j]) + (yy[i][j] + zz[j])
                        value = base[i][j] + scale[i][j] * total
                        cols = slice(LANES * j, LANES * j + LANES)
                        if k + 1 < ITERS:
                            new[m, p, rows, cols] = value
                        else:
                            out[m, p - W, rows, cols] = value
                    edge = jnp.where(gz == 0, mid[i][1], mid[i][0])
                    send_edge(edges, (m, k, rows), edge, p, gz, lane)
                for j in range(2):
                    cols = slice(LANES * j, LANES * j + LANES)
                    ends[m, k, p, 0, 0:1, cols] = mid[CY // 8 - 1][j][7:8]
                    ends[m, k, p, 1, 0:1, cols] = mid[0][j][0:1]
            return carry

        lax.fori_loop(k + 1, PX - 1 - k, body, 0)


def strip_sweeps(fields, where, table, source, ends, states, edges, out):
    gx, gy, gz = where
    sub, lane = sub_lane()
    sb = states[0]
    edges[...] = jnp.zeros(edges.shape, F32)
    wide = iota((8, CZ), 0)
    for p in range(PX):
        kind = kind_of(gx, p)
        for m in range(fields):
            halo = source(m, p) * (1.0 / radius_sq)
            sb[m, p, 0:8, :] = jnp.where(wide < 4, halo * table[kind, 0:8, :], 0.0)
            sb[m, p, 8:16, :] = jnp.where(wide < 4, 0.0, halo * table[kind, 8:16, :])
    for k in range(ITERS):
        old = states[0] if k == 0 else states[1 + (k - 1) % 2]
        new = states[1 + k % 2]

        def body(p, carry, old=old, new=new, k=k):
            scale = tiles_of(table, (kind_of(gx, p),), 2, 2)
            for m in range(fields):
                mid = tiles_of(old, (m, p), 2, 2)
                low = tiles_of(old, (m, p - 1), 2, 2)
                high = tiles_of(old, (m, p + 1), 2, 2)
                base = tiles_of(sb, (m, p), 2, 2)
                for i in range(2):
                    rows = slice(8 * i, 8 * i + 8)
                    zz = along_lanes(mid[i], lane)
                    for j in range(2):
                        cols = slice(LANES * j, LANES * j + LANES)
                        end = jnp.broadcast_to(ends[m, k, p, i, 0:1, cols], (8, LANES))
                        down = pltpu.roll(mid[i][j], 1, 0)
                        up = pltpu.roll(mid[i][j], 7, 0)
                        if i == 0:
                            down = jnp.where(sub == 4, 0.0, down) + jnp.where(sub == 0, end, 0.0)
                        else:
                            up = jnp.where(sub == 3, 0.0, up) + jnp.where(sub == 7, end, 0.0)
                        total = (low[i][j] + high[i][j]) + (down + up) + zz[j]
                        value = base[i][j] + scale[i][j] * total
                        if k + 1 < ITERS:
                            new[m, p, rows, cols] = value
                        else:
                            out[m, p - W, rows, cols] = value
                    edge = jnp.where(gz == 0, mid[i][1], mid[i][0])
                    send_edge(edges, (m, k, rows), edge, p, gz, lane)
            return carry

        lax.fori_loop(k + 1, PX - 1 - k, body, 0)


def z_sweeps(m, scale, halo, bulk_edges, strip_edges):
    sub = iota((8, LANES), 0)
    column = lax.rem(iota((PY, LANES), 1), 8)
    base = halo * (scale * (1.0 / radius_sq))
    state = base
    for k in range(ITERS):
        top, bottom = strip_edges[m, k, 0:8, :], strip_edges[m, k, 8:16, :]
        own = bulk_edges[m, k]
        fed = jnp.concatenate(
            [
                own[0:8] + jnp.where(sub < 4, bottom, 0.0),
                own[8 : CY - 8],
                own[CY - 8 : CY] + jnp.where(sub < 4, 0.0, top),
                jnp.where(sub < 4, top, bottom),
            ],
            axis=0,
        )
        total = pltpu.roll(state, 8, 1) + pltpu.roll(state, LANES - 8, 1)
        total = total + pltpu.roll(state, 1, 0) + pltpu.roll(state, PY - 1, 0)
        total = total + jnp.where(column == 0, 0.0, pltpu.roll(state, 1, 1))
        total = total + jnp.where(column == 7, 0.0, pltpu.roll(state, LANES - 1, 1))
        state = base + scale * (total + fed)
    return state


def result_tile(m, x, i, j, bulk, strips, z_state, beside, sub):
    rows, cols = slice(8 * i, 8 * i + 8), slice(LANES * j, LANES * j + LANES)
    value = bulk[m, x, rows, cols]
    if i == 0:
        value = value + jnp.where(sub < 4, strips[m, x, 8:16, cols], 0.0)
    if i == CY // 8 - 1:
        value = value + jnp.where(sub < 4, 0.0, strips[m, x, 0:8, cols])
    turned = pltpu.roll(z_state[rows], (LANES - 4 - 8 * (x + W)) % LANES, 1)
    return value + jnp.where(beside[j], turned, 0.0)


def beside_halo(gz, lane):
    return (lane < 4 * gz), (lane >= LANES - 4 * (1 - gz))


def pack_strip(gz, tile, p, acc, lane):
    first = 8 * p + 4 * gz
    turned = pltpu.roll(tile, (8 * p + 4) % LANES, 1)
    return jnp.where((lane >= first) & (lane < first + 4), turned, acc)


def edge_tiles(gz):
    return pl.ds(pl.multiple_of((1 - gz) * LANES, LANES), LANES)


def energy_terms(prev, cur):
    (paa, pad, pda, pdd), (caa, cad, cda, cdd) = prev, cur
    u, v, w = 0, 1, 2
    aad = [cad[i] + pad[i] for i in range(3)]
    ada = [cda[i] + pda[i] for i in range(3)]
    add = [cdd[i] + pdd[i] for i in range(3)]
    daa = [caa[i] - paa[i] for i in range(3)]
    dad = [cad[i] - pad[i] for i in range(3)]
    dda = [cda[i] - pda[i] for i in range(3)]
    ddd = [cdd[i] - pdd[i] for i in range(3)]

    def sq(x):
        return x * x

    trace = sq(daa[u] + ada[v] + aad[w])
    lines = sq(dda[v] + dad[w]) + sq(dda[u] + add[w]) + sq(dad[u] + add[v])
    diag = sq(daa[u]) + sq(ada[v]) + sq(aad[w])
    shear = sq(ada[u] + daa[v]) + sq(aad[u] + daa[w]) + sq(aad[v] + ada[w])
    mixed = sq(dda[u]) + sq(dda[v]) + sq(dad[u]) + sq(dad[w]) + sq(add[v]) + sq(add[w])
    cross = sq(add[u] + dad[v]) + sq(add[u] + dda[w]) + sq(dad[v] + dda[w])
    cubic = sq(ddd[u]) + sq(ddd[v]) + sq(ddd[w])
    return (
        LAME * (trace + lines * (1.0 / 3.0))
        + SHEAR * (2.0 * diag + shear + mixed + cross * (1.0 / 3.0))
        + ((LAME + 4.0 * SHEAR) / 9.0) * cubic
    )


def y_parts(pairs):
    aa = [a0 + a1 for a0, d0, a1, d1 in pairs]
    ad = [d0 + d1 for a0, d0, a1, d1 in pairs]
    da = [a1 - a0 for a0, d0, a1, d1 in pairs]
    dd = [d1 - d0 for a0, d0, a1, d1 in pairs]
    return aa, ad, da, dd


def mass_of(parts):
    return total_of([x * x for part in parts for x in part])


def z_pair(here):
    after = pltpu.roll(here, CZ - 1, 1)
    return here + after, after - here


def own_parts(load, chunk):
    sub = iota((8, CZ), 0)
    pairs = []
    for c in range(3):
        a0, d0 = z_pair(load(c, 8 * chunk))
        following = min(chunk + 1, CY // 8 - 1)
        a1, d1 = z_pair(load(c, 8 * following))

        def next_row(t, n):
            return jnp.where(sub == 7, pltpu.roll(n, 7, 0), pltpu.roll(t, 7, 0))

        pairs.append((a0, d0, next_row(a0, a1), next_row(d0, d1)))
    return y_parts(pairs)


def pack_columns(load, lane):
    first = jnp.zeros((CY, LANES), F32)
    last = first
    for m in range(MODES):
        for c in range(3):
            for x in range(CX):
                to = 32 * m + NODES * c + x
                here = lane == to
                first = jnp.where(here, pltpu.roll(load(m, c, x, 0), to, 1), first)
                last = jnp.where(here, pltpu.roll(load(m, c, x, 1), to + 1, 1), last)
    return first, last


def with_rims(packed, above, y_above, keep_x, keep_y, last):
    cols = slice(CZ - LANES, CZ) if last else slice(0, LANES)
    lane = iota((CY, LANES), 1)
    sub, short = sub_lane()
    rim = jnp.zeros((8, LANES), F32)
    for m in range(MODES):
        for c in range(3):
            to = 32 * m + NODES * c + CX
            turned = pltpu.roll(above[W + 3 * m + c, :, cols], to + last, 1)
            packed = jnp.where(lane == to, turned * keep_x, packed)
            for x in range(NODES):
                n = NODES * c + x
                to = 32 * m + n
                row = y_above[8 + 4 * m + n // 8, n % 8 : n % 8 + 1, cols]
                turned = pltpu.roll(jnp.broadcast_to(row, (8, LANES)), to + last, 1)
                rim = jnp.where((short == to) & (sub == 0), turned, rim)
    return jnp.concatenate([packed, rim * keep_y], axis=0)


def pack_x1(design, mask, modes, src, down, up):
    for x in range(CX):
        plane = design[x] * mask[x].astype(F32)
        src[x] = plane
        if x < W:
            down[x] = plane
        if x >= CX - W:
            up[x - (CX - W)] = plane
    for m in range(MODES):
        for c in range(3):
            down[W + 3 * m + c] = modes[m, c, 0]


def energy_kernel(modes, stiff, mass, columns):
    lane = iota((CY, LANES), 1)
    columns[0], columns[1] = pack_columns(
        lambda m, c, x, j: modes[m, c, x, :, LANES * j : LANES * j + LANES], lane
    )

    def mode_step(m, carry):
        for chunk in range(CY // 8):
            rows = slice(8 * chunk, 8 * chunk + 8)
            prev = prev_mass = None
            for x in range(CX):
                cur = own_parts(lambda c, r: modes[m, c, x, r : r + 8, :], chunk)
                cur_mass = mass_of(cur)
                if x:
                    stiff[m, x - 1, rows, :] = energy_terms(prev, cur)
                    mass[m, x - 1, rows, :] = cur_mass + prev_mass
                prev, prev_mass = cur, cur_mass
        return carry

    lax.fori_loop(0, MODES, mode_step, 0)


def pick_plane(own, above, below, p):
    if p < W:
        return below, p
    if p < W + CX:
        return own, p - W
    return above, p - W - CX


def pack_y1(where, src, modes, above, below, down, up):
    gx, gy, gz = pos(where)
    low = iota((8, CZ), 0) < 4
    for q in range(8):
        a, i = pick_plane(src, above, below, q)
        b, j = pick_plane(src, above, below, q + 8)
        down[q] = jnp.where(low, a[i, 0:8, :], pltpu.roll(b[j, 0:8, :], 4, 0))
        up[q] = jnp.where(low, pltpu.roll(b[j, 24:32, :], 4, 0), a[i, 24:32, :])
    keep = jnp.where(gx < 7, 1.0, 0.0)
    for m in range(MODES):
        for c in range(3):
            for x in range(NODES):
                n = c * NODES + x
                if x < CX:
                    row = modes[m, c, x, 0:1, :]
                else:
                    row = above[W + 3 * m + c, 0:1, :] * keep
                down[8 + 4 * m + n // 8, n % 8 : n % 8 + 1, :] = row
        down[8 + 4 * m + 3, 3:8, :] = jnp.zeros((5, CZ), F32)


def bulk_kernel1(
    where, src, modes, above, below, bulk, ends, edges, stiff, mass, table, sb, one, two
):
    at = pos(where)
    gx, gy, gz = at
    fill_bulk(table, gy, gz)

    def source(m, p, i):
        a, at_plane = pick_plane(src, above, below, p)
        return a[at_plane, 8 * i : 8 * i + 8, :]

    bulk_sweeps(1, at, table, source, (sb, one, two), ends, edges, bulk)
    keep = jnp.where(gx < 7, 1.0, 0.0)
    for m in range(MODES):
        for chunk in range(CY // 8):
            rows = slice(8 * chunk, 8 * chunk + 8)
            prev = own_parts(lambda c, r: modes[m, c, CX - 1, r : r + 8, :], chunk)
            cur = own_parts(lambda c, r: above[W + 3 * m + c, r : r + 8, :] * keep, chunk)
            stiff[m, rows, :] = energy_terms(prev, cur)
            mass[m, rows, :] = mass_of(cur) + mass_of(prev)


def halo_tile(y_above, y_below, p, lanes=slice(None)):
    a, b = y_above[p % 8, :, lanes], y_below[p % 8, :, lanes]
    if p >= 8:
        a, b = pltpu.roll(a, 4, 0), pltpu.roll(b, 4, 0)
    return jnp.where(iota(a.shape, 0) < 4, a, b)


def pack_z1(where, src, columns, above, below, y_above, y_below, out):
    gx, gy, gz = pos(where)
    edge = edge_tiles(gz)
    lane = iota((PY, LANES), 1)
    acc = jnp.zeros((PY, LANES), F32)
    for p in range(PX):
        a, i = pick_plane(src, above, below, p)
        tile = jnp.concatenate([a[i, :, edge], halo_tile(y_above, y_below, p, edge)], axis=0)
        acc = pack_strip(gz, tile, p, acc, lane)
    out[0] = acc
    keep_x = jnp.where(gx < 7, 1.0, 0.0)
    keep_y = jnp.where(gy < 7, 1.0, 0.0)
    out[1] = with_rims(columns[0], above, y_above, keep_x, keep_y, 0)


def strip_kernel1(
    where, modes, columns, above, y_above, y_below, ends,
    strips, edges, rim, packed, table, sb, one, two, near, far,
):
    at = pos(where)
    gx, gy, gz = at
    fill_strips(table, gy, gz)
    strip_sweeps(
        1, at, table, lambda m, p: halo_tile(y_above, y_below, p), ends, (sb, one, two), edges, strips
    )
    keep_x = jnp.where(gx < 7, 1.0, 0.0)
    keep_y = jnp.where(gy < 7, 1.0, 0.0)
    packed[...] = with_rims(columns[1], above, y_above, keep_x, keep_y, 1)
    for m in range(MODES):
        for c in range(3):
            for x in range(NODES):
                n = c * NODES + x
                row = above[W + 3 * m + c, CY - 1 : CY, :] * keep_x
                if x < CX:
                    row = modes[m, c, x, CY - 1 : CY, :]
                near[c, x : x + 1, :] = row
                far[c, x : x + 1, :] = (
                    y_above[8 + 4 * m + n // 8, n % 8 : n % 8 + 1, :] * keep_y
                )

        def parts(first):
            pairs = []
            for c in range(3):
                a0, d0 = z_pair(near[c, first : first + 8, :])
                a1, d1 = z_pair(far[c, first : first + 8, :])
                pairs.append((a0, d0, a1, d1))
            return y_parts(pairs)

        prev, cur = parts(0), parts(1)
        rim[m, 0] = energy_terms(prev, cur)
        rim[m, 1] = mass_of(cur) + mass_of(prev)


def raw_kernel(
    eigenvalues, order, where, z_in, packed, bulk, bulk_edges, strips, strip_edges,
    stiff, mass, stiff7, mass7, rim, low, high,
):
    gx, gy, gz = pos(where)
    sub, lane = sub_lane()
    z_state = z_sweeps(0, strip_scale(gx, gy), z_in[0], bulk_edges, strip_edges)
    beside = beside_halo(gz, lane)

    near, far = packed[...], z_in[1] * jnp.where(gz < 1, 1.0, 0.0)
    a0, d0 = near + far, far - near
    a1, d1 = pltpu.roll(a0, PY - 1, 0), pltpu.roll(d0, PY - 1, 0)
    parts = [(x[0][0:CY]) for x in y_parts([(a0, d0, a1, d1)])]

    def turned(t, by):
        return pltpu.roll(t, (LANES - by) % LANES, 1) if by else t

    prev = [[turned(t, NODES * c) for c in range(3)] for t in parts]
    cur = [[turned(t, NODES * c + 1) for c in range(3)] for t in parts]
    column_stiff = energy_terms(prev, cur)
    column_mass = mass_of(cur) + mass_of(prev)

    factor = 3.0 * (1.0 - stiff_floor) / 16.0
    lams = [eigenvalues[order[m]] * (0.125 * 0.25) for m in range(MODES)]
    for x in range(CX):
        for i in range(CY // 8):
            rows = slice(8 * i, 8 * i + 8)
            for j in range(2):
                cols = slice(LANES * j, LANES * j + LANES)
                phys = result_tile(0, x, i, j, bulk, strips, z_state, beside, sub)
                phys = (factor * phys) * phys
                for m in range(MODES):
                    if x < CX - 1:
                        k, e = stiff[m, x, rows, cols], mass[m, x, rows, cols]
                    else:
                        k, e = stiff7[m, rows, cols], mass7[m, rows, cols]
                    if i == CY // 8 - 1:
                        k = jnp.where(sub == 7, jnp.broadcast_to(rim[m, 0, x : x + 1, cols], (8, LANES)), k)
                        e = jnp.where(sub == 7, jnp.broadcast_to(rim[m, 1, x : x + 1, cols], (8, LANES)), e)
                    if j == 1:
                        by = LANES - 1 - (32 * m + x)
                        k = jnp.where(lane == LANES - 1, pltpu.roll(column_stiff[rows], by, 1), k)
                        e = jnp.where(lane == LANES - 1, pltpu.roll(column_mass[rows], by, 1), e)
                    raw = phys * k - lams[m] * e
                    if x < W:
                        low[x, m, rows, cols] = raw
                    else:
                        high[x - W, m, rows, cols] = raw


def raw_plane(low, high, above, below, p):
    if p < W:
        return below, p
    if p < 2 * W:
        return low, p - W
    if p < 3 * W:
        return high, p - 2 * W
    return above, p - 3 * W


def pack_y2(low, high, above, below, down, up):
    first = iota((8, CZ), 0) < 4
    for p in range(PX):
        a, i = raw_plane(low, high, above, below, p)
        down[p] = jnp.where(first, a[i, 0, 0:8, :], pltpu.roll(a[i, 1, 0:8, :], 4, 0))
        up[p] = jnp.where(first, pltpu.roll(a[i, 0, 24:32, :], 4, 0), a[i, 1, 24:32, :])


def raw_halo(y_above, y_below, m, p, lanes=slice(None)):
    a, b = y_above[p, :, lanes], y_below[p, :, lanes]
    if m == 0:
        b = pltpu.roll(b, 4, 0)
    else:
        a = pltpu.roll(a, 4, 0)
    return jnp.where(iota(a.shape, 0) < 4, a, b)


def bulk_kernel2(where, low, high, above, below, bulk, ends, edges, table, sb, one, two):
    at = pos(where)
    fill_bulk(table, at[1], at[2])

    def source(m, p, i):
        a, at_plane = raw_plane(low, high, above, below, p)
        return a[at_plane, m, 8 * i : 8 * i + 8, :]

    bulk_sweeps(MODES, at, table, source, (sb, one, two), ends, edges, bulk)


def pack_z2(where, low, high, above, below, y_above, y_below, out):
    gx, gy, gz = pos(where)
    edge = edge_tiles(gz)
    lane = iota((PY, LANES), 1)
    for m in range(MODES):
        acc = jnp.zeros((PY, LANES), F32)
        for p in range(PX):
            a, i = raw_plane(low, high, above, below, p)
            halo = raw_halo(y_above, y_below, m, p, edge)
            acc = pack_strip(gz, jnp.concatenate([a[i, m, :, edge], halo], axis=0), p, acc, lane)
        out[m] = acc


def strip_kernel2(where, y_above, y_below, ends, strips, edges, table, sb, one, two):
    at = pos(where)
    fill_strips(table, at[1], at[2])

    def source(m, p):
        return raw_halo(y_above, y_below, m, p)

    strip_sweeps(MODES, at, table, source, ends, (sb, one, two), edges, strips)


def final_kernel(where, mask, z_in, bulk, bulk_edges, strips, strip_edges, out):
    gx, gy, gz = pos(where)
    sub, lane = sub_lane()
    beside = beside_halo(gz, lane)
    scale = strip_scale(gx, gy)
    for m in range(MODES):
        z_state = z_sweeps(m, scale, z_in[m], bulk_edges, strip_edges)
        for x in range(CX):
            for i in range(CY // 8):
                rows = slice(8 * i, 8 * i + 8)
                for j in range(2):
                    cols = slice(LANES * j, LANES * j + LANES)
                    value = result_tile(m, x, i, j, bulk, strips, z_state, beside, sub)
                    out[m, x, rows, cols] = value * mask[x, rows, cols].astype(F32)


SMEM = pl.BlockSpec(memory_space=pltpu.SMEM)


def whole(x):
    return pl.BlockSpec(x.shape, lambda i: (0,) * x.ndim)


def call(kernel, name, outs, args, specs=None, scratch=(), flops=0):
    specs = specs or {}
    shapes = tuple(jax.ShapeDtypeStruct(s, F32) for s in outs)
    return pl.pallas_call(
        kernel,
        grid=(1,),
        out_shape=shapes if len(shapes) > 1 else shapes[0],
        in_specs=[specs.get(i, SMEM if a.ndim == 1 else whole(a)) for i, a in enumerate(args)],
        scratch_shapes=[pltpu.VMEM(s, F32) for s in scratch],
        compiler_params=pltpu.CompilerParams(vmem_limit_bytes=24 * 1024 * 1024),
        cost_estimate=pl.CostEstimate(flops=flops, bytes_accessed=2_000_000, transcendentals=0),
        name=name,
    )(*args)


def ring(axis, step):
    size = lax.axis_size(axis)
    return [(i, (i + step) % size) for i in range(size)]


def shift(x, axis, step):
    return lax.ppermute(x, axis, ring(axis, step))


def sweep_outs(fields):
    return (
        [(fields, CX, CY, CZ), (fields, ITERS, PX, 2, 1, CZ), (fields, ITERS, CY, LANES)],
        [(3, CY, CZ)] + [(fields, PX, CY, CZ)] * 3,
        [(fields, CX, 16, CZ), (fields, ITERS, 16, LANES)],
        [(3, 16, CZ)] + [(fields, PX, 16, CZ)] * 3,
    )


def local(mode_fields, design, solid_mask, eigenvalues, mode_order):
    where = jnp.stack([lax.axis_index(a) for a in ("gx", "gy", "gz")]).astype(jnp.int32)
    bulk_outs, bulk_scratch, strip_outs, strip_scratch = sweep_outs(1)

    block = pl.BlockSpec((MODES, 3, 1, CY, CZ), lambda i: (0, 0, 0, 0, 0))
    src, down, up = call(
        pack_x1, "pack_x1", [(CX, CY, CZ), (W + 6, CY, CZ), (W, CY, CZ)],
        (design, solid_mask, mode_fields), {2: block},
    )
    above, below = shift(down, "gx", -1), shift(up, "gx", 1)
    field = (MODES, CX - 1, CY, CZ)
    stiff, mass, columns = call(
        energy_kernel, "energy", [field, field, (2, CY, LANES)], (mode_fields,), flops=40_000_000
    )

    block = pl.BlockSpec((MODES, 3, CX, 8, CZ), lambda i: (0, 0, 0, 0, 0))
    down, up = call(
        pack_y1, "pack_y1", [(16, 8, CZ), (8, 8, CZ)],
        (where, src, mode_fields, above, below), {2: block},
    )
    y_above, y_below = shift(down, "gy", -1), shift(up, "gy", 1)
    plane = (MODES, CY, CZ)
    bulk, ends, bulk_edges, stiff7, mass7 = call(
        bulk_kernel1, "bulk1", bulk_outs + [plane, plane],
        (where, src, mode_fields, above, below), scratch=bulk_scratch, flops=30_000_000,
    )

    edge = call(
        pack_z1, "pack_z1", [(2, PY, LANES)], (where, src, columns, above, below, y_above, y_below)
    )
    z_in = shift(edge, "gz", 1)
    strips, strip_edges, rim, packed = call(
        strip_kernel1, "strips1", strip_outs + [(MODES, 2, 8, CZ), (PY, LANES)],
        (where, mode_fields, columns, above, y_above, y_below, ends),
        scratch=strip_scratch + [(3, 16, CZ)] * 2, flops=20_000_000,
    )
    low, high = call(
        raw_kernel, "raw", [(W, MODES, CY, CZ)] * 2,
        (eigenvalues, mode_order, where, z_in, packed, bulk, bulk_edges, strips, strip_edges,
         stiff, mass, stiff7, mass7, rim),
    )

    bulk_outs, bulk_scratch, strip_outs, strip_scratch = sweep_outs(MODES)
    above, below = shift(low, "gx", -1), shift(high, "gx", 1)
    planes = (low, high, above, below)
    down, up = call(pack_y2, "pack_y2", [(PX, 8, CZ)] * 2, planes)
    y_above, y_below = shift(down, "gy", -1), shift(up, "gy", 1)
    bulk, ends, bulk_edges = call(
        bulk_kernel2, "bulk2", bulk_outs, (where, *planes), scratch=bulk_scratch, flops=40_000_000
    )
    edge = call(pack_z2, "pack_z2", [(MODES, PY, LANES)], (where, *planes, y_above, y_below))
    z_in = shift(edge, "gz", 1)
    strips, strip_edges = call(
        strip_kernel2, "strips2", strip_outs, (where, y_above, y_below, ends),
        scratch=strip_scratch, flops=20_000_000,
    )
    return call(
        final_kernel, "final", [(MODES, CX, CY, CZ)],
        (where, solid_mask, z_in, bulk, bulk_edges, strips, strip_edges),
    )


def solution(mesh):
    return jax.shard_map(
        local,
        mesh=mesh,
        in_specs=(
            P(None, None, "gx", "gy", "gz"),
            P("gx", "gy", "gz"),
            P("gx", "gy", "gz"),
            P(),
            P(),
        ),
        out_specs=P(None, "gx", "gy", "gz"),
        check_vma=False,
    )
```

time: 541 us -> 70.9 us (0.13); the launches traced: 534 us -> 70.5 us
  starting transfers between devices: 152 us -> 14.2 us
  other arithmetic: 135 us -> 0.08 us
  local copies, waits for them, and re-layouts: 133 us -> 3.33 us
  waiting for transfers between devices: 90.5 us -> 24.6 us
  Pallas kernels: 0 us -> 28.1 us
  matrix products: 21.1 us -> 0 us
    ppermute x51 -> x10, starting transfers between devices: 152 us -> 14.2 us  [shift(): return lax.ppermute(x, axis, ring(axis, step))]
    concatenate x27 -> x0, other arithmetic: 79.8 us -> none  [the longest x3 64.8 us: local(): jnp.concatenate([extended, from_behind(extended[:, :, :, 0:1], 'gy', -1)]...]
    ppermute x51 -> x10, waiting for transfers between devices: 90.5 us -> 24.6 us  [shift(): return lax.ppermute(x, axis, ring(axis, step))]
    unnamed x141 -> x14, local copies, waits for them, and re-layouts: 52.5 us -> 3.33 us
    another operation x3 -> x1, other arithmetic: 33.1 us -> 0.08 us  [local(): jnp.stack([lax.axis_index(a) for a in ('gx', 'gy', 'gz')]).astype(jnp.int32)]
    pallas_call x0 -> x12, Pallas kernels: none -> 28.1 us  [call(): pl.pallas_call(kernel, grid=(1,), out_shape=shapes if len(shapes) > 1 els...]
    dot_general x2 -> x0, matrix products: 21.1 us -> none  [local(): jnp.dot(stiffness, element, precision=lax.Precision.HIGHEST, preferred_el...]
    concatenate x7 -> x0, local copies, waits for them, and re-layouts: 19.1 us -> none  [the longest x1 11.1 us: local(): jnp.concatenate([extended, from_behind(extended[:, :, :, 0:1], 'gy', -1)]...]
  transfers between devices with their start and end apart: 51 -> 10, of which waited for: 34 -> 6; matrix products, arithmetic and copies ran while one was open for 17% -> 0% of each run, Pallas kernels for 0% -> 32%
where the time goes in v2:
time: 70.9 us; the launch traced here: 70.5 us
  Pallas kernels  28.1 us (40%)
  waiting for transfers between devices  24.6 us (35%)
  starting transfers between devices  14.2 us (20%)
  local copies, waits for them, and re-layouts  3.33 us (5%)
    pallas_call x12, Pallas kernels, call(): pl.pallas_call(kernel, grid=(1,), out_shape=shapes if len(shapes) > 1 els...  28.1 us
    ppermute x10, waiting for transfers between devices, shift(): return lax.ppermute(x, axis, ring(axis, step))  24.6 us
    ppermute x10, starting transfers between devices, shift(): return lax.ppermute(x, axis, ring(axis, step))  14.2 us
    unnamed x14, local copies, waits for them, and re-layouts  3.33 us
  transfers between devices with their start and end apart: 10, of which 6 were waited for; matrix products, arithmetic and copies ran while one was open for 0% of the time, Pallas kernels for 32%

profile of v2, /device:TPU:0, one launch (start us, length us, event | category | flops | bytes accessed | tf_op | source)
XLA Modules:
  0.0 70.5 jit_solution(4693549169503930886)
XLA Ops:
  0.0 1.4 %copy-done = f32[2,3,8,32,256]{4,3,2,1,0:T(8,128)S(1)} copy-done((f32[2,3,8,32,256]{4,3,2,1,0:T(8,128)S(1)}, f32[2,3,8,32,256]{4,3,2,1,0:T(8,128)}, u32[]{:S(2)}) %copy-start) | copy-done | bytes 1572888
  1.4 0.9 %copy-done.2 = s32[8,32,256]{2,1,0:T(8,128)S(1)} copy-done((s32[8,32,256]{2,1,0:T(8,128)S(1)}, s32[8,32,256]{2,1,0:T(8,128)}, u32[]{:S(2)}) %copy-start.2) | copy-done | bytes 262168
  2.4 0.9 %copy-done.4 = f32[8,32,256]{2,1,0:T(8,128)S(1)} copy-done((f32[8,32,256]{2,1,0:T(8,128)S(1)}, f32[8,32,256]{2,1,0:T(8,128)}, u32[]{:S(2)}) %copy-start.4) | copy-done | bytes 262168
  3.3 0.1 pack_x1.1
  3.4 2.5 %collective-permute-start = (f32[10,32,256]{2,1,0:T(8,128)S(1)}, f32[10,32,256]{2,1,0:T(8,128)S(1)}, u32[]{:S(2)}, u32[]{:S(2)}) collective-permute-start(f32[10,32,256]{2,1,0:T(8,128)S(1)} %get-tuple-element.33), channel_id=1, source_target_pairs={{0,112},{16,0},{32,16},{48,32},{64,48},{80,64},{96,80},{112,96},{1... | collective-permute-start | bytes 983048 | tf_op jit(solution)/shard_map/ppermute | solution.py:673
  5.9 0.1 pad_add_fusion.where
  6.0 5.5 %collective-permute-done.1.below = f32[4,32,256]{2,1,0:T(8,128)S(1)} collective-permute-done((f32[4,32,256]{2,1,0:T(8,128)S(1)}, f32[4,32,256]{2,1,0:T(8,128)S(1)}, u32[]{:S(2)}, u32[]{:S(2)}) %collective-permute-start.1) | collective-permute-done | bytes 131104 | tf_op jit(solution)/shard_map/ppermute | solution.py:673
  11.5 0.6 pack_y1.1
  12.1 6.6 %collective-permute-start.2 = (f32[16,8,256]{2,1,0:T(8,128)S(1)}, f32[16,8,256]{2,1,0:T(8,128)S(1)}, u32[]{:S(2)}, u32[]{:S(2)}) collective-permute-start(f32[16,8,256]{2,1,0:T(8,128)S(1)} %get-tuple-element.35), channel_id=1, source_target_pairs={{0,14},{2,0},{4,2},{6,4},{8,6},{10,8},{12,10},{14,12},{1,15},{3,1}... | collective-permute-start | bytes 393224 | tf_op jit(solution)/shard_map/ppermute | solution.py:673
  18.7 3.1 %energy.1 = (f32[2,7,32,256]{3,2,1,0:T(8,128)S(1)}, f32[2,7,32,256]{3,2,1,0:T(8,128)S(1)}, f32[2,32,128]{2,1,0:T(8,128)S(1)}) custom-call(f32[2,3,8,32,256]{4,3,2,1,0:T(8,128)S(1)} %copy-done.1), custom_call_target="tpu_custom_call" | custom-call | flops 40000000 | bytes 2000000 | tf_op jit(solution)/shard_map/energy/pallas_call | solution.py:655
  21.8 4.8 %collective-permute-done.3.y_below = f32[8,8,256]{2,1,0:T(8,128)S(1)} collective-permute-done((f32[8,8,256]{2,1,0:T(8,128)S(1)}, f32[8,8,256]{2,1,0:T(8,128)S(1)}, u32[]{:S(2)}, u32[]{:S(2)}) %collective-permute-start.3) | collective-permute-done | bytes 65568 | tf_op jit(solution)/shard_map/ppermute | solution.py:673
  26.6 0.8 %pack_z1.1 = f32[2,40,128]{2,1,0:T(8,128)S(1)} custom-call(s32[3]{0:T(128)S(1)} %pad_add_fusion.where, f32[8,32,256]{2,1,0:T(8,128)S(1)} %get-tuple-element.31.src, f32[2,32,128]{2,1,0:T(8,128)S(1)} %get-tuple-element.32.columns, f32[10,32,256]{2,1,0:T(8,128)S(1)} %collective-permute-done.above, f32[4,32,256]{2,1,0:T(8,128)S(1)} %collective-permute-done.1.below, ...), custom_call_target="tpu_custom_call" | custom-call | bytes 2000000 | tf_op jit(solution)/shard_map/pack_z1/pallas_call | solution.py:655
  27.4 0.7 collective-permute-start.4
  28.0 5.1 %bulk1.1 = (f32[1,8,32,256]{3,2,1,0:T(8,128)S(1)}, f32[1,4,16,2,1,256]{5,4,3,2,1,0:T(1,128)S(1)}, f32[1,4,32,128]{3,2,1,0:T(8,128)S(1)}, f32[2,32,256]{2,1,0:T(8,128)S(1)}, f32[2,32,256]{2,1,0:T(8,128)S(1)}) custom-call(s32[3]{0:T(128)S(1)} %pad_add_fusion.where, f32[8,32,256]{2,1,0:T(8,128)S(1)} %get-tuple-element.31.src, ...), custom_call_target="tpu_custom_call" | custom-call | flops 30000000 | bytes 2000000 | tf_op jit(solution)/shard_map/bulk1/pallas_call | solution.py:655
  33.2 0.0 copy-start.5
  33.2 0.0 copy-start.6
  33.2 4.5 %strips1.1 = (f32[1,8,16,256]{3,2,1,0:T(8,128)S(1)}, f32[1,4,16,128]{3,2,1,0:T(8,128)S(1)}, f32[2,2,8,256]{3,2,1,0:T(8,128)S(1)}, f32[40,128]{1,0:T(8,128)S(1)}) custom-call(s32[3]{0:T(128)S(1)} %pad_add_fusion.where, f32[2,3,8,32,256]{4,3,2,1,0:T(8,128)S(1)} %copy-done.1, f32[2,32,128]{2,1,0:T(8,128)S(1)} %get-tuple-element.32.columns, ...), custom_call_target="tpu_custom_call" | custom-call | flops 20000000 | bytes 2000000 | tf_op jit(solution)/shard_map/strips1/pallas_call | solution.py:655
  37.7 1.2 %raw.1 = (f32[4,2,32,256]{3,2,1,0:T(8,128)S(1)}, f32[4,2,32,256]{3,2,1,0:T(8,128)S(1)}) custom-call(f32[6]{0:T(128)S(1)} %copy-done.5, s32[6]{0:T(128)S(1)} %copy-done.6, s32[3]{0:T(128)S(1)} %pad_add_fusion.where, f32[2,40,128]{2,1,0:T(8,128)S(1)} %collective-permute-done.4.z_in, f32[40,128]{1,0:T(8,128)S(1)} %get-tuple-element.38.packed, ...), custom_call_target="tpu_custom_call" | custom-call | bytes 2000000 | tf_op jit(solution)/shard_map/raw/pallas_call | solution.py:655
  38.9 0.4 collective-permute-start.5
  39.4 0.1 collective-permute-start.6
  39.5 3.8 %collective-permute-done.5.above = f32[4,2,32,256]{3,2,1,0:T(8,128)S(1)} collective-permute-done((f32[4,2,32,256]{3,2,1,0:T(8,128)S(1)}, f32[4,2,32,256]{3,2,1,0:T(8,128)S(1)}, u32[]{:S(2)}, u32[]{:S(2)}) %collective-permute-start.5) | collective-permute-done | bytes 262176 | tf_op jit(solution)/shard_map/ppermute | solution.py:673
  43.2 3.1 %collective-permute-done.6.below = f32[4,2,32,256]{3,2,1,0:T(8,128)S(1)} collective-permute-done((f32[4,2,32,256]{3,2,1,0:T(8,128)S(1)}, f32[4,2,32,256]{3,2,1,0:T(8,128)S(1)}, u32[]{:S(2)}, u32[]{:S(2)}) %collective-permute-start.6) | collective-permute-done | bytes 262176 | tf_op jit(solution)/shard_map/ppermute | solution.py:673
  46.4 0.0 copy-start.3
  46.4 2.4 %collective-permute-start.7 = (f32[16,8,256]{2,1,0:T(8,128)S(1)}, f32[16,8,256]{2,1,0:T(8,128)S(1)}, u32[]{:S(2)}, u32[]{:S(2)}) collective-permute-start(f32[16,8,256]{2,1,0:T(8,128)S(1)} %get-tuple-element.50), channel_id=1, source_target_pairs={{0,14},{2,0},{4,2},{6,4},{8,6},{10,8},{12,10},{14,12},{1,15},{3,1}... | collective-permute-start | bytes 393224 | tf_op jit(solution)/shard_map/ppermute | solution.py:673
  48.8 1.2 %collective-permute-start.8 = (f32[16,8,256]{2,1,0:T(8,128)S(1)}, f32[16,8,256]{2,1,0:T(8,128)S(1)}, u32[]{:S(2)}, u32[]{:S(2)}) collective-permute-start(f32[16,8,256]{2,1,0:T(8,128)S(1)} %get-tuple-element.51), channel_id=1, source_target_pairs={{0,2},{2,4},{4,6},{6,8},{8,10},{10,12},{12,14},{14,0},{1,3},{3,5},... | collective-permute-start | bytes 393224 | tf_op jit(solution)/shard_map/ppermute | solution.py:673
  50.0 2.9 %collective-permute-done.7.y_above = f32[16,8,256]{2,1,0:T(8,128)S(1)} collective-permute-done((f32[16,8,256]{2,1,0:T(8,128)S(1)}, f32[16,8,256]{2,1,0:T(8,128)S(1)}, u32[]{:S(2)}, u32[]{:S(2)}) %collective-permute-start.7) | collective-permute-done | bytes 131104 | tf_op jit(solution)/shard_map/ppermute | solution.py:673
  52.9 4.4 %collective-permute-done.8.y_below = f32[16,8,256]{2,1,0:T(8,128)S(1)} collective-permute-done((f32[16,8,256]{2,1,0:T(8,128)S(1)}, f32[16,8,256]{2,1,0:T(8,128)S(1)}, u32[]{:S(2)}, u32[]{:S(2)}) %collective-permute-start.8) | collective-permute-done | bytes 131104 | tf_op jit(solution)/shard_map/ppermute | solution.py:673
  57.4 0.8 %pack_z2.1 = f32[2,40,128]{2,1,0:T(8,128)S(1)} custom-call(s32[3]{0:T(128)S(1)} %pad_add_fusion.where, f32[4,2,32,256]{3,2,1,0:T(8,128)S(1)} %get-tuple-element.48.low, f32[4,2,32,256]{3,2,1,0:T(8,128)S(1)} %get-tuple-element.49.high, f32[4,2,32,256]{3,2,1,0:T(8,128)S(1)} %collective-permute-done.5.above, ...), custom_call_target="tpu_custom_call" | custom-call | bytes 2000000 | tf_op jit(solution)/shard_map/pack_z2/pallas_call | solution.py:655
  58.2 0.3 collective-permute-start.9
  58.5 5.6 %bulk2.1 = (f32[2,8,32,256]{3,2,1,0:T(8,128)S(1)}, f32[2,4,16,2,1,256]{5,4,3,2,1,0:T(1,128)S(1)}, f32[2,4,32,128]{3,2,1,0:T(8,128)S(1)}) custom-call(s32[3]{0:T(128)S(1)} %pad_add_fusion.where, f32[4,2,32,256]{3,2,1,0:T(8,128)S(1)} %get-tuple-element.48.low, f32[4,2,32,256]{3,2,1,0:T(8,128)S(1)} %get-tuple-element.49.high, ...), custom_call_target="tpu_custom_call" | custom-call | flops 40000000 | bytes 2000000 | tf_op jit(solution)/shard_map/bulk2/pallas_call | solution.py:655
  64.1 4.6 %strips2.1 = (f32[2,8,16,256]{3,2,1,0:T(8,128)S(1)}, f32[2,4,16,128]{3,2,1,0:T(8,128)S(1)}) custom-call(s32[3]{0:T(128)S(1)} %pad_add_fusion.where, f32[16,8,256]{2,1,0:T(8,128)S(1)} %collective-permute-done.7.y_above, f32[16,8,256]{2,1,0:T(8,128)S(1)} %collective-permute-done.8.y_below, f32[2,4,16,2,1,256]{5,4,3,2,1,0:T(1,128)S(1)} %get-tuple-element.54.ends), custom_call_target="tpu_custom_call" | custom-call | flops 20000000 | bytes 2000000 | tf_op jit(solution)/shard_map/strips2/pallas_call | solution.py:655
  68.7 1.9 %final.1 = f32[2,8,32,256]{3,2,1,0:T(8,128)} custom-call(s32[3]{0:T(128)S(1)} %pad_add_fusion.where, s32[8,32,256]{2,1,0:T(8,128)S(1)} %copy-done.3, f32[2,40,128]{2,1,0:T(8,128)S(1)} %collective-permute-done.9.z_in, f32[2,8,32,256]{3,2,1,0:T(8,128)S(1)} %get-tuple-element.52.bulk, f32[2,4,32,128]{3,2,1,0:T(8,128)S(1)} %get-tuple-element.53.bulk_edges, ...), custom_call_target="tpu_custom_call" | custom-call | bytes 2000000 | tf_op jit(solution)/shard_map/final/pallas_call | solution.py:655
  (15 shorter events, 0.1 us)
Async XLA Ops:
  0.0 1.4 %copy-start = (f32[2,3,8,32,256]{4,3,2,1,0:T(8,128)S(1)}, f32[2,3,8,32,256]{4,3,2,1,0:T(8,128)}, u32[]{:S(2)}) copy-start(f32[2,3,8,32,256]{4,3,2,1,0:T(8,128)} %modes.9) | copy-start | bytes 4718596
  1.4 0.9 %copy-start.2 = (s32[8,32,256]{2,1,0:T(8,128)S(1)}, s32[8,32,256]{2,1,0:T(8,128)}, u32[]{:S(2)}) copy-start(s32[8,32,256]{2,1,0:T(8,128)} %mask.3) | copy-start | bytes 786436
  2.4 0.9 %copy-start.4 = (f32[8,32,256]{2,1,0:T(8,128)S(1)}, f32[8,32,256]{2,1,0:T(8,128)}, u32[]{:S(2)}) copy-start(f32[8,32,256]{2,1,0:T(8,128)} %design.1) | copy-start | bytes 786436
  3.3 8.2 %copy-start.1 = (f32[2,3,8,32,256]{4,3,2,1,0:T(8,128)S(1)}, f32[2,3,8,32,256]{4,3,2,1,0:T(8,128)}, u32[]{:S(2)}) copy-start(f32[2,3,8,32,256]{4,3,2,1,0:T(8,128)} %modes.9) | copy-start | bytes 4718596
  3.4 8.2 %collective-permute-start = (f32[10,32,256]{2,1,0:T(8,128)S(1)}, f32[10,32,256]{2,1,0:T(8,128)S(1)}, u32[]{:S(2)}, u32[]{:S(2)}) collective-permute-start(f32[10,32,256]{2,1,0:T(8,128)S(1)} %get-tuple-element.33), channel_id=1, source_target_pairs={{0,112},{16,0},{32,16},{48,32},{64,48},{80,64},{96,80},{112,96},{1... | collective-permute-start | bytes 983048 | tf_op jit(solution)/shard_map/ppermute | solution.py:673
  5.9 5.6 %collective-permute-start.1 = (f32[4,32,256]{2,1,0:T(8,128)S(1)}, f32[4,32,256]{2,1,0:T(8,128)S(1)}, u32[]{:S(2)}, u32[]{:S(2)}) collective-permute-start(f32[4,32,256]{2,1,0:T(8,128)S(1)} %get-tuple-element.34), channel_id=1, source_target_pairs={{0,16},{16,32},{32,48},{48,64},{64,80},{80,96},{96,112},{112,0},{1... | collective-permute-start | bytes 393224 | tf_op jit(solution)/shard_map/ppermute | solution.py:673
  12.1 14.4 %collective-permute-start.2 = (f32[16,8,256]{2,1,0:T(8,128)S(1)}, f32[16,8,256]{2,1,0:T(8,128)S(1)}, u32[]{:S(2)}, u32[]{:S(2)}) collective-permute-start(f32[16,8,256]{2,1,0:T(8,128)S(1)} %get-tuple-element.35), channel_id=1, source_target_pairs={{0,14},{2,0},{4,2},{6,4},{8,6},{10,8},{12,10},{14,12},{1,15},{3,1}... | collective-permute-start | bytes 393224 | tf_op jit(solution)/shard_map/ppermute | solution.py:673
  18.7 7.9 %collective-permute-start.3 = (f32[8,8,256]{2,1,0:T(8,128)S(1)}, f32[8,8,256]{2,1,0:T(8,128)S(1)}, u32[]{:S(2)}, u32[]{:S(2)}) collective-permute-start(f32[8,8,256]{2,1,0:T(8,128)S(1)} %get-tuple-element.36), channel_id=1, source_target_pairs={{0,2},{2,4},{4,6},{6,8},{8,10},{10,12},{12,14},{14,0},{1,3},{3,5},... | collective-permute-start | bytes 196616 | tf_op jit(solution)/shard_map/ppermute | solution.py:673
  27.4 10.4 %collective-permute-start.4 = (f32[2,40,128]{2,1,0:T(8,128)S(1)}, f32[2,40,128]{2,1,0:T(8,128)S(1)}, u32[]{:S(2)}, u32[]{:S(2)}) collective-permute-start(f32[2,40,128]{2,1,0:T(8,128)S(1)} %pack_z1.1), channel_id=1, source_target_pairs={{0,1},{1,0},{2,3},{3,2},{4,5},{5,4},{6,7},{7,6},{8,9},{9,8},{10,11... | collective-permute-start | bytes 122888 | tf_op jit(solution)/shard_map/ppermute | solution.py:673
  33.2 4.5 %copy-start.5 = (f32[6]{0:T(128)S(1)}, f32[6]{0:T(128)}, u32[]{:S(2)}) copy-start(f32[6]{0:T(128)} %eigenvalues.1) | copy-start | bytes 76
  33.2 4.5 %copy-start.6 = (s32[6]{0:T(128)S(1)}, s32[6]{0:T(128)}, u32[]{:S(2)}) copy-start(s32[6]{0:T(128)} %order.1) | copy-start | bytes 76
  38.9 4.3 %collective-permute-start.5 = (f32[4,2,32,256]{3,2,1,0:T(8,128)S(1)}, f32[4,2,32,256]{3,2,1,0:T(8,128)S(1)}, u32[]{:S(2)}, u32[]{:S(2)}) collective-permute-start(f32[4,2,32,256]{3,2,1,0:T(8,128)S(1)} %get-tuple-element.48.low), channel_id=1, source_target_pairs={{0,112},{16,0},{32,16},{48,32},{64,48},{80,64},{96,80},{112,96},{1... | collective-permute-start | bytes 786440 | tf_op jit(solution)/shard_map/ppermute | solution.py:673
  39.4 7.0 %collective-permute-start.6 = (f32[4,2,32,256]{3,2,1,0:T(8,128)S(1)}, f32[4,2,32,256]{3,2,1,0:T(8,128)S(1)}, u32[]{:S(2)}, u32[]{:S(2)}) collective-permute-start(f32[4,2,32,256]{3,2,1,0:T(8,128)S(1)} %get-tuple-element.49.high), channel_id=1, source_target_pairs={{0,16},{16,32},{32,48},{48,64},{64,80},{80,96},{96,112},{112,0},{1... | collective-permute-start | bytes 786440 | tf_op jit(solution)/shard_map/ppermute | solution.py:673
  46.4 22.2 %copy-start.3 = (s32[8,32,256]{2,1,0:T(8,128)S(1)}, s32[8,32,256]{2,1,0:T(8,128)}, u32[]{:S(2)}) copy-start(s32[8,32,256]{2,1,0:T(8,128)} %mask.3) | copy-start | bytes 786436
  46.4 6.5 %collective-permute-start.7 = (f32[16,8,256]{2,1,0:T(8,128)S(1)}, f32[16,8,256]{2,1,0:T(8,128)S(1)}, u32[]{:S(2)}, u32[]{:S(2)}) collective-permute-start(f32[16,8,256]{2,1,0:T(8,128)S(1)} %get-tuple-element.50), channel_id=1, source_target_pairs={{0,14},{2,0},{4,2},{6,4},{8,6},{10,8},{12,10},{14,12},{1,15},{3,1}... | collective-permute-start | bytes 393224 | tf_op jit(solution)/shard_map/ppermute | solution.py:673
  48.8 8.6 %collective-permute-start.8 = (f32[16,8,256]{2,1,0:T(8,128)S(1)}, f32[16,8,256]{2,1,0:T(8,128)S(1)}, u32[]{:S(2)}, u32[]{:S(2)}) collective-permute-start(f32[16,8,256]{2,1,0:T(8,128)S(1)} %get-tuple-element.51), channel_id=1, source_target_pairs={{0,2},{2,4},{4,6},{6,8},{8,10},{10,12},{12,14},{14,0},{1,3},{3,5},... | collective-permute-start | bytes 393224 | tf_op jit(solution)/shard_map/ppermute | solution.py:673
  58.2 10.5 %collective-permute-start.9 = (f32[2,40,128]{2,1,0:T(8,128)S(1)}, f32[2,40,128]{2,1,0:T(8,128)S(1)}, u32[]{:S(2)}, u32[]{:S(2)}) collective-permute-start(f32[2,40,128]{2,1,0:T(8,128)S(1)} %pack_z2.1), channel_id=1, source_target_pairs={{0,1},{1,0},{2,3},{3,2},{4,5},{5,4},{6,7},{7,6},{8,9},{9,8},{10,11... | collective-permute-start | bytes 122888 | tf_op jit(solution)/shard_map/ppermute | solution.py:673

commit v3 on v2

--- a/solution.py
+++ b/solution.py
@@ -128,19 +128,20 @@
     return out
 
 
-def send_edge(edges, index, tile, p, gz, lane):
-    turned = pltpu.roll(tile, lax.rem(8 * p + 5 - 2 * gz, LANES), 1)
-    edges[index] = jnp.where(lane == 8 * p + 4 - gz, turned, edges[index])
+def turn_edge(tile, p, gz):
+    return pltpu.roll(tile, lax.rem(8 * p + 5 - 2 * gz, LANES), 1)
+
+
+def kind_at(gx, p):
+    return 2 if W < p < PX - W - 1 else kind_of(gx, p)
 
 
 def bulk_sweeps(fields, where, table, source, states, ends, edges, out):
     gx, gy, gz = where
     sub, lane = sub_lane()
     sb = states[0]
-    edges[...] = jnp.zeros(edges.shape, F32)
-    ends[...] = jnp.zeros(ends.shape, F32)
     for p in range(PX):
-        kind = kind_of(gx, p)
+        kind = kind_at(gx, p)
         for m in range(fields):
             for i in range(CY // 8):
                 rows = slice(8 * i, 8 * i + 8)
@@ -148,45 +149,41 @@
     for k in range(ITERS):
         old = states[0] if k == 0 else states[1 + (k - 1) % 2]
         new = states[1 + k % 2]
-
-        def body(p, carry, old=old, new=new, k=k):
-            scale = tiles_of(table, (kind_of(gx, p),), CY // 8, 2)
-            for m in range(fields):
+        for m in range(fields):
+            edge = [jnp.zeros((8, LANES), F32)] * (CY // 8)
+            for p in range(k + 1, PX - 1 - k):
+                kind = kind_at(gx, p)
                 mid = tiles_of(old, (m, p), CY // 8, 2)
-                low = tiles_of(old, (m, p - 1), CY // 8, 2)
-                high = tiles_of(old, (m, p + 1), CY // 8, 2)
-                base = tiles_of(sb, (m, p), CY // 8, 2)
                 yy = along_rows(mid, sub)
                 for i in range(CY // 8):
                     zz = along_lanes(mid[i], lane)
                     rows = slice(8 * i, 8 * i + 8)
                     for j in range(2):
-                        total = (low[i][j] + high[i][j]) + (yy[i][j] + zz[j])
-                        value = base[i][j] + scale[i][j] * total
                         cols = slice(LANES * j, LANES * j + LANES)
+                        total = old[m, p - 1, rows, cols] + old[m, p + 1, rows, cols]
+                        total = total + (yy[i][j] + zz[j])
+                        value = sb[m, p, rows, cols] + table[kind, rows, cols] * total
                         if k + 1 < ITERS:
                             new[m, p, rows, cols] = value
                         else:
                             out[m, p - W, rows, cols] = value
-                    edge = jnp.where(gz == 0, mid[i][1], mid[i][0])
-                    send_edge(edges, (m, k, rows), edge, p, gz, lane)
+                    side = jnp.where(gz == 0, mid[i][1], mid[i][0])
+                    edge[i] = jnp.where(lane == 8 * p + 4 - gz, turn_edge(side, p, gz), edge[i])
                 for j in range(2):
                     cols = slice(LANES * j, LANES * j + LANES)
                     ends[m, k, p, 0, 0:1, cols] = mid[CY // 8 - 1][j][7:8]
                     ends[m, k, p, 1, 0:1, cols] = mid[0][j][0:1]
-            return carry
-
-        lax.fori_loop(k + 1, PX - 1 - k, body, 0)
+            for i in range(CY // 8):
+                edges[m, k, 8 * i : 8 * i + 8, :] = edge[i]
 
 
 def strip_sweeps(fields, where, table, source, ends, states, edges, out):
     gx, gy, gz = where
     sub, lane = sub_lane()
     sb = states[0]
-    edges[...] = jnp.zeros(edges.shape, F32)
     wide = iota((8, CZ), 0)
     for p in range(PX):
-        kind = kind_of(gx, p)
+        kind = kind_at(gx, p)
         for m in range(fields):
             halo = source(m, p) * (1.0 / radius_sq)
             sb[m, p, 0:8, :] = jnp.where(wide < 4, halo * table[kind, 0:8, :], 0.0)
@@ -194,14 +191,11 @@
     for k in range(ITERS):
         old = states[0] if k == 0 else states[1 + (k - 1) % 2]
         new = states[1 + k % 2]
-
-        def body(p, carry, old=old, new=new, k=k):
-            scale = tiles_of(table, (kind_of(gx, p),), 2, 2)
-            for m in range(fields):
+        for m in range(fields):
+            edge = [jnp.zeros((8, LANES), F32)] * 2
+            for p in range(k + 1, PX - 1 - k):
+                kind = kind_at(gx, p)
                 mid = tiles_of(old, (m, p), 2, 2)
-                low = tiles_of(old, (m, p - 1), 2, 2)
-                high = tiles_of(old, (m, p + 1), 2, 2)
-                base = tiles_of(sb, (m, p), 2, 2)
                 for i in range(2):
                     rows = slice(8 * i, 8 * i + 8)
                     zz = along_lanes(mid[i], lane)
@@ -214,17 +208,17 @@
                             down = jnp.where(sub == 4, 0.0, down) + jnp.where(sub == 0, end, 0.0)
                         else:
                             up = jnp.where(sub == 3, 0.0, up) + jnp.where(sub == 7, end, 0.0)
-                        total = (low[i][j] + high[i][j]) + (down + up) + zz[j]
-                        value = base[i][j] + scale[i][j] * total
+                        total = old[m, p - 1, rows, cols] + old[m, p + 1, rows, cols]
+                        total = total + (down + up) + zz[j]
+                        value = sb[m, p, rows, cols] + table[kind, rows, cols] * total
                         if k + 1 < ITERS:
                             new[m, p, rows, cols] = value
                         else:
                             out[m, p - W, rows, cols] = value
-                    edge = jnp.where(gz == 0, mid[i][1], mid[i][0])
-                    send_edge(edges, (m, k, rows), edge, p, gz, lane)
-            return carry
-
-        lax.fori_loop(k + 1, PX - 1 - k, body, 0)
+                    side = jnp.where(gz == 0, mid[i][1], mid[i][0])
+                    edge[i] = jnp.where(lane == 8 * p + 4 - gz, turn_edge(side, p, gz), edge[i])
+            for i in range(2):
+                edges[m, k, 8 * i : 8 * i + 8, :] = edge[i]
 
 
 def z_sweeps(m, scale, halo, bulk_edges, strip_edges):
@@ -369,17 +363,27 @@
     return jnp.concatenate([packed, rim * keep_y], axis=0)
 
 
-def pack_x1(design, mask, modes, src, down, up):
+def pack_x1(design, mask, modes, src, down, up, field, solid, arrived):
+    copies = []
     for x in range(CX):
-        plane = design[x] * mask[x].astype(F32)
+        copies.append(pltpu.make_async_copy(design.at[x], field.at[x], arrived.at[2 * x]))
+        copies.append(pltpu.make_async_copy(mask.at[x], solid.at[x], arrived.at[2 * x + 1]))
+    for n in range(3 * MODES):
+        to = down.at[W + n]
+        copies.append(pltpu.make_async_copy(modes.at[n // 3, n % 3, 0], to, arrived.at[2 * CX + n]))
+    for copy in copies:
+        copy.start()
+    for x in range(CX):
+        copies[2 * x].wait()
+        copies[2 * x + 1].wait()
+        plane = field[x] * solid[x].astype(F32)
         src[x] = plane
         if x < W:
             down[x] = plane
         if x >= CX - W:
             up[x - (CX - W)] = plane
-    for m in range(MODES):
-        for c in range(3):
-            down[W + 3 * m + c] = modes[m, c, 0]
+    for copy in copies[2 * CX :]:
+        copy.wait()
 
 
 def energy_kernel(modes, stiff, mass, columns):
@@ -412,7 +416,7 @@
     return above, p - W - CX
 
 
-def pack_y1(where, src, modes, above, below, down, up):
+def pack_y1(where, src, modes, above, below, ahead, down, up):
     gx, gy, gz = pos(where)
     low = iota((8, CZ), 0) < 4
     for q in range(8):
@@ -462,7 +466,7 @@
     return jnp.where(iota(a.shape, 0) < 4, a, b)
 
 
-def pack_z1(where, src, columns, above, below, y_above, y_below, out):
+def pack_z1(where, src, columns, above, below, y_above, y_below, ahead, out):
     gx, gy, gz = pos(where)
     edge = edge_tiles(gz)
     lane = iota((PY, LANES), 1)
@@ -575,20 +579,45 @@
     return above, p - 3 * W
 
 
+SHARED = ((PX - W, PX - W + 2, 3), (W - 1, W - 3, 3), (PX - W + 1, W - 2, 2))
+
+
+def rolled(tile, by):
+    return pltpu.roll(tile, by % 8, 0) if by % 8 else tile
+
+
 def pack_y2(low, high, above, below, down, up):
-    first = iota((8, CZ), 0) < 4
-    for p in range(PX):
+    sub = iota((8, CZ), 0)
+
+    def rows(p, m, start):
         a, i = raw_plane(low, high, above, below, p)
-        down[p] = jnp.where(first, a[i, 0, 0:8, :], pltpu.roll(a[i, 1, 0:8, :], 4, 0))
-        up[p] = jnp.where(first, pltpu.roll(a[i, 0, 24:32, :], 4, 0), a[i, 1, 24:32, :])
+        return a[i, m, start : start + 8, :]
+
+    def both(tiles, first):
+        return jnp.where(sub < 4, rolled(tiles[0], -first), rolled(tiles[1], 4 - first))
+
+    for p in range(W, W + CX):
+        down[p - W] = both([rows(p, m, 0) for m in range(MODES)], 0)
+        up[p - W] = both([rows(p, m, 24) for m in range(MODES)], 4)
+    for n, (p, q, count) in enumerate(SHARED):
+        down[CX + n] = both(
+            [jnp.where(sub < count, rows(p, m, 0), rolled(rows(q, m, 0), count)) for m in range(MODES)], 0
+        )
+        up[CX + n] = both(
+            [jnp.where(sub >= 8 - count, rows(p, m, 24), rolled(rows(q, m, 24), -count)) for m in range(MODES)], 4
+        )
 
 
 def raw_halo(y_above, y_below, m, p, lanes=slice(None)):
-    a, b = y_above[p, :, lanes], y_below[p, :, lanes]
-    if m == 0:
-        b = pltpu.roll(b, 4, 0)
+    if W <= p < W + CX:
+        n, skip = p - W, 0
     else:
-        a = pltpu.roll(a, 4, 0)
+        found = [(CX + n, 0 if p == s[0] else s[2]) for n, s in enumerate(SHARED) if p in s[:2]]
+        if not found:
+            return jnp.zeros(y_above[0, :, lanes].shape, F32)
+        n, skip = found[0]
+    a = rolled(y_above[n, :, lanes], 4 * m - skip)
+    b = rolled(y_below[n, :, lanes], 4 * (1 - m) + skip)
     return jnp.where(iota(a.shape, 0) < 4, a, b)
 
 
@@ -603,7 +632,7 @@
     bulk_sweeps(MODES, at, table, source, (sb, one, two), ends, edges, bulk)
 
 
-def pack_z2(where, low, high, above, below, y_above, y_below, out):
+def pack_z2(where, low, high, above, below, y_above, y_below, ahead, out):
     gx, gy, gz = pos(where)
     edge = edge_tiles(gz)
     lane = iota((PY, LANES), 1)
@@ -626,20 +655,28 @@
     strip_sweeps(MODES, at, table, source, ends, (sb, one, two), edges, strips)
 
 
-def final_kernel(where, mask, z_in, bulk, bulk_edges, strips, strip_edges, out):
+def final_kernel(where, mask, z_in, bulk, bulk_edges, strips, strip_edges, out, held, left):
     gx, gy, gz = pos(where)
     sub, lane = sub_lane()
     beside = beside_halo(gz, lane)
     scale = strip_scale(gx, gy)
+    states = [z_sweeps(m, scale, z_in[m], bulk_edges, strip_edges) for m in range(MODES)]
+    copies = []
     for m in range(MODES):
-        z_state = z_sweeps(m, scale, z_in[m], bulk_edges, strip_edges)
         for x in range(CX):
             for i in range(CY // 8):
                 rows = slice(8 * i, 8 * i + 8)
                 for j in range(2):
                     cols = slice(LANES * j, LANES * j + LANES)
-                    value = result_tile(m, x, i, j, bulk, strips, z_state, beside, sub)
-                    out[m, x, rows, cols] = value * mask[x, rows, cols].astype(F32)
+                    value = result_tile(m, x, i, j, bulk, strips, states[m], beside, sub)
+                    held[m, x, rows, cols] = value * mask[x, rows, cols].astype(F32)
+            if x % 2:
+                part = (m, slice(x - 1, x + 1))
+                copy = pltpu.make_async_copy(held.at[part], out.at[part], left.at[len(copies)])
+                copy.start()
+                copies.append(copy)
+    for copy in copies:
+        copy.wait()
 
 
 SMEM = pl.BlockSpec(memory_space=pltpu.SMEM)
@@ -649,19 +686,25 @@
     return pl.BlockSpec(x.shape, lambda i: (0,) * x.ndim)
 
 
-def call(kernel, name, outs, args, specs=None, scratch=(), flops=0):
+def call(kernel, name, outs, args, specs=None, out_spec=None, scratch=(), flops=0):
     specs = specs or {}
     shapes = tuple(jax.ShapeDtypeStruct(s, F32) for s in outs)
+    more = {} if out_spec is None else {"out_specs": out_spec}
     return pl.pallas_call(
         kernel,
         grid=(1,),
         out_shape=shapes if len(shapes) > 1 else shapes[0],
         in_specs=[specs.get(i, SMEM if a.ndim == 1 else whole(a)) for i, a in enumerate(args)],
-        scratch_shapes=[pltpu.VMEM(s, F32) for s in scratch],
+        scratch_shapes=[pltpu.VMEM(s, F32) if isinstance(s, tuple) else s for s in scratch],
         compiler_params=pltpu.CompilerParams(vmem_limit_bytes=24 * 1024 * 1024),
         cost_estimate=pl.CostEstimate(flops=flops, bytes_accessed=2_000_000, transcendentals=0),
         name=name,
+        **more,
     )(*args)
+
+
+HBM = pl.BlockSpec(memory_space=pltpu.HBM)
+ANY = pl.BlockSpec(memory_space=pl.ANY)
 
 
 def ring(axis, step):
@@ -686,10 +729,11 @@
     where = jnp.stack([lax.axis_index(a) for a in ("gx", "gy", "gz")]).astype(jnp.int32)
     bulk_outs, bulk_scratch, strip_outs, strip_scratch = sweep_outs(1)
 
-    block = pl.BlockSpec((MODES, 3, 1, CY, CZ), lambda i: (0, 0, 0, 0, 0))
     src, down, up = call(
         pack_x1, "pack_x1", [(CX, CY, CZ), (W + 6, CY, CZ), (W, CY, CZ)],
-        (design, solid_mask, mode_fields), {2: block},
+        tuple(pltpu.with_memory_space_constraint(x, pltpu.HBM) for x in (design, solid_mask, mode_fields)),
+        {0: HBM, 1: HBM, 2: HBM},
+        scratch=[(CX, CY, CZ), pltpu.VMEM((CX, CY, CZ), jnp.int32), pltpu.SemaphoreType.DMA((2 * CX + 6,))],
     )
     above, below = shift(down, "gx", -1), shift(up, "gx", 1)
     field = (MODES, CX - 1, CY, CZ)
@@ -700,7 +744,7 @@
     block = pl.BlockSpec((MODES, 3, CX, 8, CZ), lambda i: (0, 0, 0, 0, 0))
     down, up = call(
         pack_y1, "pack_y1", [(16, 8, CZ), (8, 8, CZ)],
-        (where, src, mode_fields, above, below), {2: block},
+        (where, src, mode_fields, above, below, columns), {2: block, 5: ANY},
     )
     y_above, y_below = shift(down, "gy", -1), shift(up, "gy", 1)
     plane = (MODES, CY, CZ)
@@ -710,7 +754,8 @@
     )
 
     edge = call(
-        pack_z1, "pack_z1", [(2, PY, LANES)], (where, src, columns, above, below, y_above, y_below)
+        pack_z1, "pack_z1", [(2, PY, LANES)],
+        (where, src, columns, above, below, y_above, y_below, bulk_edges), {7: ANY},
     )
     z_in = shift(edge, "gz", 1)
     strips, strip_edges, rim, packed = call(
@@ -727,12 +772,15 @@
     bulk_outs, bulk_scratch, strip_outs, strip_scratch = sweep_outs(MODES)
     above, below = shift(low, "gx", -1), shift(high, "gx", 1)
     planes = (low, high, above, below)
-    down, up = call(pack_y2, "pack_y2", [(PX, 8, CZ)] * 2, planes)
+    down, up = call(pack_y2, "pack_y2", [(CX + 3, 8, CZ)] * 2, planes)
     y_above, y_below = shift(down, "gy", -1), shift(up, "gy", 1)
     bulk, ends, bulk_edges = call(
         bulk_kernel2, "bulk2", bulk_outs, (where, *planes), scratch=bulk_scratch, flops=40_000_000
     )
-    edge = call(pack_z2, "pack_z2", [(MODES, PY, LANES)], (where, *planes, y_above, y_below))
+    edge = call(
+        pack_z2, "pack_z2", [(MODES, PY, LANES)],
+        (where, *planes, y_above, y_below, bulk_edges), {7: ANY},
+    )
     z_in = shift(edge, "gz", 1)
     strips, strip_edges = call(
         strip_kernel2, "strips2", strip_outs, (where, y_above, y_below, ends),
@@ -740,7 +788,8 @@
     )
     return call(
         final_kernel, "final", [(MODES, CX, CY, CZ)],
-        (where, solid_mask, z_in, bulk, bulk_edges, strips, strip_edges),
+        (where, solid_mask, z_in, bulk, bulk_edges, strips, strip_edges), out_spec=HBM,
+        scratch=[(MODES, CX, CY, CZ), pltpu.SemaphoreType.DMA((MODES * CX // 2,))],
     )
 
 

time: 70.9 us -> 54 us (0.76)
  Pallas kernels: 28.1 us -> 17.5 us
  local copies, waits for them, and re-layouts: 3.33 us -> 0.02 us
  waiting for transfers between devices: 24.6 us -> 21.9 us
    pallas_call x12, Pallas kernels: 28.1 us -> 17.5 us  [call(): pl.pallas_call(kernel, grid=(1,), out_shape=shapes if len(shapes) > 1 els...]
    unnamed x14 -> x8, local copies, waits for them, and re-layouts: 3.33 us -> 0.02 us
    ppermute x10, waiting for transfers between devices: 24.6 us -> 21.9 us  [shift(): return lax.ppermute(x, axis, ring(axis, step))]
  transfers between devices with their start and end apart: 10 -> 10, of which waited for: 6 -> 7; matrix products, arithmetic and copies ran while one was open for 0% -> 0% of each run, Pallas kernels for 32% -> 20%
where the time goes in v3:
time: 54 us; the launch traced here: 53.8 us
  waiting for transfers between devices  21.9 us (41%)
  Pallas kernels  17.5 us (32%)
  starting transfers between devices  14.2 us (26%)
    ppermute x10, waiting for transfers between devices, shift(): return lax.ppermute(x, axis, ring(axis, step))  21.9 us
    pallas_call x12, Pallas kernels, call(): pl.pallas_call(kernel, grid=(1,), out_shape=shapes if len(shapes) > 1 els...  17.5 us
    ppermute x10, starting transfers between devices, shift(): return lax.ppermute(x, axis, ring(axis, step))  14.2 us
  transfers between devices with their start and end apart: 10, of which 7 were waited for; matrix products, arithmetic and copies ran while one was open for 0% of the time, Pallas kernels for 20%

profile of v3, /device:TPU:0, one launch (start us, length us, event | category | flops | bytes accessed | tf_op | source)
XLA Modules:
  0.0 53.8 jit_solution(8847370217619118706)
XLA Ops:
  0.0 1.4 %pack_x1.1 = (f32[8,32,256]{2,1,0:T(8,128)S(1)}, f32[10,32,256]{2,1,0:T(8,128)S(1)}, f32[4,32,256]{2,1,0:T(8,128)S(1)}) custom-call(f32[8,32,256]{2,1,0:T(8,128)} %design.1, s32[8,32,256]{2,1,0:T(8,128)} %mask.3, f32[2,3,8,32,256]{4,3,2,1,0:T(8,128)} %modes.9), custom_call_target="tpu_custom_call" | custom-call | bytes 2000000 | tf_op jit(solution)/shard_map/pack_x1/pallas_call | solution.py:693
  1.4 2.5 %collective-permute-start = (f32[10,32,256]{2,1,0:T(8,128)S(1)}, f32[10,32,256]{2,1,0:T(8,128)S(1)}, u32[]{:S(2)}, u32[]{:S(2)}) collective-permute-start(f32[10,32,256]{2,1,0:T(8,128)S(1)} %get-tuple-element.33), channel_id=1, source_target_pairs={{0,112},{16,0},{32,16},{48,32},{64,48},{80,64},{96,80},{112,96},{1... | collective-permute-start | bytes 983048 | tf_op jit(solution)/shard_map/ppermute | solution.py:716
  3.9 0.0 collective-permute-start.1
  3.9 3.1 %energy.1 = (f32[2,7,32,256]{3,2,1,0:T(8,128)S(1)}, f32[2,7,32,256]{3,2,1,0:T(8,128)S(1)}, f32[2,32,128]{2,1,0:T(8,128)S(1)}) custom-call(f32[2,3,8,32,256]{4,3,2,1,0:T(8,128)S(1)} %copy-done), custom_call_target="tpu_custom_call" | custom-call | flops 40000000 | bytes 2000000 | tf_op jit(solution)/shard_map/energy/pallas_call | solution.py:693
  7.0 0.1 pad_add_fusion.where
  7.1 2.4 %collective-permute-done.1.below = f32[4,32,256]{2,1,0:T(8,128)S(1)} collective-permute-done((f32[4,32,256]{2,1,0:T(8,128)S(1)}, f32[4,32,256]{2,1,0:T(8,128)S(1)}, u32[]{:S(2)}, u32[]{:S(2)}) %collective-permute-start.1) | collective-permute-done | bytes 131104 | tf_op jit(solution)/shard_map/ppermute | solution.py:716
  9.5 0.0 collective-permute-done.above
  9.5 0.6 %pack_y1.1 = (f32[16,8,256]{2,1,0:T(8,128)S(1)}, f32[8,8,256]{2,1,0:T(8,128)S(1)}) custom-call(s32[3]{0:T(128)S(1)} %pad_add_fusion.where, f32[8,32,256]{2,1,0:T(8,128)S(1)} %get-tuple-element.31.src, f32[2,3,8,32,256]{4,3,2,1,0:T(8,128)S(1)} %copy-done, f32[10,32,256]{2,1,0:T(8,128)S(1)} %collective-permute-done.above, ...), custom_call_target="tpu_custom_call" | custom-call | bytes 2000000 | tf_op jit(solution)/shard_map/pack_y1/pallas_call | solution.py:693
  10.1 6.6 %collective-permute-start.2 = (f32[16,8,256]{2,1,0:T(8,128)S(1)}, f32[16,8,256]{2,1,0:T(8,128)S(1)}, u32[]{:S(2)}, u32[]{:S(2)}) collective-permute-start(f32[16,8,256]{2,1,0:T(8,128)S(1)} %get-tuple-element.35), channel_id=1, source_target_pairs={{0,14},{2,0},{4,2},{6,4},{8,6},{10,8},{12,10},{14,12},{1,15},{3,1}... | collective-permute-start | bytes 393224 | tf_op jit(solution)/shard_map/ppermute | solution.py:716
  16.7 0.0 collective-permute-start.3
  16.7 2.1 %bulk1.1 = (f32[1,8,32,256]{3,2,1,0:T(8,128)S(1)}, f32[1,4,16,2,1,256]{5,4,3,2,1,0:T(1,128)S(1)}, f32[1,4,32,128]{3,2,1,0:T(8,128)S(1)}, f32[2,32,256]{2,1,0:T(8,128)S(1)}, f32[2,32,256]{2,1,0:T(8,128)S(1)}) custom-call(s32[3]{0:T(128)S(1)} %pad_add_fusion.where, f32[8,32,256]{2,1,0:T(8,128)S(1)} %get-tuple-element.31.src, ...), custom_call_target="tpu_custom_call" | custom-call | flops 30000000 | bytes 2000000 | tf_op jit(solution)/shard_map/bulk1/pallas_call | solution.py:693
  18.8 5.8 %collective-permute-done.3.y_below = f32[8,8,256]{2,1,0:T(8,128)S(1)} collective-permute-done((f32[8,8,256]{2,1,0:T(8,128)S(1)}, f32[8,8,256]{2,1,0:T(8,128)S(1)}, u32[]{:S(2)}, u32[]{:S(2)}) %collective-permute-start.3) | collective-permute-done | bytes 65568 | tf_op jit(solution)/shard_map/ppermute | solution.py:716
  24.6 0.8 %pack_z1.1 = f32[2,40,128]{2,1,0:T(8,128)S(1)} custom-call(s32[3]{0:T(128)S(1)} %pad_add_fusion.where, f32[8,32,256]{2,1,0:T(8,128)S(1)} %get-tuple-element.31.src, f32[2,32,128]{2,1,0:T(8,128)S(1)} %get-tuple-element.32.ahead.columns, f32[10,32,256]{2,1,0:T(8,128)S(1)} %collective-permute-done.above, f32[4,32,256]{2,1,0:T(8,128)S(1)} %collective-permute-done.1.below, ...), custom_call_target="tpu_custom_call" | custom-call | bytes 2000000 | tf_op jit(solution)/shard_map/pack_z1/pallas_call | solution.py:693
  25.4 0.7 %collective-permute-start.4 = (f32[2,40,128]{2,1,0:T(8,128)S(1)}, f32[2,40,128]{2,1,0:T(8,128)S(1)}, u32[]{:S(2)}, u32[]{:S(2)}) collective-permute-start(f32[2,40,128]{2,1,0:T(8,128)S(1)} %pack_z1.1), channel_id=1, source_target_pairs={{0,1},{1,0},{2,3},{3,2},{4,5},{5,4},{6,7},{7,6},{8,9},{9,8},{10,11... | collective-permute-start | bytes 122888 | tf_op jit(solution)/shard_map/ppermute | solution.py:716
  26.0 1.4 %strips1.1 = (f32[1,8,16,256]{3,2,1,0:T(8,128)S(1)}, f32[1,4,16,128]{3,2,1,0:T(8,128)S(1)}, f32[2,2,8,256]{3,2,1,0:T(8,128)S(1)}, f32[40,128]{1,0:T(8,128)S(1)}) custom-call(s32[3]{0:T(128)S(1)} %pad_add_fusion.where, f32[2,3,8,32,256]{4,3,2,1,0:T(8,128)S(1)} %copy-done, f32[2,32,128]{2,1,0:T(8,128)S(1)} %get-tuple-element.32.ahead.columns, ...), custom_call_target="tpu_custom_call" | custom-call | flops 20000000 | bytes 2000000 | tf_op jit(solution)/shard_map/strips1/pallas_call | solution.py:693
  27.5 2.0 %collective-permute-done.4.z_in = f32[2,40,128]{2,1,0:T(8,128)S(1)} collective-permute-done((f32[2,40,128]{2,1,0:T(8,128)S(1)}, f32[2,40,128]{2,1,0:T(8,128)S(1)}, u32[]{:S(2)}, u32[]{:S(2)}) %collective-permute-start.4) | collective-permute-done | bytes 40992 | tf_op jit(solution)/shard_map/ppermute | solution.py:716
  29.5 1.2 %raw.1 = (f32[4,2,32,256]{3,2,1,0:T(8,128)S(1)}, f32[4,2,32,256]{3,2,1,0:T(8,128)S(1)}) custom-call(f32[6]{0:T(128)S(1)} %copy-done.2, s32[6]{0:T(128)S(1)} %copy-done.3, s32[3]{0:T(128)S(1)} %pad_add_fusion.where, f32[2,40,128]{2,1,0:T(8,128)S(1)} %collective-permute-done.4.z_in, f32[40,128]{1,0:T(8,128)S(1)} %get-tuple-element.39.packed, ...), custom_call_target="tpu_custom_call" | custom-call | bytes 2000000 | tf_op jit(solution)/shard_map/raw/pallas_call | solution.py:693
  30.7 0.0 collective-permute-start.5
  30.7 0.5 collective-permute-start.6
  31.2 3.4 %collective-permute-done.5.above = f32[4,2,32,256]{3,2,1,0:T(8,128)S(1)} collective-permute-done((f32[4,2,32,256]{3,2,1,0:T(8,128)S(1)}, f32[4,2,32,256]{3,2,1,0:T(8,128)S(1)}, u32[]{:S(2)}, u32[]{:S(2)}) %collective-permute-start.5) | collective-permute-done | bytes 262176 | tf_op jit(solution)/shard_map/ppermute | solution.py:716
  34.6 3.1 %collective-permute-done.6.below = f32[4,2,32,256]{3,2,1,0:T(8,128)S(1)} collective-permute-done((f32[4,2,32,256]{3,2,1,0:T(8,128)S(1)}, f32[4,2,32,256]{3,2,1,0:T(8,128)S(1)}, u32[]{:S(2)}, u32[]{:S(2)}) %collective-permute-start.6) | collective-permute-done | bytes 262176 | tf_op jit(solution)/shard_map/ppermute | solution.py:716
  37.7 0.0 copy-start.1
  37.7 0.9 %collective-permute-start.7 = (f32[11,8,256]{2,1,0:T(8,128)S(1)}, f32[11,8,256]{2,1,0:T(8,128)S(1)}, u32[]{:S(2)}, u32[]{:S(2)}) collective-permute-start(f32[11,8,256]{2,1,0:T(8,128)S(1)} %get-tuple-element.50), channel_id=1, source_target_pairs={{0,14},{2,0},{4,2},{6,4},{8,6},{10,8},{12,10},{14,12},{1,15},{3,1}... | collective-permute-start | bytes 270344 | tf_op jit(solution)/shard_map/ppermute | solution.py:716
  38.6 2.7 %collective-permute-start.8 = (f32[11,8,256]{2,1,0:T(8,128)S(1)}, f32[11,8,256]{2,1,0:T(8,128)S(1)}, u32[]{:S(2)}, u32[]{:S(2)}) collective-permute-start(f32[11,8,256]{2,1,0:T(8,128)S(1)} %get-tuple-element.51), channel_id=1, source_target_pairs={{0,2},{2,4},{4,6},{6,8},{8,10},{10,12},{12,14},{14,0},{1,3},{3,5},... | collective-permute-start | bytes 270344 | tf_op jit(solution)/shard_map/ppermute | solution.py:716
  41.3 2.7 %bulk2.1 = (f32[2,8,32,256]{3,2,1,0:T(8,128)S(1)}, f32[2,4,16,2,1,256]{5,4,3,2,1,0:T(1,128)S(1)}, f32[2,4,32,128]{3,2,1,0:T(8,128)S(1)}) custom-call(s32[3]{0:T(128)S(1)} %pad_add_fusion.where, f32[4,2,32,256]{3,2,1,0:T(8,128)S(1)} %get-tuple-element.48.low, f32[4,2,32,256]{3,2,1,0:T(8,128)S(1)} %get-tuple-element.49.high, ...), custom_call_target="tpu_custom_call" | custom-call | flops 40000000 | bytes 2000000 | tf_op jit(solution)/shard_map/bulk2/pallas_call | solution.py:693
  44.0 0.0 collective-permute-done.7.y_above
  44.0 3.1 %collective-permute-done.8.y_below = f32[11,8,256]{2,1,0:T(8,128)S(1)} collective-permute-done((f32[11,8,256]{2,1,0:T(8,128)S(1)}, f32[11,8,256]{2,1,0:T(8,128)S(1)}, u32[]{:S(2)}, u32[]{:S(2)}) %collective-permute-start.8) | collective-permute-done | bytes 90144 | tf_op jit(solution)/shard_map/ppermute | solution.py:716
  47.1 0.8 %pack_z2.1 = f32[2,40,128]{2,1,0:T(8,128)S(1)} custom-call(s32[3]{0:T(128)S(1)} %pad_add_fusion.where, f32[4,2,32,256]{3,2,1,0:T(8,128)S(1)} %get-tuple-element.48.low, f32[4,2,32,256]{3,2,1,0:T(8,128)S(1)} %get-tuple-element.49.high, f32[4,2,32,256]{3,2,1,0:T(8,128)S(1)} %collective-permute-done.5.above, ...), custom_call_target="tpu_custom_call" | custom-call | bytes 2000000 | tf_op jit(solution)/shard_map/pack_z2/pallas_call | solution.py:693
  47.9 0.3 collective-permute-start.9
  48.2 1.7 %strips2.1 = (f32[2,8,16,256]{3,2,1,0:T(8,128)S(1)}, f32[2,4,16,128]{3,2,1,0:T(8,128)S(1)}) custom-call(s32[3]{0:T(128)S(1)} %pad_add_fusion.where, f32[11,8,256]{2,1,0:T(8,128)S(1)} %collective-permute-done.7.y_above, f32[11,8,256]{2,1,0:T(8,128)S(1)} %collective-permute-done.8.y_below, f32[2,4,16,2,1,256]{5,4,3,2,1,0:T(1,128)S(1)} %get-tuple-element.54.ends), custom_call_target="tpu_custom_call" | custom-call | flops 20000000 | bytes 2000000 | tf_op jit(solution)/shard_map/strips2/pallas_call | solution.py:693
  49.9 2.1 %collective-permute-done.9.z_in = f32[2,40,128]{2,1,0:T(8,128)S(1)} collective-permute-done((f32[2,40,128]{2,1,0:T(8,128)S(1)}, f32[2,40,128]{2,1,0:T(8,128)S(1)}, u32[]{:S(2)}, u32[]{:S(2)}) %collective-permute-start.9) | collective-permute-done | bytes 40992 | tf_op jit(solution)/shard_map/ppermute | solution.py:716
  52.0 1.8 %final.1 = f32[2,8,32,256]{3,2,1,0:T(8,128)} custom-call(s32[3]{0:T(128)S(1)} %pad_add_fusion.where, s32[8,32,256]{2,1,0:T(8,128)S(1)} %copy-done.1, f32[2,40,128]{2,1,0:T(8,128)S(1)} %collective-permute-done.9.z_in, f32[2,8,32,256]{3,2,1,0:T(8,128)S(1)} %get-tuple-element.53.bulk, f32[2,4,32,128]{3,2,1,0:T(8,128)S(1)} %get-tuple-element.52.ahead.bulk_edges, ...), custom_call_target="tpu_custom_call" | custom-call | bytes 2000000 | tf_op jit(solution)/shard_map/final/pallas_call | solution.py:693
  (9 shorter events, 0.0 us)
Async XLA Ops:
  0.0 3.9 %copy-start = (f32[2,3,8,32,256]{4,3,2,1,0:T(8,128)S(1)}, f32[2,3,8,32,256]{4,3,2,1,0:T(8,128)}, u32[]{:S(2)}) copy-start(f32[2,3,8,32,256]{4,3,2,1,0:T(8,128)} %modes.9) | copy-start | bytes 4718596
  1.4 8.2 %collective-permute-start = (f32[10,32,256]{2,1,0:T(8,128)S(1)}, f32[10,32,256]{2,1,0:T(8,128)S(1)}, u32[]{:S(2)}, u32[]{:S(2)}) collective-permute-start(f32[10,32,256]{2,1,0:T(8,128)S(1)} %get-tuple-element.33), channel_id=1, source_target_pairs={{0,112},{16,0},{32,16},{48,32},{64,48},{80,64},{96,80},{112,96},{1... | collective-permute-start | bytes 983048 | tf_op jit(solution)/shard_map/ppermute | solution.py:716
  3.9 5.6 %collective-permute-start.1 = (f32[4,32,256]{2,1,0:T(8,128)S(1)}, f32[4,32,256]{2,1,0:T(8,128)S(1)}, u32[]{:S(2)}, u32[]{:S(2)}) collective-permute-start(f32[4,32,256]{2,1,0:T(8,128)S(1)} %get-tuple-element.34), channel_id=1, source_target_pairs={{0,16},{16,32},{32,48},{48,64},{64,80},{80,96},{96,112},{112,0},{1... | collective-permute-start | bytes 393224 | tf_op jit(solution)/shard_map/ppermute | solution.py:716
  10.1 14.4 %collective-permute-start.2 = (f32[16,8,256]{2,1,0:T(8,128)S(1)}, f32[16,8,256]{2,1,0:T(8,128)S(1)}, u32[]{:S(2)}, u32[]{:S(2)}) collective-permute-start(f32[16,8,256]{2,1,0:T(8,128)S(1)} %get-tuple-element.35), channel_id=1, source_target_pairs={{0,14},{2,0},{4,2},{6,4},{8,6},{10,8},{12,10},{14,12},{1,15},{3,1}... | collective-permute-start | bytes 393224 | tf_op jit(solution)/shard_map/ppermute | solution.py:716
  16.7 7.9 %collective-permute-start.3 = (f32[8,8,256]{2,1,0:T(8,128)S(1)}, f32[8,8,256]{2,1,0:T(8,128)S(1)}, u32[]{:S(2)}, u32[]{:S(2)}) collective-permute-start(f32[8,8,256]{2,1,0:T(8,128)S(1)} %get-tuple-element.36), channel_id=1, source_target_pairs={{0,2},{2,4},{4,6},{6,8},{8,10},{10,12},{12,14},{14,0},{1,3},{3,5},... | collective-permute-start | bytes 196616 | tf_op jit(solution)/shard_map/ppermute | solution.py:716
  24.6 4.9 %copy-start.2 = (f32[6]{0:T(128)S(1)}, f32[6]{0:T(128)}, u32[]{:S(2)}) copy-start(f32[6]{0:T(128)} %eigenvalues.1) | copy-start | bytes 76
  24.6 4.9 %copy-start.3 = (s32[6]{0:T(128)S(1)}, s32[6]{0:T(128)}, u32[]{:S(2)}) copy-start(s32[6]{0:T(128)} %order.1) | copy-start | bytes 76
  25.4 4.1 %collective-permute-start.4 = (f32[2,40,128]{2,1,0:T(8,128)S(1)}, f32[2,40,128]{2,1,0:T(8,128)S(1)}, u32[]{:S(2)}, u32[]{:S(2)}) collective-permute-start(f32[2,40,128]{2,1,0:T(8,128)S(1)} %pack_z1.1), channel_id=1, source_target_pairs={{0,1},{1,0},{2,3},{3,2},{4,5},{5,4},{6,7},{7,6},{8,9},{9,8},{10,11... | collective-permute-start | bytes 122888 | tf_op jit(solution)/shard_map/ppermute | solution.py:716
  30.7 3.9 %collective-permute-start.5 = (f32[4,2,32,256]{3,2,1,0:T(8,128)S(1)}, f32[4,2,32,256]{3,2,1,0:T(8,128)S(1)}, u32[]{:S(2)}, u32[]{:S(2)}) collective-permute-start(f32[4,2,32,256]{3,2,1,0:T(8,128)S(1)} %get-tuple-element.48.low), channel_id=1, source_target_pairs={{0,112},{16,0},{32,16},{48,32},{64,48},{80,64},{96,80},{112,96},{1... | collective-permute-start | bytes 786440 | tf_op jit(solution)/shard_map/ppermute | solution.py:716
  30.7 7.0 %collective-permute-start.6 = (f32[4,2,32,256]{3,2,1,0:T(8,128)S(1)}, f32[4,2,32,256]{3,2,1,0:T(8,128)S(1)}, u32[]{:S(2)}, u32[]{:S(2)}) collective-permute-start(f32[4,2,32,256]{3,2,1,0:T(8,128)S(1)} %get-tuple-element.49.high), channel_id=1, source_target_pairs={{0,16},{16,32},{32,48},{48,64},{64,80},{80,96},{96,112},{112,0},{1... | collective-permute-start | bytes 786440 | tf_op jit(solution)/shard_map/ppermute | solution.py:716
  37.7 14.3 %copy-start.1 = (s32[8,32,256]{2,1,0:T(8,128)S(1)}, s32[8,32,256]{2,1,0:T(8,128)}, u32[]{:S(2)}) copy-start(s32[8,32,256]{2,1,0:T(8,128)} %mask.3) | copy-start | bytes 786436
  37.7 6.3 %collective-permute-start.7 = (f32[11,8,256]{2,1,0:T(8,128)S(1)}, f32[11,8,256]{2,1,0:T(8,128)S(1)}, u32[]{:S(2)}, u32[]{:S(2)}) collective-permute-start(f32[11,8,256]{2,1,0:T(8,128)S(1)} %get-tuple-element.50), channel_id=1, source_target_pairs={{0,14},{2,0},{4,2},{6,4},{8,6},{10,8},{12,10},{14,12},{1,15},{3,1}... | collective-permute-start | bytes 270344 | tf_op jit(solution)/shard_map/ppermute | solution.py:716
  38.6 8.5 %collective-permute-start.8 = (f32[11,8,256]{2,1,0:T(8,128)S(1)}, f32[11,8,256]{2,1,0:T(8,128)S(1)}, u32[]{:S(2)}, u32[]{:S(2)}) collective-permute-start(f32[11,8,256]{2,1,0:T(8,128)S(1)} %get-tuple-element.51), channel_id=1, source_target_pairs={{0,2},{2,4},{4,6},{6,8},{8,10},{10,12},{12,14},{14,0},{1,3},{3,5},... | collective-permute-start | bytes 270344 | tf_op jit(solution)/shard_map/ppermute | solution.py:716
  47.9 4.1 %collective-permute-start.9 = (f32[2,40,128]{2,1,0:T(8,128)S(1)}, f32[2,40,128]{2,1,0:T(8,128)S(1)}, u32[]{:S(2)}, u32[]{:S(2)}) collective-permute-start(f32[2,40,128]{2,1,0:T(8,128)S(1)} %pack_z2.1), channel_id=1, source_target_pairs={{0,1},{1,0},{2,3},{3,2},{4,5},{5,4},{6,7},{7,6},{8,9},{9,8},{10,11... | collective-permute-start | bytes 122888 | tf_op jit(solution)/shard_map/ppermute | solution.py:716

commit v4 on v3

--- a/solution.py
+++ b/solution.py
@@ -246,15 +246,18 @@
     return state
 
 
-def result_tile(m, x, i, j, bulk, strips, z_state, beside, sub):
+def pair_tile(m, x, i, j, bulk, strips, sub):
     rows, cols = slice(8 * i, 8 * i + 8), slice(LANES * j, LANES * j + LANES)
     value = bulk[m, x, rows, cols]
     if i == 0:
         value = value + jnp.where(sub < 4, strips[m, x, 8:16, cols], 0.0)
     if i == CY // 8 - 1:
         value = value + jnp.where(sub < 4, 0.0, strips[m, x, 0:8, cols])
-    turned = pltpu.roll(z_state[rows], (LANES - 4 - 8 * (x + W)) % LANES, 1)
-    return value + jnp.where(beside[j], turned, 0.0)
+    return value
+
+
+def z_tile(z_state, x, i):
+    return pltpu.roll(z_state[8 * i : 8 * i + 8], (LANES - 4 - 8 * (x + W)) % LANES, 1)
 
 
 def beside_halo(gz, lane):
@@ -265,6 +268,14 @@
     first = 8 * p + 4 * gz
     turned = pltpu.roll(tile, (8 * p + 4) % LANES, 1)
     return jnp.where((lane >= first) & (lane < first + 4), turned, acc)
+
+
+def own_strip(gz, load, rows=CY):
+    lane = iota((rows, LANES), 1)
+    acc = jnp.zeros((rows, LANES), F32)
+    for p in range(PX):
+        acc = pack_strip(gz, load(p), p, acc, lane)
+    return acc
 
 
 def edge_tiles(gz):
@@ -344,23 +355,22 @@
     return first, last
 
 
-def with_rims(packed, above, y_above, keep_x, keep_y, last):
+def with_plane8(packed, above, keep_x, last):
     cols = slice(CZ - LANES, CZ) if last else slice(0, LANES)
-    lane = iota((CY, LANES), 1)
-    sub, short = sub_lane()
-    rim = jnp.zeros((8, LANES), F32)
+    rows = packed.shape[0]
+    lane = iota(packed.shape, 1)
     for m in range(MODES):
         for c in range(3):
             to = 32 * m + NODES * c + CX
-            turned = pltpu.roll(above[W + 3 * m + c, :, cols], to + last, 1)
+            turned = pltpu.roll(above[W + 3 * m + c, 0:rows, cols], to + last, 1)
             packed = jnp.where(lane == to, turned * keep_x, packed)
-            for x in range(NODES):
-                n = NODES * c + x
-                to = 32 * m + n
-                row = y_above[8 + 4 * m + n // 8, n % 8 : n % 8 + 1, cols]
-                turned = pltpu.roll(jnp.broadcast_to(row, (8, LANES)), to + last, 1)
-                rim = jnp.where((short == to) & (sub == 0), turned, rim)
-    return jnp.concatenate([packed, rim * keep_y], axis=0)
+    return packed
+
+
+def with_row32(packed, y_above, keep_y, last):
+    sub, lane = sub_lane()
+    row = y_above[11, 3:4, LANES * last : LANES * last + LANES] * keep_y
+    return jnp.concatenate([packed, jnp.where(sub == 0, jnp.broadcast_to(row, (8, LANES)), 0.0)], axis=0)
 
 
 def pack_x1(design, mask, modes, src, down, up, field, solid, arrived):
@@ -386,11 +396,18 @@
         copy.wait()
 
 
-def energy_kernel(modes, stiff, mass, columns):
+def energy_kernel(modes, stiff, mass, columns, first_rows):
     lane = iota((CY, LANES), 1)
     columns[0], columns[1] = pack_columns(
         lambda m, c, x, j: modes[m, c, x, :, LANES * j : LANES * j + LANES], lane
     )
+
+    for m in range(MODES):
+        first_rows[4 * m + 3] = jnp.zeros((8, CZ), F32)
+        for c in range(3):
+            for x in range(CX):
+                n = NODES * c + x
+                first_rows[4 * m + n // 8, n % 8 : n % 8 + 1, :] = modes[m, c, x, 0:1, :]
 
     def mode_step(m, carry):
         for chunk in range(CY // 8):
@@ -416,7 +433,7 @@
     return above, p - W - CX
 
 
-def pack_y1(where, src, modes, above, below, ahead, down, up):
+def pack_y1(where, src, first_rows, columns, above, below, down, up):
     gx, gy, gz = pos(where)
     low = iota((8, CZ), 0) < 4
     for q in range(8):
@@ -425,20 +442,19 @@
         down[q] = jnp.where(low, a[i, 0:8, :], pltpu.roll(b[j, 0:8, :], 4, 0))
         up[q] = jnp.where(low, pltpu.roll(b[j, 24:32, :], 4, 0), a[i, 24:32, :])
     keep = jnp.where(gx < 7, 1.0, 0.0)
+    down[8:16] = first_rows[...]
     for m in range(MODES):
         for c in range(3):
-            for x in range(NODES):
-                n = c * NODES + x
-                if x < CX:
-                    row = modes[m, c, x, 0:1, :]
-                else:
-                    row = above[W + 3 * m + c, 0:1, :] * keep
-                down[8 + 4 * m + n // 8, n % 8 : n % 8 + 1, :] = row
-        down[8 + 4 * m + 3, 3:8, :] = jnp.zeros((5, CZ), F32)
+            n = NODES * c + CX
+            down[8 + 4 * m + n // 8, n % 8 : n % 8 + 1, :] = above[W + 3 * m + c, 0:1, :] * keep
+    for last in range(2):
+        row = with_plane8(columns[last, 0:8, :], above, keep, last)
+        down[11, 3:4, LANES * last : LANES * last + LANES] = row[0:1]
 
 
 def bulk_kernel1(
-    where, src, modes, above, below, bulk, ends, edges, stiff, mass, table, sb, one, two
+    where, src, modes, columns, above, below,
+    bulk, ends, edges, stiff, mass, own, rims, table, sb, one, two,
 ):
     at = pos(where)
     gx, gy, gz = at
@@ -449,7 +465,11 @@
         return a[at_plane, 8 * i : 8 * i + 8, :]
 
     bulk_sweeps(1, at, table, source, (sb, one, two), ends, edges, bulk)
+    edge = edge_tiles(gz)
+    own[0] = own_strip(gz, lambda p: plane_edge(src, above, below, p, edge))
     keep = jnp.where(gx < 7, 1.0, 0.0)
+    for last in range(2):
+        rims[last] = with_plane8(columns[last], above, keep, last)
     for m in range(MODES):
         for chunk in range(CY // 8):
             rows = slice(8 * chunk, 8 * chunk + 8)
@@ -466,23 +486,21 @@
     return jnp.where(iota(a.shape, 0) < 4, a, b)
 
 
-def pack_z1(where, src, columns, above, below, y_above, y_below, ahead, out):
+def plane_edge(own, above, below, p, edge):
+    a, i = pick_plane(own, above, below, p)
+    return a[i, :, edge]
+
+
+def pack_z1(where, own, rims, y_above, y_below, out):
     gx, gy, gz = pos(where)
     edge = edge_tiles(gz)
-    lane = iota((PY, LANES), 1)
-    acc = jnp.zeros((PY, LANES), F32)
-    for p in range(PX):
-        a, i = pick_plane(src, above, below, p)
-        tile = jnp.concatenate([a[i, :, edge], halo_tile(y_above, y_below, p, edge)], axis=0)
-        acc = pack_strip(gz, tile, p, acc, lane)
-    out[0] = acc
-    keep_x = jnp.where(gx < 7, 1.0, 0.0)
-    keep_y = jnp.where(gy < 7, 1.0, 0.0)
-    out[1] = with_rims(columns[0], above, y_above, keep_x, keep_y, 0)
+    out[0, 0:CY, :] = own[0]
+    out[0, CY:PY, :] = own_strip(gz, lambda p: halo_tile(y_above, y_below, p, edge), 8)
+    out[1] = with_row32(rims[0], y_above, jnp.where(gy < 7, 1.0, 0.0), 0)
 
 
 def strip_kernel1(
-    where, modes, columns, above, y_above, y_below, ends,
+    where, modes, rims, above, y_above, y_below, ends,
     strips, edges, rim, packed, table, sb, one, two, near, far,
 ):
     at = pos(where)
@@ -493,7 +511,7 @@
     )
     keep_x = jnp.where(gx < 7, 1.0, 0.0)
     keep_y = jnp.where(gy < 7, 1.0, 0.0)
-    packed[...] = with_rims(columns[1], above, y_above, keep_x, keep_y, 1)
+    packed[...] = with_row32(rims[1], y_above, keep_y, 1)
     for m in range(MODES):
         for c in range(3):
             for x in range(NODES):
@@ -519,36 +537,21 @@
         rim[m, 1] = mass_of(cur) + mass_of(prev)
 
 
-def raw_kernel(
-    eigenvalues, order, where, z_in, packed, bulk, bulk_edges, strips, strip_edges,
-    stiff, mass, stiff7, mass7, rim, low, high,
+def raw_planes(
+    planes, eigenvalues, order, gz, z_state, column_stiff, column_mass, bulk, strips,
+    stiff, mass, stiff7, mass7, rim, out,
 ):
-    gx, gy, gz = pos(where)
     sub, lane = sub_lane()
-    z_state = z_sweeps(0, strip_scale(gx, gy), z_in[0], bulk_edges, strip_edges)
     beside = beside_halo(gz, lane)
-
-    near, far = packed[...], z_in[1] * jnp.where(gz < 1, 1.0, 0.0)
-    a0, d0 = near + far, far - near
-    a1, d1 = pltpu.roll(a0, PY - 1, 0), pltpu.roll(d0, PY - 1, 0)
-    parts = [(x[0][0:CY]) for x in y_parts([(a0, d0, a1, d1)])]
-
-    def turned(t, by):
-        return pltpu.roll(t, (LANES - by) % LANES, 1) if by else t
-
-    prev = [[turned(t, NODES * c) for c in range(3)] for t in parts]
-    cur = [[turned(t, NODES * c + 1) for c in range(3)] for t in parts]
-    column_stiff = energy_terms(prev, cur)
-    column_mass = mass_of(cur) + mass_of(prev)
-
     factor = 3.0 * (1.0 - stiff_floor) / 16.0
     lams = [eigenvalues[order[m]] * (0.125 * 0.25) for m in range(MODES)]
-    for x in range(CX):
+    for x in planes:
         for i in range(CY // 8):
             rows = slice(8 * i, 8 * i + 8)
+            correction = z_tile(z_state, x, i)
             for j in range(2):
                 cols = slice(LANES * j, LANES * j + LANES)
-                phys = result_tile(0, x, i, j, bulk, strips, z_state, beside, sub)
+                phys = pair_tile(0, x, i, j, bulk, strips, sub) + jnp.where(beside[j], correction, 0.0)
                 phys = (factor * phys) * phys
                 for m in range(MODES):
                     if x < CX - 1:
@@ -560,13 +563,45 @@
                         e = jnp.where(sub == 7, jnp.broadcast_to(rim[m, 1, x : x + 1, cols], (8, LANES)), e)
                     if j == 1:
                         by = LANES - 1 - (32 * m + x)
-                        k = jnp.where(lane == LANES - 1, pltpu.roll(column_stiff[rows], by, 1), k)
-                        e = jnp.where(lane == LANES - 1, pltpu.roll(column_mass[rows], by, 1), e)
-                    raw = phys * k - lams[m] * e
-                    if x < W:
-                        low[x, m, rows, cols] = raw
-                    else:
-                        high[x - W, m, rows, cols] = raw
+                        k = jnp.where(lane == LANES - 1, pltpu.roll(column_stiff[rows, :], by, 1), k)
+                        e = jnp.where(lane == LANES - 1, pltpu.roll(column_mass[rows, :], by, 1), e)
+                    out[x % W, m, rows, cols] = phys * k - lams[m] * e
+
+
+def raw_kernel1(
+    eigenvalues, order, where, z_in, packed, bulk, bulk_edges, strips, strip_edges,
+    stiff, mass, stiff7, mass7, rim, low, z_parts,
+):
+    gx, gy, gz = pos(where)
+    z_state = z_sweeps(0, strip_scale(gx, gy), z_in[0], bulk_edges, strip_edges)
+
+    near, far = packed[...], z_in[1] * jnp.where(gz < 1, 1.0, 0.0)
+    a0, d0 = near + far, far - near
+    a1, d1 = pltpu.roll(a0, PY - 1, 0), pltpu.roll(d0, PY - 1, 0)
+    parts = [(x[0][0:CY]) for x in y_parts([(a0, d0, a1, d1)])]
+
+    def turned(t, by):
+        return pltpu.roll(t, (LANES - by) % LANES, 1) if by else t
+
+    prev = [[turned(t, NODES * c) for c in range(3)] for t in parts]
+    cur = [[turned(t, NODES * c + 1) for c in range(3)] for t in parts]
+    column_stiff = energy_terms(prev, cur)
+    column_mass = mass_of(cur) + mass_of(prev)
+    z_parts[0], z_parts[1], z_parts[2] = z_state[0:CY], column_stiff, column_mass
+    raw_planes(
+        range(W), eigenvalues, order, gz, z_state, column_stiff, column_mass, bulk, strips,
+        stiff, mass, stiff7, mass7, rim, low,
+    )
+
+
+def raw_kernel2(
+    eigenvalues, order, where, z_parts, bulk, strips, stiff, mass, stiff7, mass7, rim, high
+):
+    gx, gy, gz = pos(where)
+    raw_planes(
+        range(W, CX), eigenvalues, order, gz, z_parts[0], z_parts.at[1], z_parts.at[2], bulk, strips,
+        stiff, mass, stiff7, mass7, rim, high,
+    )
 
 
 def raw_plane(low, high, above, below, p):
@@ -621,7 +656,7 @@
     return jnp.where(iota(a.shape, 0) < 4, a, b)
 
 
-def bulk_kernel2(where, low, high, above, below, bulk, ends, edges, table, sb, one, two):
+def bulk_kernel2(where, low, high, above, below, bulk, ends, edges, own, table, sb, one, two):
     at = pos(where)
     fill_bulk(table, at[1], at[2])
 
@@ -630,48 +665,49 @@
         return a[at_plane, m, 8 * i : 8 * i + 8, :]
 
     bulk_sweeps(MODES, at, table, source, (sb, one, two), ends, edges, bulk)
-
-
-def pack_z2(where, low, high, above, below, y_above, y_below, ahead, out):
+    edge = edge_tiles(at[2])
+    for m in range(MODES):
+
+        def load(p, m=m):
+            a, i = raw_plane(low, high, above, below, p)
+            return a[i, m, :, edge]
+
+        own[m] = own_strip(at[2], load)
+
+
+def pack_z2(where, own, y_above, y_below, out):
     gx, gy, gz = pos(where)
     edge = edge_tiles(gz)
-    lane = iota((PY, LANES), 1)
-    for m in range(MODES):
-        acc = jnp.zeros((PY, LANES), F32)
-        for p in range(PX):
-            a, i = raw_plane(low, high, above, below, p)
-            halo = raw_halo(y_above, y_below, m, p, edge)
-            acc = pack_strip(gz, jnp.concatenate([a[i, m, :, edge], halo], axis=0), p, acc, lane)
-        out[m] = acc
-
-
-def strip_kernel2(where, y_above, y_below, ends, strips, edges, table, sb, one, two):
-    at = pos(where)
-    fill_strips(table, at[1], at[2])
+    for m in range(MODES):
+        out[m, 0:CY, :] = own[m]
+        out[m, CY:PY, :] = own_strip(gz, lambda p, m=m: raw_halo(y_above, y_below, m, p, edge), 8)
+
+
+def strip_kernel2(
+    where, mask, y_above, y_below, ends, bulk, out, side, edges, strips, table, sb, one, two, held, left
+):
+    gx, gy, gz = at = pos(where)
+    sub, lane = sub_lane()
+    fill_strips(table, gy, gz)
 
     def source(m, p):
         return raw_halo(y_above, y_below, m, p)
 
     strip_sweeps(MODES, at, table, source, ends, (sb, one, two), edges, strips)
-
-
-def final_kernel(where, mask, z_in, bulk, bulk_edges, strips, strip_edges, out, held, left):
-    gx, gy, gz = pos(where)
-    sub, lane = sub_lane()
-    beside = beside_halo(gz, lane)
-    scale = strip_scale(gx, gy)
-    states = [z_sweeps(m, scale, z_in[m], bulk_edges, strip_edges) for m in range(MODES)]
     copies = []
     for m in range(MODES):
         for x in range(CX):
             for i in range(CY // 8):
                 rows = slice(8 * i, 8 * i + 8)
+                pair = []
                 for j in range(2):
                     cols = slice(LANES * j, LANES * j + LANES)
-                    value = result_tile(m, x, i, j, bulk, strips, states[m], beside, sub)
+                    value = pair_tile(m, x, i, j, bulk, strips, sub)
                     held[m, x, rows, cols] = value * mask[x, rows, cols].astype(F32)
-            if x % 2:
-                part = (m, slice(x - 1, x + 1))
+                    pair.append(value)
+                side[m, x, rows, :] = jnp.where(gz == 0, pair[1], pair[0])
+            if x % 4 == 3:
+                part = (m, slice(x - 3, x + 1))
                 copy = pltpu.make_async_copy(held.at[part], out.at[part], left.at[len(copies)])
                 copy.start()
                 copies.append(copy)
@@ -679,6 +715,32 @@
         copy.wait()
 
 
+def final_kernel(where, mask, z_in, bulk_edges, strip_edges, side, given, out, held, left):
+    gx, gy, gz = pos(where)
+    sub, lane = sub_lane()
+    at_end = beside_halo(gz, lane)
+    beside = at_end[0] | at_end[1]
+    edge = edge_tiles(gz)
+    scale = strip_scale(gx, gy)
+    copies = []
+    for m in range(MODES):
+        z_state = z_sweeps(m, scale, z_in[m], bulk_edges, strip_edges)
+        for x in range(CX):
+            for i in range(CY // 8):
+                rows = slice(8 * i, 8 * i + 8)
+                value = side[m, x, rows, :] + jnp.where(beside, z_tile(z_state, x, i), 0.0)
+                held[m, x, rows, :] = value * mask[x, rows, edge].astype(F32)
+            if x % 4 == 3:
+                planes = slice(x - 3, x + 1)
+                copy = pltpu.make_async_copy(
+                    held.at[m, planes], out.at[m, planes, :, edge], left.at[len(copies)]
+                )
+                copy.start()
+                copies.append(copy)
+    for copy in copies:
+        copy.wait()
+
+
 SMEM = pl.BlockSpec(memory_space=pltpu.SMEM)
 
 
@@ -686,10 +748,11 @@
     return pl.BlockSpec(x.shape, lambda i: (0,) * x.ndim)
 
 
-def call(kernel, name, outs, args, specs=None, out_spec=None, scratch=(), flops=0):
+def call(kernel, name, outs, args, specs=None, out_specs=None, scratch=(), flops=0, aliases=None):
     specs = specs or {}
     shapes = tuple(jax.ShapeDtypeStruct(s, F32) for s in outs)
-    more = {} if out_spec is None else {"out_specs": out_spec}
+    out_specs = out_specs or {}
+    out_specs = tuple(out_specs.get(i, whole(s)) for i, s in enumerate(shapes))
     return pl.pallas_call(
         kernel,
         grid=(1,),
@@ -699,12 +762,12 @@
         compiler_params=pltpu.CompilerParams(vmem_limit_bytes=24 * 1024 * 1024),
         cost_estimate=pl.CostEstimate(flops=flops, bytes_accessed=2_000_000, transcendentals=0),
         name=name,
-        **more,
+        out_specs=out_specs if len(shapes) > 1 else out_specs[0],
+        input_output_aliases=aliases or {},
     )(*args)
 
 
 HBM = pl.BlockSpec(memory_space=pltpu.HBM)
-ANY = pl.BlockSpec(memory_space=pl.ANY)
 
 
 def ring(axis, step):
@@ -737,59 +800,57 @@
     )
     above, below = shift(down, "gx", -1), shift(up, "gx", 1)
     field = (MODES, CX - 1, CY, CZ)
-    stiff, mass, columns = call(
-        energy_kernel, "energy", [field, field, (2, CY, LANES)], (mode_fields,), flops=40_000_000
-    )
-
-    block = pl.BlockSpec((MODES, 3, CX, 8, CZ), lambda i: (0, 0, 0, 0, 0))
+    stiff, mass, columns, first_rows = call(
+        energy_kernel, "energy", [field, field, (2, CY, LANES), (8, 8, CZ)], (mode_fields,), flops=40_000_000
+    )
+
     down, up = call(
-        pack_y1, "pack_y1", [(16, 8, CZ), (8, 8, CZ)],
-        (where, src, mode_fields, above, below, columns), {2: block, 5: ANY},
+        pack_y1, "pack_y1", [(16, 8, CZ), (8, 8, CZ)], (where, src, first_rows, columns, above, below)
     )
     y_above, y_below = shift(down, "gy", -1), shift(up, "gy", 1)
     plane = (MODES, CY, CZ)
-    bulk, ends, bulk_edges, stiff7, mass7 = call(
-        bulk_kernel1, "bulk1", bulk_outs + [plane, plane],
-        (where, src, mode_fields, above, below), scratch=bulk_scratch, flops=30_000_000,
-    )
-
-    edge = call(
-        pack_z1, "pack_z1", [(2, PY, LANES)],
-        (where, src, columns, above, below, y_above, y_below, bulk_edges), {7: ANY},
-    )
-    z_in = shift(edge, "gz", 1)
+    bulk, ends, bulk_edges, stiff7, mass7, own, rims = call(
+        bulk_kernel1, "bulk1", bulk_outs + [plane, plane, (1, CY, LANES), (2, CY, LANES)],
+        (where, src, mode_fields, columns, above, below), scratch=bulk_scratch, flops=30_000_000,
+    )
+
+    z_in = shift(call(pack_z1, "pack_z1", [(2, PY, LANES)], (where, own, rims, y_above, y_below)), "gz", 1)
     strips, strip_edges, rim, packed = call(
         strip_kernel1, "strips1", strip_outs + [(MODES, 2, 8, CZ), (PY, LANES)],
-        (where, mode_fields, columns, above, y_above, y_below, ends),
+        (where, mode_fields, rims, above, y_above, y_below, ends),
         scratch=strip_scratch + [(3, 16, CZ)] * 2, flops=20_000_000,
     )
-    low, high = call(
-        raw_kernel, "raw", [(W, MODES, CY, CZ)] * 2,
-        (eigenvalues, mode_order, where, z_in, packed, bulk, bulk_edges, strips, strip_edges,
-         stiff, mass, stiff7, mass7, rim),
-    )
+    half = (W, MODES, CY, CZ)
+    scalars = (eigenvalues, mode_order, where)
+    energies = (stiff, mass, stiff7, mass7, rim)
+    low, z_parts = call(
+        raw_kernel1, "raw1", [half, (3, CY, LANES)],
+        (*scalars, z_in, packed, bulk, bulk_edges, strips, strip_edges, *energies),
+    )
+    above = shift(low, "gx", -1)
+    high = call(raw_kernel2, "raw2", [half], (*scalars, z_parts, bulk, strips, *energies), flops=60_000_000)
+    below = shift(high, "gx", 1)
 
     bulk_outs, bulk_scratch, strip_outs, strip_scratch = sweep_outs(MODES)
-    above, below = shift(low, "gx", -1), shift(high, "gx", 1)
     planes = (low, high, above, below)
     down, up = call(pack_y2, "pack_y2", [(CX + 3, 8, CZ)] * 2, planes)
     y_above, y_below = shift(down, "gy", -1), shift(up, "gy", 1)
-    bulk, ends, bulk_edges = call(
-        bulk_kernel2, "bulk2", bulk_outs, (where, *planes), scratch=bulk_scratch, flops=40_000_000
-    )
-    edge = call(
-        pack_z2, "pack_z2", [(MODES, PY, LANES)],
-        (where, *planes, y_above, y_below, bulk_edges), {7: ANY},
-    )
-    z_in = shift(edge, "gz", 1)
-    strips, strip_edges = call(
-        strip_kernel2, "strips2", strip_outs, (where, y_above, y_below, ends),
-        scratch=strip_scratch, flops=20_000_000,
+    bulk, ends, bulk_edges, own = call(
+        bulk_kernel2, "bulk2", bulk_outs + [(MODES, CY, LANES)], (where, *planes),
+        scratch=bulk_scratch, flops=40_000_000,
+    )
+    z_in = shift(call(pack_z2, "pack_z2", [(MODES, PY, LANES)], (where, own, y_above, y_below)), "gz", 1)
+    result = (MODES, CX, CY, CZ)
+    out, side, strip_edges = call(
+        strip_kernel2, "strips2", [result, (MODES, CX, CY, LANES), strip_outs[1]],
+        (where, solid_mask, y_above, y_below, ends, bulk), out_specs={0: HBM},
+        scratch=[strip_outs[0]] + strip_scratch + [result, pltpu.SemaphoreType.DMA((4,))],
+        flops=20_000_000,
     )
     return call(
-        final_kernel, "final", [(MODES, CX, CY, CZ)],
-        (where, solid_mask, z_in, bulk, bulk_edges, strips, strip_edges), out_spec=HBM,
-        scratch=[(MODES, CX, CY, CZ), pltpu.SemaphoreType.DMA((MODES * CX // 2,))],
+        final_kernel, "final", [result],
+        (where, solid_mask, z_in, bulk_edges, strip_edges, side, out), {6: HBM}, {0: HBM},
+        scratch=[(MODES, CX, CY, LANES), pltpu.SemaphoreType.DMA((4,))], aliases={6: 0},
     )
 
 

time: 54 us -> 53.7 us (level)
  waiting for transfers between devices: 21.9 us -> 17.4 us
  starting transfers between devices: 14.2 us -> 17.2 us
  Pallas kernels: 17.5 us -> 18.7 us
    ppermute x10, waiting for transfers between devices: 21.9 us -> 17.4 us  [shift(): return lax.ppermute(x, axis, ring(axis, step))]
    ppermute x10, starting transfers between devices: 14.2 us -> 17.2 us  [shift(): return lax.ppermute(x, axis, ring(axis, step))]
    pallas_call x12 -> x13, Pallas kernels: 17.5 us -> 18.7 us  [call(): pl.pallas_call(kernel, grid=(1,), out_shape=shapes if len(shapes) > 1 els...]
  transfers between devices with their start and end apart: 10 -> 10, of which waited for: 7 -> 6; matrix products, arithmetic and copies ran while one was open for 0% -> 0% of each run, Pallas kernels for 20% -> 22%
where the time goes in v4:
time: 53.7 us; the launch traced here: 53.6 us
  Pallas kernels  18.7 us (35%)
  waiting for transfers between devices  17.4 us (32%)
  starting transfers between devices  17.2 us (32%)
    pallas_call x13, Pallas kernels, call(): pl.pallas_call(kernel, grid=(1,), out_shape=shapes if len(shapes) > 1 els...  18.7 us
    ppermute x10, waiting for transfers between devices, shift(): return lax.ppermute(x, axis, ring(axis, step))  17.4 us
    ppermute x10, starting transfers between devices, shift(): return lax.ppermute(x, axis, ring(axis, step))  17.2 us
  transfers between devices with their start and end apart: 10, of which 6 were waited for; matrix products, arithmetic and copies ran while one was open for 0% of the time, Pallas kernels for 22%

profile of v4, /device:TPU:0, one launch (start us, length us, event | category | flops | bytes accessed | tf_op | source)
XLA Modules:
  0.0 53.6 jit_solution(987187122395274476)
XLA Ops:
  0.0 1.4 %pack_x1.1 = (f32[8,32,256]{2,1,0:T(8,128)S(1)}, f32[10,32,256]{2,1,0:T(8,128)S(1)}, f32[4,32,256]{2,1,0:T(8,128)S(1)}) custom-call(f32[8,32,256]{2,1,0:T(8,128)} %design.1, s32[8,32,256]{2,1,0:T(8,128)} %mask.5, f32[2,3,8,32,256]{4,3,2,1,0:T(8,128)} %modes.7), custom_call_target="tpu_custom_call" | custom-call | bytes 2000000 | tf_op jit(solution)/shard_map/pack_x1/pallas_call | solution.py:756
  1.4 2.5 %collective-permute-start = (f32[10,32,256]{2,1,0:T(8,128)S(1)}, f32[10,32,256]{2,1,0:T(8,128)S(1)}, u32[]{:S(2)}, u32[]{:S(2)}) collective-permute-start(f32[10,32,256]{2,1,0:T(8,128)S(1)} %get-tuple-element.38), channel_id=1, source_target_pairs={{0,112},{16,0},{32,16},{48,32},{64,48},{80,64},{96,80},{112,96},{1... | collective-permute-start | bytes 983048 | tf_op jit(solution)/shard_map/ppermute | solution.py:779
  3.9 0.0 collective-permute-start.1
  3.9 3.1 %energy.1 = (f32[2,7,32,256]{3,2,1,0:T(8,128)S(1)}, f32[2,7,32,256]{3,2,1,0:T(8,128)S(1)}, f32[2,32,128]{2,1,0:T(8,128)S(1)}, f32[8,8,256]{2,1,0:T(8,128)S(1)}) custom-call(f32[2,3,8,32,256]{4,3,2,1,0:T(8,128)S(1)} %copy-done), custom_call_target="tpu_custom_call" | custom-call | flops 40000000 | bytes 2000000 | tf_op jit(solution)/shard_map/energy/pallas_call | solution.py:756
  7.0 0.1 pad_add_fusion.where
  7.1 2.4 %collective-permute-done.1.below = f32[4,32,256]{2,1,0:T(8,128)S(1)} collective-permute-done((f32[4,32,256]{2,1,0:T(8,128)S(1)}, f32[4,32,256]{2,1,0:T(8,128)S(1)}, u32[]{:S(2)}, u32[]{:S(2)}) %collective-permute-start.1) | collective-permute-done | bytes 131104 | tf_op jit(solution)/shard_map/ppermute | solution.py:779
  9.5 0.6 %pack_y1.1 = (f32[16,8,256]{2,1,0:T(8,128)S(1)}, f32[8,8,256]{2,1,0:T(8,128)S(1)}) custom-call(s32[3]{0:T(128)S(1)} %pad_add_fusion.where, f32[8,32,256]{2,1,0:T(8,128)S(1)} %get-tuple-element.36.src, f32[8,8,256]{2,1,0:T(8,128)S(1)} %get-tuple-element.42.first_rows, f32[2,32,128]{2,1,0:T(8,128)S(1)} %get-tuple-element.37.columns, ...), custom_call_target="tpu_custom_call" | custom-call | bytes 2000000 | tf_op jit(solution)/shard_map/pack_y1/pallas_call | solution.py:756
  10.2 6.6 %collective-permute-start.2 = (f32[16,8,256]{2,1,0:T(8,128)S(1)}, f32[16,8,256]{2,1,0:T(8,128)S(1)}, u32[]{:S(2)}, u32[]{:S(2)}) collective-permute-start(f32[16,8,256]{2,1,0:T(8,128)S(1)} %get-tuple-element.43), channel_id=1, source_target_pairs={{0,14},{2,0},{4,2},{6,4},{8,6},{10,8},{12,10},{14,12},{1,15},{3,1}... | collective-permute-start | bytes 393224 | tf_op jit(solution)/shard_map/ppermute | solution.py:779
  16.7 0.0 collective-permute-start.3
  16.7 2.2 %bulk1.1 = (f32[1,8,32,256]{3,2,1,0:T(8,128)S(1)}, f32[1,4,16,2,1,256]{5,4,3,2,1,0:T(1,128)S(1)}, f32[1,4,32,128]{3,2,1,0:T(8,128)S(1)}, f32[2,32,256]{2,1,0:T(8...) custom-call(s32[3]{0:T(128)S(1)} %pad_add_fusion.where, ...), custom_call_target="tpu_custom_call" | custom-call | flops 30000000 | bytes 2000000 | tf_op jit(solution)/shard_map/bulk1/pallas_call | solution.py:756
  19.0 0.0 copy-start.2
  19.0 0.0 copy-start.3
  19.0 5.6 %collective-permute-done.3.y_below = f32[8,8,256]{2,1,0:T(8,128)S(1)} collective-permute-done((f32[8,8,256]{2,1,0:T(8,128)S(1)}, f32[8,8,256]{2,1,0:T(8,128)S(1)}, u32[]{:S(2)}, u32[]{:S(2)}) %collective-permute-start.3) | collective-permute-done | bytes 65568 | tf_op jit(solution)/shard_map/ppermute | solution.py:779
  24.6 0.6 %pack_z1.1 = f32[2,40,128]{2,1,0:T(8,128)S(1)} custom-call(s32[3]{0:T(128)S(1)} %pad_add_fusion.where, f32[1,32,128]{2,1,0:T(8,128)S(1)} %get-tuple-element.40.own, f32[2,32,128]{2,1,0:T(8,128)S(1)} %get-tuple-element.41.rims, f32[16,8,256]{2,1,0:T(8,128)S(1)} %collective-permute-done.2.y_above, f32[8,8,256]{2,1,0:T(8,128)S(1)} %collective-permute-done.3.y_below), custom_call_target="tpu_custom_call" | custom-call | bytes 2000000 | tf_op jit(solution)/shard_map/pack_z1/pallas_call | solution.py:756
  25.2 0.7 %collective-permute-start.4 = (f32[2,40,128]{2,1,0:T(8,128)S(1)}, f32[2,40,128]{2,1,0:T(8,128)S(1)}, u32[]{:S(2)}, u32[]{:S(2)}) collective-permute-start(f32[2,40,128]{2,1,0:T(8,128)S(1)} %pack_z1.1), channel_id=1, source_target_pairs={{0,1},{1,0},{2,3},{3,2},{4,5},{5,4},{6,7},{7,6},{8,9},{9,8},{10,11... | collective-permute-start | bytes 122888 | tf_op jit(solution)/shard_map/ppermute | solution.py:779
  25.9 1.4 %strips1.1 = (f32[1,8,16,256]{3,2,1,0:T(8,128)S(1)}, f32[1,4,16,128]{3,2,1,0:T(8,128)S(1)}, f32[2,2,8,256]{3,2,1,0:T(8,128)S(1)}, f32[40,128]{1,0:T(8,128)S(1)}) custom-call(s32[3]{0:T(128)S(1)} %pad_add_fusion.where, f32[2,3,8,32,256]{4,3,2,1,0:T(8,128)S(1)} %copy-done, f32[2,32,128]{2,1,0:T(8,128)S(1)} %get-tuple-element.41.rims, ...), custom_call_target="tpu_custom_call" | custom-call | flops 20000000 | bytes 2000000 | tf_op jit(solution)/shard_map/strips1/pallas_call | solution.py:756
  27.3 2.0 %collective-permute-done.4.z_in = f32[2,40,128]{2,1,0:T(8,128)S(1)} collective-permute-done((f32[2,40,128]{2,1,0:T(8,128)S(1)}, f32[2,40,128]{2,1,0:T(8,128)S(1)}, u32[]{:S(2)}, u32[]{:S(2)}) %collective-permute-start.4) | collective-permute-done | bytes 40992 | tf_op jit(solution)/shard_map/ppermute | solution.py:779
  29.3 1.1 %raw1.1 = (f32[4,2,32,256]{3,2,1,0:T(8,128)S(1)}, f32[3,32,128]{2,1,0:T(8,128)S(1)}) custom-call(f32[6]{0:T(128)S(1)} %copy-done.2, s32[6]{0:T(128)S(1)} %copy-done.3, s32[3]{0:T(128)S(1)} %pad_add_fusion.where, f32[2,40,128]{2,1,0:T(8,128)S(1)} %collective-permute-done.4.z_in, f32[40,128]{1,0:T(8,128)S(1)} %get-tuple-element.46.packed, ...), custom_call_target="tpu_custom_call" | custom-call | bytes 2000000 | tf_op jit(solution)/shard_map/raw1/pallas_call | solution.py:756
  30.4 0.7 %raw2.1.high = f32[4,2,32,256]{3,2,1,0:T(8,128)S(1)} custom-call(f32[6]{0:T(128)S(1)} %copy-done.2, s32[6]{0:T(128)S(1)} %copy-done.3, s32[3]{0:T(128)S(1)} %pad_add_fusion.where, f32[3,32,128]{2,1,0:T(8,128)S(1)} %get-tuple-element.57.z_parts, f32[1,8,32,256]{3,2,1,0:T(8,128)S(1)} %get-tuple-element.47.bulk, ...), custom_call_target="tpu_custom_call" | custom-call | flops 60000000 | bytes 2000000 | tf_op jit(solution)/shard_map/raw2/pallas_call | solution.py:756
  31.2 0.0 copy-start.1
  31.2 0.0 collective-permute-start.6
  31.2 2.9 %collective-permute-start.5 = (f32[4,2,32,256]{3,2,1,0:T(8,128)S(1)}, f32[4,2,32,256]{3,2,1,0:T(8,128)S(1)}, u32[]{:S(2)}, u32[]{:S(2)}) collective-permute-start(f32[4,2,32,256]{3,2,1,0:T(8,128)S(1)} %get-tuple-element.56.low), channel_id=1, source_target_pairs={{0,112},{16,0},{32,16},{48,32},{64,48},{80,64},{96,80},{112,96},{1... | collective-permute-start | bytes 786440 | tf_op jit(solution)/shard_map/ppermute | solution.py:779
  34.1 4.1 %collective-permute-done.6.below = f32[4,2,32,256]{3,2,1,0:T(8,128)S(1)} collective-permute-done((f32[4,2,32,256]{3,2,1,0:T(8,128)S(1)}, f32[4,2,32,256]{3,2,1,0:T(8,128)S(1)}, u32[]{:S(2)}, u32[]{:S(2)}) %collective-permute-start.6) | collective-permute-done | bytes 262176 | tf_op jit(solution)/shard_map/ppermute | solution.py:779
  38.2 0.8 %collective-permute-start.7 = (f32[11,8,256]{2,1,0:T(8,128)S(1)}, f32[11,8,256]{2,1,0:T(8,128)S(1)}, u32[]{:S(2)}, u32[]{:S(2)}) collective-permute-start(f32[11,8,256]{2,1,0:T(8,128)S(1)} %get-tuple-element.59), channel_id=1, source_target_pairs={{0,14},{2,0},{4,2},{6,4},{8,6},{10,8},{12,10},{14,12},{1,15},{3,1}... | collective-permute-start | bytes 270344 | tf_op jit(solution)/shard_map/ppermute | solution.py:779
  39.0 2.8 %collective-permute-start.8 = (f32[11,8,256]{2,1,0:T(8,128)S(1)}, f32[11,8,256]{2,1,0:T(8,128)S(1)}, u32[]{:S(2)}, u32[]{:S(2)}) collective-permute-start(f32[11,8,256]{2,1,0:T(8,128)S(1)} %get-tuple-element.60), channel_id=1, source_target_pairs={{0,2},{2,4},{4,6},{6,8},{8,10},{10,12},{12,14},{14,0},{1,3},{3,5},... | collective-permute-start | bytes 270344 | tf_op jit(solution)/shard_map/ppermute | solution.py:779
  41.8 2.8 %bulk2.1 = (f32[2,8,32,256]{3,2,1,0:T(8,128)S(1)}, f32[2,4,16,2,1,256]{5,4,3,2,1,0:T(1,128)S(1)}, f32[2,4,32,128]{3,2,1,0:T(8,128)S(1)}, f32[2,32,128]{2,1,0:T(8,128)S(1)}) custom-call(s32[3]{0:T(128)S(1)} %pad_add_fusion.where, f32[4,2,32,256]{3,2,1,0:T(8,128)S(1)} %get-tuple-element.56.low, f32[4,2,32,256]{3,2,1,0:T(8,128)S(1)} %raw2.1.high, ...), custom_call_target="tpu_custom_call" | custom-call | flops 40000000 | bytes 2000000 | tf_op jit(solution)/shard_map/bulk2/pallas_call | solution.py:756
  44.6 2.5 %collective-permute-done.8.y_below = f32[11,8,256]{2,1,0:T(8,128)S(1)} collective-permute-done((f32[11,8,256]{2,1,0:T(8,128)S(1)}, f32[11,8,256]{2,1,0:T(8,128)S(1)}, u32[]{:S(2)}, u32[]{:S(2)}) %collective-permute-start.8) | collective-permute-done | bytes 90144 | tf_op jit(solution)/shard_map/ppermute | solution.py:779
  47.1 0.6 %pack_z2.1 = f32[2,40,128]{2,1,0:T(8,128)S(1)} custom-call(s32[3]{0:T(128)S(1)} %pad_add_fusion.where, f32[2,32,128]{2,1,0:T(8,128)S(1)} %get-tuple-element.58.own, f32[11,8,256]{2,1,0:T(8,128)S(1)} %collective-permute-done.7.y_above, f32[11,8,256]{2,1,0:T(8,128)S(1)} %collective-permute-done.8.y_below), custom_call_target="tpu_custom_call" | custom-call | bytes 2000000 | tf_op jit(solution)/shard_map/pack_z2/pallas_call | solution.py:756
  47.8 0.9 %collective-permute-start.9 = (f32[2,40,128]{2,1,0:T(8,128)S(1)}, f32[2,40,128]{2,1,0:T(8,128)S(1)}, u32[]{:S(2)}, u32[]{:S(2)}) collective-permute-start(f32[2,40,128]{2,1,0:T(8,128)S(1)} %pack_z2.1), channel_id=1, source_target_pairs={{0,1},{1,0},{2,3},{3,2},{4,5},{5,4},{6,7},{7,6},{8,9},{9,8},{10,11... | collective-permute-start | bytes 122888 | tf_op jit(solution)/shard_map/ppermute | solution.py:779
  48.6 2.4 %strips2.1 = (f32[2,8,32,256]{3,2,1,0:T(8,128)}, f32[2,8,32,128]{3,2,1,0:T(8,128)S(1)}, f32[2,4,16,128]{3,2,1,0:T(8,128)S(1)}) custom-call(s32[3]{0:T(128)S(1)} %pad_add_fusion.where, s32[8,32,256]{2,1,0:T(8,128)S(1)} %copy-done.1, f32[11,8,256]{2,1,0:T(8,128)S(1)} %collective-permute-done.7.y_above, f32[11,8,256]{2,1,0:T(8,128)S(1)} %collective-permute-done.8.y_below, ...), custom_call_target="tpu_custom_call" | custom-call | flops 20000000 | bytes 2000000 | tf_op jit(solution)/shard_map/strips2/pallas_call | solution.py:756
  51.1 0.8 %collective-permute-done.9.z_in = f32[2,40,128]{2,1,0:T(8,128)S(1)} collective-permute-done((f32[2,40,128]{2,1,0:T(8,128)S(1)}, f32[2,40,128]{2,1,0:T(8,128)S(1)}, u32[]{:S(2)}, u32[]{:S(2)}) %collective-permute-start.9) | collective-permute-done | bytes 40992 | tf_op jit(solution)/shard_map/ppermute | solution.py:779
  51.9 1.7 %final.1 = f32[2,8,32,256]{3,2,1,0:T(8,128)} custom-call(s32[3]{0:T(128)S(1)} %pad_add_fusion.where, s32[8,32,256]{2,1,0:T(8,128)S(1)} %copy-done.1, f32[2,40,128]{2,1,0:T(8,128)S(1)} %collective-permute-done.9.z_in, f32[2,4,32,128]{3,2,1,0:T(8,128)S(1)} %get-tuple-element.61.bulk_edges, ...), custom_call_target="tpu_custom_call", output_to_operand_aliasing={{}: (6, {})} | custom-call | bytes 2000000 | tf_op jit(solution)/shard_map/final/pallas_call | solution.py:756
  (10 shorter events, 0.0 us)
Async XLA Ops:
  0.0 3.9 %copy-start = (f32[2,3,8,32,256]{4,3,2,1,0:T(8,128)S(1)}, f32[2,3,8,32,256]{4,3,2,1,0:T(8,128)}, u32[]{:S(2)}) copy-start(f32[2,3,8,32,256]{4,3,2,1,0:T(8,128)} %modes.7) | copy-start | bytes 4718596
  1.4 8.2 %collective-permute-start = (f32[10,32,256]{2,1,0:T(8,128)S(1)}, f32[10,32,256]{2,1,0:T(8,128)S(1)}, u32[]{:S(2)}, u32[]{:S(2)}) collective-permute-start(f32[10,32,256]{2,1,0:T(8,128)S(1)} %get-tuple-element.38), channel_id=1, source_target_pairs={{0,112},{16,0},{32,16},{48,32},{64,48},{80,64},{96,80},{112,96},{1... | collective-permute-start | bytes 983048 | tf_op jit(solution)/shard_map/ppermute | solution.py:779
  3.9 5.6 %collective-permute-start.1 = (f32[4,32,256]{2,1,0:T(8,128)S(1)}, f32[4,32,256]{2,1,0:T(8,128)S(1)}, u32[]{:S(2)}, u32[]{:S(2)}) collective-permute-start(f32[4,32,256]{2,1,0:T(8,128)S(1)} %get-tuple-element.39), channel_id=1, source_target_pairs={{0,16},{16,32},{32,48},{48,64},{64,80},{80,96},{96,112},{112,0},{1... | collective-permute-start | bytes 393224 | tf_op jit(solution)/shard_map/ppermute | solution.py:779
  10.2 14.4 %collective-permute-start.2 = (f32[16,8,256]{2,1,0:T(8,128)S(1)}, f32[16,8,256]{2,1,0:T(8,128)S(1)}, u32[]{:S(2)}, u32[]{:S(2)}) collective-permute-start(f32[16,8,256]{2,1,0:T(8,128)S(1)} %get-tuple-element.43), channel_id=1, source_target_pairs={{0,14},{2,0},{4,2},{6,4},{8,6},{10,8},{12,10},{14,12},{1,15},{3,1}... | collective-permute-start | bytes 393224 | tf_op jit(solution)/shard_map/ppermute | solution.py:779
  16.7 7.9 %collective-permute-start.3 = (f32[8,8,256]{2,1,0:T(8,128)S(1)}, f32[8,8,256]{2,1,0:T(8,128)S(1)}, u32[]{:S(2)}, u32[]{:S(2)}) collective-permute-start(f32[8,8,256]{2,1,0:T(8,128)S(1)} %get-tuple-element.44), channel_id=1, source_target_pairs={{0,2},{2,4},{4,6},{6,8},{8,10},{10,12},{12,14},{14,0},{1,3},{3,5},... | collective-permute-start | bytes 196616 | tf_op jit(solution)/shard_map/ppermute | solution.py:779
  19.0 10.3 %copy-start.2 = (f32[6]{0:T(128)S(1)}, f32[6]{0:T(128)}, u32[]{:S(2)}) copy-start(f32[6]{0:T(128)} %eigenvalues.3) | copy-start | bytes 76
  19.0 10.3 %copy-start.3 = (s32[6]{0:T(128)S(1)}, s32[6]{0:T(128)}, u32[]{:S(2)}) copy-start(s32[6]{0:T(128)} %order.3) | copy-start | bytes 76
  25.2 4.1 %collective-permute-start.4 = (f32[2,40,128]{2,1,0:T(8,128)S(1)}, f32[2,40,128]{2,1,0:T(8,128)S(1)}, u32[]{:S(2)}, u32[]{:S(2)}) collective-permute-start(f32[2,40,128]{2,1,0:T(8,128)S(1)} %pack_z1.1), channel_id=1, source_target_pairs={{0,1},{1,0},{2,3},{3,2},{4,5},{5,4},{6,7},{7,6},{8,9},{9,8},{10,11... | collective-permute-start | bytes 122888 | tf_op jit(solution)/shard_map/ppermute | solution.py:779
  31.2 17.5 %copy-start.1 = (s32[8,32,256]{2,1,0:T(8,128)S(1)}, s32[8,32,256]{2,1,0:T(8,128)}, u32[]{:S(2)}) copy-start(s32[8,32,256]{2,1,0:T(8,128)} %mask.5) | copy-start | bytes 786436
  31.2 7.0 %collective-permute-start.6 = (f32[4,2,32,256]{3,2,1,0:T(8,128)S(1)}, f32[4,2,32,256]{3,2,1,0:T(8,128)S(1)}, u32[]{:S(2)}, u32[]{:S(2)}) collective-permute-start(f32[4,2,32,256]{3,2,1,0:T(8,128)S(1)} %raw2.1.high), channel_id=1, source_target_pairs={{0,16},{16,32},{32,48},{48,64},{64,80},{80,96},{96,112},{112,0},{1... | collective-permute-start | bytes 786440 | tf_op jit(solution)/shard_map/ppermute | solution.py:779
  31.2 7.0 %collective-permute-start.5 = (f32[4,2,32,256]{3,2,1,0:T(8,128)S(1)}, f32[4,2,32,256]{3,2,1,0:T(8,128)S(1)}, u32[]{:S(2)}, u32[]{:S(2)}) collective-permute-start(f32[4,2,32,256]{3,2,1,0:T(8,128)S(1)} %get-tuple-element.56.low), channel_id=1, source_target_pairs={{0,112},{16,0},{32,16},{48,32},{64,48},{80,64},{96,80},{112,96},{1... | collective-permute-start | bytes 786440 | tf_op jit(solution)/shard_map/ppermute | solution.py:779
  38.2 6.4 %collective-permute-start.7 = (f32[11,8,256]{2,1,0:T(8,128)S(1)}, f32[11,8,256]{2,1,0:T(8,128)S(1)}, u32[]{:S(2)}, u32[]{:S(2)}) collective-permute-start(f32[11,8,256]{2,1,0:T(8,128)S(1)} %get-tuple-element.59), channel_id=1, source_target_pairs={{0,14},{2,0},{4,2},{6,4},{8,6},{10,8},{12,10},{14,12},{1,15},{3,1}... | collective-permute-start | bytes 270344 | tf_op jit(solution)/shard_map/ppermute | solution.py:779
  39.0 8.1 %collective-permute-start.8 = (f32[11,8,256]{2,1,0:T(8,128)S(1)}, f32[11,8,256]{2,1,0:T(8,128)S(1)}, u32[]{:S(2)}, u32[]{:S(2)}) collective-permute-start(f32[11,8,256]{2,1,0:T(8,128)S(1)} %get-tuple-element.60), channel_id=1, source_target_pairs={{0,2},{2,4},{4,6},{6,8},{8,10},{10,12},{12,14},{14,0},{1,3},{3,5},... | collective-permute-start | bytes 270344 | tf_op jit(solution)/shard_map/ppermute | solution.py:779
  47.8 4.1 %collective-permute-start.9 = (f32[2,40,128]{2,1,0:T(8,128)S(1)}, f32[2,40,128]{2,1,0:T(8,128)S(1)}, u32[]{:S(2)}, u32[]{:S(2)}) collective-permute-start(f32[2,40,128]{2,1,0:T(8,128)S(1)} %pack_z2.1), channel_id=1, source_target_pairs={{0,1},{1,0},{2,3},{3,2},{4,5},{5,4},{6,7},{7,6},{8,9},{9,8},{10,11... | collective-permute-start | bytes 122888 | tf_op jit(solution)/shard_map/ppermute | solution.py:779

commit v5 on v4

--- a/solution.py
+++ b/solution.py
@@ -27,8 +27,8 @@
     return lax.broadcasted_iota(jnp.int32, shape, dim)
 
 
-def pos(ref):
-    return ref[0], ref[1], ref[2]
+def pos():
+    return tuple(lax.axis_index(a) for a in ("gx", "gy", "gz"))
 
 
 def sub_lane():
@@ -433,8 +433,8 @@
     return above, p - W - CX
 
 
-def pack_y1(where, src, first_rows, columns, above, below, down, up):
-    gx, gy, gz = pos(where)
+def pack_y1(src, first_rows, columns, above, below, down, up):
+    gx, gy, gz = pos()
     low = iota((8, CZ), 0) < 4
     for q in range(8):
         a, i = pick_plane(src, above, below, q)
@@ -453,10 +453,10 @@
 
 
 def bulk_kernel1(
-    where, src, modes, columns, above, below,
+    src, modes, columns, above, below,
     bulk, ends, edges, stiff, mass, own, rims, table, sb, one, two,
 ):
-    at = pos(where)
+    at = pos()
     gx, gy, gz = at
     fill_bulk(table, gy, gz)
 
@@ -491,8 +491,8 @@
     return a[i, :, edge]
 
 
-def pack_z1(where, own, rims, y_above, y_below, out):
-    gx, gy, gz = pos(where)
+def pack_z1(own, rims, y_above, y_below, out):
+    gx, gy, gz = pos()
     edge = edge_tiles(gz)
     out[0, 0:CY, :] = own[0]
     out[0, CY:PY, :] = own_strip(gz, lambda p: halo_tile(y_above, y_below, p, edge), 8)
@@ -500,10 +500,10 @@
 
 
 def strip_kernel1(
-    where, modes, rims, above, y_above, y_below, ends,
+    modes, rims, above, y_above, y_below, ends,
     strips, edges, rim, packed, table, sb, one, two, near, far,
 ):
-    at = pos(where)
+    at = pos()
     gx, gy, gz = at
     fill_strips(table, gy, gz)
     strip_sweeps(
@@ -538,13 +538,12 @@
 
 
 def raw_planes(
-    planes, eigenvalues, order, gz, z_state, column_stiff, column_mass, bulk, strips,
+    planes, lams, gz, z_state, column_stiff, column_mass, bulk, strips,
     stiff, mass, stiff7, mass7, rim, out,
 ):
     sub, lane = sub_lane()
     beside = beside_halo(gz, lane)
     factor = 3.0 * (1.0 - stiff_floor) / 16.0
-    lams = [eigenvalues[order[m]] * (0.125 * 0.25) for m in range(MODES)]
     for x in planes:
         for i in range(CY // 8):
             rows = slice(8 * i, 8 * i + 8)
@@ -569,10 +568,10 @@
 
 
 def raw_kernel1(
-    eigenvalues, order, where, z_in, packed, bulk, bulk_edges, strips, strip_edges,
+    lams, z_in, packed, bulk, bulk_edges, strips, strip_edges,
     stiff, mass, stiff7, mass7, rim, low, z_parts,
 ):
-    gx, gy, gz = pos(where)
+    gx, gy, gz = pos()
     z_state = z_sweeps(0, strip_scale(gx, gy), z_in[0], bulk_edges, strip_edges)
 
     near, far = packed[...], z_in[1] * jnp.where(gz < 1, 1.0, 0.0)
@@ -589,17 +588,17 @@
     column_mass = mass_of(cur) + mass_of(prev)
     z_parts[0], z_parts[1], z_parts[2] = z_state[0:CY], column_stiff, column_mass
     raw_planes(
-        range(W), eigenvalues, order, gz, z_state, column_stiff, column_mass, bulk, strips,
+        range(W), lams, gz, z_state, column_stiff, column_mass, bulk, strips,
         stiff, mass, stiff7, mass7, rim, low,
     )
 
 
 def raw_kernel2(
-    eigenvalues, order, where, z_parts, bulk, strips, stiff, mass, stiff7, mass7, rim, high
+    lams, z_parts, bulk, strips, stiff, mass, stiff7, mass7, rim, high
 ):
-    gx, gy, gz = pos(where)
+    gx, gy, gz = pos()
     raw_planes(
-        range(W, CX), eigenvalues, order, gz, z_parts[0], z_parts.at[1], z_parts.at[2], bulk, strips,
+        range(W, CX), lams, gz, z_parts[0], z_parts.at[1], z_parts.at[2], bulk, strips,
         stiff, mass, stiff7, mass7, rim, high,
     )
 
@@ -656,8 +655,8 @@
     return jnp.where(iota(a.shape, 0) < 4, a, b)
 
 
-def bulk_kernel2(where, low, high, above, below, bulk, ends, edges, own, table, sb, one, two):
-    at = pos(where)
+def bulk_kernel2(low, high, above, below, bulk, ends, edges, own, table, sb, one, two):
+    at = pos()
     fill_bulk(table, at[1], at[2])
 
     def source(m, p, i):
@@ -675,8 +674,8 @@
         own[m] = own_strip(at[2], load)
 
 
-def pack_z2(where, own, y_above, y_below, out):
-    gx, gy, gz = pos(where)
+def pack_z2(own, y_above, y_below, out):
+    gx, gy, gz = pos()
     edge = edge_tiles(gz)
     for m in range(MODES):
         out[m, 0:CY, :] = own[m]
@@ -684,9 +683,9 @@
 
 
 def strip_kernel2(
-    where, mask, y_above, y_below, ends, bulk, out, side, edges, strips, table, sb, one, two, held, left
+    mask, y_above, y_below, ends, bulk, out, side, edges, strips, table, sb, one, two, held, left
 ):
-    gx, gy, gz = at = pos(where)
+    gx, gy, gz = at = pos()
     sub, lane = sub_lane()
     fill_strips(table, gy, gz)
 
@@ -715,8 +714,8 @@
         copy.wait()
 
 
-def final_kernel(where, mask, z_in, bulk_edges, strip_edges, side, given, out, held, left):
-    gx, gy, gz = pos(where)
+def final_kernel(mask, z_in, bulk_edges, strip_edges, side, given, out, held, left):
+    gx, gy, gz = pos()
     sub, lane = sub_lane()
     at_end = beside_halo(gz, lane)
     beside = at_end[0] | at_end[1]
@@ -741,9 +740,6 @@
         copy.wait()
 
 
-SMEM = pl.BlockSpec(memory_space=pltpu.SMEM)
-
-
 def whole(x):
     return pl.BlockSpec(x.shape, lambda i: (0,) * x.ndim)
 
@@ -757,7 +753,7 @@
         kernel,
         grid=(1,),
         out_shape=shapes if len(shapes) > 1 else shapes[0],
-        in_specs=[specs.get(i, SMEM if a.ndim == 1 else whole(a)) for i, a in enumerate(args)],
+        in_specs=[specs.get(i, whole(a)) for i, a in enumerate(args)],
         scratch_shapes=[pltpu.VMEM(s, F32) if isinstance(s, tuple) else s for s in scratch],
         compiler_params=pltpu.CompilerParams(vmem_limit_bytes=24 * 1024 * 1024),
         cost_estimate=pl.CostEstimate(flops=flops, bytes_accessed=2_000_000, transcendentals=0),
@@ -789,7 +785,9 @@
 
 
 def local(mode_fields, design, solid_mask, eigenvalues, mode_order):
-    where = jnp.stack([lax.axis_index(a) for a in ("gx", "gy", "gz")]).astype(jnp.int32)
+    selector = (mode_order[:MODES, None] == jnp.arange(eigenvalues.shape[0], dtype=jnp.int32)).astype(F32)
+    chosen = jnp.sum(selector * eigenvalues[None, :], axis=1) * (0.125 * 0.25)
+    lams = jnp.broadcast_to(chosen[:, None, None], (MODES, 8, LANES))
     bulk_outs, bulk_scratch, strip_outs, strip_scratch = sweep_outs(1)
 
     src, down, up = call(
@@ -805,30 +803,29 @@
     )
 
     down, up = call(
-        pack_y1, "pack_y1", [(16, 8, CZ), (8, 8, CZ)], (where, src, first_rows, columns, above, below)
+        pack_y1, "pack_y1", [(16, 8, CZ), (8, 8, CZ)], (src, first_rows, columns, above, below)
     )
     y_above, y_below = shift(down, "gy", -1), shift(up, "gy", 1)
     plane = (MODES, CY, CZ)
     bulk, ends, bulk_edges, stiff7, mass7, own, rims = call(
         bulk_kernel1, "bulk1", bulk_outs + [plane, plane, (1, CY, LANES), (2, CY, LANES)],
-        (where, src, mode_fields, columns, above, below), scratch=bulk_scratch, flops=30_000_000,
-    )
-
-    z_in = shift(call(pack_z1, "pack_z1", [(2, PY, LANES)], (where, own, rims, y_above, y_below)), "gz", 1)
+        (src, mode_fields, columns, above, below), scratch=bulk_scratch, flops=30_000_000,
+    )
+
+    z_in = shift(call(pack_z1, "pack_z1", [(2, PY, LANES)], (own, rims, y_above, y_below)), "gz", 1)
     strips, strip_edges, rim, packed = call(
         strip_kernel1, "strips1", strip_outs + [(MODES, 2, 8, CZ), (PY, LANES)],
-        (where, mode_fields, rims, above, y_above, y_below, ends),
+        (mode_fields, rims, above, y_above, y_below, ends),
         scratch=strip_scratch + [(3, 16, CZ)] * 2, flops=20_000_000,
     )
     half = (W, MODES, CY, CZ)
-    scalars = (eigenvalues, mode_order, where)
     energies = (stiff, mass, stiff7, mass7, rim)
     low, z_parts = call(
         raw_kernel1, "raw1", [half, (3, CY, LANES)],
-        (*scalars, z_in, packed, bulk, bulk_edges, strips, strip_edges, *energies),
+        (lams, z_in, packed, bulk, bulk_edges, strips, strip_edges, *energies),
     )
     above = shift(low, "gx", -1)
-    high = call(raw_kernel2, "raw2", [half], (*scalars, z_parts, bulk, strips, *energies), flops=60_000_000)
+    high = call(raw_kernel2, "raw2", [half], (lams, z_parts, bulk, strips, *energies), flops=60_000_000)
     below = shift(high, "gx", 1)
 
     bulk_outs, bulk_scratch, strip_outs, strip_scratch = sweep_outs(MODES)
@@ -836,21 +833,21 @@
     down, up = call(pack_y2, "pack_y2", [(CX + 3, 8, CZ)] * 2, planes)
     y_above, y_below = shift(down, "gy", -1), shift(up, "gy", 1)
     bulk, ends, bulk_edges, own = call(
-        bulk_kernel2, "bulk2", bulk_outs + [(MODES, CY, LANES)], (where, *planes),
+        bulk_kernel2, "bulk2", bulk_outs + [(MODES, CY, LANES)], planes,
         scratch=bulk_scratch, flops=40_000_000,
     )
-    z_in = shift(call(pack_z2, "pack_z2", [(MODES, PY, LANES)], (where, own, y_above, y_below)), "gz", 1)
+    z_in = shift(call(pack_z2, "pack_z2", [(MODES, PY, LANES)], (own, y_above, y_below)), "gz", 1)
     result = (MODES, CX, CY, CZ)
     out, side, strip_edges = call(
         strip_kernel2, "strips2", [result, (MODES, CX, CY, LANES), strip_outs[1]],
-        (where, solid_mask, y_above, y_below, ends, bulk), out_specs={0: HBM},
+        (solid_mask, y_above, y_below, ends, bulk), out_specs={0: HBM},
         scratch=[strip_outs[0]] + strip_scratch + [result, pltpu.SemaphoreType.DMA((4,))],
         flops=20_000_000,
     )
     return call(
         final_kernel, "final", [result],
-        (where, solid_mask, z_in, bulk_edges, strip_edges, side, out), {6: HBM}, {0: HBM},
-        scratch=[(MODES, CX, CY, LANES), pltpu.SemaphoreType.DMA((4,))], aliases={6: 0},
+        (solid_mask, z_in, bulk_edges, strip_edges, side, out), {5: HBM}, {0: HBM},
+        scratch=[(MODES, CX, CY, LANES), pltpu.SemaphoreType.DMA((4,))], aliases={5: 0},
     )
 
 

time: 53.7 us -> 51 us (0.950)
  Pallas kernels: 18.7 us -> 13.2 us
  waiting for transfers between devices: 17.4 us -> 20.2 us
    pallas_call x13, Pallas kernels: 18.7 us -> 13.2 us  [call(): pl.pallas_call(kernel, grid=(1,), out_shape=shapes if len(shapes) > 1 els...]
    ppermute x10, waiting for transfers between devices: 17.4 us -> 20.2 us  [shift(): return lax.ppermute(x, axis, ring(axis, step))]
  transfers between devices with their start and end apart: 10 -> 10, of which waited for: 6 -> 7; matrix products, arithmetic and copies ran while one was open for 0% -> 0% of each run, Pallas kernels for 22% -> 19%
where the time goes in v5:
time: 51 us; the launch traced here: 50.9 us
  waiting for transfers between devices  20.2 us (40%)
  starting transfers between devices  17 us (33%)
  Pallas kernels  13.2 us (26%)
    ppermute x10, waiting for transfers between devices, shift(): return lax.ppermute(x, axis, ring(axis, step))  20.2 us
    ppermute x10, starting transfers between devices, shift(): return lax.ppermute(x, axis, ring(axis, step))  17 us
    pallas_call x13, Pallas kernels, call(): pl.pallas_call(kernel, grid=(1,), out_shape=shapes if len(shapes) > 1 els...  13.2 us
  transfers between devices with their start and end apart: 10, of which 7 were waited for; matrix products, arithmetic and copies ran while one was open for 0% of the time, Pallas kernels for 19%

profile of v5, /device:TPU:0, one launch (start us, length us, event | category | flops | bytes accessed | tf_op | source)
XLA Modules:
  0.0 50.9 jit_solution(17270071701350824817)
XLA Ops:
  0.0 1.4 %pack_x1.1 = (f32[8,32,256]{2,1,0:T(8,128)S(1)}, f32[10,32,256]{2,1,0:T(8,128)S(1)}, f32[4,32,256]{2,1,0:T(8,128)S(1)}) custom-call(f32[8,32,256]{2,1,0:T(8,128)} %design.1, s32[8,32,256]{2,1,0:T(8,128)} %mask.5, f32[2,3,8,32,256]{4,3,2,1,0:T(8,128)} %modes.7), custom_call_target="tpu_custom_call" | custom-call | bytes 2000000 | tf_op jit(solution)/shard_map/pack_x1/pallas_call | solution.py:752
  1.4 0.0 copy-start.2
  1.4 0.0 copy-start.3
  1.4 2.5 %collective-permute-start = (f32[10,32,256]{2,1,0:T(8,128)S(1)}, f32[10,32,256]{2,1,0:T(8,128)S(1)}, u32[]{:S(2)}, u32[]{:S(2)}) collective-permute-start(f32[10,32,256]{2,1,0:T(8,128)S(1)} %get-tuple-element.38), channel_id=1, source_target_pairs={{0,112},{16,0},{32,16},{48,32},{64,48},{80,64},{96,80},{112,96},{1... | collective-permute-start | bytes 983048 | tf_op jit(solution)/shard_map/ppermute | solution.py:775
  4.0 3.1 %energy.1 = (f32[2,7,32,256]{3,2,1,0:T(8,128)S(1)}, f32[2,7,32,256]{3,2,1,0:T(8,128)S(1)}, f32[2,32,128]{2,1,0:T(8,128)S(1)}, f32[8,8,256]{2,1,0:T(8,128)S(1)}) custom-call(f32[2,3,8,32,256]{4,3,2,1,0:T(8,128)S(1)} %copy-done), custom_call_target="tpu_custom_call" | custom-call | flops 40000000 | bytes 2000000 | tf_op jit(solution)/shard_map/energy/pallas_call | solution.py:752
  7.0 2.5 %collective-permute-done.1.below = f32[4,32,256]{2,1,0:T(8,128)S(1)} collective-permute-done((f32[4,32,256]{2,1,0:T(8,128)S(1)}, f32[4,32,256]{2,1,0:T(8,128)S(1)}, u32[]{:S(2)}, u32[]{:S(2)}) %collective-permute-start.1) | collective-permute-done | bytes 131104 | tf_op jit(solution)/shard_map/ppermute | solution.py:775
  9.6 0.1 pack_y1.1
  9.6 6.6 %collective-permute-start.2 = (f32[16,8,256]{2,1,0:T(8,128)S(1)}, f32[16,8,256]{2,1,0:T(8,128)S(1)}, u32[]{:S(2)}, u32[]{:S(2)}) collective-permute-start(f32[16,8,256]{2,1,0:T(8,128)S(1)} %get-tuple-element.43), channel_id=1, source_target_pairs={{0,14},{2,0},{4,2},{6,4},{8,6},{10,8},{12,10},{14,12},{1,15},{3,1}... | collective-permute-start | bytes 393224 | tf_op jit(solution)/shard_map/ppermute | solution.py:775
  16.2 0.2 fusion
  16.4 1.7 %bulk1.1 = (f32[1,8,32,256]{3,2,1,0:T(8,128)S(1)}, f32[1,4,16,2,1,256]{5,4,3,2,1,0:T(1,128)S(1)}, f32[1,4,32,128]{3,2,1,0:T(8,128)S(1)}, f32[2,32,256]{2,1,0:T(8...) custom-call(f32[8,32,256]{2,1,0:T(8,128)S(1)} %get-tuple-element.36.src, ...), custom_call_target="tpu_custom_call" | custom-call | flops 30000000 | bytes 2000000 | tf_op jit(solution)/shard_map/bulk1/pallas_call | solution.py:752
  18.1 6.1 %collective-permute-done.3.y_below = f32[8,8,256]{2,1,0:T(8,128)S(1)} collective-permute-done((f32[8,8,256]{2,1,0:T(8,128)S(1)}, f32[8,8,256]{2,1,0:T(8,128)S(1)}, u32[]{:S(2)}, u32[]{:S(2)}) %collective-permute-start.3) | collective-permute-done | bytes 65568 | tf_op jit(solution)/shard_map/ppermute | solution.py:775
  24.3 0.1 pack_z1.1
  24.4 0.9 %collective-permute-start.4 = (f32[2,40,128]{2,1,0:T(8,128)S(1)}, f32[2,40,128]{2,1,0:T(8,128)S(1)}, u32[]{:S(2)}, u32[]{:S(2)}) collective-permute-start(f32[2,40,128]{2,1,0:T(8,128)S(1)} %pack_z1.1), channel_id=1, source_target_pairs={{0,1},{1,0},{2,3},{3,2},{4,5},{5,4},{6,7},{7,6},{8,9},{9,8},{10,11... | collective-permute-start | bytes 122888 | tf_op jit(solution)/shard_map/ppermute | solution.py:775
  25.3 0.8 %strips1.1 = (f32[1,8,16,256]{3,2,1,0:T(8,128)S(1)}, f32[1,4,16,128]{3,2,1,0:T(8,128)S(1)}, f32[2,2,8,256]{3,2,1,0:T(8,128)S(1)}, f32[40,128]{1,0:T(8,128)S(1)}) custom-call(f32[2,3,8,32,256]{4,3,2,1,0:T(8,128)S(1)} %copy-done, f32[2,32,128]{2,1,0:T(8,128)S(1)} %get-tuple-element.41.rims, f32[10,32,256]{2,1,0:T(8,128)S(1)} %collective-permute-done.above, ...), custom_call_target="tpu_custom_call" | custom-call | flops 20000000 | bytes 2000000 | tf_op jit(solution)/shard_map/strips1/pallas_call | solution.py:752
  26.1 2.3 %collective-permute-done.4.z_in = f32[2,40,128]{2,1,0:T(8,128)S(1)} collective-permute-done((f32[2,40,128]{2,1,0:T(8,128)S(1)}, f32[2,40,128]{2,1,0:T(8,128)S(1)}, u32[]{:S(2)}, u32[]{:S(2)}) %collective-permute-start.4) | collective-permute-done | bytes 40992 | tf_op jit(solution)/shard_map/ppermute | solution.py:775
  28.5 0.1 broadcast_in_dim.2.lams
  28.5 0.5 %raw1.1 = (f32[4,2,32,256]{3,2,1,0:T(8,128)S(1)}, f32[3,32,128]{2,1,0:T(8,128)S(1)}) custom-call(f32[2,8,128]{2,1,0:T(8,128)S(1)} %broadcast_in_dim.2.lams, f32[2,40,128]{2,1,0:T(8,128)S(1)} %collective-permute-done.4.z_in, f32[40,128]{1,0:T(8,128)S(1)} %get-tuple-element.46.packed, f32[1,8,32,256]{3,2,1,0:T(8,128)S(1)} %get-tuple-element.47.bulk, ...), custom_call_target="tpu_custom_call" | custom-call | bytes 2000000 | tf_op jit(solution)/shard_map/raw1/pallas_call | solution.py:752
  29.1 0.2 raw2.1.high
  29.2 0.0 copy-start.1
  29.2 0.0 collective-permute-start.6
  29.3 2.9 %collective-permute-start.5 = (f32[4,2,32,256]{3,2,1,0:T(8,128)S(1)}, f32[4,2,32,256]{3,2,1,0:T(8,128)S(1)}, u32[]{:S(2)}, u32[]{:S(2)}) collective-permute-start(f32[4,2,32,256]{3,2,1,0:T(8,128)S(1)} %get-tuple-element.56.low), channel_id=1, source_target_pairs={{0,112},{16,0},{32,16},{48,32},{64,48},{80,64},{96,80},{112,96},{1... | collective-permute-start | bytes 786440 | tf_op jit(solution)/shard_map/ppermute | solution.py:775
  32.2 4.1 %collective-permute-done.6.below = f32[4,2,32,256]{3,2,1,0:T(8,128)S(1)} collective-permute-done((f32[4,2,32,256]{3,2,1,0:T(8,128)S(1)}, f32[4,2,32,256]{3,2,1,0:T(8,128)S(1)}, u32[]{:S(2)}, u32[]{:S(2)}) %collective-permute-start.6) | collective-permute-done | bytes 262176 | tf_op jit(solution)/shard_map/ppermute | solution.py:775
  36.3 0.6 %collective-permute-start.7 = (f32[11,8,256]{2,1,0:T(8,128)S(1)}, f32[11,8,256]{2,1,0:T(8,128)S(1)}, u32[]{:S(2)}, u32[]{:S(2)}) collective-permute-start(f32[11,8,256]{2,1,0:T(8,128)S(1)} %get-tuple-element.59), channel_id=1, source_target_pairs={{0,14},{2,0},{4,2},{6,4},{8,6},{10,8},{12,10},{14,12},{1,15},{3,1}... | collective-permute-start | bytes 270344 | tf_op jit(solution)/shard_map/ppermute | solution.py:775
  36.9 3.0 %collective-permute-start.8 = (f32[11,8,256]{2,1,0:T(8,128)S(1)}, f32[11,8,256]{2,1,0:T(8,128)S(1)}, u32[]{:S(2)}, u32[]{:S(2)}) collective-permute-start(f32[11,8,256]{2,1,0:T(8,128)S(1)} %get-tuple-element.60), channel_id=1, source_target_pairs={{0,2},{2,4},{4,6},{6,8},{8,10},{10,12},{12,14},{14,0},{1,3},{3,5},... | collective-permute-start | bytes 270344 | tf_op jit(solution)/shard_map/ppermute | solution.py:775
  39.9 2.2 %bulk2.1 = (f32[2,8,32,256]{3,2,1,0:T(8,128)S(1)}, f32[2,4,16,2,1,256]{5,4,3,2,1,0:T(1,128)S(1)}, f32[2,4,32,128]{3,2,1,0:T(8,128)S(1)}, f32[2,32,128]{2,1,0:T(8,128)S(1)}) custom-call(f32[4,2,32,256]{3,2,1,0:T(8,128)S(1)} %get-tuple-element.56.low, f32[4,2,32,256]{3,2,1,0:T(8,128)S(1)} %raw2.1.high, f32[4,2,32,256]{3,2,1,0:T(8,128)S(1)} %collective-permute-done.5.above, ...), custom_call_target="tpu_custom_call" | custom-call | flops 40000000 | bytes 2000000 | tf_op jit(solution)/shard_map/bulk2/pallas_call | solution.py:752
  42.2 0.2 collective-permute-done.7.y_above
  42.4 3.1 %collective-permute-done.8.y_below = f32[11,8,256]{2,1,0:T(8,128)S(1)} collective-permute-done((f32[11,8,256]{2,1,0:T(8,128)S(1)}, f32[11,8,256]{2,1,0:T(8,128)S(1)}, u32[]{:S(2)}, u32[]{:S(2)}) %collective-permute-start.8) | collective-permute-done | bytes 90144 | tf_op jit(solution)/shard_map/ppermute | solution.py:775
  45.5 0.1 pack_z2.1
  45.6 0.4 collective-permute-start.9
  46.0 1.8 %strips2.1 = (f32[2,8,32,256]{3,2,1,0:T(8,128)}, f32[2,8,32,128]{3,2,1,0:T(8,128)S(1)}, f32[2,4,16,128]{3,2,1,0:T(8,128)S(1)}) custom-call(s32[8,32,256]{2,1,0:T(8,128)S(1)} %copy-done.1, f32[11,8,256]{2,1,0:T(8,128)S(1)} %collective-permute-done.7.y_above, f32[11,8,256]{2,1,0:T(8,128)S(1)} %collective-permute-done.8.y_below, ...), custom_call_target="tpu_custom_call" | custom-call | flops 20000000 | bytes 2000000 | tf_op jit(solution)/shard_map/strips2/pallas_call | solution.py:752
  47.8 1.9 %collective-permute-done.9.z_in = f32[2,40,128]{2,1,0:T(8,128)S(1)} collective-permute-done((f32[2,40,128]{2,1,0:T(8,128)S(1)}, f32[2,40,128]{2,1,0:T(8,128)S(1)}, u32[]{:S(2)}, u32[]{:S(2)}) %collective-permute-start.9) | collective-permute-done | bytes 40992 | tf_op jit(solution)/shard_map/ppermute | solution.py:775
  49.7 1.2 %final.1 = f32[2,8,32,256]{3,2,1,0:T(8,128)} custom-call(s32[8,32,256]{2,1,0:T(8,128)S(1)} %copy-done.1, f32[2,40,128]{2,1,0:T(8,128)S(1)} %collective-permute-done.9.z_in, f32[2,4,32,128]{3,2,1,0:T(8,128)S(1)} %get-tuple-element.61.bulk_edges, f32[2,4,16,128]{3,2,1,0:T(8,128)S(1)} %get-tuple-element.64.strip_edges, ...), custom_call_target="tpu_custom_call", output_to_operand_aliasing={{}: (5, {})} | custom-call | bytes 2000000 | tf_op jit(solution)/shard_map/final/pallas_call | solution.py:752
  (12 shorter events, 0.1 us)
Async XLA Ops:
  0.0 4.0 %copy-start = (f32[2,3,8,32,256]{4,3,2,1,0:T(8,128)S(1)}, f32[2,3,8,32,256]{4,3,2,1,0:T(8,128)}, u32[]{:S(2)}) copy-start(f32[2,3,8,32,256]{4,3,2,1,0:T(8,128)} %modes.7) | copy-start | bytes 4718596
  1.4 14.8 %copy-start.2 = (f32[6]{0:T(128)S(1)}, f32[6]{0:T(128)}, u32[]{:S(2)}) copy-start(f32[6]{0:T(128)} %param.8) | copy-start | bytes 76
  1.4 14.8 %copy-start.3 = (s32[6]{0:T(128)S(1)}, s32[6]{0:T(128)}, u32[]{:S(2)}) copy-start(s32[6]{0:T(128)} %param.9) | copy-start | bytes 76
  1.4 8.2 %collective-permute-start = (f32[10,32,256]{2,1,0:T(8,128)S(1)}, f32[10,32,256]{2,1,0:T(8,128)S(1)}, u32[]{:S(2)}, u32[]{:S(2)}) collective-permute-start(f32[10,32,256]{2,1,0:T(8,128)S(1)} %get-tuple-element.38), channel_id=1, source_target_pairs={{0,112},{16,0},{32,16},{48,32},{64,48},{80,64},{96,80},{112,96},{1... | collective-permute-start | bytes 983048 | tf_op jit(solution)/shard_map/ppermute | solution.py:775
  4.0 5.6 %collective-permute-start.1 = (f32[4,32,256]{2,1,0:T(8,128)S(1)}, f32[4,32,256]{2,1,0:T(8,128)S(1)}, u32[]{:S(2)}, u32[]{:S(2)}) collective-permute-start(f32[4,32,256]{2,1,0:T(8,128)S(1)} %get-tuple-element.39), channel_id=1, source_target_pairs={{0,16},{16,32},{32,48},{48,64},{64,80},{80,96},{96,112},{112,0},{1... | collective-permute-start | bytes 393224 | tf_op jit(solution)/shard_map/ppermute | solution.py:775
  9.6 14.6 %collective-permute-start.2 = (f32[16,8,256]{2,1,0:T(8,128)S(1)}, f32[16,8,256]{2,1,0:T(8,128)S(1)}, u32[]{:S(2)}, u32[]{:S(2)}) collective-permute-start(f32[16,8,256]{2,1,0:T(8,128)S(1)} %get-tuple-element.43), channel_id=1, source_target_pairs={{0,14},{2,0},{4,2},{6,4},{8,6},{10,8},{12,10},{14,12},{1,15},{3,1}... | collective-permute-start | bytes 393224 | tf_op jit(solution)/shard_map/ppermute | solution.py:775
  16.2 8.1 %collective-permute-start.3 = (f32[8,8,256]{2,1,0:T(8,128)S(1)}, f32[8,8,256]{2,1,0:T(8,128)S(1)}, u32[]{:S(2)}, u32[]{:S(2)}) collective-permute-start(f32[8,8,256]{2,1,0:T(8,128)S(1)} %get-tuple-element.44), channel_id=1, source_target_pairs={{0,2},{2,4},{4,6},{6,8},{8,10},{10,12},{12,14},{14,0},{1,3},{3,5},... | collective-permute-start | bytes 196616 | tf_op jit(solution)/shard_map/ppermute | solution.py:775
  24.4 4.1 %collective-permute-start.4 = (f32[2,40,128]{2,1,0:T(8,128)S(1)}, f32[2,40,128]{2,1,0:T(8,128)S(1)}, u32[]{:S(2)}, u32[]{:S(2)}) collective-permute-start(f32[2,40,128]{2,1,0:T(8,128)S(1)} %pack_z1.1), channel_id=1, source_target_pairs={{0,1},{1,0},{2,3},{3,2},{4,5},{5,4},{6,7},{7,6},{8,9},{9,8},{10,11... | collective-permute-start | bytes 122888 | tf_op jit(solution)/shard_map/ppermute | solution.py:775
  29.2 16.7 %copy-start.1 = (s32[8,32,256]{2,1,0:T(8,128)S(1)}, s32[8,32,256]{2,1,0:T(8,128)}, u32[]{:S(2)}) copy-start(s32[8,32,256]{2,1,0:T(8,128)} %mask.5) | copy-start | bytes 786436
  29.2 7.0 %collective-permute-start.6 = (f32[4,2,32,256]{3,2,1,0:T(8,128)S(1)}, f32[4,2,32,256]{3,2,1,0:T(8,128)S(1)}, u32[]{:S(2)}, u32[]{:S(2)}) collective-permute-start(f32[4,2,32,256]{3,2,1,0:T(8,128)S(1)} %raw2.1.high), channel_id=1, source_target_pairs={{0,16},{16,32},{32,48},{48,64},{64,80},{80,96},{96,112},{112,0},{1... | collective-permute-start | bytes 786440 | tf_op jit(solution)/shard_map/ppermute | solution.py:775
  29.3 7.0 %collective-permute-start.5 = (f32[4,2,32,256]{3,2,1,0:T(8,128)S(1)}, f32[4,2,32,256]{3,2,1,0:T(8,128)S(1)}, u32[]{:S(2)}, u32[]{:S(2)}) collective-permute-start(f32[4,2,32,256]{3,2,1,0:T(8,128)S(1)} %get-tuple-element.56.low), channel_id=1, source_target_pairs={{0,112},{16,0},{32,16},{48,32},{64,48},{80,64},{96,80},{112,96},{1... | collective-permute-start | bytes 786440 | tf_op jit(solution)/shard_map/ppermute | solution.py:775
  36.3 6.1 %collective-permute-start.7 = (f32[11,8,256]{2,1,0:T(8,128)S(1)}, f32[11,8,256]{2,1,0:T(8,128)S(1)}, u32[]{:S(2)}, u32[]{:S(2)}) collective-permute-start(f32[11,8,256]{2,1,0:T(8,128)S(1)} %get-tuple-element.59), channel_id=1, source_target_pairs={{0,14},{2,0},{4,2},{6,4},{8,6},{10,8},{12,10},{14,12},{1,15},{3,1}... | collective-permute-start | bytes 270344 | tf_op jit(solution)/shard_map/ppermute | solution.py:775
  36.9 8.6 %collective-permute-start.8 = (f32[11,8,256]{2,1,0:T(8,128)S(1)}, f32[11,8,256]{2,1,0:T(8,128)S(1)}, u32[]{:S(2)}, u32[]{:S(2)}) collective-permute-start(f32[11,8,256]{2,1,0:T(8,128)S(1)} %get-tuple-element.60), channel_id=1, source_target_pairs={{0,2},{2,4},{4,6},{6,8},{8,10},{10,12},{12,14},{14,0},{1,3},{3,5},... | collective-permute-start | bytes 270344 | tf_op jit(solution)/shard_map/ppermute | solution.py:775
  45.6 4.1 %collective-permute-start.9 = (f32[2,40,128]{2,1,0:T(8,128)S(1)}, f32[2,40,128]{2,1,0:T(8,128)S(1)}, u32[]{:S(2)}, u32[]{:S(2)}) collective-permute-start(f32[2,40,128]{2,1,0:T(8,128)S(1)} %pack_z2.1), channel_id=1, source_target_pairs={{0,1},{1,0},{2,3},{3,2},{4,5},{5,4},{6,7},{7,6},{8,9},{9,8},{10,11... | collective-permute-start | bytes 122888 | tf_op jit(solution)/shard_map/ppermute | solution.py:775

commit v6 on v5

--- a/solution.py
+++ b/solution.py
@@ -367,10 +367,29 @@
     return packed
 
 
-def with_row32(packed, y_above, keep_y, last):
+def row32_of(y_above, last):
+    cols = slice(CZ - LANES, CZ) if last else slice(0, LANES)
     sub, lane = sub_lane()
-    row = y_above[11, 3:4, LANES * last : LANES * last + LANES] * keep_y
-    return jnp.concatenate([packed, jnp.where(sub == 0, jnp.broadcast_to(row, (8, LANES)), 0.0)], axis=0)
+    tile = jnp.zeros((8, LANES), F32)
+    for m in range(MODES):
+        for c in range(3):
+            for x in range(CX):
+                to = 32 * m + NODES * c + x
+                row = jnp.broadcast_to(y_above[W + 3 * m + c, x : x + 1, cols], (8, LANES))
+                tile = jnp.where(lane == to, pltpu.roll(row, to + last, 1), tile)
+    return jnp.where(sub == 0, tile, 0.0)
+
+
+def with_row32(packed, row, from_above, keep_x, keep_y, last):
+    cols = slice(CZ - LANES, CZ) if last else slice(0, LANES)
+    sub, lane = sub_lane()
+    for m in range(MODES):
+        for c in range(3):
+            to = 32 * m + NODES * c + CX
+            n = 3 * m + c
+            corner = jnp.broadcast_to(from_above[W - 1, n : n + 1, cols] * keep_x, (8, LANES))
+            row = jnp.where((lane == to) & (sub == 0), pltpu.roll(corner, to + last, 1), row)
+    return jnp.concatenate([packed, row * keep_y], axis=0)
 
 
 def pack_x1(design, mask, modes, src, down, up, field, solid, arrived):
@@ -396,18 +415,11 @@
         copy.wait()
 
 
-def energy_kernel(modes, stiff, mass, columns, first_rows):
+def energy_kernel(modes, stiff, mass, columns):
     lane = iota((CY, LANES), 1)
     columns[0], columns[1] = pack_columns(
         lambda m, c, x, j: modes[m, c, x, :, LANES * j : LANES * j + LANES], lane
     )
-
-    for m in range(MODES):
-        first_rows[4 * m + 3] = jnp.zeros((8, CZ), F32)
-        for c in range(3):
-            for x in range(CX):
-                n = NODES * c + x
-                first_rows[4 * m + n // 8, n % 8 : n % 8 + 1, :] = modes[m, c, x, 0:1, :]
 
     def mode_step(m, carry):
         for chunk in range(CY // 8):
@@ -433,28 +445,46 @@
     return above, p - W - CX
 
 
-def pack_y1(src, first_rows, columns, above, below, down, up):
-    gx, gy, gz = pos()
+def pack_y1(src, modes, down, up):
     low = iota((8, CZ), 0) < 4
-    for q in range(8):
-        a, i = pick_plane(src, above, below, q)
-        b, j = pick_plane(src, above, below, q + 8)
-        down[q] = jnp.where(low, a[i, 0:8, :], pltpu.roll(b[j, 0:8, :], 4, 0))
-        up[q] = jnp.where(low, pltpu.roll(b[j, 24:32, :], 4, 0), a[i, 24:32, :])
-    keep = jnp.where(gx < 7, 1.0, 0.0)
-    down[8:16] = first_rows[...]
+    for q in range(W):
+        down[q] = jnp.where(low, src[q, 0:8, :], pltpu.roll(src[q + W, 0:8, :], 4, 0))
+        up[q] = jnp.where(low, pltpu.roll(src[q + W, 24:32, :], 4, 0), src[q, 24:32, :])
     for m in range(MODES):
         for c in range(3):
-            n = NODES * c + CX
-            down[8 + 4 * m + n // 8, n % 8 : n % 8 + 1, :] = above[W + 3 * m + c, 0:1, :] * keep
-    for last in range(2):
-        row = with_plane8(columns[last, 0:8, :], above, keep, last)
-        down[11, 3:4, LANES * last : LANES * last + LANES] = row[0:1]
+            for x in range(CX):
+                down[W + 3 * m + c, x : x + 1, :] = modes[m, c, x, 0:1, :]
+
+
+def own_halo(y_above, y_below, x, lanes=slice(None)):
+    a, b = y_above[x % W, :, lanes], y_below[x % W, :, lanes]
+    if x >= W:
+        a, b = pltpu.roll(a, 4, 0), pltpu.roll(b, 4, 0)
+    return jnp.where(iota(a.shape, 0) < 4, a, b)
+
+
+def pack_e1(y_above, y_below, ahead, down, up):
+    for i in range(W - 1):
+        down[i] = own_halo(y_above, y_below, i)
+        up[i] = own_halo(y_above, y_below, CX - 1 - i)
+    down[W - 1] = jnp.zeros((8, CZ), F32)
+    for n in range(3 * MODES):
+        down[W - 1, n : n + 1, :] = y_above[W + n, 0:1, :]
+
+
+def halo_tile(y_above, y_below, from_above, from_below, p, lanes=slice(None)):
+    if W <= p < W + CX:
+        return own_halo(y_above, y_below, p - W, lanes)
+    if 0 < p < W:
+        return from_below[W - 1 - p, :, lanes]
+    if W + CX <= p < PX - 1:
+        return from_above[p - W - CX, :, lanes]
+    return jnp.zeros(y_above[0, :, lanes].shape, F32)
 
 
 def bulk_kernel1(
-    src, modes, columns, above, below,
-    bulk, ends, edges, stiff, mass, own, rims, table, sb, one, two,
+    src, modes, columns, above, below, y_above,
+    bulk, ends, edges, stiff, mass, own, rims, row32, table, sb, one, two,
 ):
     at = pos()
     gx, gy, gz = at
@@ -470,6 +500,7 @@
     keep = jnp.where(gx < 7, 1.0, 0.0)
     for last in range(2):
         rims[last] = with_plane8(columns[last], above, keep, last)
+        row32[last] = row32_of(y_above, last)
     for m in range(MODES):
         for chunk in range(CY // 8):
             rows = slice(8 * chunk, 8 * chunk + 8)
@@ -479,50 +510,44 @@
             mass[m, rows, :] = mass_of(cur) + mass_of(prev)
 
 
-def halo_tile(y_above, y_below, p, lanes=slice(None)):
-    a, b = y_above[p % 8, :, lanes], y_below[p % 8, :, lanes]
-    if p >= 8:
-        a, b = pltpu.roll(a, 4, 0), pltpu.roll(b, 4, 0)
-    return jnp.where(iota(a.shape, 0) < 4, a, b)
-
-
 def plane_edge(own, above, below, p, edge):
     a, i = pick_plane(own, above, below, p)
     return a[i, :, edge]
 
 
-def pack_z1(own, rims, y_above, y_below, out):
+def pack_z1(own, rims, row32, y_above, y_below, from_above, from_below, out):
     gx, gy, gz = pos()
     edge = edge_tiles(gz)
+    halos = (y_above, y_below, from_above, from_below)
     out[0, 0:CY, :] = own[0]
-    out[0, CY:PY, :] = own_strip(gz, lambda p: halo_tile(y_above, y_below, p, edge), 8)
-    out[1] = with_row32(rims[0], y_above, jnp.where(gy < 7, 1.0, 0.0), 0)
+    out[0, CY:PY, :] = own_strip(gz, lambda p: halo_tile(*halos, p, edge), 8)
+    keep_x = jnp.where(gx < 7, 1.0, 0.0)
+    keep_y = jnp.where(gy < 7, 1.0, 0.0)
+    out[1] = with_row32(rims[0], row32[0], from_above, keep_x, keep_y, 0)
 
 
 def strip_kernel1(
-    modes, rims, above, y_above, y_below, ends,
+    modes, rims, row32, above, y_above, y_below, from_above, from_below, ends,
     strips, edges, rim, packed, table, sb, one, two, near, far,
 ):
     at = pos()
     gx, gy, gz = at
     fill_strips(table, gy, gz)
+    halos = (y_above, y_below, from_above, from_below)
     strip_sweeps(
-        1, at, table, lambda m, p: halo_tile(y_above, y_below, p), ends, (sb, one, two), edges, strips
+        1, at, table, lambda m, p: halo_tile(*halos, p), ends, (sb, one, two), edges, strips
     )
     keep_x = jnp.where(gx < 7, 1.0, 0.0)
     keep_y = jnp.where(gy < 7, 1.0, 0.0)
-    packed[...] = with_row32(rims[1], y_above, keep_y, 1)
+    packed[...] = with_row32(rims[1], row32[1], from_above, keep_x, keep_y, 1)
     for m in range(MODES):
         for c in range(3):
-            for x in range(NODES):
-                n = c * NODES + x
-                row = above[W + 3 * m + c, CY - 1 : CY, :] * keep_x
-                if x < CX:
-                    row = modes[m, c, x, CY - 1 : CY, :]
-                near[c, x : x + 1, :] = row
-                far[c, x : x + 1, :] = (
-                    y_above[8 + 4 * m + n // 8, n % 8 : n % 8 + 1, :] * keep_y
-                )
+            n = 3 * m + c
+            for x in range(CX):
+                near[c, x : x + 1, :] = modes[m, c, x, CY - 1 : CY, :]
+            near[c, CX : CX + 1, :] = above[W + n, CY - 1 : CY, :] * keep_x
+            far[c, 0:CX, :] = y_above[W + n] * keep_y
+            far[c, CX : CX + 1, :] = from_above[W - 1, n : n + 1, :] * (keep_x * keep_y)
 
         def parts(first):
             pairs = []
@@ -613,46 +638,38 @@
     return above, p - 3 * W
 
 
-SHARED = ((PX - W, PX - W + 2, 3), (W - 1, W - 3, 3), (PX - W + 1, W - 2, 2))
-
-
-def rolled(tile, by):
-    return pltpu.roll(tile, by % 8, 0) if by % 8 else tile
-
-
-def pack_y2(low, high, above, below, down, up):
-    sub = iota((8, CZ), 0)
-
-    def rows(p, m, start):
-        a, i = raw_plane(low, high, above, below, p)
-        return a[i, m, start : start + 8, :]
-
-    def both(tiles, first):
-        return jnp.where(sub < 4, rolled(tiles[0], -first), rolled(tiles[1], 4 - first))
-
-    for p in range(W, W + CX):
-        down[p - W] = both([rows(p, m, 0) for m in range(MODES)], 0)
-        up[p - W] = both([rows(p, m, 24) for m in range(MODES)], 4)
-    for n, (p, q, count) in enumerate(SHARED):
-        down[CX + n] = both(
-            [jnp.where(sub < count, rows(p, m, 0), rolled(rows(q, m, 0), count)) for m in range(MODES)], 0
-        )
-        up[CX + n] = both(
-            [jnp.where(sub >= 8 - count, rows(p, m, 24), rolled(rows(q, m, 24), -count)) for m in range(MODES)], 4
-        )
-
-
-def raw_halo(y_above, y_below, m, p, lanes=slice(None)):
+def pack_y2(low, high, down, up):
+    first = iota((8, CZ), 0) < 4
+    for x in range(CX):
+        a, i = (low, x) if x < W else (high, x - W)
+        down[x] = jnp.where(first, a[i, 0, 0:8, :], pltpu.roll(a[i, 1, 0:8, :], 4, 0))
+        up[x] = jnp.where(first, pltpu.roll(a[i, 0, 24:32, :], 4, 0), a[i, 1, 24:32, :])
+
+
+def own_raw_halo(y_above, y_below, m, x, lanes=slice(None)):
+    a, b = y_above[x, :, lanes], y_below[x, :, lanes]
+    if m == 0:
+        b = pltpu.roll(b, 4, 0)
+    else:
+        a = pltpu.roll(a, 4, 0)
+    return jnp.where(iota(a.shape, 0) < 4, a, b)
+
+
+def pack_e2(y_above, y_below, down, up):
+    for i in range(W - 1):
+        for m in range(MODES):
+            down[MODES * i + m] = own_raw_halo(y_above, y_below, m, i)
+            up[MODES * i + m] = own_raw_halo(y_above, y_below, m, CX - 1 - i)
+
+
+def raw_halo(y_above, y_below, from_above, from_below, m, p, lanes=slice(None)):
     if W <= p < W + CX:
-        n, skip = p - W, 0
-    else:
-        found = [(CX + n, 0 if p == s[0] else s[2]) for n, s in enumerate(SHARED) if p in s[:2]]
-        if not found:
-            return jnp.zeros(y_above[0, :, lanes].shape, F32)
-        n, skip = found[0]
-    a = rolled(y_above[n, :, lanes], 4 * m - skip)
-    b = rolled(y_below[n, :, lanes], 4 * (1 - m) + skip)
-    return jnp.where(iota(a.shape, 0) < 4, a, b)
+        return own_raw_halo(y_above, y_below, m, p - W, lanes)
+    if 0 < p < W:
+        return from_below[MODES * (W - 1 - p) + m, :, lanes]
+    if W + CX <= p < PX - 1:
+        return from_above[MODES * (p - W - CX) + m, :, lanes]
+    return jnp.zeros(y_above[0, :, lanes].shape, F32)
 
 
 def bulk_kernel2(low, high, above, below, bulk, ends, edges, own, table, sb, one, two):
@@ -674,23 +691,25 @@
         own[m] = own_strip(at[2], load)
 
 
-def pack_z2(own, y_above, y_below, out):
+def pack_z2(own, y_above, y_below, from_above, from_below, out):
     gx, gy, gz = pos()
     edge = edge_tiles(gz)
+    halos = (y_above, y_below, from_above, from_below)
     for m in range(MODES):
         out[m, 0:CY, :] = own[m]
-        out[m, CY:PY, :] = own_strip(gz, lambda p, m=m: raw_halo(y_above, y_below, m, p, edge), 8)
+        out[m, CY:PY, :] = own_strip(gz, lambda p, m=m: raw_halo(*halos, m, p, edge), 8)
 
 
 def strip_kernel2(
-    mask, y_above, y_below, ends, bulk, out, side, edges, strips, table, sb, one, two, held, left
+    mask, y_above, y_below, from_above, from_below, ends, bulk,
+    out, side, edges, strips, table, sb, one, two, held, left,
 ):
     gx, gy, gz = at = pos()
     sub, lane = sub_lane()
     fill_strips(table, gy, gz)
 
     def source(m, p):
-        return raw_halo(y_above, y_below, m, p)
+        return raw_halo(y_above, y_below, from_above, from_below, m, p)
 
     strip_sweeps(MODES, at, table, source, ends, (sb, one, two), edges, strips)
     copies = []
@@ -798,24 +817,25 @@
     )
     above, below = shift(down, "gx", -1), shift(up, "gx", 1)
     field = (MODES, CX - 1, CY, CZ)
-    stiff, mass, columns, first_rows = call(
-        energy_kernel, "energy", [field, field, (2, CY, LANES), (8, 8, CZ)], (mode_fields,), flops=40_000_000
-    )
-
-    down, up = call(
-        pack_y1, "pack_y1", [(16, 8, CZ), (8, 8, CZ)], (src, first_rows, columns, above, below)
-    )
+    down, up = call(pack_y1, "pack_y1", [(W + 6, 8, CZ), (W, 8, CZ)], (src, mode_fields))
     y_above, y_below = shift(down, "gy", -1), shift(up, "gy", 1)
+    stiff, mass, columns = call(
+        energy_kernel, "energy", [field, field, (2, CY, LANES)], (mode_fields,), flops=40_000_000
+    )
+
+    down, up = call(pack_e1, "pack_e1", [(W, 8, CZ), (W - 1, 8, CZ)], (y_above, y_below, columns))
+    halos = (y_above, y_below, shift(down, "gx", -1), shift(up, "gx", 1))
     plane = (MODES, CY, CZ)
-    bulk, ends, bulk_edges, stiff7, mass7, own, rims = call(
-        bulk_kernel1, "bulk1", bulk_outs + [plane, plane, (1, CY, LANES), (2, CY, LANES)],
-        (src, mode_fields, columns, above, below), scratch=bulk_scratch, flops=30_000_000,
-    )
-
-    z_in = shift(call(pack_z1, "pack_z1", [(2, PY, LANES)], (own, rims, y_above, y_below)), "gz", 1)
+    bulk, ends, bulk_edges, stiff7, mass7, own, rims, row32 = call(
+        bulk_kernel1, "bulk1",
+        bulk_outs + [plane, plane, (1, CY, LANES), (2, CY, LANES), (2, 8, LANES)],
+        (src, mode_fields, columns, above, below, y_above), scratch=bulk_scratch, flops=30_000_000,
+    )
+
+    z_in = shift(call(pack_z1, "pack_z1", [(2, PY, LANES)], (own, rims, row32, *halos)), "gz", 1)
     strips, strip_edges, rim, packed = call(
         strip_kernel1, "strips1", strip_outs + [(MODES, 2, 8, CZ), (PY, LANES)],
-        (mode_fields, rims, above, y_above, y_below, ends),
+        (mode_fields, rims, row32, above, *halos, ends),
         scratch=strip_scratch + [(3, 16, CZ)] * 2, flops=20_000_000,
     )
     half = (W, MODES, CY, CZ)
@@ -830,17 +850,20 @@
 
     bulk_outs, bulk_scratch, strip_outs, strip_scratch = sweep_outs(MODES)
     planes = (low, high, above, below)
-    down, up = call(pack_y2, "pack_y2", [(CX + 3, 8, CZ)] * 2, planes)
+    down, up = call(pack_y2, "pack_y2", [(CX, 8, CZ)] * 2, (low, high))
     y_above, y_below = shift(down, "gy", -1), shift(up, "gy", 1)
+    edge = (MODES * (W - 1), 8, CZ)
+    down, up = call(pack_e2, "pack_e2", [edge] * 2, (y_above, y_below))
+    halos = (y_above, y_below, shift(down, "gx", -1), shift(up, "gx", 1))
     bulk, ends, bulk_edges, own = call(
         bulk_kernel2, "bulk2", bulk_outs + [(MODES, CY, LANES)], planes,
         scratch=bulk_scratch, flops=40_000_000,
     )
-    z_in = shift(call(pack_z2, "pack_z2", [(MODES, PY, LANES)], (own, y_above, y_below)), "gz", 1)
+    z_in = shift(call(pack_z2, "pack_z2", [(MODES, PY, LANES)], (own, *halos)), "gz", 1)
     result = (MODES, CX, CY, CZ)
     out, side, strip_edges = call(
         strip_kernel2, "strips2", [result, (MODES, CX, CY, LANES), strip_outs[1]],
-        (solid_mask, y_above, y_below, ends, bulk), out_specs={0: HBM},
+        (solid_mask, *halos, ends, bulk), out_specs={0: HBM},
         scratch=[strip_outs[0]] + strip_scratch + [result, pltpu.SemaphoreType.DMA((4,))],
         flops=20_000_000,
     )

time: 51 us -> 48.8 us (0.957)
  waiting for transfers between devices: 20.2 us -> 14.7 us
  starting transfers between devices: 17 us -> 20.2 us
    ppermute x10 -> x14, waiting for transfers between devices: 20.2 us -> 14.7 us  [shift(): return lax.ppermute(x, axis, ring(axis, step))]
    ppermute x10 -> x14, starting transfers between devices: 17 us -> 20.2 us  [shift(): return lax.ppermute(x, axis, ring(axis, step))]
    pallas_call x13 -> x15, Pallas kernels: 13.2 us -> 13.3 us  [call(): pl.pallas_call(kernel, grid=(1,), out_shape=shapes if len(shapes) > 1 els...]
  transfers between devices with their start and end apart: 10 -> 14, of which waited for: 7 -> 6; matrix products, arithmetic and copies ran while one was open for 0% -> 0% of each run, Pallas kernels for 19% -> 20%
where the time goes in v6:
time: 48.8 us; the launch traced here: 48.7 us
  starting transfers between devices  20.2 us (41%)
  waiting for transfers between devices  14.7 us (30%)
  Pallas kernels  13.3 us (27%)
    ppermute x14, starting transfers between devices, shift(): return lax.ppermute(x, axis, ring(axis, step))  20.2 us
    ppermute x14, waiting for transfers between devices, shift(): return lax.ppermute(x, axis, ring(axis, step))  14.7 us
    pallas_call x15, Pallas kernels, call(): pl.pallas_call(kernel, grid=(1,), out_shape=shapes if len(shapes) > 1 els...  13.3 us
  transfers between devices with their start and end apart: 14, of which 6 were waited for; matrix products, arithmetic and copies ran while one was open for 0% of the time, Pallas kernels for 20%

profile of v6, /device:TPU:0, one launch (start us, length us, event | category | flops | bytes accessed | tf_op | source)
XLA Modules:
  0.0 48.7 jit_solution(18388492302436091466)
XLA Ops:
  0.0 1.4 %pack_x1.1 = (f32[8,32,256]{2,1,0:T(8,128)S(1)}, f32[10,32,256]{2,1,0:T(8,128)S(1)}, f32[4,32,256]{2,1,0:T(8,128)S(1)}) custom-call(f32[8,32,256]{2,1,0:T(8,128)} %design.1, s32[8,32,256]{2,1,0:T(8,128)} %mask.5, f32[2,3,8,32,256]{4,3,2,1,0:T(8,128)} %modes.9), custom_call_target="tpu_custom_call" | custom-call | bytes 2000000 | tf_op jit(solution)/shard_map/pack_x1/pallas_call | solution.py:771
  1.4 2.5 %collective-permute-start = (f32[10,32,256]{2,1,0:T(8,128)S(1)}, f32[10,32,256]{2,1,0:T(8,128)S(1)}, u32[]{:S(2)}, u32[]{:S(2)}) collective-permute-start(f32[10,32,256]{2,1,0:T(8,128)S(1)} %get-tuple-element.42), channel_id=1, source_target_pairs={{0,112},{16,0},{32,16},{48,32},{64,48},{80,64},{96,80},{112,96},{1... | collective-permute-start | bytes 983048 | tf_op jit(solution)/shard_map/ppermute | solution.py:794
  4.0 6.6 %collective-permute-start.2 = (f32[10,8,256]{2,1,0:T(8,128)S(1)}, f32[10,8,256]{2,1,0:T(8,128)S(1)}, u32[]{:S(2)}, u32[]{:S(2)}) collective-permute-start(f32[10,8,256]{2,1,0:T(8,128)S(1)} %get-tuple-element.44), channel_id=1, source_target_pairs={{0,14},{2,0},{4,2},{6,4},{8,6},{10,8},{12,10},{14,12},{1,15},{3,1}... | collective-permute-start | bytes 245768 | tf_op jit(solution)/shard_map/ppermute | solution.py:794
  10.5 3.1 %energy.1 = (f32[2,7,32,256]{3,2,1,0:T(8,128)S(1)}, f32[2,7,32,256]{3,2,1,0:T(8,128)S(1)}, f32[2,32,128]{2,1,0:T(8,128)S(1)}) custom-call(f32[2,3,8,32,256]{4,3,2,1,0:T(8,128)S(1)} %copy-done), custom_call_target="tpu_custom_call" | custom-call | flops 40000000 | bytes 2000000 | tf_op jit(solution)/shard_map/energy/pallas_call | solution.py:771
  13.7 4.4 %collective-permute-done.3.y_below = f32[4,8,256]{2,1,0:T(8,128)S(1)} collective-permute-done((f32[4,8,256]{2,1,0:T(8,128)S(1)}, f32[4,8,256]{2,1,0:T(8,128)S(1)}, u32[]{:S(2)}, u32[]{:S(2)}) %collective-permute-start.3) | collective-permute-done | bytes 32800 | tf_op jit(solution)/shard_map/ppermute | solution.py:794
  18.1 0.0 collective-permute-start.4
  18.1 0.5 %collective-permute-start.5 = (f32[3,8,256]{2,1,0:T(8,128)S(1)}, f32[3,8,256]{2,1,0:T(8,128)S(1)}, u32[]{:S(2)}, u32[]{:S(2)}) collective-permute-start(f32[3,8,256]{2,1,0:T(8,128)S(1)} %get-tuple-element.50), channel_id=1, source_target_pairs={{0,16},{16,32},{32,48},{48,64},{64,80},{80,96},{96,112},{112,0},{1... | collective-permute-start | bytes 73736 | tf_op jit(solution)/shard_map/ppermute | solution.py:794
  18.6 0.2 fusion
  18.8 1.8 %bulk1.1 = (f32[1,8,32,256]{3,2,1,0:T(8,128)S(1)}, f32[1,4,16,2,1,256]{5,4,3,2,1,0:T(1,128)S(1)}, f32[1,4,32,128]{3,2,1,0:T(8,128)S(1)}, f32[2,32,256]{2,1,0:T(8...) custom-call(f32[8,32,256]{2,1,0:T(8,128)S(1)} %get-tuple-element.40., ...), custom_call_target="tpu_custom_call" | custom-call | flops 30000000 | bytes 2000000 | tf_op jit(solution)/shard_map/bulk1/pallas_call | solution.py:771
  20.6 1.9 %collective-permute-done.5.from_below = f32[3,8,256]{2,1,0:T(8,128)S(1)} collective-permute-done((f32[3,8,256]{2,1,0:T(8,128)S(1)}, f32[3,8,256]{2,1,0:T(8,128)S(1)}, u32[]{:S(2)}, u32[]{:S(2)}) %collective-permute-start.5) | collective-permute-done | bytes 24608 | tf_op jit(solution)/shard_map/ppermute | solution.py:794
  22.6 0.1 pack_z1.1
  22.7 0.7 %collective-permute-start.6 = (f32[2,40,128]{2,1,0:T(8,128)S(1)}, f32[2,40,128]{2,1,0:T(8,128)S(1)}, u32[]{:S(2)}, u32[]{:S(2)}) collective-permute-start(f32[2,40,128]{2,1,0:T(8,128)S(1)} %pack_z1.1), channel_id=1, source_target_pairs={{0,1},{1,0},{2,3},{3,2},{4,5},{5,4},{6,7},{7,6},{8,9},{9,8},{10,11... | collective-permute-start | bytes 122888 | tf_op jit(solution)/shard_map/ppermute | solution.py:794
  23.4 0.8 %strips1.1 = (f32[1,8,16,256]{3,2,1,0:T(8,128)S(1)}, f32[1,4,16,128]{3,2,1,0:T(8,128)S(1)}, f32[2,2,8,256]{3,2,1,0:T(8,128)S(1)}, f32[40,128]{1,0:T(8,128)S(1)}) custom-call(f32[2,3,8,32,256]{4,3,2,1,0:T(8,128)S(1)} %copy-done, f32[2,32,128]{2,1,0:T(8,128)S(1)} %get-tuple-element.46.rims, f32[2,8,128]{2,1,0:T(8,128)S(1)} %get-tuple-element.47.row32, ...), custom_call_target="tpu_custom_call" | custom-call | flops 20000000 | bytes 2000000 | tf_op jit(solution)/shard_map/strips1/pallas_call | solution.py:771
  24.2 2.6 %collective-permute-done.6.z_in = f32[2,40,128]{2,1,0:T(8,128)S(1)} collective-permute-done((f32[2,40,128]{2,1,0:T(8,128)S(1)}, f32[2,40,128]{2,1,0:T(8,128)S(1)}, u32[]{:S(2)}, u32[]{:S(2)}) %collective-permute-start.6) | collective-permute-done | bytes 40992 | tf_op jit(solution)/shard_map/ppermute | solution.py:794
  26.8 0.1 broadcast_in_dim.2.lams
  26.8 0.5 %raw1.1 = (f32[4,2,32,256]{3,2,1,0:T(8,128)S(1)}, f32[3,32,128]{2,1,0:T(8,128)S(1)}) custom-call(f32[2,8,128]{2,1,0:T(8,128)S(1)} %broadcast_in_dim.2.lams, f32[2,40,128]{2,1,0:T(8,128)S(1)} %collective-permute-done.6.z_in, f32[40,128]{1,0:T(8,128)S(1)} %get-tuple-element.52.packed, f32[1,8,32,256]{3,2,1,0:T(8,128)S(1)} %get-tuple-element.53.bulk, ...), custom_call_target="tpu_custom_call" | custom-call | bytes 2000000 | tf_op jit(solution)/shard_map/raw1/pallas_call | solution.py:771
  27.4 0.0 copy-start.1
  27.4 0.2 raw2.1.high
  27.6 0.0 collective-permute-start.8
  27.6 2.9 %collective-permute-start.7 = (f32[4,2,32,256]{3,2,1,0:T(8,128)S(1)}, f32[4,2,32,256]{3,2,1,0:T(8,128)S(1)}, u32[]{:S(2)}, u32[]{:S(2)}) collective-permute-start(f32[4,2,32,256]{3,2,1,0:T(8,128)S(1)} %get-tuple-element.62.low), channel_id=1, source_target_pairs={{0,112},{16,0},{32,16},{48,32},{64,48},{80,64},{96,80},{112,96},{1... | collective-permute-start | bytes 786440 | tf_op jit(solution)/shard_map/ppermute | solution.py:794
  30.6 0.1 collective-permute-start.10
  30.6 5.6 %collective-permute-start.9 = (f32[8,8,256]{2,1,0:T(8,128)S(1)}, f32[8,8,256]{2,1,0:T(8,128)S(1)}, u32[]{:S(2)}, u32[]{:S(2)}) collective-permute-start(f32[8,8,256]{2,1,0:T(8,128)S(1)} %get-tuple-element.65), channel_id=1, source_target_pairs={{0,14},{2,0},{4,2},{6,4},{8,6},{10,8},{12,10},{14,12},{1,15},{3,1}... | collective-permute-start | bytes 196616 | tf_op jit(solution)/shard_map/ppermute | solution.py:794
  36.3 2.2 %collective-permute-done.10.y_below = f32[8,8,256]{2,1,0:T(8,128)S(1)} collective-permute-done((f32[8,8,256]{2,1,0:T(8,128)S(1)}, f32[8,8,256]{2,1,0:T(8,128)S(1)}, u32[]{:S(2)}, u32[]{:S(2)}) %collective-permute-start.10) | collective-permute-done | bytes 65568 | tf_op jit(solution)/shard_map/ppermute | solution.py:794
  38.5 0.0 collective-permute-start.11
  38.6 0.5 %collective-permute-start.12 = (f32[6,8,256]{2,1,0:T(8,128)S(1)}, f32[6,8,256]{2,1,0:T(8,128)S(1)}, u32[]{:S(2)}, u32[]{:S(2)}) collective-permute-start(f32[6,8,256]{2,1,0:T(8,128)S(1)} %get-tuple-element.68), channel_id=1, source_target_pairs={{0,16},{16,32},{32,48},{48,64},{64,80},{80,96},{96,112},{112,0},{1... | collective-permute-start | bytes 147464 | tf_op jit(solution)/shard_map/ppermute | solution.py:794
  39.1 2.3 %bulk2.1 = (f32[2,8,32,256]{3,2,1,0:T(8,128)S(1)}, f32[2,4,16,2,1,256]{5,4,3,2,1,0:T(1,128)S(1)}, f32[2,4,32,128]{3,2,1,0:T(8,128)S(1)}, f32[2,32,128]{2,1,0:T(8,128)S(1)}) custom-call(f32[4,2,32,256]{3,2,1,0:T(8,128)S(1)} %get-tuple-element.62.low, f32[4,2,32,256]{3,2,1,0:T(8,128)S(1)} %raw2.1.high, f32[4,2,32,256]{3,2,1,0:T(8,128)S(1)} %collective-permute-done.7.above, ...), custom_call_target="tpu_custom_call" | custom-call | flops 40000000 | bytes 2000000 | tf_op jit(solution)/shard_map/bulk2/pallas_call | solution.py:771
  41.3 2.0 %collective-permute-done.12.from_below = f32[6,8,256]{2,1,0:T(8,128)S(1)} collective-permute-done((f32[6,8,256]{2,1,0:T(8,128)S(1)}, f32[6,8,256]{2,1,0:T(8,128)S(1)}, u32[]{:S(2)}, u32[]{:S(2)}) %collective-permute-start.12) | collective-permute-done | bytes 49184 | tf_op jit(solution)/shard_map/ppermute | solution.py:794
  43.3 0.1 pack_z2.1
  43.4 0.7 %collective-permute-start.13 = (f32[2,40,128]{2,1,0:T(8,128)S(1)}, f32[2,40,128]{2,1,0:T(8,128)S(1)}, u32[]{:S(2)}, u32[]{:S(2)}) collective-permute-start(f32[2,40,128]{2,1,0:T(8,128)S(1)} %pack_z2.1), channel_id=1, source_target_pairs={{0,1},{1,0},{2,3},{3,2},{4,5},{5,4},{6,7},{7,6},{8,9},{9,8},{10,11... | collective-permute-start | bytes 122888 | tf_op jit(solution)/shard_map/ppermute | solution.py:794
  44.1 1.8 %strips2.1 = (f32[2,8,32,256]{3,2,1,0:T(8,128)}, f32[2,8,32,128]{3,2,1,0:T(8,128)S(1)}, f32[2,4,16,128]{3,2,1,0:T(8,128)S(1)}) custom-call(s32[8,32,256]{2,1,0:T(8,128)S(1)} %copy-done.1, f32[8,8,256]{2,1,0:T(8,128)S(1)} %collective-permute-done.9.y_above, f32[8,8,256]{2,1,0:T(8,128)S(1)} %collective-permute-done.10.y_below, ...), custom_call_target="tpu_custom_call" | custom-call | flops 20000000 | bytes 2000000 | tf_op jit(solution)/shard_map/strips2/pallas_call | solution.py:771
  45.9 1.6 %collective-permute-done.13.z_in = f32[2,40,128]{2,1,0:T(8,128)S(1)} collective-permute-done((f32[2,40,128]{2,1,0:T(8,128)S(1)}, f32[2,40,128]{2,1,0:T(8,128)S(1)}, u32[]{:S(2)}, u32[]{:S(2)}) %collective-permute-start.13) | collective-permute-done | bytes 40992 | tf_op jit(solution)/shard_map/ppermute | solution.py:794
  47.5 1.2 %final.1 = f32[2,8,32,256]{3,2,1,0:T(8,128)} custom-call(s32[8,32,256]{2,1,0:T(8,128)S(1)} %copy-done.1, f32[2,40,128]{2,1,0:T(8,128)S(1)} %collective-permute-done.13.z_in, f32[2,4,32,128]{3,2,1,0:T(8,128)S(1)} %get-tuple-element.69.bulk_edges, f32[2,4,16,128]{3,2,1,0:T(8,128)S(1)} %get-tuple-element.72.strip_edges, ...), custom_call_target="tpu_custom_call", output_to_operand_aliasing={{}: (5, {})} | custom-call | bytes 2000000 | tf_op jit(solution)/shard_map/final/pallas_call | solution.py:771
  (22 shorter events, 0.1 us)
Async XLA Ops:
  0.0 3.9 %copy-start = (f32[2,3,8,32,256]{4,3,2,1,0:T(8,128)S(1)}, f32[2,3,8,32,256]{4,3,2,1,0:T(8,128)}, u32[]{:S(2)}) copy-start(f32[2,3,8,32,256]{4,3,2,1,0:T(8,128)} %modes.9) | copy-start | bytes 4718596
  1.4 17.4 %collective-permute-start = (f32[10,32,256]{2,1,0:T(8,128)S(1)}, f32[10,32,256]{2,1,0:T(8,128)S(1)}, u32[]{:S(2)}, u32[]{:S(2)}) collective-permute-start(f32[10,32,256]{2,1,0:T(8,128)S(1)} %get-tuple-element.42), channel_id=1, source_target_pairs={{0,112},{16,0},{32,16},{48,32},{64,48},{80,64},{96,80},{112,96},{1... | collective-permute-start | bytes 983048 | tf_op jit(solution)/shard_map/ppermute | solution.py:794
  3.9 14.7 %copy-start.2 = (f32[6]{0:T(128)S(1)}, f32[6]{0:T(128)}, u32[]{:S(2)}) copy-start(f32[6]{0:T(128)} %param.8) | copy-start | bytes 76
  3.9 14.7 %copy-start.3 = (s32[6]{0:T(128)S(1)}, s32[6]{0:T(128)}, u32[]{:S(2)}) copy-start(s32[6]{0:T(128)} %param.9) | copy-start | bytes 76
  4.0 14.1 %collective-permute-start.2 = (f32[10,8,256]{2,1,0:T(8,128)S(1)}, f32[10,8,256]{2,1,0:T(8,128)S(1)}, u32[]{:S(2)}, u32[]{:S(2)}) collective-permute-start(f32[10,8,256]{2,1,0:T(8,128)S(1)} %get-tuple-element.44), channel_id=1, source_target_pairs={{0,14},{2,0},{4,2},{6,4},{8,6},{10,8},{12,10},{14,12},{1,15},{3,1}... | collective-permute-start | bytes 245768 | tf_op jit(solution)/shard_map/ppermute | solution.py:794
  10.5 7.5 %collective-permute-start.3 = (f32[4,8,256]{2,1,0:T(8,128)S(1)}, f32[4,8,256]{2,1,0:T(8,128)S(1)}, u32[]{:S(2)}, u32[]{:S(2)}) collective-permute-start(f32[4,8,256]{2,1,0:T(8,128)S(1)} %get-tuple-element.48), channel_id=1, source_target_pairs={{0,2},{2,4},{4,6},{6,8},{8,10},{10,12},{12,14},{14,0},{1,3},{3,5},... | collective-permute-start | bytes 98312 | tf_op jit(solution)/shard_map/ppermute | solution.py:794
  10.5 8.3 %collective-permute-start.1 = (f32[4,32,256]{2,1,0:T(8,128)S(1)}, f32[4,32,256]{2,1,0:T(8,128)S(1)}, u32[]{:S(2)}, u32[]{:S(2)}) collective-permute-start(f32[4,32,256]{2,1,0:T(8,128)S(1)} %get-tuple-element.43), channel_id=1, source_target_pairs={{0,16},{16,32},{32,48},{48,64},{64,80},{80,96},{96,112},{112,0},{1... | collective-permute-start | bytes 393224 | tf_op jit(solution)/shard_map/ppermute | solution.py:794
  18.1 4.5 %collective-permute-start.4 = (f32[4,8,256]{2,1,0:T(8,128)S(1)}, f32[4,8,256]{2,1,0:T(8,128)S(1)}, u32[]{:S(2)}, u32[]{:S(2)}) collective-permute-start(f32[4,8,256]{2,1,0:T(8,128)S(1)} %get-tuple-element.49), channel_id=1, source_target_pairs={{0,112},{16,0},{32,16},{48,32},{64,48},{80,64},{96,80},{112,96},{1... | collective-permute-start | bytes 98312 | tf_op jit(solution)/shard_map/ppermute | solution.py:794
  18.1 4.5 %collective-permute-start.5 = (f32[3,8,256]{2,1,0:T(8,128)S(1)}, f32[3,8,256]{2,1,0:T(8,128)S(1)}, u32[]{:S(2)}, u32[]{:S(2)}) collective-permute-start(f32[3,8,256]{2,1,0:T(8,128)S(1)} %get-tuple-element.50), channel_id=1, source_target_pairs={{0,16},{16,32},{32,48},{48,64},{64,80},{80,96},{96,112},{112,0},{1... | collective-permute-start | bytes 73736 | tf_op jit(solution)/shard_map/ppermute | solution.py:794
  22.7 4.1 %collective-permute-start.6 = (f32[2,40,128]{2,1,0:T(8,128)S(1)}, f32[2,40,128]{2,1,0:T(8,128)S(1)}, u32[]{:S(2)}, u32[]{:S(2)}) collective-permute-start(f32[2,40,128]{2,1,0:T(8,128)S(1)} %pack_z1.1), channel_id=1, source_target_pairs={{0,1},{1,0},{2,3},{3,2},{4,5},{5,4},{6,7},{7,6},{8,9},{9,8},{10,11... | collective-permute-start | bytes 122888 | tf_op jit(solution)/shard_map/ppermute | solution.py:794
  27.4 16.7 %copy-start.1 = (s32[8,32,256]{2,1,0:T(8,128)S(1)}, s32[8,32,256]{2,1,0:T(8,128)}, u32[]{:S(2)}) copy-start(s32[8,32,256]{2,1,0:T(8,128)} %mask.5) | copy-start | bytes 786436
  27.6 11.5 %collective-permute-start.8 = (f32[4,2,32,256]{3,2,1,0:T(8,128)S(1)}, f32[4,2,32,256]{3,2,1,0:T(8,128)S(1)}, u32[]{:S(2)}, u32[]{:S(2)}) collective-permute-start(f32[4,2,32,256]{3,2,1,0:T(8,128)S(1)} %raw2.1.high), channel_id=1, source_target_pairs={{0,16},{16,32},{32,48},{48,64},{64,80},{80,96},{96,112},{112,0},{1... | collective-permute-start | bytes 786440 | tf_op jit(solution)/shard_map/ppermute | solution.py:794
  27.6 11.5 %collective-permute-start.7 = (f32[4,2,32,256]{3,2,1,0:T(8,128)S(1)}, f32[4,2,32,256]{3,2,1,0:T(8,128)S(1)}, u32[]{:S(2)}, u32[]{:S(2)}) collective-permute-start(f32[4,2,32,256]{3,2,1,0:T(8,128)S(1)} %get-tuple-element.62.low), channel_id=1, source_target_pairs={{0,112},{16,0},{32,16},{48,32},{64,48},{80,64},{96,80},{112,96},{1... | collective-permute-start | bytes 786440 | tf_op jit(solution)/shard_map/ppermute | solution.py:794
  30.6 7.9 %collective-permute-start.10 = (f32[8,8,256]{2,1,0:T(8,128)S(1)}, f32[8,8,256]{2,1,0:T(8,128)S(1)}, u32[]{:S(2)}, u32[]{:S(2)}) collective-permute-start(f32[8,8,256]{2,1,0:T(8,128)S(1)} %get-tuple-element.66), channel_id=1, source_target_pairs={{0,2},{2,4},{4,6},{6,8},{8,10},{10,12},{12,14},{14,0},{1,3},{3,5},... | collective-permute-start | bytes 196616 | tf_op jit(solution)/shard_map/ppermute | solution.py:794
  30.6 7.9 %collective-permute-start.9 = (f32[8,8,256]{2,1,0:T(8,128)S(1)}, f32[8,8,256]{2,1,0:T(8,128)S(1)}, u32[]{:S(2)}, u32[]{:S(2)}) collective-permute-start(f32[8,8,256]{2,1,0:T(8,128)S(1)} %get-tuple-element.65), channel_id=1, source_target_pairs={{0,14},{2,0},{4,2},{6,4},{8,6},{10,8},{12,10},{14,12},{1,15},{3,1}... | collective-permute-start | bytes 196616 | tf_op jit(solution)/shard_map/ppermute | solution.py:794
  38.5 2.8 %collective-permute-start.11 = (f32[6,8,256]{2,1,0:T(8,128)S(1)}, f32[6,8,256]{2,1,0:T(8,128)S(1)}, u32[]{:S(2)}, u32[]{:S(2)}) collective-permute-start(f32[6,8,256]{2,1,0:T(8,128)S(1)} %get-tuple-element.67), channel_id=1, source_target_pairs={{0,112},{16,0},{32,16},{48,32},{64,48},{80,64},{96,80},{112,96},{1... | collective-permute-start | bytes 147464 | tf_op jit(solution)/shard_map/ppermute | solution.py:794
  38.6 4.7 %collective-permute-start.12 = (f32[6,8,256]{2,1,0:T(8,128)S(1)}, f32[6,8,256]{2,1,0:T(8,128)S(1)}, u32[]{:S(2)}, u32[]{:S(2)}) collective-permute-start(f32[6,8,256]{2,1,0:T(8,128)S(1)} %get-tuple-element.68), channel_id=1, source_target_pairs={{0,16},{16,32},{32,48},{48,64},{64,80},{80,96},{96,112},{112,0},{1... | collective-permute-start | bytes 147464 | tf_op jit(solution)/shard_map/ppermute | solution.py:794
  43.4 4.1 %collective-permute-start.13 = (f32[2,40,128]{2,1,0:T(8,128)S(1)}, f32[2,40,128]{2,1,0:T(8,128)S(1)}, u32[]{:S(2)}, u32[]{:S(2)}) collective-permute-start(f32[2,40,128]{2,1,0:T(8,128)S(1)} %pack_z2.1), channel_id=1, source_target_pairs={{0,1},{1,0},{2,3},{3,2},{4,5},{5,4},{6,7},{7,6},{8,9},{9,8},{10,11... | collective-permute-start | bytes 122888 | tf_op jit(solution)/shard_map/ppermute | solution.py:794

commit v7 on v6

--- a/solution.py
+++ b/solution.py
@@ -1,3 +1,5 @@
+import functools
+
 import jax
 import jax.numpy as jnp
 from jax import lax
@@ -392,27 +394,33 @@
     return jnp.concatenate([packed, row * keep_y], axis=0)
 
 
-def pack_x1(design, mask, modes, src, down, up, field, solid, arrived):
+def pack_x1(
+    design, mask, modes, eigenvalues, order, src, down, up, lams, field, solid, values, chosen, arrived
+):
     copies = []
-    for x in range(CX):
-        copies.append(pltpu.make_async_copy(design.at[x], field.at[x], arrived.at[2 * x]))
-        copies.append(pltpu.make_async_copy(mask.at[x], solid.at[x], arrived.at[2 * x + 1]))
-    for n in range(3 * MODES):
-        to = down.at[W + n]
-        copies.append(pltpu.make_async_copy(modes.at[n // 3, n % 3, 0], to, arrived.at[2 * CX + n]))
+    for half in (slice(0, W), slice(W, CX)):
+        copies.append((design.at[half], field.at[half]))
+        copies.append((mask.at[half], solid.at[half]))
+    for m in range(MODES):
+        copies.append((modes.at[m, :, 0], down.at[W + 3 * m : W + 3 * m + 3]))
+    copies += [(eigenvalues, values), (order, chosen)]
+    copies = [pltpu.make_async_copy(a, b, arrived.at[n]) for n, (a, b) in enumerate(copies)]
     for copy in copies:
         copy.start()
     for x in range(CX):
-        copies[2 * x].wait()
-        copies[2 * x + 1].wait()
+        if x % W == 0:
+            copies[2 * (x // W)].wait()
+            copies[2 * (x // W) + 1].wait()
         plane = field[x] * solid[x].astype(F32)
         src[x] = plane
         if x < W:
             down[x] = plane
-        if x >= CX - W:
-            up[x - (CX - W)] = plane
-    for copy in copies[2 * CX :]:
+        else:
+            up[x - W] = plane
+    for copy in copies[4:]:
         copy.wait()
+    for m in range(MODES):
+        lams[m] = jnp.full((8, LANES), values[chosen[m]] * (0.125 * 0.25), F32)
 
 
 def energy_kernel(modes, stiff, mass, columns):
@@ -655,7 +663,7 @@
     return jnp.where(iota(a.shape, 0) < 4, a, b)
 
 
-def pack_e2(y_above, y_below, down, up):
+def pack_e2(y_above, y_below, ahead, down, up):
     for i in range(W - 1):
         for m in range(MODES):
             down[MODES * i + m] = own_raw_halo(y_above, y_below, m, i)
@@ -672,55 +680,57 @@
     return jnp.zeros(y_above[0, :, lanes].shape, F32)
 
 
-def bulk_kernel2(low, high, above, below, bulk, ends, edges, own, table, sb, one, two):
+def bulk_kernel2(m, low, high, above, below, bulk, ends, edges, own, table, sb, one, two):
     at = pos()
     fill_bulk(table, at[1], at[2])
 
-    def source(m, p, i):
+    def source(_, p, i):
         a, at_plane = raw_plane(low, high, above, below, p)
         return a[at_plane, m, 8 * i : 8 * i + 8, :]
 
-    bulk_sweeps(MODES, at, table, source, (sb, one, two), ends, edges, bulk)
+    bulk_sweeps(1, at, table, source, (sb, one, two), ends, edges, bulk)
     edge = edge_tiles(at[2])
-    for m in range(MODES):
-
-        def load(p, m=m):
-            a, i = raw_plane(low, high, above, below, p)
-            return a[i, m, :, edge]
-
-        own[m] = own_strip(at[2], load)
-
-
-def pack_z2(own, y_above, y_below, from_above, from_below, out):
+
+    def load(p):
+        a, i = raw_plane(low, high, above, below, p)
+        return a[i, m, :, edge]
+
+    own[0] = own_strip(at[2], load)
+
+
+def pack_z2(own0, own1, y_above, y_below, from_above, from_below, out):
     gx, gy, gz = pos()
     edge = edge_tiles(gz)
     halos = (y_above, y_below, from_above, from_below)
-    for m in range(MODES):
-        out[m, 0:CY, :] = own[m]
+    for m, own in enumerate((own0, own1)):
+        out[m, 0:CY, :] = own[0]
         out[m, CY:PY, :] = own_strip(gz, lambda p, m=m: raw_halo(*halos, m, p, edge), 8)
 
 
 def strip_kernel2(
-    mask, y_above, y_below, from_above, from_below, ends, bulk,
-    out, side, edges, strips, table, sb, one, two, held, left,
+    mask, y_above, y_below, from_above, from_below, ends0, ends1, bulk0, bulk1,
+    out, side, edges0, edges1, table, strips0, strips1, a0, a1, b0, b1, c0, c1, held, left,
 ):
     gx, gy, gz = at = pos()
     sub, lane = sub_lane()
     fill_strips(table, gy, gz)
-
-    def source(m, p):
-        return raw_halo(y_above, y_below, from_above, from_below, m, p)
-
-    strip_sweeps(MODES, at, table, source, ends, (sb, one, two), edges, strips)
+    states = ((a0, b0, c0), (a1, b1, c1))
     copies = []
     for m in range(MODES):
+        ends, bulk, edges = (ends0, ends1)[m], (bulk0, bulk1)[m], (edges0, edges1)[m]
+        strips = (strips0, strips1)[m]
+
+        def source(_, p, m=m):
+            return raw_halo(y_above, y_below, from_above, from_below, m, p)
+
+        strip_sweeps(1, at, table, source, ends, states[m], edges, strips)
         for x in range(CX):
             for i in range(CY // 8):
                 rows = slice(8 * i, 8 * i + 8)
                 pair = []
                 for j in range(2):
                     cols = slice(LANES * j, LANES * j + LANES)
-                    value = pair_tile(m, x, i, j, bulk, strips, sub)
+                    value = pair_tile(0, x, i, j, bulk, strips, sub)
                     held[m, x, rows, cols] = value * mask[x, rows, cols].astype(F32)
                     pair.append(value)
                 side[m, x, rows, :] = jnp.where(gz == 0, pair[1], pair[0])
@@ -733,7 +743,7 @@
         copy.wait()
 
 
-def final_kernel(mask, z_in, bulk_edges, strip_edges, side, given, out, held, left):
+def final_kernel(mask, z_in, bulk_edges0, bulk_edges1, strip_edges0, strip_edges1, side, given, out, held, left):
     gx, gy, gz = pos()
     sub, lane = sub_lane()
     at_end = beside_halo(gz, lane)
@@ -742,7 +752,8 @@
     scale = strip_scale(gx, gy)
     copies = []
     for m in range(MODES):
-        z_state = z_sweeps(m, scale, z_in[m], bulk_edges, strip_edges)
+        edges = ((bulk_edges0, strip_edges0), (bulk_edges1, strip_edges1))[m]
+        z_state = z_sweeps(0, scale, z_in[m], *edges)
         for x in range(CX):
             for i in range(CY // 8):
                 rows = slice(8 * i, 8 * i + 8)
@@ -804,16 +815,17 @@
 
 
 def local(mode_fields, design, solid_mask, eigenvalues, mode_order):
-    selector = (mode_order[:MODES, None] == jnp.arange(eigenvalues.shape[0], dtype=jnp.int32)).astype(F32)
-    chosen = jnp.sum(selector * eigenvalues[None, :], axis=1) * (0.125 * 0.25)
-    lams = jnp.broadcast_to(chosen[:, None, None], (MODES, 8, LANES))
     bulk_outs, bulk_scratch, strip_outs, strip_scratch = sweep_outs(1)
 
-    src, down, up = call(
-        pack_x1, "pack_x1", [(CX, CY, CZ), (W + 6, CY, CZ), (W, CY, CZ)],
-        tuple(pltpu.with_memory_space_constraint(x, pltpu.HBM) for x in (design, solid_mask, mode_fields)),
-        {0: HBM, 1: HBM, 2: HBM},
-        scratch=[(CX, CY, CZ), pltpu.VMEM((CX, CY, CZ), jnp.int32), pltpu.SemaphoreType.DMA((2 * CX + 6,))],
+    inputs = (design, solid_mask, mode_fields, eigenvalues, mode_order)
+    src, down, up, lams = call(
+        pack_x1, "pack_x1", [(CX, CY, CZ), (W + 6, CY, CZ), (W, CY, CZ), (MODES, 8, LANES)],
+        tuple(pltpu.with_memory_space_constraint(x, pltpu.HBM) for x in inputs),
+        {i: HBM for i in range(5)},
+        scratch=[
+            (CX, CY, CZ), pltpu.VMEM((CX, CY, CZ), jnp.int32), pltpu.SMEM((eigenvalues.size,), F32),
+            pltpu.SMEM((mode_order.size,), jnp.int32), pltpu.SemaphoreType.DMA((8,)),
+        ],
     )
     above, below = shift(down, "gx", -1), shift(up, "gx", 1)
     field = (MODES, CX - 1, CY, CZ)
@@ -848,29 +860,34 @@
     high = call(raw_kernel2, "raw2", [half], (lams, z_parts, bulk, strips, *energies), flops=60_000_000)
     below = shift(high, "gx", 1)
 
-    bulk_outs, bulk_scratch, strip_outs, strip_scratch = sweep_outs(MODES)
     planes = (low, high, above, below)
     down, up = call(pack_y2, "pack_y2", [(CX, 8, CZ)] * 2, (low, high))
     y_above, y_below = shift(down, "gy", -1), shift(up, "gy", 1)
+    bulks = [
+        call(
+            functools.partial(bulk_kernel2, m), f"bulk2_{m}", bulk_outs + [(1, CY, LANES)], planes,
+            scratch=bulk_scratch, flops=20_000_000,
+        )
+        for m in range(MODES)
+    ]
+    bulk, ends, bulk_edges, own = zip(*bulks)
     edge = (MODES * (W - 1), 8, CZ)
-    down, up = call(pack_e2, "pack_e2", [edge] * 2, (y_above, y_below))
+    down, up = call(pack_e2, "pack_e2", [edge] * 2, (y_above, y_below, own[0]))
     halos = (y_above, y_below, shift(down, "gx", -1), shift(up, "gx", 1))
-    bulk, ends, bulk_edges, own = call(
-        bulk_kernel2, "bulk2", bulk_outs + [(MODES, CY, LANES)], planes,
-        scratch=bulk_scratch, flops=40_000_000,
-    )
-    z_in = shift(call(pack_z2, "pack_z2", [(MODES, PY, LANES)], (own, *halos)), "gz", 1)
+    z_in = shift(call(pack_z2, "pack_z2", [(MODES, PY, LANES)], (*own, *halos)), "gz", 1)
     result = (MODES, CX, CY, CZ)
-    out, side, strip_edges = call(
-        strip_kernel2, "strips2", [result, (MODES, CX, CY, LANES), strip_outs[1]],
-        (solid_mask, *halos, ends, bulk), out_specs={0: HBM},
-        scratch=[strip_outs[0]] + strip_scratch + [result, pltpu.SemaphoreType.DMA((4,))],
+    strips, edges = strip_outs
+    table, state = strip_scratch[0], strip_scratch[1]
+    out, side, *strip_edges = call(
+        strip_kernel2, "strips2", [result, (MODES, CX, CY, LANES), edges, edges],
+        (solid_mask, *halos, *ends, *bulk), out_specs={0: HBM},
+        scratch=[table, strips, strips] + [state] * 6 + [result, pltpu.SemaphoreType.DMA((4,))],
         flops=20_000_000,
     )
     return call(
         final_kernel, "final", [result],
-        (solid_mask, z_in, bulk_edges, strip_edges, side, out), {5: HBM}, {0: HBM},
-        scratch=[(MODES, CX, CY, LANES), pltpu.SemaphoreType.DMA((4,))], aliases={5: 0},
+        (solid_mask, z_in, *bulk_edges, *strip_edges, side, out), {7: HBM}, {0: HBM},
+        scratch=[(MODES, CX, CY, LANES), pltpu.SemaphoreType.DMA((4,))], aliases={7: 0},
     )
 
 

time: 48.8 us -> 50.9 us (1.043)
  waiting for transfers between devices: 14.7 us -> 20 us
  starting transfers between devices: 20.2 us -> 17.2 us
    ppermute x14, waiting for transfers between devices: 14.7 us -> 20 us  [shift(): return lax.ppermute(x, axis, ring(axis, step))]
    ppermute x14, starting transfers between devices: 20.2 us -> 17.2 us  [shift(): return lax.ppermute(x, axis, ring(axis, step))]
    pallas_call x15 -> x16, Pallas kernels: 13.3 us -> 13.5 us  [call(): pl.pallas_call(kernel, grid=(1,), out_shape=shapes if len(shapes) > 1 els...]
  transfers between devices with their start and end apart: 14 -> 14, of which waited for: 6 -> 8; matrix products, arithmetic and copies ran while one was open for 0% -> 0% of each run, Pallas kernels for 20% -> 20%
where the time goes in v7:
time: 50.9 us; the launch traced here: 50.8 us
  waiting for transfers between devices  20 us (39%)
  starting transfers between devices  17.2 us (34%)
  Pallas kernels  13.5 us (27%)
    ppermute x14, waiting for transfers between devices, shift(): return lax.ppermute(x, axis, ring(axis, step))  20 us
    ppermute x14, starting transfers between devices, shift(): return lax.ppermute(x, axis, ring(axis, step))  17.2 us
    pallas_call x16, Pallas kernels, call(): pl.pallas_call(kernel, grid=(1,), out_shape=shapes if len(shapes) > 1 els...  13.5 us
  transfers between devices with their start and end apart: 14, of which 8 were waited for; matrix products, arithmetic and copies ran while one was open for 0% of the time, Pallas kernels for 20%

profile of v7, /device:TPU:0, one launch (start us, length us, event | category | flops | bytes accessed | tf_op | source)
XLA Modules:
  0.0 50.8 jit_solution(18421024990238964641)
XLA Ops:
  0.0 1.4 %pack_x1.1 = (f32[8,32,256]{2,1,0:T(8,128)S(1)}, f32[10,32,256]{2,1,0:T(8,128)S(1)}, f32[4,32,256]{2,1,0:T(8,128)S(1)}, f32[2,8,128]{2,1,0:T(8,128)S(1)}) custom-call(f32[8,32,256]{2,1,0:T(8,128)} %design.1, s32[8,32,256]{2,1,0:T(8,128)} %mask.5, f32[2,3,8,32,256]{4,3,2,1,0:T(8,128)} %modes.9, f32[6]{0:T(128)} %eigenvalues.1, s32[6]{0:T(128)} %order.1), custom_call_target="tpu_custom_call" | custom-call | bytes 2000000 | tf_op jit(solution)/shard_map/pack_x1/pallas_call | solution.py:782
  1.4 2.5 %collective-permute-start = (f32[10,32,256]{2,1,0:T(8,128)S(1)}, f32[10,32,256]{2,1,0:T(8,128)S(1)}, u32[]{:S(2)}, u32[]{:S(2)}) collective-permute-start(f32[10,32,256]{2,1,0:T(8,128)S(1)} %get-tuple-element.49), channel_id=1, source_target_pairs={{0,112},{16,0},{32,16},{48,32},{64,48},{80,64},{96,80},{112,96},{1... | collective-permute-start | bytes 983048 | tf_op jit(solution)/shard_map/ppermute | solution.py:805
  4.0 6.6 %collective-permute-start.2 = (f32[10,8,256]{2,1,0:T(8,128)S(1)}, f32[10,8,256]{2,1,0:T(8,128)S(1)}, u32[]{:S(2)}, u32[]{:S(2)}) collective-permute-start(f32[10,8,256]{2,1,0:T(8,128)S(1)} %get-tuple-element.51), channel_id=1, source_target_pairs={{0,14},{2,0},{4,2},{6,4},{8,6},{10,8},{12,10},{14,12},{1,15},{3,1}... | collective-permute-start | bytes 245768 | tf_op jit(solution)/shard_map/ppermute | solution.py:805
  10.6 3.1 %energy.1 = (f32[2,7,32,256]{3,2,1,0:T(8,128)S(1)}, f32[2,7,32,256]{3,2,1,0:T(8,128)S(1)}, f32[2,32,128]{2,1,0:T(8,128)S(1)}) custom-call(f32[2,3,8,32,256]{4,3,2,1,0:T(8,128)S(1)} %copy-done), custom_call_target="tpu_custom_call" | custom-call | flops 40000000 | bytes 2000000 | tf_op jit(solution)/shard_map/energy/pallas_call | solution.py:782
  13.7 4.4 %collective-permute-done.3.y_below = f32[4,8,256]{2,1,0:T(8,128)S(1)} collective-permute-done((f32[4,8,256]{2,1,0:T(8,128)S(1)}, f32[4,8,256]{2,1,0:T(8,128)S(1)}, u32[]{:S(2)}, u32[]{:S(2)}) %collective-permute-start.3) | collective-permute-done | bytes 32800 | tf_op jit(solution)/shard_map/ppermute | solution.py:805
  18.1 0.0 collective-permute-done.2.y_above
  18.1 1.5 %collective-permute-start.4 = (f32[4,8,256]{2,1,0:T(8,128)S(1)}, f32[4,8,256]{2,1,0:T(8,128)S(1)}, u32[]{:S(2)}, u32[]{:S(2)}) collective-permute-start(f32[4,8,256]{2,1,0:T(8,128)S(1)} %get-tuple-element.56), channel_id=1, source_target_pairs={{0,112},{16,0},{32,16},{48,32},{64,48},{80,64},{96,80},{112,96},{1... | collective-permute-start | bytes 98312 | tf_op jit(solution)/shard_map/ppermute | solution.py:805
  19.7 1.8 %bulk1.1 = (f32[1,8,32,256]{3,2,1,0:T(8,128)S(1)}, f32[1,4,16,2,1,256]{5,4,3,2,1,0:T(1,128)S(1)}, f32[1,4,32,128]{3,2,1,0:T(8,128)S(1)}, f32[2,32,256]{2,1,0:T(8...) custom-call(f32[8,32,256]{2,1,0:T(8,128)S(1)} %get-tuple-element.47., ...), custom_call_target="tpu_custom_call" | custom-call | flops 30000000 | bytes 2000000 | tf_op jit(solution)/shard_map/bulk1/pallas_call | solution.py:782
  21.5 2.6 %collective-permute-done.5.from_below = f32[3,8,256]{2,1,0:T(8,128)S(1)} collective-permute-done((f32[3,8,256]{2,1,0:T(8,128)S(1)}, f32[3,8,256]{2,1,0:T(8,128)S(1)}, u32[]{:S(2)}, u32[]{:S(2)}) %collective-permute-start.5) | collective-permute-done | bytes 24608 | tf_op jit(solution)/shard_map/ppermute | solution.py:805
  24.1 0.1 pack_z1.1
  24.2 0.7 %collective-permute-start.6 = (f32[2,40,128]{2,1,0:T(8,128)S(1)}, f32[2,40,128]{2,1,0:T(8,128)S(1)}, u32[]{:S(2)}, u32[]{:S(2)}) collective-permute-start(f32[2,40,128]{2,1,0:T(8,128)S(1)} %pack_z1.1), channel_id=1, source_target_pairs={{0,1},{1,0},{2,3},{3,2},{4,5},{5,4},{6,7},{7,6},{8,9},{9,8},{10,11... | collective-permute-start | bytes 122888 | tf_op jit(solution)/shard_map/ppermute | solution.py:805
  24.9 0.8 %strips1.1 = (f32[1,8,16,256]{3,2,1,0:T(8,128)S(1)}, f32[1,4,16,128]{3,2,1,0:T(8,128)S(1)}, f32[2,2,8,256]{3,2,1,0:T(8,128)S(1)}, f32[40,128]{1,0:T(8,128)S(1)}) custom-call(f32[2,3,8,32,256]{4,3,2,1,0:T(8,128)S(1)} %copy-done, f32[2,32,128]{2,1,0:T(8,128)S(1)} %get-tuple-element.53.rims, f32[2,8,128]{2,1,0:T(8,128)S(1)} %get-tuple-element.54.row32, ...), custom_call_target="tpu_custom_call" | custom-call | flops 20000000 | bytes 2000000 | tf_op jit(solution)/shard_map/strips1/pallas_call | solution.py:782
  25.7 2.6 %collective-permute-done.6.z_in = f32[2,40,128]{2,1,0:T(8,128)S(1)} collective-permute-done((f32[2,40,128]{2,1,0:T(8,128)S(1)}, f32[2,40,128]{2,1,0:T(8,128)S(1)}, u32[]{:S(2)}, u32[]{:S(2)}) %collective-permute-start.6) | collective-permute-done | bytes 40992 | tf_op jit(solution)/shard_map/ppermute | solution.py:805
  28.3 0.5 %raw1.1 = (f32[4,2,32,256]{3,2,1,0:T(8,128)S(1)}, f32[3,32,128]{2,1,0:T(8,128)S(1)}) custom-call(f32[2,8,128]{2,1,0:T(8,128)S(1)} %get-tuple-element.46.lams, f32[2,40,128]{2,1,0:T(8,128)S(1)} %collective-permute-done.6.z_in, f32[40,128]{1,0:T(8,128)S(1)} %get-tuple-element.59.packed, f32[1,8,32,256]{3,2,1,0:T(8,128)S(1)} %get-tuple-element.60.bulk, ...), custom_call_target="tpu_custom_call" | custom-call | bytes 2000000 | tf_op jit(solution)/shard_map/raw1/pallas_call | solution.py:782
  28.8 0.2 raw2.1.high
  29.0 0.0 copy-start.1
  29.0 0.0 collective-permute-start.7
  29.0 0.5 collective-permute-start.8
  29.6 2.2 %collective-permute-start.9 = (f32[8,8,256]{2,1,0:T(8,128)S(1)}, f32[8,8,256]{2,1,0:T(8,128)S(1)}, u32[]{:S(2)}, u32[]{:S(2)}) collective-permute-start(f32[8,8,256]{2,1,0:T(8,128)S(1)} %get-tuple-element.73), channel_id=1, source_target_pairs={{0,14},{2,0},{4,2},{6,4},{8,6},{10,8},{12,10},{14,12},{1,15},{3,1}... | collective-permute-start | bytes 196616 | tf_op jit(solution)/shard_map/ppermute | solution.py:805
  31.8 1.4 %collective-permute-start.10 = (f32[8,8,256]{2,1,0:T(8,128)S(1)}, f32[8,8,256]{2,1,0:T(8,128)S(1)}, u32[]{:S(2)}, u32[]{:S(2)}) collective-permute-start(f32[8,8,256]{2,1,0:T(8,128)S(1)} %get-tuple-element.74), channel_id=1, source_target_pairs={{0,2},{2,4},{4,6},{6,8},{8,10},{10,12},{12,14},{14,0},{1,3},{3,5},... | collective-permute-start | bytes 196616 | tf_op jit(solution)/shard_map/ppermute | solution.py:805
  33.2 2.9 %collective-permute-done.8.below = f32[4,2,32,256]{3,2,1,0:T(8,128)S(1)} collective-permute-done((f32[4,2,32,256]{3,2,1,0:T(8,128)S(1)}, f32[4,2,32,256]{3,2,1,0:T(8,128)S(1)}, u32[]{:S(2)}, u32[]{:S(2)}) %collective-permute-start.8) | collective-permute-done | bytes 262176 | tf_op jit(solution)/shard_map/ppermute | solution.py:805
  36.1 1.2 %bulk2_0.1 = (f32[1,8,32,256]{3,2,1,0:T(8,128)S(1)}, f32[1,4,16,2,1,256]{5,4,3,2,1,0:T(1,128)S(1)}, f32[1,4,32,128]{3,2,1,0:T(8,128)S(1)}, f32[1,32,128]{2,1,0:T(8,128)S(1)}) custom-call(f32[4,2,32,256]{3,2,1,0:T(8,128)S(1)} %get-tuple-element.69.low, f32[4,2,32,256]{3,2,1,0:T(8,128)S(1)} %raw2.1.high, f32[4,2,32,256]{3,2,1,0:T(8,128)S(1)} %collective-permute-done.7.above, ...), custom_call_target="tpu_custom_call" | custom-call | flops 20000000 | bytes 2000000 | tf_op jit(solution)/shard_map/bulk2_0/pallas_call | solution.py:782
  37.3 2.4 %collective-permute-done.10.y_below = f32[8,8,256]{2,1,0:T(8,128)S(1)} collective-permute-done((f32[8,8,256]{2,1,0:T(8,128)S(1)}, f32[8,8,256]{2,1,0:T(8,128)S(1)}, u32[]{:S(2)}, u32[]{:S(2)}) %collective-permute-start.10) | collective-permute-done | bytes 65568 | tf_op jit(solution)/shard_map/ppermute | solution.py:805
  39.6 1.1 %collective-permute-start.11 = (f32[6,8,256]{2,1,0:T(8,128)S(1)}, f32[6,8,256]{2,1,0:T(8,128)S(1)}, u32[]{:S(2)}, u32[]{:S(2)}) collective-permute-start(f32[6,8,256]{2,1,0:T(8,128)S(1)} %get-tuple-element.75), channel_id=1, source_target_pairs={{0,112},{16,0},{32,16},{48,32},{64,48},{80,64},{96,80},{112,96},{1... | collective-permute-start | bytes 147464 | tf_op jit(solution)/shard_map/ppermute | solution.py:805
  40.7 1.2 %bulk2_1.1 = (f32[1,8,32,256]{3,2,1,0:T(8,128)S(1)}, f32[1,4,16,2,1,256]{5,4,3,2,1,0:T(1,128)S(1)}, f32[1,4,32,128]{3,2,1,0:T(8,128)S(1)}, f32[1,32,128]{2,1,0:T(8,128)S(1)}) custom-call(f32[4,2,32,256]{3,2,1,0:T(8,128)S(1)} %get-tuple-element.69.low, f32[4,2,32,256]{3,2,1,0:T(8,128)S(1)} %raw2.1.high, f32[4,2,32,256]{3,2,1,0:T(8,128)S(1)} %collective-permute-done.7.above, ...), custom_call_target="tpu_custom_call" | custom-call | flops 20000000 | bytes 2000000 | tf_op jit(solution)/shard_map/bulk2_1/pallas_call | solution.py:782
  41.9 0.6 %collective-permute-done.11.from_above = f32[6,8,256]{2,1,0:T(8,128)S(1)} collective-permute-done((f32[6,8,256]{2,1,0:T(8,128)S(1)}, f32[6,8,256]{2,1,0:T(8,128)S(1)}, u32[]{:S(2)}, u32[]{:S(2)}) %collective-permute-start.11) | collective-permute-done | bytes 49184 | tf_op jit(solution)/shard_map/ppermute | solution.py:805
  42.5 3.0 %collective-permute-done.12.from_below = f32[6,8,256]{2,1,0:T(8,128)S(1)} collective-permute-done((f32[6,8,256]{2,1,0:T(8,128)S(1)}, f32[6,8,256]{2,1,0:T(8,128)S(1)}, u32[]{:S(2)}, u32[]{:S(2)}) %collective-permute-start.12) | collective-permute-done | bytes 49184 | tf_op jit(solution)/shard_map/ppermute | solution.py:805
  45.4 0.1 pack_z2.1
  45.5 0.7 %collective-permute-start.13 = (f32[2,40,128]{2,1,0:T(8,128)S(1)}, f32[2,40,128]{2,1,0:T(8,128)S(1)}, u32[]{:S(2)}, u32[]{:S(2)}) collective-permute-start(f32[2,40,128]{2,1,0:T(8,128)S(1)} %pack_z2.1), channel_id=1, source_target_pairs={{0,1},{1,0},{2,3},{3,2},{4,5},{5,4},{6,7},{7,6},{8,9},{9,8},{10,11... | collective-permute-start | bytes 122888 | tf_op jit(solution)/shard_map/ppermute | solution.py:805
  46.2 1.8 %strips2.1 = (f32[2,8,32,256]{3,2,1,0:T(8,128)}, f32[2,8,32,128]{3,2,1,0:T(8,128)S(1)}, f32[1,4,16,128]{3,2,1,0:T(8,128)S(1)}, f32[1,4,16,128]{3,2,1,0:T(8,128)S(1)}) custom-call(s32[8,32,256]{2,1,0:T(8,128)S(1)} %copy-done.1, f32[8,8,256]{2,1,0:T(8,128)S(1)} %collective-permute-done.9.y_above, f32[8,8,256]{2,1,0:T(8,128)S(1)} %collective-permute-done.10.y_below, ...), custom_call_target="tpu_custom_call" | custom-call | flops 20000000 | bytes 2000000 | tf_op jit(solution)/shard_map/strips2/pallas_call | solution.py:782
  48.0 1.6 %collective-permute-done.13.z_in = f32[2,40,128]{2,1,0:T(8,128)S(1)} collective-permute-done((f32[2,40,128]{2,1,0:T(8,128)S(1)}, f32[2,40,128]{2,1,0:T(8,128)S(1)}, u32[]{:S(2)}, u32[]{:S(2)}) %collective-permute-start.13) | collective-permute-done | bytes 40992 | tf_op jit(solution)/shard_map/ppermute | solution.py:805
  49.6 1.2 %final.1 = f32[2,8,32,256]{3,2,1,0:T(8,128)} custom-call(s32[8,32,256]{2,1,0:T(8,128)S(1)} %copy-done.1, f32[2,40,128]{2,1,0:T(8,128)S(1)} %collective-permute-done.13.z_in, f32[1,4,32,128]{3,2,1,0:T(8,128)S(1)} %get-tuple-element.77.bulk_edges0, f32[1,4,32,128]{3,2,1,0:T(8,128)S(1)} %get-tuple-element.78.bulk_edges1, ...), custom_call_target="tpu_custom_call", output_to_operand_aliasing={{}: (7, {})} | custom-call | bytes 2000000 | tf_op jit(solution)/shard_map/final/pallas_call | solution.py:782
  (16 shorter events, 0.1 us)
Async XLA Ops:
  0.0 4.0 %copy-start = (f32[2,3,8,32,256]{4,3,2,1,0:T(8,128)S(1)}, f32[2,3,8,32,256]{4,3,2,1,0:T(8,128)}, u32[]{:S(2)}) copy-start(f32[2,3,8,32,256]{4,3,2,1,0:T(8,128)} %modes.9) | copy-start | bytes 4718596
  1.4 18.3 %collective-permute-start = (f32[10,32,256]{2,1,0:T(8,128)S(1)}, f32[10,32,256]{2,1,0:T(8,128)S(1)}, u32[]{:S(2)}, u32[]{:S(2)}) collective-permute-start(f32[10,32,256]{2,1,0:T(8,128)S(1)} %get-tuple-element.49), channel_id=1, source_target_pairs={{0,112},{16,0},{32,16},{48,32},{64,48},{80,64},{96,80},{112,96},{1... | collective-permute-start | bytes 983048 | tf_op jit(solution)/shard_map/ppermute | solution.py:805
  3.9 15.7 %collective-permute-start.1 = (f32[4,32,256]{2,1,0:T(8,128)S(1)}, f32[4,32,256]{2,1,0:T(8,128)S(1)}, u32[]{:S(2)}, u32[]{:S(2)}) collective-permute-start(f32[4,32,256]{2,1,0:T(8,128)S(1)} %get-tuple-element.50), channel_id=1, source_target_pairs={{0,16},{16,32},{32,48},{48,64},{64,80},{80,96},{96,112},{112,0},{1... | collective-permute-start | bytes 393224 | tf_op jit(solution)/shard_map/ppermute | solution.py:805
  4.0 14.1 %collective-permute-start.2 = (f32[10,8,256]{2,1,0:T(8,128)S(1)}, f32[10,8,256]{2,1,0:T(8,128)S(1)}, u32[]{:S(2)}, u32[]{:S(2)}) collective-permute-start(f32[10,8,256]{2,1,0:T(8,128)S(1)} %get-tuple-element.51), channel_id=1, source_target_pairs={{0,14},{2,0},{4,2},{6,4},{8,6},{10,8},{12,10},{14,12},{1,15},{3,1}... | collective-permute-start | bytes 245768 | tf_op jit(solution)/shard_map/ppermute | solution.py:805
  10.6 7.5 %collective-permute-start.3 = (f32[4,8,256]{2,1,0:T(8,128)S(1)}, f32[4,8,256]{2,1,0:T(8,128)S(1)}, u32[]{:S(2)}, u32[]{:S(2)}) collective-permute-start(f32[4,8,256]{2,1,0:T(8,128)S(1)} %get-tuple-element.55), channel_id=1, source_target_pairs={{0,2},{2,4},{4,6},{6,8},{8,10},{10,12},{12,14},{14,0},{1,3},{3,5},... | collective-permute-start | bytes 98312 | tf_op jit(solution)/shard_map/ppermute | solution.py:805
  18.1 6.0 %collective-permute-start.4 = (f32[4,8,256]{2,1,0:T(8,128)S(1)}, f32[4,8,256]{2,1,0:T(8,128)S(1)}, u32[]{:S(2)}, u32[]{:S(2)}) collective-permute-start(f32[4,8,256]{2,1,0:T(8,128)S(1)} %get-tuple-element.56), channel_id=1, source_target_pairs={{0,112},{16,0},{32,16},{48,32},{64,48},{80,64},{96,80},{112,96},{1... | collective-permute-start | bytes 98312 | tf_op jit(solution)/shard_map/ppermute | solution.py:805
  19.6 4.5 %collective-permute-start.5 = (f32[3,8,256]{2,1,0:T(8,128)S(1)}, f32[3,8,256]{2,1,0:T(8,128)S(1)}, u32[]{:S(2)}, u32[]{:S(2)}) collective-permute-start(f32[3,8,256]{2,1,0:T(8,128)S(1)} %get-tuple-element.57), channel_id=1, source_target_pairs={{0,16},{16,32},{32,48},{48,64},{64,80},{80,96},{96,112},{112,0},{1... | collective-permute-start | bytes 73736 | tf_op jit(solution)/shard_map/ppermute | solution.py:805
  24.2 4.1 %collective-permute-start.6 = (f32[2,40,128]{2,1,0:T(8,128)S(1)}, f32[2,40,128]{2,1,0:T(8,128)S(1)}, u32[]{:S(2)}, u32[]{:S(2)}) collective-permute-start(f32[2,40,128]{2,1,0:T(8,128)S(1)} %pack_z1.1), channel_id=1, source_target_pairs={{0,1},{1,0},{2,3},{3,2},{4,5},{5,4},{6,7},{7,6},{8,9},{9,8},{10,11... | collective-permute-start | bytes 122888 | tf_op jit(solution)/shard_map/ppermute | solution.py:805
  29.0 17.2 %copy-start.1 = (s32[8,32,256]{2,1,0:T(8,128)S(1)}, s32[8,32,256]{2,1,0:T(8,128)}, u32[]{:S(2)}) copy-start(s32[8,32,256]{2,1,0:T(8,128)} %mask.5) | copy-start | bytes 786436
  29.0 4.1 %collective-permute-start.7 = (f32[4,2,32,256]{3,2,1,0:T(8,128)S(1)}, f32[4,2,32,256]{3,2,1,0:T(8,128)S(1)}, u32[]{:S(2)}, u32[]{:S(2)}) collective-permute-start(f32[4,2,32,256]{3,2,1,0:T(8,128)S(1)} %get-tuple-element.69.low), channel_id=1, source_target_pairs={{0,112},{16,0},{32,16},{48,32},{64,48},{80,64},{96,80},{112,96},{1... | collective-permute-start | bytes 786440 | tf_op jit(solution)/shard_map/ppermute | solution.py:805
  29.0 7.0 %collective-permute-start.8 = (f32[4,2,32,256]{3,2,1,0:T(8,128)S(1)}, f32[4,2,32,256]{3,2,1,0:T(8,128)S(1)}, u32[]{:S(2)}, u32[]{:S(2)}) collective-permute-start(f32[4,2,32,256]{3,2,1,0:T(8,128)S(1)} %raw2.1.high), channel_id=1, source_target_pairs={{0,16},{16,32},{32,48},{48,64},{64,80},{80,96},{96,112},{112,0},{1... | collective-permute-start | bytes 786440 | tf_op jit(solution)/shard_map/ppermute | solution.py:805
  29.6 7.7 %collective-permute-start.9 = (f32[8,8,256]{2,1,0:T(8,128)S(1)}, f32[8,8,256]{2,1,0:T(8,128)S(1)}, u32[]{:S(2)}, u32[]{:S(2)}) collective-permute-start(f32[8,8,256]{2,1,0:T(8,128)S(1)} %get-tuple-element.73), channel_id=1, source_target_pairs={{0,14},{2,0},{4,2},{6,4},{8,6},{10,8},{12,10},{14,12},{1,15},{3,1}... | collective-permute-start | bytes 196616 | tf_op jit(solution)/shard_map/ppermute | solution.py:805
  31.8 7.9 %collective-permute-start.10 = (f32[8,8,256]{2,1,0:T(8,128)S(1)}, f32[8,8,256]{2,1,0:T(8,128)S(1)}, u32[]{:S(2)}, u32[]{:S(2)}) collective-permute-start(f32[8,8,256]{2,1,0:T(8,128)S(1)} %get-tuple-element.74), channel_id=1, source_target_pairs={{0,2},{2,4},{4,6},{6,8},{8,10},{10,12},{12,14},{14,0},{1,3},{3,5},... | collective-permute-start | bytes 196616 | tf_op jit(solution)/shard_map/ppermute | solution.py:805
  39.6 2.8 %collective-permute-start.11 = (f32[6,8,256]{2,1,0:T(8,128)S(1)}, f32[6,8,256]{2,1,0:T(8,128)S(1)}, u32[]{:S(2)}, u32[]{:S(2)}) collective-permute-start(f32[6,8,256]{2,1,0:T(8,128)S(1)} %get-tuple-element.75), channel_id=1, source_target_pairs={{0,112},{16,0},{32,16},{48,32},{64,48},{80,64},{96,80},{112,96},{1... | collective-permute-start | bytes 147464 | tf_op jit(solution)/shard_map/ppermute | solution.py:805
  40.7 4.7 %collective-permute-start.12 = (f32[6,8,256]{2,1,0:T(8,128)S(1)}, f32[6,8,256]{2,1,0:T(8,128)S(1)}, u32[]{:S(2)}, u32[]{:S(2)}) collective-permute-start(f32[6,8,256]{2,1,0:T(8,128)S(1)} %get-tuple-element.76), channel_id=1, source_target_pairs={{0,16},{16,32},{32,48},{48,64},{64,80},{80,96},{96,112},{112,0},{1... | collective-permute-start | bytes 147464 | tf_op jit(solution)/shard_map/ppermute | solution.py:805
  45.5 4.1 %collective-permute-start.13 = (f32[2,40,128]{2,1,0:T(8,128)S(1)}, f32[2,40,128]{2,1,0:T(8,128)S(1)}, u32[]{:S(2)}, u32[]{:S(2)}) collective-permute-start(f32[2,40,128]{2,1,0:T(8,128)S(1)} %pack_z2.1), channel_id=1, source_target_pairs={{0,1},{1,0},{2,3},{3,2},{4,5},{5,4},{6,7},{7,6},{8,9},{9,8},{10,11... | collective-permute-start | bytes 122888 | tf_op jit(solution)/shard_map/ppermute | solution.py:805

commit v8 on v7

--- a/solution.py
+++ b/solution.py
@@ -35,6 +35,29 @@
 
 def sub_lane():
     return iota((8, LANES), 0), iota((8, LANES), 1)
+
+
+def even(axis):
+    return lax.rem(lax.axis_index(axis), 2) == 0
+
+
+class Pick:
+    def __init__(self, cond, yes, no):
+        self.cond, self.yes, self.no = cond, yes, no
+
+    def __getitem__(self, index):
+        return jnp.where(self.cond, self.yes[index], self.no[index])
+
+
+def neighbours(axis, first, second):
+    cond = even(axis)
+    return Pick(cond, first, second), Pick(cond, second, first)
+
+
+def put(axis, first, second, index, down, up):
+    cond = even(axis)
+    first[index] = jnp.where(cond, up, down)
+    second[index] = jnp.where(cond, down, up)
 
 
 def total_of(terms):
@@ -395,30 +418,28 @@
 
 
 def pack_x1(
-    design, mask, modes, eigenvalues, order, src, down, up, lams, field, solid, values, chosen, arrived
+    design, mask, modes, eigenvalues, order, src, first, second, lams, field, solid, rim, values, chosen, arrived
 ):
     copies = []
     for half in (slice(0, W), slice(W, CX)):
         copies.append((design.at[half], field.at[half]))
         copies.append((mask.at[half], solid.at[half]))
     for m in range(MODES):
-        copies.append((modes.at[m, :, 0], down.at[W + 3 * m : W + 3 * m + 3]))
+        copies.append((modes.at[m, :, 0], rim.at[3 * m : 3 * m + 3]))
     copies += [(eigenvalues, values), (order, chosen)]
     copies = [pltpu.make_async_copy(a, b, arrived.at[n]) for n, (a, b) in enumerate(copies)]
     for copy in copies:
         copy.start()
-    for x in range(CX):
-        if x % W == 0:
-            copies[2 * (x // W)].wait()
-            copies[2 * (x // W) + 1].wait()
-        plane = field[x] * solid[x].astype(F32)
-        src[x] = plane
-        if x < W:
-            down[x] = plane
-        else:
-            up[x - W] = plane
+    for copy in copies[:4]:
+        copy.wait()
+    for x in range(W):
+        low, high = (field[p] * solid[p].astype(F32) for p in (x, x + W))
+        src[x], src[x + W] = low, high
+        put("gx", first, second, x, low, high)
     for copy in copies[4:]:
         copy.wait()
+    first[W : W + 6] = rim[...]
+    second[W : W + 6] = rim[...]
     for m in range(MODES):
         lams[m] = jnp.full((8, LANES), values[chosen[m]] * (0.125 * 0.25), F32)
 
@@ -453,15 +474,17 @@
     return above, p - W - CX
 
 
-def pack_y1(src, modes, down, up):
+def pack_y1(src, modes, first, second):
     low = iota((8, CZ), 0) < 4
     for q in range(W):
-        down[q] = jnp.where(low, src[q, 0:8, :], pltpu.roll(src[q + W, 0:8, :], 4, 0))
-        up[q] = jnp.where(low, pltpu.roll(src[q + W, 24:32, :], 4, 0), src[q, 24:32, :])
+        down = jnp.where(low, src[q, 0:8, :], pltpu.roll(src[q + W, 0:8, :], 4, 0))
+        up = jnp.where(low, pltpu.roll(src[q + W, 24:32, :], 4, 0), src[q, 24:32, :])
+        put("gy", first, second, q, down, up)
     for m in range(MODES):
         for c in range(3):
             for x in range(CX):
-                down[W + 3 * m + c, x : x + 1, :] = modes[m, c, x, 0:1, :]
+                for out in (first, second):
+                    out[W + 3 * m + c, x : x + 1, :] = modes[m, c, x, 0:1, :]
 
 
 def own_halo(y_above, y_below, x, lanes=slice(None)):
@@ -471,13 +494,15 @@
     return jnp.where(iota(a.shape, 0) < 4, a, b)
 
 
-def pack_e1(y_above, y_below, ahead, down, up):
+def pack_e1(y_first, y_second, ahead, first, second):
+    y_above, y_below = neighbours("gy", y_first, y_second)
     for i in range(W - 1):
-        down[i] = own_halo(y_above, y_below, i)
-        up[i] = own_halo(y_above, y_below, CX - 1 - i)
-    down[W - 1] = jnp.zeros((8, CZ), F32)
-    for n in range(3 * MODES):
-        down[W - 1, n : n + 1, :] = y_above[W + n, 0:1, :]
+        down, up = (own_halo(y_above, y_below, x) for x in (i, CX - 1 - i))
+        put("gx", first, second, i, down, up)
+    for out in (first, second):
+        out[W - 1] = jnp.zeros((8, CZ), F32)
+        for n in range(3 * MODES):
+            out[W - 1, n : n + 1, :] = y_above[W + n, 0:1, :]
 
 
 def halo_tile(y_above, y_below, from_above, from_below, p, lanes=slice(None)):
@@ -491,9 +516,11 @@
 
 
 def bulk_kernel1(
-    src, modes, columns, above, below, y_above,
+    src, modes, columns, x_first, x_second, y_first, y_second,
     bulk, ends, edges, stiff, mass, own, rims, row32, table, sb, one, two,
 ):
+    above, below = neighbours("gx", x_first, x_second)
+    y_above, y_below = neighbours("gy", y_first, y_second)
     at = pos()
     gx, gy, gz = at
     fill_bulk(table, gy, gz)
@@ -523,10 +550,11 @@
     return a[i, :, edge]
 
 
-def pack_z1(own, rims, row32, y_above, y_below, from_above, from_below, out):
+def pack_z1(own, rims, row32, y_first, y_second, e_first, e_second, out):
     gx, gy, gz = pos()
     edge = edge_tiles(gz)
-    halos = (y_above, y_below, from_above, from_below)
+    halos = (*neighbours("gy", y_first, y_second), *neighbours("gx", e_first, e_second))
+    from_above = halos[2]
     out[0, 0:CY, :] = own[0]
     out[0, CY:PY, :] = own_strip(gz, lambda p: halo_tile(*halos, p, edge), 8)
     keep_x = jnp.where(gx < 7, 1.0, 0.0)
@@ -535,13 +563,15 @@
 
 
 def strip_kernel1(
-    modes, rims, row32, above, y_above, y_below, from_above, from_below, ends,
+    modes, rims, row32, x_first, x_second, y_first, y_second, e_first, e_second, ends,
     strips, edges, rim, packed, table, sb, one, two, near, far,
 ):
     at = pos()
     gx, gy, gz = at
     fill_strips(table, gy, gz)
-    halos = (y_above, y_below, from_above, from_below)
+    halos = (*neighbours("gy", y_first, y_second), *neighbours("gx", e_first, e_second))
+    y_above, y_below, from_above, from_below = halos
+    above, below = neighbours("gx", x_first, x_second)
     strip_sweeps(
         1, at, table, lambda m, p: halo_tile(*halos, p), ends, (sb, one, two), edges, strips
     )
@@ -572,7 +602,7 @@
 
 def raw_planes(
     planes, lams, gz, z_state, column_stiff, column_mass, bulk, strips,
-    stiff, mass, stiff7, mass7, rim, out,
+    stiff, mass, stiff7, mass7, rim, store,
 ):
     sub, lane = sub_lane()
     beside = beside_halo(gz, lane)
@@ -597,7 +627,7 @@
                         by = LANES - 1 - (32 * m + x)
                         k = jnp.where(lane == LANES - 1, pltpu.roll(column_stiff[rows, :], by, 1), k)
                         e = jnp.where(lane == LANES - 1, pltpu.roll(column_mass[rows, :], by, 1), e)
-                    out[x % W, m, rows, cols] = phys * k - lams[m] * e
+                    store((x % W, m, rows, cols), phys * k - lams[m] * e)
 
 
 def raw_kernel1(
@@ -622,17 +652,22 @@
     z_parts[0], z_parts[1], z_parts[2] = z_state[0:CY], column_stiff, column_mass
     raw_planes(
         range(W), lams, gz, z_state, column_stiff, column_mass, bulk, strips,
-        stiff, mass, stiff7, mass7, rim, low,
+        stiff, mass, stiff7, mass7, rim, low.__setitem__,
     )
 
 
 def raw_kernel2(
-    lams, z_parts, bulk, strips, stiff, mass, stiff7, mass7, rim, high
+    lams, z_parts, bulk, strips, stiff, mass, stiff7, mass7, rim, low, high, first, second
 ):
     gx, gy, gz = pos()
+
+    def store(index, value):
+        high[index] = value
+        put("gx", first, second, index, low[index], value)
+
     raw_planes(
         range(W, CX), lams, gz, z_parts[0], z_parts.at[1], z_parts.at[2], bulk, strips,
-        stiff, mass, stiff7, mass7, rim, high,
+        stiff, mass, stiff7, mass7, rim, store,
     )
 
 
@@ -646,12 +681,13 @@
     return above, p - 3 * W
 
 
-def pack_y2(low, high, down, up):
-    first = iota((8, CZ), 0) < 4
+def pack_y2(low, high, first, second):
+    top = iota((8, CZ), 0) < 4
     for x in range(CX):
         a, i = (low, x) if x < W else (high, x - W)
-        down[x] = jnp.where(first, a[i, 0, 0:8, :], pltpu.roll(a[i, 1, 0:8, :], 4, 0))
-        up[x] = jnp.where(first, pltpu.roll(a[i, 0, 24:32, :], 4, 0), a[i, 1, 24:32, :])
+        down = jnp.where(top, a[i, 0, 0:8, :], pltpu.roll(a[i, 1, 0:8, :], 4, 0))
+        up = jnp.where(top, pltpu.roll(a[i, 0, 24:32, :], 4, 0), a[i, 1, 24:32, :])
+        put("gy", first, second, x, down, up)
 
 
 def own_raw_halo(y_above, y_below, m, x, lanes=slice(None)):
@@ -663,11 +699,12 @@
     return jnp.where(iota(a.shape, 0) < 4, a, b)
 
 
-def pack_e2(y_above, y_below, ahead, down, up):
+def pack_e2(y_first, y_second, ahead, first, second):
+    y_above, y_below = neighbours("gy", y_first, y_second)
     for i in range(W - 1):
         for m in range(MODES):
-            down[MODES * i + m] = own_raw_halo(y_above, y_below, m, i)
-            up[MODES * i + m] = own_raw_halo(y_above, y_below, m, CX - 1 - i)
+            down, up = (own_raw_halo(y_above, y_below, m, x) for x in (i, CX - 1 - i))
+            put("gx", first, second, MODES * i + m, down, up)
 
 
 def raw_halo(y_above, y_below, from_above, from_below, m, p, lanes=slice(None)):
@@ -680,7 +717,8 @@
     return jnp.zeros(y_above[0, :, lanes].shape, F32)
 
 
-def bulk_kernel2(m, low, high, above, below, bulk, ends, edges, own, table, sb, one, two):
+def bulk_kernel2(m, low, high, x_first, x_second, bulk, ends, edges, own, table, sb, one, two):
+    above, below = neighbours("gx", x_first, x_second)
     at = pos()
     fill_bulk(table, at[1], at[2])
 
@@ -698,20 +736,21 @@
     own[0] = own_strip(at[2], load)
 
 
-def pack_z2(own0, own1, y_above, y_below, from_above, from_below, out):
+def pack_z2(own0, own1, y_first, y_second, e_first, e_second, out):
     gx, gy, gz = pos()
     edge = edge_tiles(gz)
-    halos = (y_above, y_below, from_above, from_below)
+    halos = (*neighbours("gy", y_first, y_second), *neighbours("gx", e_first, e_second))
     for m, own in enumerate((own0, own1)):
         out[m, 0:CY, :] = own[0]
         out[m, CY:PY, :] = own_strip(gz, lambda p, m=m: raw_halo(*halos, m, p, edge), 8)
 
 
 def strip_kernel2(
-    mask, y_above, y_below, from_above, from_below, ends0, ends1, bulk0, bulk1,
+    mask, y_first, y_second, e_first, e_second, ends0, ends1, bulk0, bulk1,
     out, side, edges0, edges1, table, strips0, strips1, a0, a1, b0, b1, c0, c1, held, left,
 ):
     gx, gy, gz = at = pos()
+    halos = (*neighbours("gy", y_first, y_second), *neighbours("gx", e_first, e_second))
     sub, lane = sub_lane()
     fill_strips(table, gy, gz)
     states = ((a0, b0, c0), (a1, b1, c1))
@@ -721,7 +760,7 @@
         strips = (strips0, strips1)[m]
 
         def source(_, p, m=m):
-            return raw_halo(y_above, y_below, from_above, from_below, m, p)
+            return raw_halo(*halos, m, p)
 
         strip_sweeps(1, at, table, source, ends, states[m], edges, strips)
         for x in range(CX):
@@ -796,13 +835,15 @@
 HBM = pl.BlockSpec(memory_space=pltpu.HBM)
 
 
-def ring(axis, step):
+def swap(x, axis, start):
     size = lax.axis_size(axis)
-    return [(i, (i + step) % size) for i in range(size)]
-
-
-def shift(x, axis, step):
-    return lax.ppermute(x, axis, ring(axis, step))
+    other = {i: i + 1 if i % 2 == start else i - 1 for i in range(size)}
+    return lax.ppermute(x, axis, [(i, j if 0 <= j < size else i) for i, j in other.items()])
+
+
+def swaps(axis, pair):
+    second = swap(pair[1], axis, 1)
+    return swap(pair[0], axis, 0), second
 
 
 def sweep_outs(fields):
@@ -818,36 +859,35 @@
     bulk_outs, bulk_scratch, strip_outs, strip_scratch = sweep_outs(1)
 
     inputs = (design, solid_mask, mode_fields, eigenvalues, mode_order)
-    src, down, up, lams = call(
-        pack_x1, "pack_x1", [(CX, CY, CZ), (W + 6, CY, CZ), (W, CY, CZ), (MODES, 8, LANES)],
+    src, first, second, lams = call(
+        pack_x1, "pack_x1", [(CX, CY, CZ), (W + 6, CY, CZ), (W + 6, CY, CZ), (MODES, 8, LANES)],
         tuple(pltpu.with_memory_space_constraint(x, pltpu.HBM) for x in inputs),
         {i: HBM for i in range(5)},
         scratch=[
-            (CX, CY, CZ), pltpu.VMEM((CX, CY, CZ), jnp.int32), pltpu.SMEM((eigenvalues.size,), F32),
+            (CX, CY, CZ), pltpu.VMEM((CX, CY, CZ), jnp.int32), (6, CY, CZ), pltpu.SMEM((eigenvalues.size,), F32),
             pltpu.SMEM((mode_order.size,), jnp.int32), pltpu.SemaphoreType.DMA((8,)),
         ],
     )
-    above, below = shift(down, "gx", -1), shift(up, "gx", 1)
+    x_pair = swaps("gx", (first, second))
     field = (MODES, CX - 1, CY, CZ)
-    down, up = call(pack_y1, "pack_y1", [(W + 6, 8, CZ), (W, 8, CZ)], (src, mode_fields))
-    y_above, y_below = shift(down, "gy", -1), shift(up, "gy", 1)
+    y_pair = swaps("gy", call(pack_y1, "pack_y1", [(W + 6, 8, CZ)] * 2, (src, mode_fields)))
     stiff, mass, columns = call(
         energy_kernel, "energy", [field, field, (2, CY, LANES)], (mode_fields,), flops=40_000_000
     )
 
-    down, up = call(pack_e1, "pack_e1", [(W, 8, CZ), (W - 1, 8, CZ)], (y_above, y_below, columns))
-    halos = (y_above, y_below, shift(down, "gx", -1), shift(up, "gx", 1))
+    edge_pair = swaps("gx", call(pack_e1, "pack_e1", [(W, 8, CZ)] * 2, (*y_pair, columns)))
+    halos = (*y_pair, *edge_pair)
     plane = (MODES, CY, CZ)
     bulk, ends, bulk_edges, stiff7, mass7, own, rims, row32 = call(
         bulk_kernel1, "bulk1",
         bulk_outs + [plane, plane, (1, CY, LANES), (2, CY, LANES), (2, 8, LANES)],
-        (src, mode_fields, columns, above, below, y_above), scratch=bulk_scratch, flops=30_000_000,
-    )
-
-    z_in = shift(call(pack_z1, "pack_z1", [(2, PY, LANES)], (own, rims, row32, *halos)), "gz", 1)
+        (src, mode_fields, columns, *x_pair, *y_pair), scratch=bulk_scratch, flops=30_000_000,
+    )
+
+    z_in = swap(call(pack_z1, "pack_z1", [(2, PY, LANES)], (own, rims, row32, *halos)), "gz", 0)
     strips, strip_edges, rim, packed = call(
         strip_kernel1, "strips1", strip_outs + [(MODES, 2, 8, CZ), (PY, LANES)],
-        (mode_fields, rims, row32, above, *halos, ends),
+        (mode_fields, rims, row32, *x_pair, *halos, ends),
         scratch=strip_scratch + [(3, 16, CZ)] * 2, flops=20_000_000,
     )
     half = (W, MODES, CY, CZ)
@@ -856,13 +896,11 @@
         raw_kernel1, "raw1", [half, (3, CY, LANES)],
         (lams, z_in, packed, bulk, bulk_edges, strips, strip_edges, *energies),
     )
-    above = shift(low, "gx", -1)
-    high = call(raw_kernel2, "raw2", [half], (lams, z_parts, bulk, strips, *energies), flops=60_000_000)
-    below = shift(high, "gx", 1)
-
-    planes = (low, high, above, below)
-    down, up = call(pack_y2, "pack_y2", [(CX, 8, CZ)] * 2, (low, high))
-    y_above, y_below = shift(down, "gy", -1), shift(up, "gy", 1)
+    high, first, second = call(
+        raw_kernel2, "raw2", [half] * 3, (lams, z_parts, bulk, strips, *energies, low), flops=5_000_000
+    )
+    planes = (low, high, *swaps("gx", (first, second)))
+    y_pair = swaps("gy", call(pack_y2, "pack_y2", [(CX, 8, CZ)] * 2, (low, high)))
     bulks = [
         call(
             functools.partial(bulk_kernel2, m), f"bulk2_{m}", bulk_outs + [(1, CY, LANES)], planes,
@@ -872,9 +910,8 @@
     ]
     bulk, ends, bulk_edges, own = zip(*bulks)
     edge = (MODES * (W - 1), 8, CZ)
-    down, up = call(pack_e2, "pack_e2", [edge] * 2, (y_above, y_below, own[0]))
-    halos = (y_above, y_below, shift(down, "gx", -1), shift(up, "gx", 1))
-    z_in = shift(call(pack_z2, "pack_z2", [(MODES, PY, LANES)], (*own, *halos)), "gz", 1)
+    halos = (*y_pair, *swaps("gx", call(pack_e2, "pack_e2", [edge] * 2, (*y_pair, own[0]))))
+    z_in = swap(call(pack_z2, "pack_z2", [(MODES, PY, LANES)], (*own, *halos)), "gz", 0)
     result = (MODES, CX, CY, CZ)
     strips, edges = strip_outs
     table, state = strip_scratch[0], strip_scratch[1]

time: 50.9 us -> 51.2 us (level)
  the two profiles are of different devices: /device:TPU:0 before, /device:TPU:48 now
where the time goes in v8:
time: 51.2 us; the launch traced here: 50.9 us
  starting transfers between devices  23.7 us (46%)
  Pallas kernels  13.6 us (27%)
  waiting for transfers between devices  13.3 us (26%)
    ppermute x14, starting transfers between devices, swap(): lax.ppermute(x, axis, [(i, j if 0 <= j < size else i) for i, j in other.i...  23.7 us
    pallas_call x16, Pallas kernels, call(): pl.pallas_call(kernel, grid=(1,), out_shape=shapes if len(shapes) > 1 els...  13.6 us
    ppermute x14, waiting for transfers between devices, swap(): lax.ppermute(x, axis, [(i, j if 0 <= j < size else i) for i, j in other.i...  13.3 us
  transfers between devices with their start and end apart: 14, of which 7 were waited for; matrix products, arithmetic and copies ran while one was open for 0% of the time, Pallas kernels for 20%

profile of v8, /device:TPU:48, one launch (start us, length us, event | category | flops | bytes accessed | tf_op | source)
XLA Modules:
  0.0 50.9 jit_solution(8553136720453927129)
XLA Ops:
  0.0 1.4 %pack_x1.1 = (f32[8,32,256]{2,1,0:T(8,128)S(1)}, f32[10,32,256]{2,1,0:T(8,128)S(1)}, f32[10,32,256]{2,1,0:T(8,128)S(1)}, f32[2,8,128]{2,1,0:T(8,128)S(1)}) custom-call(f32[8,32,256]{2,1,0:T(8,128)} %design.1, s32[8,32,256]{2,1,0:T(8,128)} %mask.5, f32[2,3,8,32,256]{4,3,2,1,0:T(8,128)} %modes.9, f32[6]{0:T(128)} %eigenvalues.1, s32[6]{0:T(128)} %order.1), custom_call_target="tpu_custom_call" | custom-call | bytes 2000000 | tf_op jit(solution)/shard_map/pack_x1/pallas_call | solution.py:821
  1.4 0.1 collective-permute-start
  1.5 2.4 %collective-permute-start.1 = (f32[10,32,256]{2,1,0:T(8,128)S(1)}, f32[10,32,256]{2,1,0:T(8,128)S(1)}, u32[]{:S(2)}, u32[]{:S(2)}) collective-permute-start(f32[10,32,256]{2,1,0:T(8,128)S(1)} %get-tuple-element.53), channel_id=1, source_target_pairs={{0,0},{16,32},{32,16},{48,64},{64,48},{80,96},{96,80},{112,112},{1... | collective-permute-start | bytes 983048 | tf_op jit(solution)/shard_map/ppermute | solution.py:841
  4.0 3.1 %collective-permute-start.2 = (f32[10,8,256]{2,1,0:T(8,128)S(1)}, f32[10,8,256]{2,1,0:T(8,128)S(1)}, u32[]{:S(2)}, u32[]{:S(2)}) collective-permute-start(f32[10,8,256]{2,1,0:T(8,128)S(1)} %get-tuple-element.54), channel_id=1, source_target_pairs={{0,2},{2,0},{4,6},{6,4},{8,10},{10,8},{12,14},{14,12},{1,3},{3,1},... | collective-permute-start | bytes 245768 | tf_op jit(solution)/shard_map/ppermute | solution.py:841
  7.1 1.9 %collective-permute-start.3 = (f32[10,8,256]{2,1,0:T(8,128)S(1)}, f32[10,8,256]{2,1,0:T(8,128)S(1)}, u32[]{:S(2)}, u32[]{:S(2)}) collective-permute-start(f32[10,8,256]{2,1,0:T(8,128)S(1)} %get-tuple-element.55), channel_id=1, source_target_pairs={{0,0},{2,4},{4,2},{6,8},{8,6},{10,12},{12,10},{14,14},{1,1},{3,5},... | collective-permute-start | bytes 245768 | tf_op jit(solution)/shard_map/ppermute | solution.py:841
  9.1 3.1 %energy.1 = (f32[2,7,32,256]{3,2,1,0:T(8,128)S(1)}, f32[2,7,32,256]{3,2,1,0:T(8,128)S(1)}, f32[2,32,128]{2,1,0:T(8,128)S(1)}) custom-call(f32[2,3,8,32,256]{4,3,2,1,0:T(8,128)S(1)} %copy-done), custom_call_target="tpu_custom_call" | custom-call | flops 40000000 | bytes 2000000 | tf_op jit(solution)/shard_map/energy/pallas_call | solution.py:821
  12.2 4.1 %collective-permute-done.3.y_second = f32[10,8,256]{2,1,0:T(8,128)S(1)} collective-permute-done((f32[10,8,256]{2,1,0:T(8,128)S(1)}, f32[10,8,256]{2,1,0:T(8,128)S(1)}, u32[]{:S(2)}, u32[]{:S(2)}) %collective-permute-start.3) | collective-permute-done | bytes 81952 | tf_op jit(solution)/shard_map/ppermute | solution.py:841
  16.4 0.1 collective-permute-start.4
  16.5 2.7 %collective-permute-start.5 = (f32[4,8,256]{2,1,0:T(8,128)S(1)}, f32[4,8,256]{2,1,0:T(8,128)S(1)}, u32[]{:S(2)}, u32[]{:S(2)}) collective-permute-start(f32[4,8,256]{2,1,0:T(8,128)S(1)} %get-tuple-element.60), channel_id=1, source_target_pairs={{0,0},{16,32},{32,16},{48,64},{64,48},{80,96},{96,80},{112,112},{1... | collective-permute-start | bytes 98312 | tf_op jit(solution)/shard_map/ppermute | solution.py:841
  19.2 1.8 %bulk1.1 = (f32[1,8,32,256]{3,2,1,0:T(8,128)S(1)}, f32[1,4,16,2,1,256]{5,4,3,2,1,0:T(1,128)S(1)}, f32[1,4,32,128]{3,2,1,0:T(8,128)S(1)}, f32[2,32,256]{2,1,0:T(8...) custom-call(f32[8,32,256]{2,1,0:T(8,128)S(1)} %get-tuple-element.50., ...), custom_call_target="tpu_custom_call" | custom-call | flops 30000000 | bytes 2000000 | tf_op jit(solution)/shard_map/bulk1/pallas_call | solution.py:821
  21.1 0.6 %collective-permute-done.5.e_second = f32[4,8,256]{2,1,0:T(8,128)S(1)} collective-permute-done((f32[4,8,256]{2,1,0:T(8,128)S(1)}, f32[4,8,256]{2,1,0:T(8,128)S(1)}, u32[]{:S(2)}, u32[]{:S(2)}) %collective-permute-start.5) | collective-permute-done | bytes 32800 | tf_op jit(solution)/shard_map/ppermute | solution.py:841
  21.7 0.1 pack_z1.1
  21.8 0.7 %collective-permute-start.6 = (f32[2,40,128]{2,1,0:T(8,128)S(1)}, f32[2,40,128]{2,1,0:T(8,128)S(1)}, u32[]{:S(2)}, u32[]{:S(2)}) collective-permute-start(f32[2,40,128]{2,1,0:T(8,128)S(1)} %pack_z1.1), channel_id=1, source_target_pairs={{0,1},{1,0},{2,3},{3,2},{4,5},{5,4},{6,7},{7,6},{8,9},{9,8},{10,11... | collective-permute-start | bytes 122888 | tf_op jit(solution)/shard_map/ppermute | solution.py:841
  22.5 0.8 %strips1.1 = (f32[1,8,16,256]{3,2,1,0:T(8,128)S(1)}, f32[1,4,16,128]{3,2,1,0:T(8,128)S(1)}, f32[2,2,8,256]{3,2,1,0:T(8,128)S(1)}, f32[40,128]{1,0:T(8,128)S(1)}) custom-call(f32[2,3,8,32,256]{4,3,2,1,0:T(8,128)S(1)} %copy-done, f32[2,32,128]{2,1,0:T(8,128)S(1)} %get-tuple-element.57.rims, f32[2,8,128]{2,1,0:T(8,128)S(1)} %get-tuple-element.58.row32, ...), custom_call_target="tpu_custom_call" | custom-call | flops 20000000 | bytes 2000000 | tf_op jit(solution)/shard_map/strips1/pallas_call | solution.py:821
  23.3 2.6 %collective-permute-done.6.z_in = f32[2,40,128]{2,1,0:T(8,128)S(1)} collective-permute-done((f32[2,40,128]{2,1,0:T(8,128)S(1)}, f32[2,40,128]{2,1,0:T(8,128)S(1)}, u32[]{:S(2)}, u32[]{:S(2)}) %collective-permute-start.6) | collective-permute-done | bytes 40992 | tf_op jit(solution)/shard_map/ppermute | solution.py:841
  25.9 0.5 %raw1.1 = (f32[4,2,32,256]{3,2,1,0:T(8,128)S(1)}, f32[3,32,128]{2,1,0:T(8,128)S(1)}) custom-call(f32[2,8,128]{2,1,0:T(8,128)S(1)} %get-tuple-element.49.lams, f32[2,40,128]{2,1,0:T(8,128)S(1)} %collective-permute-done.6.z_in, f32[40,128]{1,0:T(8,128)S(1)} %get-tuple-element.62.packed, f32[1,8,32,256]{3,2,1,0:T(8,128)S(1)} %get-tuple-element.63.bulk, ...), custom_call_target="tpu_custom_call" | custom-call | bytes 2000000 | tf_op jit(solution)/shard_map/raw1/pallas_call | solution.py:821
  26.4 0.2 raw2.1
  26.6 0.1 collective-permute-start.7
  26.7 2.7 %collective-permute-start.8 = (f32[4,2,32,256]{3,2,1,0:T(8,128)S(1)}, f32[4,2,32,256]{3,2,1,0:T(8,128)S(1)}, u32[]{:S(2)}, u32[]{:S(2)}) collective-permute-start(f32[4,2,32,256]{3,2,1,0:T(8,128)S(1)} %get-tuple-element.76), channel_id=1, source_target_pairs={{0,0},{16,32},{32,16},{48,64},{64,48},{80,96},{96,80},{112,112},{1... | collective-permute-start | bytes 786440 | tf_op jit(solution)/shard_map/ppermute | solution.py:841
  29.5 2.5 %collective-permute-start.10 = (f32[8,8,256]{2,1,0:T(8,128)S(1)}, f32[8,8,256]{2,1,0:T(8,128)S(1)}, u32[]{:S(2)}, u32[]{:S(2)}) collective-permute-start(f32[8,8,256]{2,1,0:T(8,128)S(1)} %get-tuple-element.80), channel_id=1, source_target_pairs={{0,0},{2,4},{4,2},{6,8},{8,6},{10,12},{12,10},{14,14},{1,1},{3,5},... | collective-permute-start | bytes 196616 | tf_op jit(solution)/shard_map/ppermute | solution.py:841
  32.0 4.4 %collective-permute-start.9 = (f32[8,8,256]{2,1,0:T(8,128)S(1)}, f32[8,8,256]{2,1,0:T(8,128)S(1)}, u32[]{:S(2)}, u32[]{:S(2)}) collective-permute-start(f32[8,8,256]{2,1,0:T(8,128)S(1)} %get-tuple-element.79), channel_id=1, source_target_pairs={{0,2},{2,0},{4,6},{6,4},{8,10},{10,8},{12,14},{14,12},{1,3},{3,1},... | collective-permute-start | bytes 196616 | tf_op jit(solution)/shard_map/ppermute | solution.py:841
  36.4 1.2 %bulk2_0.1 = (f32[1,8,32,256]{3,2,1,0:T(8,128)S(1)}, f32[1,4,16,2,1,256]{5,4,3,2,1,0:T(1,128)S(1)}, f32[1,4,32,128]{3,2,1,0:T(8,128)S(1)}, f32[1,32,128]{2,1,0:T(8,128)S(1)}) custom-call(f32[4,2,32,256]{3,2,1,0:T(8,128)S(1)} %get-tuple-element.72.low, f32[4,2,32,256]{3,2,1,0:T(8,128)S(1)} %get-tuple-element.74.high, ...), custom_call_target="tpu_custom_call" | custom-call | flops 20000000 | bytes 2000000 | tf_op jit(solution)/shard_map/bulk2_0/pallas_call | solution.py:821
  37.6 1.1 %collective-permute-done.10.y_second = f32[8,8,256]{2,1,0:T(8,128)S(1)} collective-permute-done((f32[8,8,256]{2,1,0:T(8,128)S(1)}, f32[8,8,256]{2,1,0:T(8,128)S(1)}, u32[]{:S(2)}, u32[]{:S(2)}) %collective-permute-start.10) | collective-permute-done | bytes 65568 | tf_op jit(solution)/shard_map/ppermute | solution.py:841
  38.7 1.3 %collective-permute-done.9.y_first = f32[8,8,256]{2,1,0:T(8,128)S(1)} collective-permute-done((f32[8,8,256]{2,1,0:T(8,128)S(1)}, f32[8,8,256]{2,1,0:T(8,128)S(1)}, u32[]{:S(2)}, u32[]{:S(2)}) %collective-permute-start.9) | collective-permute-done | bytes 65568 | tf_op jit(solution)/shard_map/ppermute | solution.py:841
  40.1 2.2 %collective-permute-start.12 = (f32[6,8,256]{2,1,0:T(8,128)S(1)}, f32[6,8,256]{2,1,0:T(8,128)S(1)}, u32[]{:S(2)}, u32[]{:S(2)}) collective-permute-start(f32[6,8,256]{2,1,0:T(8,128)S(1)} %get-tuple-element.82), channel_id=1, source_target_pairs={{0,0},{16,32},{32,16},{48,64},{64,48},{80,96},{96,80},{112,112},{1... | collective-permute-start | bytes 147464 | tf_op jit(solution)/shard_map/ppermute | solution.py:841
  42.3 1.2 %bulk2_1.1 = (f32[1,8,32,256]{3,2,1,0:T(8,128)S(1)}, f32[1,4,16,2,1,256]{5,4,3,2,1,0:T(1,128)S(1)}, f32[1,4,32,128]{3,2,1,0:T(8,128)S(1)}, f32[1,32,128]{2,1,0:T(8,128)S(1)}) custom-call(f32[4,2,32,256]{3,2,1,0:T(8,128)S(1)} %get-tuple-element.72.low, f32[4,2,32,256]{3,2,1,0:T(8,128)S(1)} %get-tuple-element.74.high, ...), custom_call_target="tpu_custom_call" | custom-call | flops 20000000 | bytes 2000000 | tf_op jit(solution)/shard_map/bulk2_1/pallas_call | solution.py:821
  43.6 2.0 %collective-permute-done.12.e_second = f32[6,8,256]{2,1,0:T(8,128)S(1)} collective-permute-done((f32[6,8,256]{2,1,0:T(8,128)S(1)}, f32[6,8,256]{2,1,0:T(8,128)S(1)}, u32[]{:S(2)}, u32[]{:S(2)}) %collective-permute-start.12) | collective-permute-done | bytes 49184 | tf_op jit(solution)/shard_map/ppermute | solution.py:841
  45.5 0.1 pack_z2.1
  45.6 0.7 %collective-permute-start.13 = (f32[2,40,128]{2,1,0:T(8,128)S(1)}, f32[2,40,128]{2,1,0:T(8,128)S(1)}, u32[]{:S(2)}, u32[]{:S(2)}) collective-permute-start(f32[2,40,128]{2,1,0:T(8,128)S(1)} %pack_z2.1), channel_id=1, source_target_pairs={{0,1},{1,0},{2,3},{3,2},{4,5},{5,4},{6,7},{7,6},{8,9},{9,8},{10,11... | collective-permute-start | bytes 122888 | tf_op jit(solution)/shard_map/ppermute | solution.py:841
  46.3 1.8 %strips2.1 = (f32[2,8,32,256]{3,2,1,0:T(8,128)}, f32[2,8,32,128]{3,2,1,0:T(8,128)S(1)}, f32[1,4,16,128]{3,2,1,0:T(8,128)S(1)}, f32[1,4,16,128]{3,2,1,0:T(8,128)S(1)}) custom-call(s32[8,32,256]{2,1,0:T(8,128)S(1)} %copy-done.1, f32[8,8,256]{2,1,0:T(8,128)S(1)} %collective-permute-done.9.y_first, f32[8,8,256]{2,1,0:T(8,128)S(1)} %collective-permute-done.10.y_second, ...), custom_call_target="tpu_custom_call" | custom-call | flops 20000000 | bytes 2000000 | tf_op jit(solution)/shard_map/strips2/pallas_call | solution.py:821
  48.1 1.6 %collective-permute-done.13.z_in = f32[2,40,128]{2,1,0:T(8,128)S(1)} collective-permute-done((f32[2,40,128]{2,1,0:T(8,128)S(1)}, f32[2,40,128]{2,1,0:T(8,128)S(1)}, u32[]{:S(2)}, u32[]{:S(2)}) %collective-permute-start.13) | collective-permute-done | bytes 40992 | tf_op jit(solution)/shard_map/ppermute | solution.py:841
  49.7 1.2 %final.1 = f32[2,8,32,256]{3,2,1,0:T(8,128)} custom-call(s32[8,32,256]{2,1,0:T(8,128)S(1)} %copy-done.1, f32[2,40,128]{2,1,0:T(8,128)S(1)} %collective-permute-done.13.z_in, f32[1,4,32,128]{3,2,1,0:T(8,128)S(1)} %get-tuple-element.83.bulk_edges0, f32[1,4,32,128]{3,2,1,0:T(8,128)S(1)} %get-tuple-element.84.bulk_edges1, ...), custom_call_target="tpu_custom_call", output_to_operand_aliasing={{}: (7, {})} | custom-call | bytes 2000000 | tf_op jit(solution)/shard_map/final/pallas_call | solution.py:821
  (16 shorter events, 0.2 us)
Async XLA Ops:
  0.0 4.0 %copy-start = (f32[2,3,8,32,256]{4,3,2,1,0:T(8,128)S(1)}, f32[2,3,8,32,256]{4,3,2,1,0:T(8,128)}, u32[]{:S(2)}) copy-start(f32[2,3,8,32,256]{4,3,2,1,0:T(8,128)} %modes.9) | copy-start | bytes 4718596
  1.4 17.8 %collective-permute-start = (f32[10,32,256]{2,1,0:T(8,128)S(1)}, f32[10,32,256]{2,1,0:T(8,128)S(1)}, u32[]{:S(2)}, u32[]{:S(2)}) collective-permute-start(f32[10,32,256]{2,1,0:T(8,128)S(1)} %get-tuple-element.52), channel_id=1, source_target_pairs={{0,16},{16,0},{32,48},{48,32},{64,80},{80,64},{96,112},{112,96},{1... | collective-permute-start | bytes 983048 | tf_op jit(solution)/shard_map/ppermute | solution.py:841
  1.5 17.7 %collective-permute-start.1 = (f32[10,32,256]{2,1,0:T(8,128)S(1)}, f32[10,32,256]{2,1,0:T(8,128)S(1)}, u32[]{:S(2)}, u32[]{:S(2)}) collective-permute-start(f32[10,32,256]{2,1,0:T(8,128)S(1)} %get-tuple-element.53), channel_id=1, source_target_pairs={{0,0},{16,32},{32,16},{48,64},{64,48},{80,96},{96,80},{112,112},{1... | collective-permute-start | bytes 983048 | tf_op jit(solution)/shard_map/ppermute | solution.py:841
  4.0 8.2 %collective-permute-start.2 = (f32[10,8,256]{2,1,0:T(8,128)S(1)}, f32[10,8,256]{2,1,0:T(8,128)S(1)}, u32[]{:S(2)}, u32[]{:S(2)}) collective-permute-start(f32[10,8,256]{2,1,0:T(8,128)S(1)} %get-tuple-element.54), channel_id=1, source_target_pairs={{0,2},{2,0},{4,6},{6,4},{8,10},{10,8},{12,14},{14,12},{1,3},{3,1},... | collective-permute-start | bytes 245768 | tf_op jit(solution)/shard_map/ppermute | solution.py:841
  7.1 9.2 %collective-permute-start.3 = (f32[10,8,256]{2,1,0:T(8,128)S(1)}, f32[10,8,256]{2,1,0:T(8,128)S(1)}, u32[]{:S(2)}, u32[]{:S(2)}) collective-permute-start(f32[10,8,256]{2,1,0:T(8,128)S(1)} %get-tuple-element.55), channel_id=1, source_target_pairs={{0,0},{2,4},{4,2},{6,8},{8,6},{10,12},{12,10},{14,14},{1,1},{3,5},... | collective-permute-start | bytes 245768 | tf_op jit(solution)/shard_map/ppermute | solution.py:841
  16.4 4.7 %collective-permute-start.4 = (f32[4,8,256]{2,1,0:T(8,128)S(1)}, f32[4,8,256]{2,1,0:T(8,128)S(1)}, u32[]{:S(2)}, u32[]{:S(2)}) collective-permute-start(f32[4,8,256]{2,1,0:T(8,128)S(1)} %get-tuple-element.59), channel_id=1, source_target_pairs={{0,16},{16,0},{32,48},{48,32},{64,80},{80,64},{96,112},{112,96},{1... | collective-permute-start | bytes 98312 | tf_op jit(solution)/shard_map/ppermute | solution.py:841
  16.5 5.2 %collective-permute-start.5 = (f32[4,8,256]{2,1,0:T(8,128)S(1)}, f32[4,8,256]{2,1,0:T(8,128)S(1)}, u32[]{:S(2)}, u32[]{:S(2)}) collective-permute-start(f32[4,8,256]{2,1,0:T(8,128)S(1)} %get-tuple-element.60), channel_id=1, source_target_pairs={{0,0},{16,32},{32,16},{48,64},{64,48},{80,96},{96,80},{112,112},{1... | collective-permute-start | bytes 98312 | tf_op jit(solution)/shard_map/ppermute | solution.py:841
  21.8 4.1 %collective-permute-start.6 = (f32[2,40,128]{2,1,0:T(8,128)S(1)}, f32[2,40,128]{2,1,0:T(8,128)S(1)}, u32[]{:S(2)}, u32[]{:S(2)}) collective-permute-start(f32[2,40,128]{2,1,0:T(8,128)S(1)} %pack_z1.1), channel_id=1, source_target_pairs={{0,1},{1,0},{2,3},{3,2},{4,5},{5,4},{6,7},{7,6},{8,9},{9,8},{10,11... | collective-permute-start | bytes 122888 | tf_op jit(solution)/shard_map/ppermute | solution.py:841
  26.6 19.7 %copy-start.1 = (s32[8,32,256]{2,1,0:T(8,128)S(1)}, s32[8,32,256]{2,1,0:T(8,128)}, u32[]{:S(2)}) copy-start(s32[8,32,256]{2,1,0:T(8,128)} %mask.5) | copy-start | bytes 786436
  26.6 9.8 %collective-permute-start.7 = (f32[4,2,32,256]{3,2,1,0:T(8,128)S(1)}, f32[4,2,32,256]{3,2,1,0:T(8,128)S(1)}, u32[]{:S(2)}, u32[]{:S(2)}) collective-permute-start(f32[4,2,32,256]{3,2,1,0:T(8,128)S(1)} %get-tuple-element.75), channel_id=1, source_target_pairs={{0,16},{16,0},{32,48},{48,32},{64,80},{80,64},{96,112},{112,96},{1... | collective-permute-start | bytes 786440 | tf_op jit(solution)/shard_map/ppermute | solution.py:841
  26.7 9.7 %collective-permute-start.8 = (f32[4,2,32,256]{3,2,1,0:T(8,128)S(1)}, f32[4,2,32,256]{3,2,1,0:T(8,128)S(1)}, u32[]{:S(2)}, u32[]{:S(2)}) collective-permute-start(f32[4,2,32,256]{3,2,1,0:T(8,128)S(1)} %get-tuple-element.76), channel_id=1, source_target_pairs={{0,0},{16,32},{32,16},{48,64},{64,48},{80,96},{96,80},{112,112},{1... | collective-permute-start | bytes 786440 | tf_op jit(solution)/shard_map/ppermute | solution.py:841
  29.5 9.2 %collective-permute-start.10 = (f32[8,8,256]{2,1,0:T(8,128)S(1)}, f32[8,8,256]{2,1,0:T(8,128)S(1)}, u32[]{:S(2)}, u32[]{:S(2)}) collective-permute-start(f32[8,8,256]{2,1,0:T(8,128)S(1)} %get-tuple-element.80), channel_id=1, source_target_pairs={{0,0},{2,4},{4,2},{6,8},{8,6},{10,12},{12,10},{14,14},{1,1},{3,5},... | collective-permute-start | bytes 196616 | tf_op jit(solution)/shard_map/ppermute | solution.py:841
  32.0 8.1 %collective-permute-start.9 = (f32[8,8,256]{2,1,0:T(8,128)S(1)}, f32[8,8,256]{2,1,0:T(8,128)S(1)}, u32[]{:S(2)}, u32[]{:S(2)}) collective-permute-start(f32[8,8,256]{2,1,0:T(8,128)S(1)} %get-tuple-element.79), channel_id=1, source_target_pairs={{0,2},{2,0},{4,6},{6,4},{8,10},{10,8},{12,14},{14,12},{1,3},{3,1},... | collective-permute-start | bytes 196616 | tf_op jit(solution)/shard_map/ppermute | solution.py:841
  40.0 3.5 %collective-permute-start.11 = (f32[6,8,256]{2,1,0:T(8,128)S(1)}, f32[6,8,256]{2,1,0:T(8,128)S(1)}, u32[]{:S(2)}, u32[]{:S(2)}) collective-permute-start(f32[6,8,256]{2,1,0:T(8,128)S(1)} %get-tuple-element.81), channel_id=1, source_target_pairs={{0,16},{16,0},{32,48},{48,32},{64,80},{80,64},{96,112},{112,96},{1... | collective-permute-start | bytes 147464 | tf_op jit(solution)/shard_map/ppermute | solution.py:841
  40.1 5.4 %collective-permute-start.12 = (f32[6,8,256]{2,1,0:T(8,128)S(1)}, f32[6,8,256]{2,1,0:T(8,128)S(1)}, u32[]{:S(2)}, u32[]{:S(2)}) collective-permute-start(f32[6,8,256]{2,1,0:T(8,128)S(1)} %get-tuple-element.82), channel_id=1, source_target_pairs={{0,0},{16,32},{32,16},{48,64},{64,48},{80,96},{96,80},{112,112},{1... | collective-permute-start | bytes 147464 | tf_op jit(solution)/shard_map/ppermute | solution.py:841
  45.6 4.1 %collective-permute-start.13 = (f32[2,40,128]{2,1,0:T(8,128)S(1)}, f32[2,40,128]{2,1,0:T(8,128)S(1)}, u32[]{:S(2)}, u32[]{:S(2)}) collective-permute-start(f32[2,40,128]{2,1,0:T(8,128)S(1)} %pack_z2.1), channel_id=1, source_target_pairs={{0,1},{1,0},{2,3},{3,2},{4,5},{5,4},{6,7},{7,6},{8,9},{9,8},{10,11... | collective-permute-start | bytes 122888 | tf_op jit(solution)/shard_map/ppermute | solution.py:841

commit v9 on v8

--- a/solution.py
+++ b/solution.py
@@ -2,6 +2,7 @@
 
 import jax
 import jax.numpy as jnp
+import numpy as np
 from jax import lax
 from jax.experimental import pallas as pl
 from jax.experimental.pallas import tpu as pltpu
@@ -835,10 +836,22 @@
 HBM = pl.BlockSpec(memory_space=pltpu.HBM)
 
 
+AXES = ("gx", "gy", "gz")
+BESIDE = {"gx": "gz", "gy": "gx"}
+
+
 def swap(x, axis, start):
-    size = lax.axis_size(axis)
-    other = {i: i + 1 if i % 2 == start else i - 1 for i in range(size)}
-    return lax.ppermute(x, axis, [(i, j if 0 <= j < size else i) for i, j in other.items()])
+    sizes = [lax.axis_size(a) for a in AXES]
+    pairs = []
+    for place in np.ndindex(*sizes):
+        other = list(place)
+        at = AXES.index(axis)
+        other[at] += 1 if place[at] % 2 == start else -1
+        if not 0 <= other[at] < sizes[at]:
+            other = list(place)
+            other[AXES.index(BESIDE[axis])] ^= 1
+        pairs.append(tuple(int(np.ravel_multi_index(p, sizes)) for p in (place, other)))
+    return lax.ppermute(x, AXES, pairs)
 
 
 def swaps(axis, pair):

time: 51.2 us -> 43.9 us (0.86)
  the two profiles are of different devices: /device:TPU:48 before, /device:TPU:0 now
where the time goes in v9:
time: 43.9 us; the launch traced here: 43.8 us
  waiting for transfers between devices  18.4 us (42%)
  Pallas kernels  13.6 us (31%)
  starting transfers between devices  11.6 us (26%)
    ppermute x14, waiting for transfers between devices, swap(): return lax.ppermute(x, AXES, pairs)  18.4 us
    pallas_call x16, Pallas kernels, call(): pl.pallas_call(kernel, grid=(1,), out_shape=shapes if len(shapes) > 1 els...  13.6 us
    ppermute x14, starting transfers between devices, swap(): return lax.ppermute(x, AXES, pairs)  11.6 us
  transfers between devices with their start and end apart: 14, of which 7 were waited for; matrix products, arithmetic and copies ran while one was open for 0% of the time, Pallas kernels for 23%

profile of v9, /device:TPU:0, one launch (start us, length us, event | category | flops | bytes accessed | tf_op | source)
XLA Modules:
  0.0 43.8 jit_solution(2204052317195541270)
XLA Ops:
  0.0 1.4 %pack_x1.1 = (f32[8,32,256]{2,1,0:T(8,128)S(1)}, f32[10,32,256]{2,1,0:T(8,128)S(1)}, f32[10,32,256]{2,1,0:T(8,128)S(1)}, f32[2,8,128]{2,1,0:T(8,128)S(1)}) custom-call(f32[8,32,256]{2,1,0:T(8,128)} %design.1, s32[8,32,256]{2,1,0:T(8,128)} %mask.5, f32[2,3,8,32,256]{4,3,2,1,0:T(8,128)} %modes.9, f32[6]{0:T(128)} %eigenvalues.1, s32[6]{0:T(128)} %order.1), custom_call_target="tpu_custom_call" | custom-call | bytes 2000000 | tf_op jit(solution)/shard_map/pack_x1/pallas_call | solution.py:822
  1.4 0.1 collective-permute-start
  1.5 1.7 %collective-permute-start.1 = (f32[10,32,256]{2,1,0:T(8,128)S(1)}, f32[10,32,256]{2,1,0:T(8,128)S(1)}, u32[]{:S(2)}, u32[]{:S(2)}) collective-permute-start(f32[10,32,256]{2,1,0:T(8,128)S(1)} %get-tuple-element.53), channel_id=1, source_target_pairs={{0,1},{1,0},{2,3},{3,2},{4,5},{5,4},{6,7},{7,6},{8,9},{9,8},{10,11... | collective-permute-start | bytes 983048 | tf_op jit(solution)/shard_map/ppermute | solution.py:854
  3.2 2.8 %collective-permute-start.2 = (f32[10,8,256]{2,1,0:T(8,128)S(1)}, f32[10,8,256]{2,1,0:T(8,128)S(1)}, u32[]{:S(2)}, u32[]{:S(2)}) collective-permute-start(f32[10,8,256]{2,1,0:T(8,128)S(1)} %get-tuple-element.54), channel_id=1, source_target_pairs={{0,2},{1,3},{2,0},{3,1},{4,6},{5,7},{6,4},{7,5},{8,10},{9,11},{10,... | collective-permute-start | bytes 245768 | tf_op jit(solution)/shard_map/ppermute | solution.py:854
  6.0 0.2 collective-permute-start.3
  6.2 3.1 %energy.1 = (f32[2,7,32,256]{3,2,1,0:T(8,128)S(1)}, f32[2,7,32,256]{3,2,1,0:T(8,128)S(1)}, f32[2,32,128]{2,1,0:T(8,128)S(1)}) custom-call(f32[2,3,8,32,256]{4,3,2,1,0:T(8,128)S(1)} %copy-done), custom_call_target="tpu_custom_call" | custom-call | flops 40000000 | bytes 2000000 | tf_op jit(solution)/shard_map/energy/pallas_call | solution.py:822
  9.4 4.2 %collective-permute-done.2.y_first = f32[10,8,256]{2,1,0:T(8,128)S(1)} collective-permute-done((f32[10,8,256]{2,1,0:T(8,128)S(1)}, f32[10,8,256]{2,1,0:T(8,128)S(1)}, u32[]{:S(2)}, u32[]{:S(2)}) %collective-permute-start.2) | collective-permute-done | bytes 81952 | tf_op jit(solution)/shard_map/ppermute | solution.py:854
  13.6 0.1 collective-permute-start.4
  13.7 0.1 collective-permute-start.5
  13.8 1.8 %bulk1.1 = (f32[1,8,32,256]{3,2,1,0:T(8,128)S(1)}, f32[1,4,16,2,1,256]{5,4,3,2,1,0:T(1,128)S(1)}, f32[1,4,32,128]{3,2,1,0:T(8,128)S(1)}, f32[2,32,256]{2,1,0:T(8...) custom-call(f32[8,32,256]{2,1,0:T(8,128)S(1)} %get-tuple-element.50., ...), custom_call_target="tpu_custom_call" | custom-call | flops 30000000 | bytes 2000000 | tf_op jit(solution)/shard_map/bulk1/pallas_call | solution.py:822
  15.7 2.0 %collective-permute-done.5.e_second = f32[4,8,256]{2,1,0:T(8,128)S(1)} collective-permute-done((f32[4,8,256]{2,1,0:T(8,128)S(1)}, f32[4,8,256]{2,1,0:T(8,128)S(1)}, u32[]{:S(2)}, u32[]{:S(2)}) %collective-permute-start.5) | collective-permute-done | bytes 32800 | tf_op jit(solution)/shard_map/ppermute | solution.py:854
  17.7 0.1 pack_z1.1
  17.9 0.8 %strips1.1 = (f32[1,8,16,256]{3,2,1,0:T(8,128)S(1)}, f32[1,4,16,128]{3,2,1,0:T(8,128)S(1)}, f32[2,2,8,256]{3,2,1,0:T(8,128)S(1)}, f32[40,128]{1,0:T(8,128)S(1)}) custom-call(f32[2,3,8,32,256]{4,3,2,1,0:T(8,128)S(1)} %copy-done, f32[2,32,128]{2,1,0:T(8,128)S(1)} %get-tuple-element.57.rims, f32[2,8,128]{2,1,0:T(8,128)S(1)} %get-tuple-element.58.row32, ...), custom_call_target="tpu_custom_call" | custom-call | flops 20000000 | bytes 2000000 | tf_op jit(solution)/shard_map/strips1/pallas_call | solution.py:822
  18.7 3.2 %collective-permute-done.6.z_in = f32[2,40,128]{2,1,0:T(8,128)S(1)} collective-permute-done((f32[2,40,128]{2,1,0:T(8,128)S(1)}, f32[2,40,128]{2,1,0:T(8,128)S(1)}, u32[]{:S(2)}, u32[]{:S(2)}) %collective-permute-start.6) | collective-permute-done | bytes 40992 | tf_op jit(solution)/shard_map/ppermute | solution.py:854
  21.9 0.5 %raw1.1 = (f32[4,2,32,256]{3,2,1,0:T(8,128)S(1)}, f32[3,32,128]{2,1,0:T(8,128)S(1)}) custom-call(f32[2,8,128]{2,1,0:T(8,128)S(1)} %get-tuple-element.49.lams, f32[2,40,128]{2,1,0:T(8,128)S(1)} %collective-permute-done.6.z_in, f32[40,128]{1,0:T(8,128)S(1)} %get-tuple-element.62.packed, f32[1,8,32,256]{3,2,1,0:T(8,128)S(1)} %get-tuple-element.63.bulk, ...), custom_call_target="tpu_custom_call" | custom-call | bytes 2000000 | tf_op jit(solution)/shard_map/raw1/pallas_call | solution.py:822
  22.4 0.2 raw2.1
  22.6 0.1 collective-permute-start.7
  22.7 0.1 collective-permute-start.8
  22.8 0.5 %collective-permute-start.10 = (f32[8,8,256]{2,1,0:T(8,128)S(1)}, f32[8,8,256]{2,1,0:T(8,128)S(1)}, u32[]{:S(2)}, u32[]{:S(2)}) collective-permute-start(f32[8,8,256]{2,1,0:T(8,128)S(1)} %get-tuple-element.80), channel_id=1, source_target_pairs={{0,16},{1,17},{2,4},{3,5},{4,2},{5,3},{6,8},{7,9},{8,6},{9,7},{10,... | collective-permute-start | bytes 196616 | tf_op jit(solution)/shard_map/ppermute | solution.py:854
  23.3 5.1 %collective-permute-start.9 = (f32[8,8,256]{2,1,0:T(8,128)S(1)}, f32[8,8,256]{2,1,0:T(8,128)S(1)}, u32[]{:S(2)}, u32[]{:S(2)}) collective-permute-start(f32[8,8,256]{2,1,0:T(8,128)S(1)} %get-tuple-element.79), channel_id=1, source_target_pairs={{0,2},{1,3},{2,0},{3,1},{4,6},{5,7},{6,4},{7,5},{8,10},{9,11},{10,... | collective-permute-start | bytes 196616 | tf_op jit(solution)/shard_map/ppermute | solution.py:854
  28.4 0.7 %collective-permute-done.8.x_second = f32[4,2,32,256]{3,2,1,0:T(8,128)S(1)} collective-permute-done((f32[4,2,32,256]{3,2,1,0:T(8,128)S(1)}, f32[4,2,32,256]{3,2,1,0:T(8,128)S(1)}, u32[]{:S(2)}, u32[]{:S(2)}) %collective-permute-start.8) | collective-permute-done | bytes 262176 | tf_op jit(solution)/shard_map/ppermute | solution.py:854
  29.2 1.2 %bulk2_0.1 = (f32[1,8,32,256]{3,2,1,0:T(8,128)S(1)}, f32[1,4,16,2,1,256]{5,4,3,2,1,0:T(1,128)S(1)}, f32[1,4,32,128]{3,2,1,0:T(8,128)S(1)}, f32[1,32,128]{2,1,0:T(8,128)S(1)}) custom-call(f32[4,2,32,256]{3,2,1,0:T(8,128)S(1)} %get-tuple-element.72.low, f32[4,2,32,256]{3,2,1,0:T(8,128)S(1)} %get-tuple-element.74.high, ...), custom_call_target="tpu_custom_call" | custom-call | flops 20000000 | bytes 2000000 | tf_op jit(solution)/shard_map/bulk2_0/pallas_call | solution.py:822
  30.4 3.7 %collective-permute-done.9.y_first = f32[8,8,256]{2,1,0:T(8,128)S(1)} collective-permute-done((f32[8,8,256]{2,1,0:T(8,128)S(1)}, f32[8,8,256]{2,1,0:T(8,128)S(1)}, u32[]{:S(2)}, u32[]{:S(2)}) %collective-permute-start.9) | collective-permute-done | bytes 65568 | tf_op jit(solution)/shard_map/ppermute | solution.py:854
  34.1 0.1 collective-permute-start.11
  34.2 0.4 collective-permute-start.12
  34.6 1.2 %bulk2_1.1 = (f32[1,8,32,256]{3,2,1,0:T(8,128)S(1)}, f32[1,4,16,2,1,256]{5,4,3,2,1,0:T(1,128)S(1)}, f32[1,4,32,128]{3,2,1,0:T(8,128)S(1)}, f32[1,32,128]{2,1,0:T(8,128)S(1)}) custom-call(f32[4,2,32,256]{3,2,1,0:T(8,128)S(1)} %get-tuple-element.72.low, f32[4,2,32,256]{3,2,1,0:T(8,128)S(1)} %get-tuple-element.74.high, ...), custom_call_target="tpu_custom_call" | custom-call | flops 20000000 | bytes 2000000 | tf_op jit(solution)/shard_map/bulk2_1/pallas_call | solution.py:822
  35.8 2.6 %collective-permute-done.12.e_second = f32[6,8,256]{2,1,0:T(8,128)S(1)} collective-permute-done((f32[6,8,256]{2,1,0:T(8,128)S(1)}, f32[6,8,256]{2,1,0:T(8,128)S(1)}, u32[]{:S(2)}, u32[]{:S(2)}) %collective-permute-start.12) | collective-permute-done | bytes 49184 | tf_op jit(solution)/shard_map/ppermute | solution.py:854
  38.4 0.1 pack_z2.1
  38.5 0.4 collective-permute-start.13
  38.9 1.8 %strips2.1 = (f32[2,8,32,256]{3,2,1,0:T(8,128)}, f32[2,8,32,128]{3,2,1,0:T(8,128)S(1)}, f32[1,4,16,128]{3,2,1,0:T(8,128)S(1)}, f32[1,4,16,128]{3,2,1,0:T(8,128)S(1)}) custom-call(s32[8,32,256]{2,1,0:T(8,128)S(1)} %copy-done.1, f32[8,8,256]{2,1,0:T(8,128)S(1)} %collective-permute-done.9.y_first, f32[8,8,256]{2,1,0:T(8,128)S(1)} %collective-permute-done.10.y_second, ...), custom_call_target="tpu_custom_call" | custom-call | flops 20000000 | bytes 2000000 | tf_op jit(solution)/shard_map/strips2/pallas_call | solution.py:822
  40.7 1.9 %collective-permute-done.13.z_in = f32[2,40,128]{2,1,0:T(8,128)S(1)} collective-permute-done((f32[2,40,128]{2,1,0:T(8,128)S(1)}, f32[2,40,128]{2,1,0:T(8,128)S(1)}, u32[]{:S(2)}, u32[]{:S(2)}) %collective-permute-start.13) | collective-permute-done | bytes 40992 | tf_op jit(solution)/shard_map/ppermute | solution.py:854
  42.6 1.2 %final.1 = f32[2,8,32,256]{3,2,1,0:T(8,128)} custom-call(s32[8,32,256]{2,1,0:T(8,128)S(1)} %copy-done.1, f32[2,40,128]{2,1,0:T(8,128)S(1)} %collective-permute-done.13.z_in, f32[1,4,32,128]{3,2,1,0:T(8,128)S(1)} %get-tuple-element.83.bulk_edges0, f32[1,4,32,128]{3,2,1,0:T(8,128)S(1)} %get-tuple-element.84.bulk_edges1, ...), custom_call_target="tpu_custom_call", output_to_operand_aliasing={{}: (7, {})} | custom-call | bytes 2000000 | tf_op jit(solution)/shard_map/final/pallas_call | solution.py:822
  (16 shorter events, 0.2 us)
Async XLA Ops:
  0.0 3.2 %copy-start = (f32[2,3,8,32,256]{4,3,2,1,0:T(8,128)S(1)}, f32[2,3,8,32,256]{4,3,2,1,0:T(8,128)}, u32[]{:S(2)}) copy-start(f32[2,3,8,32,256]{4,3,2,1,0:T(8,128)} %modes.9) | copy-start | bytes 4718596
  1.4 12.4 %collective-permute-start = (f32[10,32,256]{2,1,0:T(8,128)S(1)}, f32[10,32,256]{2,1,0:T(8,128)S(1)}, u32[]{:S(2)}, u32[]{:S(2)}) collective-permute-start(f32[10,32,256]{2,1,0:T(8,128)S(1)} %get-tuple-element.52), channel_id=1, source_target_pairs={{0,16},{1,17},{2,18},{3,19},{4,20},{5,21},{6,22},{7,23},{8,24},{9,... | collective-permute-start | bytes 983048 | tf_op jit(solution)/shard_map/ppermute | solution.py:854
  1.5 12.3 %collective-permute-start.1 = (f32[10,32,256]{2,1,0:T(8,128)S(1)}, f32[10,32,256]{2,1,0:T(8,128)S(1)}, u32[]{:S(2)}, u32[]{:S(2)}) collective-permute-start(f32[10,32,256]{2,1,0:T(8,128)S(1)} %get-tuple-element.53), channel_id=1, source_target_pairs={{0,1},{1,0},{2,3},{3,2},{4,5},{5,4},{6,7},{7,6},{8,9},{9,8},{10,11... | collective-permute-start | bytes 983048 | tf_op jit(solution)/shard_map/ppermute | solution.py:854
  3.2 10.4 %collective-permute-start.2 = (f32[10,8,256]{2,1,0:T(8,128)S(1)}, f32[10,8,256]{2,1,0:T(8,128)S(1)}, u32[]{:S(2)}, u32[]{:S(2)}) collective-permute-start(f32[10,8,256]{2,1,0:T(8,128)S(1)} %get-tuple-element.54), channel_id=1, source_target_pairs={{0,2},{1,3},{2,0},{3,1},{4,6},{5,7},{6,4},{7,5},{8,10},{9,11},{10,... | collective-permute-start | bytes 245768 | tf_op jit(solution)/shard_map/ppermute | solution.py:854
  6.0 7.5 %collective-permute-start.3 = (f32[10,8,256]{2,1,0:T(8,128)S(1)}, f32[10,8,256]{2,1,0:T(8,128)S(1)}, u32[]{:S(2)}, u32[]{:S(2)}) collective-permute-start(f32[10,8,256]{2,1,0:T(8,128)S(1)} %get-tuple-element.55), channel_id=1, source_target_pairs={{0,16},{1,17},{2,4},{3,5},{4,2},{5,3},{6,8},{7,9},{8,6},{9,7},{10,... | collective-permute-start | bytes 245768 | tf_op jit(solution)/shard_map/ppermute | solution.py:854
  13.6 2.0 %collective-permute-start.4 = (f32[4,8,256]{2,1,0:T(8,128)S(1)}, f32[4,8,256]{2,1,0:T(8,128)S(1)}, u32[]{:S(2)}, u32[]{:S(2)}) collective-permute-start(f32[4,8,256]{2,1,0:T(8,128)S(1)} %get-tuple-element.59), channel_id=1, source_target_pairs={{0,16},{1,17},{2,18},{3,19},{4,20},{5,21},{6,22},{7,23},{8,24},{9,... | collective-permute-start | bytes 98312 | tf_op jit(solution)/shard_map/ppermute | solution.py:854
  13.7 4.0 %collective-permute-start.5 = (f32[4,8,256]{2,1,0:T(8,128)S(1)}, f32[4,8,256]{2,1,0:T(8,128)S(1)}, u32[]{:S(2)}, u32[]{:S(2)}) collective-permute-start(f32[4,8,256]{2,1,0:T(8,128)S(1)} %get-tuple-element.60), channel_id=1, source_target_pairs={{0,1},{1,0},{2,3},{3,2},{4,5},{5,4},{6,7},{7,6},{8,9},{9,8},{10,11... | collective-permute-start | bytes 98312 | tf_op jit(solution)/shard_map/ppermute | solution.py:854
  17.8 4.1 %collective-permute-start.6 = (f32[2,40,128]{2,1,0:T(8,128)S(1)}, f32[2,40,128]{2,1,0:T(8,128)S(1)}, u32[]{:S(2)}, u32[]{:S(2)}) collective-permute-start(f32[2,40,128]{2,1,0:T(8,128)S(1)} %pack_z1.1), channel_id=1, source_target_pairs={{0,1},{1,0},{2,3},{3,2},{4,5},{5,4},{6,7},{7,6},{8,9},{9,8},{10,11... | collective-permute-start | bytes 122888 | tf_op jit(solution)/shard_map/ppermute | solution.py:854
  22.6 16.3 %copy-start.1 = (s32[8,32,256]{2,1,0:T(8,128)S(1)}, s32[8,32,256]{2,1,0:T(8,128)}, u32[]{:S(2)}) copy-start(s32[8,32,256]{2,1,0:T(8,128)} %mask.5) | copy-start | bytes 786436
  22.6 5.8 %collective-permute-start.7 = (f32[4,2,32,256]{3,2,1,0:T(8,128)S(1)}, f32[4,2,32,256]{3,2,1,0:T(8,128)S(1)}, u32[]{:S(2)}, u32[]{:S(2)}) collective-permute-start(f32[4,2,32,256]{3,2,1,0:T(8,128)S(1)} %get-tuple-element.75), channel_id=1, source_target_pairs={{0,16},{1,17},{2,18},{3,19},{4,20},{5,21},{6,22},{7,23},{8,24},{9,... | collective-permute-start | bytes 786440 | tf_op jit(solution)/shard_map/ppermute | solution.py:854
  22.7 6.5 %collective-permute-start.8 = (f32[4,2,32,256]{3,2,1,0:T(8,128)S(1)}, f32[4,2,32,256]{3,2,1,0:T(8,128)S(1)}, u32[]{:S(2)}, u32[]{:S(2)}) collective-permute-start(f32[4,2,32,256]{3,2,1,0:T(8,128)S(1)} %get-tuple-element.76), channel_id=1, source_target_pairs={{0,1},{1,0},{2,3},{3,2},{4,5},{5,4},{6,7},{7,6},{8,9},{9,8},{10,11... | collective-permute-start | bytes 786440 | tf_op jit(solution)/shard_map/ppermute | solution.py:854
  22.8 7.5 %collective-permute-start.10 = (f32[8,8,256]{2,1,0:T(8,128)S(1)}, f32[8,8,256]{2,1,0:T(8,128)S(1)}, u32[]{:S(2)}, u32[]{:S(2)}) collective-permute-start(f32[8,8,256]{2,1,0:T(8,128)S(1)} %get-tuple-element.80), channel_id=1, source_target_pairs={{0,16},{1,17},{2,4},{3,5},{4,2},{5,3},{6,8},{7,9},{8,6},{9,7},{10,... | collective-permute-start | bytes 196616 | tf_op jit(solution)/shard_map/ppermute | solution.py:854
  23.3 10.8 %collective-permute-start.9 = (f32[8,8,256]{2,1,0:T(8,128)S(1)}, f32[8,8,256]{2,1,0:T(8,128)S(1)}, u32[]{:S(2)}, u32[]{:S(2)}) collective-permute-start(f32[8,8,256]{2,1,0:T(8,128)S(1)} %get-tuple-element.79), channel_id=1, source_target_pairs={{0,2},{1,3},{2,0},{3,1},{4,6},{5,7},{6,4},{7,5},{8,10},{9,11},{10,... | collective-permute-start | bytes 196616 | tf_op jit(solution)/shard_map/ppermute | solution.py:854
  34.1 1.7 %collective-permute-start.11 = (f32[6,8,256]{2,1,0:T(8,128)S(1)}, f32[6,8,256]{2,1,0:T(8,128)S(1)}, u32[]{:S(2)}, u32[]{:S(2)}) collective-permute-start(f32[6,8,256]{2,1,0:T(8,128)S(1)} %get-tuple-element.81), channel_id=1, source_target_pairs={{0,16},{1,17},{2,18},{3,19},{4,20},{5,21},{6,22},{7,23},{8,24},{9,... | collective-permute-start | bytes 147464 | tf_op jit(solution)/shard_map/ppermute | solution.py:854
  34.2 4.2 %collective-permute-start.12 = (f32[6,8,256]{2,1,0:T(8,128)S(1)}, f32[6,8,256]{2,1,0:T(8,128)S(1)}, u32[]{:S(2)}, u32[]{:S(2)}) collective-permute-start(f32[6,8,256]{2,1,0:T(8,128)S(1)} %get-tuple-element.82), channel_id=1, source_target_pairs={{0,1},{1,0},{2,3},{3,2},{4,5},{5,4},{6,7},{7,6},{8,9},{9,8},{10,11... | collective-permute-start | bytes 147464 | tf_op jit(solution)/shard_map/ppermute | solution.py:854
  38.5 4.1 %collective-permute-start.13 = (f32[2,40,128]{2,1,0:T(8,128)S(1)}, f32[2,40,128]{2,1,0:T(8,128)S(1)}, u32[]{:S(2)}, u32[]{:S(2)}) collective-permute-start(f32[2,40,128]{2,1,0:T(8,128)S(1)} %pack_z2.1), channel_id=1, source_target_pairs={{0,1},{1,0},{2,3},{3,2},{4,5},{5,4},{6,7},{7,6},{8,9},{9,8},{10,11... | collective-permute-start | bytes 122888 | tf_op jit(solution)/shard_map/ppermute | solution.py:854

commit v10 on v9

--- a/solution.py
+++ b/solution.py
@@ -38,8 +38,8 @@
     return iota((8, LANES), 0), iota((8, LANES), 1)
 
 
-def even(axis):
-    return lax.rem(lax.axis_index(axis), 2) == 0
+def odd(axis):
+    return lax.rem(lax.axis_index(axis), 2) == 1
 
 
 class Pick:
@@ -51,12 +51,12 @@
 
 
 def neighbours(axis, first, second):
-    cond = even(axis)
+    cond = odd(axis)
     return Pick(cond, first, second), Pick(cond, second, first)
 
 
 def put(axis, first, second, index, down, up):
-    cond = even(axis)
+    cond = odd(axis)
     first[index] = jnp.where(cond, up, down)
     second[index] = jnp.where(cond, down, up)
 
@@ -702,20 +702,33 @@
 
 def pack_e2(y_first, y_second, ahead, first, second):
     y_above, y_below = neighbours("gy", y_first, y_second)
-    for i in range(W - 1):
-        for m in range(MODES):
-            down, up = (own_raw_halo(y_above, y_below, m, x) for x in (i, CX - 1 - i))
-            put("gx", first, second, MODES * i + m, down, up)
+    sub = iota((8, CZ), 0)
+
+    def merged(near, far, rows):
+        moved = jnp.where(sub < 4, pltpu.roll(far, rows, 0), pltpu.roll(far, 8 - rows, 0))
+        return jnp.where((sub < rows) | (sub >= 8 - rows), near, moved)
+
+    tiles = []
+    for order in (range(W - 1), range(CX - 1, CX - W, -1)):
+        halo = [[own_raw_halo(y_above, y_below, m, x) for m in range(MODES)] for x in order]
+        side = [merged(halo[0][m], halo[2][m], 3) for m in range(MODES)]
+        tiles.append(side + [merged(halo[1][0], halo[1][1], 2)])
+    for n in range(MODES + 1):
+        put("gx", first, second, n, tiles[0][n], tiles[1][n])
 
 
 def raw_halo(y_above, y_below, from_above, from_below, m, p, lanes=slice(None)):
     if W <= p < W + CX:
         return own_raw_halo(y_above, y_below, m, p - W, lanes)
-    if 0 < p < W:
-        return from_below[MODES * (W - 1 - p) + m, :, lanes]
-    if W + CX <= p < PX - 1:
-        return from_above[MODES * (p - W - CX) + m, :, lanes]
-    return jnp.zeros(y_above[0, :, lanes].shape, F32)
+    away, side = (W - p, from_below) if p < W else (p - W - CX + 1, from_above)
+    if away == W:
+        return jnp.zeros(y_above[0, :, lanes].shape, F32)
+    tile = side[MODES if away == 2 else m, :, lanes]
+    inwards = 3 if away == 3 else 2 * m if away == 2 else 0
+    if inwards:
+        sub = iota(tile.shape, 0)
+        tile = jnp.where(sub < 4, pltpu.roll(tile, 8 - inwards, 0), pltpu.roll(tile, inwards, 0))
+    return tile
 
 
 def bulk_kernel2(m, low, high, x_first, x_second, bulk, ends, edges, own, table, sb, one, two):
@@ -791,9 +804,10 @@
     edge = edge_tiles(gz)
     scale = strip_scale(gx, gy)
     copies = []
-    for m in range(MODES):
-        edges = ((bulk_edges0, strip_edges0), (bulk_edges1, strip_edges1))[m]
-        z_state = z_sweeps(0, scale, z_in[m], *edges)
+    fed = ((bulk_edges0, strip_edges0), (bulk_edges1, strip_edges1))
+    z_states = [z_sweeps(0, scale, z_in[m], *fed[m]) for m in range(MODES)]
+    for m in range(MODES):
+        z_state = z_states[m]
         for x in range(CX):
             for i in range(CY // 8):
                 rows = slice(8 * i, 8 * i + 8)
@@ -855,8 +869,8 @@
 
 
 def swaps(axis, pair):
-    second = swap(pair[1], axis, 1)
-    return swap(pair[0], axis, 0), second
+    first = swap(pair[0], axis, 1)
+    return first, swap(pair[1], axis, 0)
 
 
 def sweep_outs(fields):
@@ -922,7 +936,7 @@
         for m in range(MODES)
     ]
     bulk, ends, bulk_edges, own = zip(*bulks)
-    edge = (MODES * (W - 1), 8, CZ)
+    edge = (MODES + 1, 8, CZ)
     halos = (*y_pair, *swaps("gx", call(pack_e2, "pack_e2", [edge] * 2, (*y_pair, own[0]))))
     z_in = swap(call(pack_z2, "pack_z2", [(MODES, PY, LANES)], (*own, *halos)), "gz", 0)
     result = (MODES, CX, CY, CZ)

time: 43.9 us -> 43.2 us (0.984)
  the two profiles are of different devices: /device:TPU:0 before, /device:TPU:38 now
where the time goes in v10:
time: 43.2 us; the launch traced here: 43.1 us
  waiting for transfers between devices  15.3 us (35%)
  starting transfers between devices  14.1 us (33%)
  Pallas kernels  13.6 us (31%)
    ppermute x14, waiting for transfers between devices, swap(): return lax.ppermute(x, AXES, pairs)  15.3 us
    ppermute x14, starting transfers between devices, swap(): return lax.ppermute(x, AXES, pairs)  14.1 us
    pallas_call x16, Pallas kernels, call(): pl.pallas_call(kernel, grid=(1,), out_shape=shapes if len(shapes) > 1 els...  13.6 us
  transfers between devices with their start and end apart: 14, of which 8 were waited for; matrix products, arithmetic and copies ran while one was open for 0% of the time, Pallas kernels for 23%

profile of v10, /device:TPU:38, one launch (start us, length us, event | category | flops | bytes accessed | tf_op | source)
XLA Modules:
  0.0 43.1 jit_solution(16221633294809119754)
XLA Ops:
  0.0 1.4 %pack_x1.1 = (f32[8,32,256]{2,1,0:T(8,128)S(1)}, f32[10,32,256]{2,1,0:T(8,128)S(1)}, f32[10,32,256]{2,1,0:T(8,128)S(1)}, f32[2,8,128]{2,1,0:T(8,128)S(1)}) custom-call(f32[8,32,256]{2,1,0:T(8,128)} %design.1, s32[8,32,256]{2,1,0:T(8,128)} %mask.5, f32[2,3,8,32,256]{4,3,2,1,0:T(8,128)} %modes.9, f32[6]{0:T(128)} %eigenvalues.1, s32[6]{0:T(128)} %order.1), custom_call_target="tpu_custom_call" | custom-call | bytes 2000000 | tf_op jit(solution)/shard_map/pack_x1/pallas_call | solution.py:836
  1.4 0.9 %collective-permute-start = (f32[10,32,256]{2,1,0:T(8,128)S(1)}, f32[10,32,256]{2,1,0:T(8,128)S(1)}, u32[]{:S(2)}, u32[]{:S(2)}) collective-permute-start(f32[10,32,256]{2,1,0:T(8,128)S(1)} %get-tuple-element.52), channel_id=1, source_target_pairs={{0,1},{1,0},{2,3},{3,2},{4,5},{5,4},{6,7},{7,6},{8,9},{9,8},{10,11... | collective-permute-start | bytes 983048 | tf_op jit(solution)/shard_map/ppermute | solution.py:868
  2.3 0.9 %collective-permute-start.1 = (f32[10,32,256]{2,1,0:T(8,128)S(1)}, f32[10,32,256]{2,1,0:T(8,128)S(1)}, u32[]{:S(2)}, u32[]{:S(2)}) collective-permute-start(f32[10,32,256]{2,1,0:T(8,128)S(1)} %get-tuple-element.53), channel_id=1, source_target_pairs={{0,16},{1,17},{2,18},{3,19},{4,20},{5,21},{6,22},{7,23},{8,24},{9,... | collective-permute-start | bytes 983048 | tf_op jit(solution)/shard_map/ppermute | solution.py:868
  3.2 2.8 %collective-permute-start.2 = (f32[10,8,256]{2,1,0:T(8,128)S(1)}, f32[10,8,256]{2,1,0:T(8,128)S(1)}, u32[]{:S(2)}, u32[]{:S(2)}) collective-permute-start(f32[10,8,256]{2,1,0:T(8,128)S(1)} %get-tuple-element.54), channel_id=1, source_target_pairs={{0,16},{1,17},{2,4},{3,5},{4,2},{5,3},{6,8},{7,9},{8,6},{9,7},{10,... | collective-permute-start | bytes 245768 | tf_op jit(solution)/shard_map/ppermute | solution.py:868
  6.1 0.3 collective-permute-start.3
  6.4 3.1 %energy.1 = (f32[2,7,32,256]{3,2,1,0:T(8,128)S(1)}, f32[2,7,32,256]{3,2,1,0:T(8,128)S(1)}, f32[2,32,128]{2,1,0:T(8,128)S(1)}) custom-call(f32[2,3,8,32,256]{4,3,2,1,0:T(8,128)S(1)} %copy-done), custom_call_target="tpu_custom_call" | custom-call | flops 40000000 | bytes 2000000 | tf_op jit(solution)/shard_map/energy/pallas_call | solution.py:836
  9.5 2.6 %collective-permute-done.2.y_first = f32[10,8,256]{2,1,0:T(8,128)S(1)} collective-permute-done((f32[10,8,256]{2,1,0:T(8,128)S(1)}, f32[10,8,256]{2,1,0:T(8,128)S(1)}, u32[]{:S(2)}, u32[]{:S(2)}) %collective-permute-start.2) | collective-permute-done | bytes 81952 | tf_op jit(solution)/shard_map/ppermute | solution.py:868
  12.2 1.3 %collective-permute-start.4 = (f32[4,8,256]{2,1,0:T(8,128)S(1)}, f32[4,8,256]{2,1,0:T(8,128)S(1)}, u32[]{:S(2)}, u32[]{:S(2)}) collective-permute-start(f32[4,8,256]{2,1,0:T(8,128)S(1)} %get-tuple-element.59), channel_id=1, source_target_pairs={{0,1},{1,0},{2,3},{3,2},{4,5},{5,4},{6,7},{7,6},{8,9},{9,8},{10,11... | collective-permute-start | bytes 98312 | tf_op jit(solution)/shard_map/ppermute | solution.py:868
  13.5 0.4 collective-permute-start.5
  13.8 1.8 %bulk1.1 = (f32[1,8,32,256]{3,2,1,0:T(8,128)S(1)}, f32[1,4,16,2,1,256]{5,4,3,2,1,0:T(1,128)S(1)}, f32[1,4,32,128]{3,2,1,0:T(8,128)S(1)}, f32[2,32,256]{2,1,0:T(8...) custom-call(f32[8,32,256]{2,1,0:T(8,128)S(1)} %get-tuple-element.50., ...), custom_call_target="tpu_custom_call" | custom-call | flops 30000000 | bytes 2000000 | tf_op jit(solution)/shard_map/bulk1/pallas_call | solution.py:836
  15.7 0.5 %collective-permute-done.4.e_first = f32[4,8,256]{2,1,0:T(8,128)S(1)} collective-permute-done((f32[4,8,256]{2,1,0:T(8,128)S(1)}, f32[4,8,256]{2,1,0:T(8,128)S(1)}, u32[]{:S(2)}, u32[]{:S(2)}) %collective-permute-start.4) | collective-permute-done | bytes 32800 | tf_op jit(solution)/shard_map/ppermute | solution.py:868
  16.2 0.1 pack_z1.1
  16.3 1.3 %collective-permute-start.6 = (f32[2,40,128]{2,1,0:T(8,128)S(1)}, f32[2,40,128]{2,1,0:T(8,128)S(1)}, u32[]{:S(2)}, u32[]{:S(2)}) collective-permute-start(f32[2,40,128]{2,1,0:T(8,128)S(1)} %pack_z1.1), channel_id=1, source_target_pairs={{0,1},{1,0},{2,3},{3,2},{4,5},{5,4},{6,7},{7,6},{8,9},{9,8},{10,11... | collective-permute-start | bytes 122888 | tf_op jit(solution)/shard_map/ppermute | solution.py:868
  17.6 0.8 %strips1.1 = (f32[1,8,16,256]{3,2,1,0:T(8,128)S(1)}, f32[1,4,16,128]{3,2,1,0:T(8,128)S(1)}, f32[2,2,8,256]{3,2,1,0:T(8,128)S(1)}, f32[40,128]{1,0:T(8,128)S(1)}) custom-call(f32[2,3,8,32,256]{4,3,2,1,0:T(8,128)S(1)} %copy-done, f32[2,32,128]{2,1,0:T(8,128)S(1)} %get-tuple-element.57.rims, f32[2,8,128]{2,1,0:T(8,128)S(1)} %get-tuple-element.58.row32, ...), custom_call_target="tpu_custom_call" | custom-call | flops 20000000 | bytes 2000000 | tf_op jit(solution)/shard_map/strips1/pallas_call | solution.py:836
  18.4 2.0 %collective-permute-done.6.z_in = f32[2,40,128]{2,1,0:T(8,128)S(1)} collective-permute-done((f32[2,40,128]{2,1,0:T(8,128)S(1)}, f32[2,40,128]{2,1,0:T(8,128)S(1)}, u32[]{:S(2)}, u32[]{:S(2)}) %collective-permute-start.6) | collective-permute-done | bytes 40992 | tf_op jit(solution)/shard_map/ppermute | solution.py:868
  20.4 0.5 %raw1.1 = (f32[4,2,32,256]{3,2,1,0:T(8,128)S(1)}, f32[3,32,128]{2,1,0:T(8,128)S(1)}) custom-call(f32[2,8,128]{2,1,0:T(8,128)S(1)} %get-tuple-element.49.lams, f32[2,40,128]{2,1,0:T(8,128)S(1)} %collective-permute-done.6.z_in, f32[40,128]{1,0:T(8,128)S(1)} %get-tuple-element.62.packed, f32[1,8,32,256]{3,2,1,0:T(8,128)S(1)} %get-tuple-element.63.bulk, ...), custom_call_target="tpu_custom_call" | custom-call | bytes 2000000 | tf_op jit(solution)/shard_map/raw1/pallas_call | solution.py:836
  20.9 0.2 raw2.1
  21.1 1.3 %collective-permute-start.7 = (f32[4,2,32,256]{3,2,1,0:T(8,128)S(1)}, f32[4,2,32,256]{3,2,1,0:T(8,128)S(1)}, u32[]{:S(2)}, u32[]{:S(2)}) collective-permute-start(f32[4,2,32,256]{3,2,1,0:T(8,128)S(1)} %get-tuple-element.75), channel_id=1, source_target_pairs={{0,1},{1,0},{2,3},{3,2},{4,5},{5,4},{6,7},{7,6},{8,9},{9,8},{10,11... | collective-permute-start | bytes 786440 | tf_op jit(solution)/shard_map/ppermute | solution.py:868
  22.4 2.9 %collective-permute-start.10 = (f32[8,8,256]{2,1,0:T(8,128)S(1)}, f32[8,8,256]{2,1,0:T(8,128)S(1)}, u32[]{:S(2)}, u32[]{:S(2)}) collective-permute-start(f32[8,8,256]{2,1,0:T(8,128)S(1)} %get-tuple-element.80), channel_id=1, source_target_pairs={{0,2},{1,3},{2,0},{3,1},{4,6},{5,7},{6,4},{7,5},{8,10},{9,11},{10,... | collective-permute-start | bytes 196616 | tf_op jit(solution)/shard_map/ppermute | solution.py:868
  25.3 1.7 %collective-permute-start.9 = (f32[8,8,256]{2,1,0:T(8,128)S(1)}, f32[8,8,256]{2,1,0:T(8,128)S(1)}, u32[]{:S(2)}, u32[]{:S(2)}) collective-permute-start(f32[8,8,256]{2,1,0:T(8,128)S(1)} %get-tuple-element.79), channel_id=1, source_target_pairs={{0,16},{1,17},{2,4},{3,5},{4,2},{5,3},{6,8},{7,9},{8,6},{9,7},{10,... | collective-permute-start | bytes 196616 | tf_op jit(solution)/shard_map/ppermute | solution.py:868
  27.1 1.2 %collective-permute-done.7.x_first = f32[4,2,32,256]{3,2,1,0:T(8,128)S(1)} collective-permute-done((f32[4,2,32,256]{3,2,1,0:T(8,128)S(1)}, f32[4,2,32,256]{3,2,1,0:T(8,128)S(1)}, u32[]{:S(2)}, u32[]{:S(2)}) %collective-permute-start.7) | collective-permute-done | bytes 262176 | tf_op jit(solution)/shard_map/ppermute | solution.py:868
  28.3 1.2 %bulk2_0.1 = (f32[1,8,32,256]{3,2,1,0:T(8,128)S(1)}, f32[1,4,16,2,1,256]{5,4,3,2,1,0:T(1,128)S(1)}, f32[1,4,32,128]{3,2,1,0:T(8,128)S(1)}, f32[1,32,128]{2,1,0:T(8,128)S(1)}) custom-call(f32[4,2,32,256]{3,2,1,0:T(8,128)S(1)} %get-tuple-element.72.low, f32[4,2,32,256]{3,2,1,0:T(8,128)S(1)} %get-tuple-element.74.high, ...), custom_call_target="tpu_custom_call" | custom-call | flops 20000000 | bytes 2000000 | tf_op jit(solution)/shard_map/bulk2_0/pallas_call | solution.py:836
  29.5 2.2 %collective-permute-done.10.y_second = f32[8,8,256]{2,1,0:T(8,128)S(1)} collective-permute-done((f32[8,8,256]{2,1,0:T(8,128)S(1)}, f32[8,8,256]{2,1,0:T(8,128)S(1)}, u32[]{:S(2)}, u32[]{:S(2)}) %collective-permute-start.10) | collective-permute-done | bytes 65568 | tf_op jit(solution)/shard_map/ppermute | solution.py:868
  31.7 2.1 %collective-permute-done.9.y_first = f32[8,8,256]{2,1,0:T(8,128)S(1)} collective-permute-done((f32[8,8,256]{2,1,0:T(8,128)S(1)}, f32[8,8,256]{2,1,0:T(8,128)S(1)}, u32[]{:S(2)}, u32[]{:S(2)}) %collective-permute-start.9) | collective-permute-done | bytes 65568 | tf_op jit(solution)/shard_map/ppermute | solution.py:868
  33.8 0.1 collective-permute-start.11
  33.9 0.1 collective-permute-start.12
  34.0 1.2 %bulk2_1.1 = (f32[1,8,32,256]{3,2,1,0:T(8,128)S(1)}, f32[1,4,16,2,1,256]{5,4,3,2,1,0:T(1,128)S(1)}, f32[1,4,32,128]{3,2,1,0:T(8,128)S(1)}, f32[1,32,128]{2,1,0:T(8,128)S(1)}) custom-call(f32[4,2,32,256]{3,2,1,0:T(8,128)S(1)} %get-tuple-element.72.low, f32[4,2,32,256]{3,2,1,0:T(8,128)S(1)} %get-tuple-element.74.high, ...), custom_call_target="tpu_custom_call" | custom-call | flops 20000000 | bytes 2000000 | tf_op jit(solution)/shard_map/bulk2_1/pallas_call | solution.py:836
  35.2 2.5 %collective-permute-done.11.e_first = f32[3,8,256]{2,1,0:T(8,128)S(1)} collective-permute-done((f32[3,8,256]{2,1,0:T(8,128)S(1)}, f32[3,8,256]{2,1,0:T(8,128)S(1)}, u32[]{:S(2)}, u32[]{:S(2)}) %collective-permute-start.11) | collective-permute-done | bytes 24608 | tf_op jit(solution)/shard_map/ppermute | solution.py:868
  37.7 0.1 pack_z2.1
  37.9 1.8 %strips2.1 = (f32[2,8,32,256]{3,2,1,0:T(8,128)}, f32[2,8,32,128]{3,2,1,0:T(8,128)S(1)}, f32[1,4,16,128]{3,2,1,0:T(8,128)S(1)}, f32[1,4,16,128]{3,2,1,0:T(8,128)S(1)}) custom-call(s32[8,32,256]{2,1,0:T(8,128)S(1)} %copy-done.1, f32[8,8,256]{2,1,0:T(8,128)S(1)} %collective-permute-done.9.y_first, f32[8,8,256]{2,1,0:T(8,128)S(1)} %collective-permute-done.10.y_second, ...), custom_call_target="tpu_custom_call" | custom-call | flops 20000000 | bytes 2000000 | tf_op jit(solution)/shard_map/strips2/pallas_call | solution.py:836
  39.7 2.2 %collective-permute-done.13.z_in = f32[2,40,128]{2,1,0:T(8,128)S(1)} collective-permute-done((f32[2,40,128]{2,1,0:T(8,128)S(1)}, f32[2,40,128]{2,1,0:T(8,128)S(1)}, u32[]{:S(2)}, u32[]{:S(2)}) %collective-permute-start.13) | collective-permute-done | bytes 40992 | tf_op jit(solution)/shard_map/ppermute | solution.py:868
  41.9 1.2 %final.1 = f32[2,8,32,256]{3,2,1,0:T(8,128)} custom-call(s32[8,32,256]{2,1,0:T(8,128)S(1)} %copy-done.1, f32[2,40,128]{2,1,0:T(8,128)S(1)} %collective-permute-done.13.z_in, f32[1,4,32,128]{3,2,1,0:T(8,128)S(1)} %get-tuple-element.83.bulk_edges0, f32[1,4,32,128]{3,2,1,0:T(8,128)S(1)} %get-tuple-element.84.bulk_edges1, ...), custom_call_target="tpu_custom_call", output_to_operand_aliasing={{}: (7, {})} | custom-call | bytes 2000000 | tf_op jit(solution)/shard_map/final/pallas_call | solution.py:836
  (16 shorter events, 0.2 us)
Async XLA Ops:
  0.0 3.2 %copy-start = (f32[2,3,8,32,256]{4,3,2,1,0:T(8,128)S(1)}, f32[2,3,8,32,256]{4,3,2,1,0:T(8,128)}, u32[]{:S(2)}) copy-start(f32[2,3,8,32,256]{4,3,2,1,0:T(8,128)} %modes.9) | copy-start | bytes 4718596
  1.4 12.4 %collective-permute-start = (f32[10,32,256]{2,1,0:T(8,128)S(1)}, f32[10,32,256]{2,1,0:T(8,128)S(1)}, u32[]{:S(2)}, u32[]{:S(2)}) collective-permute-start(f32[10,32,256]{2,1,0:T(8,128)S(1)} %get-tuple-element.52), channel_id=1, source_target_pairs={{0,1},{1,0},{2,3},{3,2},{4,5},{5,4},{6,7},{7,6},{8,9},{9,8},{10,11... | collective-permute-start | bytes 983048 | tf_op jit(solution)/shard_map/ppermute | solution.py:868
  2.3 11.5 %collective-permute-start.1 = (f32[10,32,256]{2,1,0:T(8,128)S(1)}, f32[10,32,256]{2,1,0:T(8,128)S(1)}, u32[]{:S(2)}, u32[]{:S(2)}) collective-permute-start(f32[10,32,256]{2,1,0:T(8,128)S(1)} %get-tuple-element.53), channel_id=1, source_target_pairs={{0,16},{1,17},{2,18},{3,19},{4,20},{5,21},{6,22},{7,23},{8,24},{9,... | collective-permute-start | bytes 983048 | tf_op jit(solution)/shard_map/ppermute | solution.py:868
  3.2 8.9 %collective-permute-start.2 = (f32[10,8,256]{2,1,0:T(8,128)S(1)}, f32[10,8,256]{2,1,0:T(8,128)S(1)}, u32[]{:S(2)}, u32[]{:S(2)}) collective-permute-start(f32[10,8,256]{2,1,0:T(8,128)S(1)} %get-tuple-element.54), channel_id=1, source_target_pairs={{0,16},{1,17},{2,4},{3,5},{4,2},{5,3},{6,8},{7,9},{8,6},{9,7},{10,... | collective-permute-start | bytes 245768 | tf_op jit(solution)/shard_map/ppermute | solution.py:868
  6.1 6.1 %collective-permute-start.3 = (f32[10,8,256]{2,1,0:T(8,128)S(1)}, f32[10,8,256]{2,1,0:T(8,128)S(1)}, u32[]{:S(2)}, u32[]{:S(2)}) collective-permute-start(f32[10,8,256]{2,1,0:T(8,128)S(1)} %get-tuple-element.55), channel_id=1, source_target_pairs={{0,2},{1,3},{2,0},{3,1},{4,6},{5,7},{6,4},{7,5},{8,10},{9,11},{10,... | collective-permute-start | bytes 245768 | tf_op jit(solution)/shard_map/ppermute | solution.py:868
  12.2 4.0 %collective-permute-start.4 = (f32[4,8,256]{2,1,0:T(8,128)S(1)}, f32[4,8,256]{2,1,0:T(8,128)S(1)}, u32[]{:S(2)}, u32[]{:S(2)}) collective-permute-start(f32[4,8,256]{2,1,0:T(8,128)S(1)} %get-tuple-element.59), channel_id=1, source_target_pairs={{0,1},{1,0},{2,3},{3,2},{4,5},{5,4},{6,7},{7,6},{8,9},{9,8},{10,11... | collective-permute-start | bytes 98312 | tf_op jit(solution)/shard_map/ppermute | solution.py:868
  13.5 2.7 %collective-permute-start.5 = (f32[4,8,256]{2,1,0:T(8,128)S(1)}, f32[4,8,256]{2,1,0:T(8,128)S(1)}, u32[]{:S(2)}, u32[]{:S(2)}) collective-permute-start(f32[4,8,256]{2,1,0:T(8,128)S(1)} %get-tuple-element.60), channel_id=1, source_target_pairs={{0,16},{1,17},{2,18},{3,19},{4,20},{5,21},{6,22},{7,23},{8,24},{9,... | collective-permute-start | bytes 98312 | tf_op jit(solution)/shard_map/ppermute | solution.py:868
  16.3 4.1 %collective-permute-start.6 = (f32[2,40,128]{2,1,0:T(8,128)S(1)}, f32[2,40,128]{2,1,0:T(8,128)S(1)}, u32[]{:S(2)}, u32[]{:S(2)}) collective-permute-start(f32[2,40,128]{2,1,0:T(8,128)S(1)} %pack_z1.1), channel_id=1, source_target_pairs={{0,1},{1,0},{2,3},{3,2},{4,5},{5,4},{6,7},{7,6},{8,9},{9,8},{10,11... | collective-permute-start | bytes 122888 | tf_op jit(solution)/shard_map/ppermute | solution.py:868
  21.1 16.8 %copy-start.1 = (s32[8,32,256]{2,1,0:T(8,128)S(1)}, s32[8,32,256]{2,1,0:T(8,128)}, u32[]{:S(2)}) copy-start(s32[8,32,256]{2,1,0:T(8,128)} %mask.5) | copy-start | bytes 786436
  21.1 7.2 %collective-permute-start.7 = (f32[4,2,32,256]{3,2,1,0:T(8,128)S(1)}, f32[4,2,32,256]{3,2,1,0:T(8,128)S(1)}, u32[]{:S(2)}, u32[]{:S(2)}) collective-permute-start(f32[4,2,32,256]{3,2,1,0:T(8,128)S(1)} %get-tuple-element.75), channel_id=1, source_target_pairs={{0,1},{1,0},{2,3},{3,2},{4,5},{5,4},{6,7},{7,6},{8,9},{9,8},{10,11... | collective-permute-start | bytes 786440 | tf_op jit(solution)/shard_map/ppermute | solution.py:868
  22.4 5.9 %collective-permute-start.8 = (f32[4,2,32,256]{3,2,1,0:T(8,128)S(1)}, f32[4,2,32,256]{3,2,1,0:T(8,128)S(1)}, u32[]{:S(2)}, u32[]{:S(2)}) collective-permute-start(f32[4,2,32,256]{3,2,1,0:T(8,128)S(1)} %get-tuple-element.76), channel_id=1, source_target_pairs={{0,16},{1,17},{2,18},{3,19},{4,20},{5,21},{6,22},{7,23},{8,24},{9,... | collective-permute-start | bytes 786440 | tf_op jit(solution)/shard_map/ppermute | solution.py:868
  22.4 9.3 %collective-permute-start.10 = (f32[8,8,256]{2,1,0:T(8,128)S(1)}, f32[8,8,256]{2,1,0:T(8,128)S(1)}, u32[]{:S(2)}, u32[]{:S(2)}) collective-permute-start(f32[8,8,256]{2,1,0:T(8,128)S(1)} %get-tuple-element.80), channel_id=1, source_target_pairs={{0,2},{1,3},{2,0},{3,1},{4,6},{5,7},{6,4},{7,5},{8,10},{9,11},{10,... | collective-permute-start | bytes 196616 | tf_op jit(solution)/shard_map/ppermute | solution.py:868
  25.3 8.4 %collective-permute-start.9 = (f32[8,8,256]{2,1,0:T(8,128)S(1)}, f32[8,8,256]{2,1,0:T(8,128)S(1)}, u32[]{:S(2)}, u32[]{:S(2)}) collective-permute-start(f32[8,8,256]{2,1,0:T(8,128)S(1)} %get-tuple-element.79), channel_id=1, source_target_pairs={{0,16},{1,17},{2,4},{3,5},{4,2},{5,3},{6,8},{7,9},{8,6},{9,7},{10,... | collective-permute-start | bytes 196616 | tf_op jit(solution)/shard_map/ppermute | solution.py:868
  33.8 3.9 %collective-permute-start.11 = (f32[3,8,256]{2,1,0:T(8,128)S(1)}, f32[3,8,256]{2,1,0:T(8,128)S(1)}, u32[]{:S(2)}, u32[]{:S(2)}) collective-permute-start(f32[3,8,256]{2,1,0:T(8,128)S(1)} %get-tuple-element.81), channel_id=1, source_target_pairs={{0,1},{1,0},{2,3},{3,2},{4,5},{5,4},{6,7},{7,6},{8,9},{9,8},{10,11... | collective-permute-start | bytes 73736 | tf_op jit(solution)/shard_map/ppermute | solution.py:868
  33.9 3.8 %collective-permute-start.12 = (f32[3,8,256]{2,1,0:T(8,128)S(1)}, f32[3,8,256]{2,1,0:T(8,128)S(1)}, u32[]{:S(2)}, u32[]{:S(2)}) collective-permute-start(f32[3,8,256]{2,1,0:T(8,128)S(1)} %get-tuple-element.82), channel_id=1, source_target_pairs={{0,16},{1,17},{2,18},{3,19},{4,20},{5,21},{6,22},{7,23},{8,24},{9,... | collective-permute-start | bytes 73736 | tf_op jit(solution)/shard_map/ppermute | solution.py:868
  37.8 4.1 %collective-permute-start.13 = (f32[2,40,128]{2,1,0:T(8,128)S(1)}, f32[2,40,128]{2,1,0:T(8,128)S(1)}, u32[]{:S(2)}, u32[]{:S(2)}) collective-permute-start(f32[2,40,128]{2,1,0:T(8,128)S(1)} %pack_z2.1), channel_id=1, source_target_pairs={{0,1},{1,0},{2,3},{3,2},{4,5},{5,4},{6,7},{7,6},{8,9},{9,8},{10,11... | collective-permute-start | bytes 122888 | tf_op jit(solution)/shard_map/ppermute | solution.py:868

commit v11 on v10

--- a/solution.py
+++ b/solution.py
@@ -813,8 +813,8 @@
                 rows = slice(8 * i, 8 * i + 8)
                 value = side[m, x, rows, :] + jnp.where(beside, z_tile(z_state, x, i), 0.0)
                 held[m, x, rows, :] = value * mask[x, rows, edge].astype(F32)
-            if x % 4 == 3:
-                planes = slice(x - 3, x + 1)
+            if x % 2:
+                planes = slice(x - 1, x + 1)
                 copy = pltpu.make_async_copy(
                     held.at[m, planes], out.at[m, planes, :, edge], left.at[len(copies)]
                 )
@@ -951,7 +951,7 @@
     return call(
         final_kernel, "final", [result],
         (solid_mask, z_in, *bulk_edges, *strip_edges, side, out), {7: HBM}, {0: HBM},
-        scratch=[(MODES, CX, CY, LANES), pltpu.SemaphoreType.DMA((4,))], aliases={7: 0},
+        scratch=[(MODES, CX, CY, LANES), pltpu.SemaphoreType.DMA((8,))], aliases={7: 0},
     )
 
 

time: 43.2 us -> 43.2 us (level)
  no operation moved by 1% of the time
where the time goes in v11:
time: 43.2 us; the launch traced here: 43.1 us
  waiting for transfers between devices  15.3 us (35%)
  starting transfers between devices  14.1 us (33%)
  Pallas kernels  13.6 us (31%)
    ppermute x14, waiting for transfers between devices, swap(): return lax.ppermute(x, AXES, pairs)  15.3 us
    ppermute x14, starting transfers between devices, swap(): return lax.ppermute(x, AXES, pairs)  14.1 us
    pallas_call x16, Pallas kernels, call(): pl.pallas_call(kernel, grid=(1,), out_shape=shapes if len(shapes) > 1 els...  13.6 us
  transfers between devices with their start and end apart: 14, of which 8 were waited for; matrix products, arithmetic and copies ran while one was open for 0% of the time, Pallas kernels for 23%

profile of v11, /device:TPU:38, one launch (start us, length us, event | category | flops | bytes accessed | tf_op | source)
XLA Modules:
  0.0 43.1 jit_solution(1032677812462092433)
XLA Ops:
  0.0 1.4 %pack_x1.1 = (f32[8,32,256]{2,1,0:T(8,128)S(1)}, f32[10,32,256]{2,1,0:T(8,128)S(1)}, f32[10,32,256]{2,1,0:T(8,128)S(1)}, f32[2,8,128]{2,1,0:T(8,128)S(1)}) custom-call(f32[8,32,256]{2,1,0:T(8,128)} %design.1, s32[8,32,256]{2,1,0:T(8,128)} %mask.5, f32[2,3,8,32,256]{4,3,2,1,0:T(8,128)} %modes.9, f32[6]{0:T(128)} %eigenvalues.1, s32[6]{0:T(128)} %order.1), custom_call_target="tpu_custom_call" | custom-call | bytes 2000000 | tf_op jit(solution)/shard_map/pack_x1/pallas_call | solution.py:836
  1.4 0.9 %collective-permute-start = (f32[10,32,256]{2,1,0:T(8,128)S(1)}, f32[10,32,256]{2,1,0:T(8,128)S(1)}, u32[]{:S(2)}, u32[]{:S(2)}) collective-permute-start(f32[10,32,256]{2,1,0:T(8,128)S(1)} %get-tuple-element.52), channel_id=1, source_target_pairs={{0,1},{1,0},{2,3},{3,2},{4,5},{5,4},{6,7},{7,6},{8,9},{9,8},{10,11... | collective-permute-start | bytes 983048 | tf_op jit(solution)/shard_map/ppermute | solution.py:868
  2.3 0.9 %collective-permute-start.1 = (f32[10,32,256]{2,1,0:T(8,128)S(1)}, f32[10,32,256]{2,1,0:T(8,128)S(1)}, u32[]{:S(2)}, u32[]{:S(2)}) collective-permute-start(f32[10,32,256]{2,1,0:T(8,128)S(1)} %get-tuple-element.53), channel_id=1, source_target_pairs={{0,16},{1,17},{2,18},{3,19},{4,20},{5,21},{6,22},{7,23},{8,24},{9,... | collective-permute-start | bytes 983048 | tf_op jit(solution)/shard_map/ppermute | solution.py:868
  3.2 2.8 %collective-permute-start.2 = (f32[10,8,256]{2,1,0:T(8,128)S(1)}, f32[10,8,256]{2,1,0:T(8,128)S(1)}, u32[]{:S(2)}, u32[]{:S(2)}) collective-permute-start(f32[10,8,256]{2,1,0:T(8,128)S(1)} %get-tuple-element.54), channel_id=1, source_target_pairs={{0,16},{1,17},{2,4},{3,5},{4,2},{5,3},{6,8},{7,9},{8,6},{9,7},{10,... | collective-permute-start | bytes 245768 | tf_op jit(solution)/shard_map/ppermute | solution.py:868
  6.1 0.3 collective-permute-start.3
  6.4 3.1 %energy.1 = (f32[2,7,32,256]{3,2,1,0:T(8,128)S(1)}, f32[2,7,32,256]{3,2,1,0:T(8,128)S(1)}, f32[2,32,128]{2,1,0:T(8,128)S(1)}) custom-call(f32[2,3,8,32,256]{4,3,2,1,0:T(8,128)S(1)} %copy-done), custom_call_target="tpu_custom_call" | custom-call | flops 40000000 | bytes 2000000 | tf_op jit(solution)/shard_map/energy/pallas_call | solution.py:836
  9.5 2.6 %collective-permute-done.2.y_first = f32[10,8,256]{2,1,0:T(8,128)S(1)} collective-permute-done((f32[10,8,256]{2,1,0:T(8,128)S(1)}, f32[10,8,256]{2,1,0:T(8,128)S(1)}, u32[]{:S(2)}, u32[]{:S(2)}) %collective-permute-start.2) | collective-permute-done | bytes 81952 | tf_op jit(solution)/shard_map/ppermute | solution.py:868
  12.2 1.3 %collective-permute-start.4 = (f32[4,8,256]{2,1,0:T(8,128)S(1)}, f32[4,8,256]{2,1,0:T(8,128)S(1)}, u32[]{:S(2)}, u32[]{:S(2)}) collective-permute-start(f32[4,8,256]{2,1,0:T(8,128)S(1)} %get-tuple-element.59), channel_id=1, source_target_pairs={{0,1},{1,0},{2,3},{3,2},{4,5},{5,4},{6,7},{7,6},{8,9},{9,8},{10,11... | collective-permute-start | bytes 98312 | tf_op jit(solution)/shard_map/ppermute | solution.py:868
  13.5 0.4 collective-permute-start.5
  13.8 1.8 %bulk1.1 = (f32[1,8,32,256]{3,2,1,0:T(8,128)S(1)}, f32[1,4,16,2,1,256]{5,4,3,2,1,0:T(1,128)S(1)}, f32[1,4,32,128]{3,2,1,0:T(8,128)S(1)}, f32[2,32,256]{2,1,0:T(8...) custom-call(f32[8,32,256]{2,1,0:T(8,128)S(1)} %get-tuple-element.50., ...), custom_call_target="tpu_custom_call" | custom-call | flops 30000000 | bytes 2000000 | tf_op jit(solution)/shard_map/bulk1/pallas_call | solution.py:836
  15.7 0.5 %collective-permute-done.4.e_first = f32[4,8,256]{2,1,0:T(8,128)S(1)} collective-permute-done((f32[4,8,256]{2,1,0:T(8,128)S(1)}, f32[4,8,256]{2,1,0:T(8,128)S(1)}, u32[]{:S(2)}, u32[]{:S(2)}) %collective-permute-start.4) | collective-permute-done | bytes 32800 | tf_op jit(solution)/shard_map/ppermute | solution.py:868
  16.2 0.1 pack_z1.1
  16.3 1.3 %collective-permute-start.6 = (f32[2,40,128]{2,1,0:T(8,128)S(1)}, f32[2,40,128]{2,1,0:T(8,128)S(1)}, u32[]{:S(2)}, u32[]{:S(2)}) collective-permute-start(f32[2,40,128]{2,1,0:T(8,128)S(1)} %pack_z1.1), channel_id=1, source_target_pairs={{0,1},{1,0},{2,3},{3,2},{4,5},{5,4},{6,7},{7,6},{8,9},{9,8},{10,11... | collective-permute-start | bytes 122888 | tf_op jit(solution)/shard_map/ppermute | solution.py:868
  17.6 0.8 %strips1.1 = (f32[1,8,16,256]{3,2,1,0:T(8,128)S(1)}, f32[1,4,16,128]{3,2,1,0:T(8,128)S(1)}, f32[2,2,8,256]{3,2,1,0:T(8,128)S(1)}, f32[40,128]{1,0:T(8,128)S(1)}) custom-call(f32[2,3,8,32,256]{4,3,2,1,0:T(8,128)S(1)} %copy-done, f32[2,32,128]{2,1,0:T(8,128)S(1)} %get-tuple-element.57.rims, f32[2,8,128]{2,1,0:T(8,128)S(1)} %get-tuple-element.58.row32, ...), custom_call_target="tpu_custom_call" | custom-call | flops 20000000 | bytes 2000000 | tf_op jit(solution)/shard_map/strips1/pallas_call | solution.py:836
  18.4 2.0 %collective-permute-done.6.z_in = f32[2,40,128]{2,1,0:T(8,128)S(1)} collective-permute-done((f32[2,40,128]{2,1,0:T(8,128)S(1)}, f32[2,40,128]{2,1,0:T(8,128)S(1)}, u32[]{:S(2)}, u32[]{:S(2)}) %collective-permute-start.6) | collective-permute-done | bytes 40992 | tf_op jit(solution)/shard_map/ppermute | solution.py:868
  20.4 0.5 %raw1.1 = (f32[4,2,32,256]{3,2,1,0:T(8,128)S(1)}, f32[3,32,128]{2,1,0:T(8,128)S(1)}) custom-call(f32[2,8,128]{2,1,0:T(8,128)S(1)} %get-tuple-element.49.lams, f32[2,40,128]{2,1,0:T(8,128)S(1)} %collective-permute-done.6.z_in, f32[40,128]{1,0:T(8,128)S(1)} %get-tuple-element.62.packed, f32[1,8,32,256]{3,2,1,0:T(8,128)S(1)} %get-tuple-element.63.bulk, ...), custom_call_target="tpu_custom_call" | custom-call | bytes 2000000 | tf_op jit(solution)/shard_map/raw1/pallas_call | solution.py:836
  20.9 0.2 raw2.1
  21.1 1.3 %collective-permute-start.7 = (f32[4,2,32,256]{3,2,1,0:T(8,128)S(1)}, f32[4,2,32,256]{3,2,1,0:T(8,128)S(1)}, u32[]{:S(2)}, u32[]{:S(2)}) collective-permute-start(f32[4,2,32,256]{3,2,1,0:T(8,128)S(1)} %get-tuple-element.75), channel_id=1, source_target_pairs={{0,1},{1,0},{2,3},{3,2},{4,5},{5,4},{6,7},{7,6},{8,9},{9,8},{10,11... | collective-permute-start | bytes 786440 | tf_op jit(solution)/shard_map/ppermute | solution.py:868
  22.4 2.9 %collective-permute-start.10 = (f32[8,8,256]{2,1,0:T(8,128)S(1)}, f32[8,8,256]{2,1,0:T(8,128)S(1)}, u32[]{:S(2)}, u32[]{:S(2)}) collective-permute-start(f32[8,8,256]{2,1,0:T(8,128)S(1)} %get-tuple-element.80), channel_id=1, source_target_pairs={{0,2},{1,3},{2,0},{3,1},{4,6},{5,7},{6,4},{7,5},{8,10},{9,11},{10,... | collective-permute-start | bytes 196616 | tf_op jit(solution)/shard_map/ppermute | solution.py:868
  25.3 1.7 %collective-permute-start.9 = (f32[8,8,256]{2,1,0:T(8,128)S(1)}, f32[8,8,256]{2,1,0:T(8,128)S(1)}, u32[]{:S(2)}, u32[]{:S(2)}) collective-permute-start(f32[8,8,256]{2,1,0:T(8,128)S(1)} %get-tuple-element.79), channel_id=1, source_target_pairs={{0,16},{1,17},{2,4},{3,5},{4,2},{5,3},{6,8},{7,9},{8,6},{9,7},{10,... | collective-permute-start | bytes 196616 | tf_op jit(solution)/shard_map/ppermute | solution.py:868
  27.1 1.2 %collective-permute-done.7.x_first = f32[4,2,32,256]{3,2,1,0:T(8,128)S(1)} collective-permute-done((f32[4,2,32,256]{3,2,1,0:T(8,128)S(1)}, f32[4,2,32,256]{3,2,1,0:T(8,128)S(1)}, u32[]{:S(2)}, u32[]{:S(2)}) %collective-permute-start.7) | collective-permute-done | bytes 262176 | tf_op jit(solution)/shard_map/ppermute | solution.py:868
  28.3 1.2 %bulk2_0.1 = (f32[1,8,32,256]{3,2,1,0:T(8,128)S(1)}, f32[1,4,16,2,1,256]{5,4,3,2,1,0:T(1,128)S(1)}, f32[1,4,32,128]{3,2,1,0:T(8,128)S(1)}, f32[1,32,128]{2,1,0:T(8,128)S(1)}) custom-call(f32[4,2,32,256]{3,2,1,0:T(8,128)S(1)} %get-tuple-element.72.low, f32[4,2,32,256]{3,2,1,0:T(8,128)S(1)} %get-tuple-element.74.high, ...), custom_call_target="tpu_custom_call" | custom-call | flops 20000000 | bytes 2000000 | tf_op jit(solution)/shard_map/bulk2_0/pallas_call | solution.py:836
  29.5 2.2 %collective-permute-done.10.y_second = f32[8,8,256]{2,1,0:T(8,128)S(1)} collective-permute-done((f32[8,8,256]{2,1,0:T(8,128)S(1)}, f32[8,8,256]{2,1,0:T(8,128)S(1)}, u32[]{:S(2)}, u32[]{:S(2)}) %collective-permute-start.10) | collective-permute-done | bytes 65568 | tf_op jit(solution)/shard_map/ppermute | solution.py:868
  31.7 2.1 %collective-permute-done.9.y_first = f32[8,8,256]{2,1,0:T(8,128)S(1)} collective-permute-done((f32[8,8,256]{2,1,0:T(8,128)S(1)}, f32[8,8,256]{2,1,0:T(8,128)S(1)}, u32[]{:S(2)}, u32[]{:S(2)}) %collective-permute-start.9) | collective-permute-done | bytes 65568 | tf_op jit(solution)/shard_map/ppermute | solution.py:868
  33.8 0.1 collective-permute-start.11
  33.9 0.1 collective-permute-start.12
  34.0 1.2 %bulk2_1.1 = (f32[1,8,32,256]{3,2,1,0:T(8,128)S(1)}, f32[1,4,16,2,1,256]{5,4,3,2,1,0:T(1,128)S(1)}, f32[1,4,32,128]{3,2,1,0:T(8,128)S(1)}, f32[1,32,128]{2,1,0:T(8,128)S(1)}) custom-call(f32[4,2,32,256]{3,2,1,0:T(8,128)S(1)} %get-tuple-element.72.low, f32[4,2,32,256]{3,2,1,0:T(8,128)S(1)} %get-tuple-element.74.high, ...), custom_call_target="tpu_custom_call" | custom-call | flops 20000000 | bytes 2000000 | tf_op jit(solution)/shard_map/bulk2_1/pallas_call | solution.py:836
  35.2 2.5 %collective-permute-done.11.e_first = f32[3,8,256]{2,1,0:T(8,128)S(1)} collective-permute-done((f32[3,8,256]{2,1,0:T(8,128)S(1)}, f32[3,8,256]{2,1,0:T(8,128)S(1)}, u32[]{:S(2)}, u32[]{:S(2)}) %collective-permute-start.11) | collective-permute-done | bytes 24608 | tf_op jit(solution)/shard_map/ppermute | solution.py:868
  37.7 0.1 pack_z2.1
  37.9 1.8 %strips2.1 = (f32[2,8,32,256]{3,2,1,0:T(8,128)}, f32[2,8,32,128]{3,2,1,0:T(8,128)S(1)}, f32[1,4,16,128]{3,2,1,0:T(8,128)S(1)}, f32[1,4,16,128]{3,2,1,0:T(8,128)S(1)}) custom-call(s32[8,32,256]{2,1,0:T(8,128)S(1)} %copy-done.1, f32[8,8,256]{2,1,0:T(8,128)S(1)} %collective-permute-done.9.y_first, f32[8,8,256]{2,1,0:T(8,128)S(1)} %collective-permute-done.10.y_second, ...), custom_call_target="tpu_custom_call" | custom-call | flops 20000000 | bytes 2000000 | tf_op jit(solution)/shard_map/strips2/pallas_call | solution.py:836
  39.7 2.2 %collective-permute-done.13.z_in = f32[2,40,128]{2,1,0:T(8,128)S(1)} collective-permute-done((f32[2,40,128]{2,1,0:T(8,128)S(1)}, f32[2,40,128]{2,1,0:T(8,128)S(1)}, u32[]{:S(2)}, u32[]{:S(2)}) %collective-permute-start.13) | collective-permute-done | bytes 40992 | tf_op jit(solution)/shard_map/ppermute | solution.py:868
  41.9 1.2 %final.1 = f32[2,8,32,256]{3,2,1,0:T(8,128)} custom-call(s32[8,32,256]{2,1,0:T(8,128)S(1)} %copy-done.1, f32[2,40,128]{2,1,0:T(8,128)S(1)} %collective-permute-done.13.z_in, f32[1,4,32,128]{3,2,1,0:T(8,128)S(1)} %get-tuple-element.83.bulk_edges0, f32[1,4,32,128]{3,2,1,0:T(8,128)S(1)} %get-tuple-element.84.bulk_edges1, ...), custom_call_target="tpu_custom_call", output_to_operand_aliasing={{}: (7, {})} | custom-call | bytes 2000000 | tf_op jit(solution)/shard_map/final/pallas_call | solution.py:836
  (16 shorter events, 0.2 us)
Async XLA Ops:
  0.0 3.2 %copy-start = (f32[2,3,8,32,256]{4,3,2,1,0:T(8,128)S(1)}, f32[2,3,8,32,256]{4,3,2,1,0:T(8,128)}, u32[]{:S(2)}) copy-start(f32[2,3,8,32,256]{4,3,2,1,0:T(8,128)} %modes.9) | copy-start | bytes 4718596
  1.4 12.4 %collective-permute-start = (f32[10,32,256]{2,1,0:T(8,128)S(1)}, f32[10,32,256]{2,1,0:T(8,128)S(1)}, u32[]{:S(2)}, u32[]{:S(2)}) collective-permute-start(f32[10,32,256]{2,1,0:T(8,128)S(1)} %get-tuple-element.52), channel_id=1, source_target_pairs={{0,1},{1,0},{2,3},{3,2},{4,5},{5,4},{6,7},{7,6},{8,9},{9,8},{10,11... | collective-permute-start | bytes 983048 | tf_op jit(solution)/shard_map/ppermute | solution.py:868
  2.3 11.5 %collective-permute-start.1 = (f32[10,32,256]{2,1,0:T(8,128)S(1)}, f32[10,32,256]{2,1,0:T(8,128)S(1)}, u32[]{:S(2)}, u32[]{:S(2)}) collective-permute-start(f32[10,32,256]{2,1,0:T(8,128)S(1)} %get-tuple-element.53), channel_id=1, source_target_pairs={{0,16},{1,17},{2,18},{3,19},{4,20},{5,21},{6,22},{7,23},{8,24},{9,... | collective-permute-start | bytes 983048 | tf_op jit(solution)/shard_map/ppermute | solution.py:868
  3.2 8.9 %collective-permute-start.2 = (f32[10,8,256]{2,1,0:T(8,128)S(1)}, f32[10,8,256]{2,1,0:T(8,128)S(1)}, u32[]{:S(2)}, u32[]{:S(2)}) collective-permute-start(f32[10,8,256]{2,1,0:T(8,128)S(1)} %get-tuple-element.54), channel_id=1, source_target_pairs={{0,16},{1,17},{2,4},{3,5},{4,2},{5,3},{6,8},{7,9},{8,6},{9,7},{10,... | collective-permute-start | bytes 245768 | tf_op jit(solution)/shard_map/ppermute | solution.py:868
  6.1 6.1 %collective-permute-start.3 = (f32[10,8,256]{2,1,0:T(8,128)S(1)}, f32[10,8,256]{2,1,0:T(8,128)S(1)}, u32[]{:S(2)}, u32[]{:S(2)}) collective-permute-start(f32[10,8,256]{2,1,0:T(8,128)S(1)} %get-tuple-element.55), channel_id=1, source_target_pairs={{0,2},{1,3},{2,0},{3,1},{4,6},{5,7},{6,4},{7,5},{8,10},{9,11},{10,... | collective-permute-start | bytes 245768 | tf_op jit(solution)/shard_map/ppermute | solution.py:868
  12.2 4.0 %collective-permute-start.4 = (f32[4,8,256]{2,1,0:T(8,128)S(1)}, f32[4,8,256]{2,1,0:T(8,128)S(1)}, u32[]{:S(2)}, u32[]{:S(2)}) collective-permute-start(f32[4,8,256]{2,1,0:T(8,128)S(1)} %get-tuple-element.59), channel_id=1, source_target_pairs={{0,1},{1,0},{2,3},{3,2},{4,5},{5,4},{6,7},{7,6},{8,9},{9,8},{10,11... | collective-permute-start | bytes 98312 | tf_op jit(solution)/shard_map/ppermute | solution.py:868
  13.5 2.7 %collective-permute-start.5 = (f32[4,8,256]{2,1,0:T(8,128)S(1)}, f32[4,8,256]{2,1,0:T(8,128)S(1)}, u32[]{:S(2)}, u32[]{:S(2)}) collective-permute-start(f32[4,8,256]{2,1,0:T(8,128)S(1)} %get-tuple-element.60), channel_id=1, source_target_pairs={{0,16},{1,17},{2,18},{3,19},{4,20},{5,21},{6,22},{7,23},{8,24},{9,... | collective-permute-start | bytes 98312 | tf_op jit(solution)/shard_map/ppermute | solution.py:868
  16.3 4.1 %collective-permute-start.6 = (f32[2,40,128]{2,1,0:T(8,128)S(1)}, f32[2,40,128]{2,1,0:T(8,128)S(1)}, u32[]{:S(2)}, u32[]{:S(2)}) collective-permute-start(f32[2,40,128]{2,1,0:T(8,128)S(1)} %pack_z1.1), channel_id=1, source_target_pairs={{0,1},{1,0},{2,3},{3,2},{4,5},{5,4},{6,7},{7,6},{8,9},{9,8},{10,11... | collective-permute-start | bytes 122888 | tf_op jit(solution)/shard_map/ppermute | solution.py:868
  21.1 16.8 %copy-start.1 = (s32[8,32,256]{2,1,0:T(8,128)S(1)}, s32[8,32,256]{2,1,0:T(8,128)}, u32[]{:S(2)}) copy-start(s32[8,32,256]{2,1,0:T(8,128)} %mask.5) | copy-start | bytes 786436
  21.1 7.2 %collective-permute-start.7 = (f32[4,2,32,256]{3,2,1,0:T(8,128)S(1)}, f32[4,2,32,256]{3,2,1,0:T(8,128)S(1)}, u32[]{:S(2)}, u32[]{:S(2)}) collective-permute-start(f32[4,2,32,256]{3,2,1,0:T(8,128)S(1)} %get-tuple-element.75), channel_id=1, source_target_pairs={{0,1},{1,0},{2,3},{3,2},{4,5},{5,4},{6,7},{7,6},{8,9},{9,8},{10,11... | collective-permute-start | bytes 786440 | tf_op jit(solution)/shard_map/ppermute | solution.py:868
  22.4 5.9 %collective-permute-start.8 = (f32[4,2,32,256]{3,2,1,0:T(8,128)S(1)}, f32[4,2,32,256]{3,2,1,0:T(8,128)S(1)}, u32[]{:S(2)}, u32[]{:S(2)}) collective-permute-start(f32[4,2,32,256]{3,2,1,0:T(8,128)S(1)} %get-tuple-element.76), channel_id=1, source_target_pairs={{0,16},{1,17},{2,18},{3,19},{4,20},{5,21},{6,22},{7,23},{8,24},{9,... | collective-permute-start | bytes 786440 | tf_op jit(solution)/shard_map/ppermute | solution.py:868
  22.4 9.3 %collective-permute-start.10 = (f32[8,8,256]{2,1,0:T(8,128)S(1)}, f32[8,8,256]{2,1,0:T(8,128)S(1)}, u32[]{:S(2)}, u32[]{:S(2)}) collective-permute-start(f32[8,8,256]{2,1,0:T(8,128)S(1)} %get-tuple-element.80), channel_id=1, source_target_pairs={{0,2},{1,3},{2,0},{3,1},{4,6},{5,7},{6,4},{7,5},{8,10},{9,11},{10,... | collective-permute-start | bytes 196616 | tf_op jit(solution)/shard_map/ppermute | solution.py:868
  25.3 8.4 %collective-permute-start.9 = (f32[8,8,256]{2,1,0:T(8,128)S(1)}, f32[8,8,256]{2,1,0:T(8,128)S(1)}, u32[]{:S(2)}, u32[]{:S(2)}) collective-permute-start(f32[8,8,256]{2,1,0:T(8,128)S(1)} %get-tuple-element.79), channel_id=1, source_target_pairs={{0,16},{1,17},{2,4},{3,5},{4,2},{5,3},{6,8},{7,9},{8,6},{9,7},{10,... | collective-permute-start | bytes 196616 | tf_op jit(solution)/shard_map/ppermute | solution.py:868
  33.8 3.9 %collective-permute-start.11 = (f32[3,8,256]{2,1,0:T(8,128)S(1)}, f32[3,8,256]{2,1,0:T(8,128)S(1)}, u32[]{:S(2)}, u32[]{:S(2)}) collective-permute-start(f32[3,8,256]{2,1,0:T(8,128)S(1)} %get-tuple-element.81), channel_id=1, source_target_pairs={{0,1},{1,0},{2,3},{3,2},{4,5},{5,4},{6,7},{7,6},{8,9},{9,8},{10,11... | collective-permute-start | bytes 73736 | tf_op jit(solution)/shard_map/ppermute | solution.py:868
  33.9 3.8 %collective-permute-start.12 = (f32[3,8,256]{2,1,0:T(8,128)S(1)}, f32[3,8,256]{2,1,0:T(8,128)S(1)}, u32[]{:S(2)}, u32[]{:S(2)}) collective-permute-start(f32[3,8,256]{2,1,0:T(8,128)S(1)} %get-tuple-element.82), channel_id=1, source_target_pairs={{0,16},{1,17},{2,18},{3,19},{4,20},{5,21},{6,22},{7,23},{8,24},{9,... | collective-permute-start | bytes 73736 | tf_op jit(solution)/shard_map/ppermute | solution.py:868
  37.8 4.1 %collective-permute-start.13 = (f32[2,40,128]{2,1,0:T(8,128)S(1)}, f32[2,40,128]{2,1,0:T(8,128)S(1)}, u32[]{:S(2)}, u32[]{:S(2)}) collective-permute-start(f32[2,40,128]{2,1,0:T(8,128)S(1)} %pack_z2.1), channel_id=1, source_target_pairs={{0,1},{1,0},{2,3},{3,2},{4,5},{5,4},{6,7},{7,6},{8,9},{9,8},{10,11... | collective-permute-start | bytes 122888 | tf_op jit(solution)/shard_map/ppermute | solution.py:868
